TPU v7x, 32 devices: a whole 2x2x4 slice. The times are simulated.
32 devices in a mesh: grp: 1, row: 32 (over z, y, x, core).
Axes of the slice: x: 2, y: 2, z: 4, core: 2. Of those that a mesh axis runs over, the one named last changes fastest.
Arguments:
- pair: bfloat16 [384, 384, 128], P(('grp', 'row')), may hold values from -6 to 6
- residue_mask: int32 [384], P('grp'), may hold values 0 or 1
- chain_ids: int32 [384], P('grp'), may hold values from 0 to 5, never falling along the last dimension, each value on 1 to 96 neighbouring positions
- ln_in_gain: float32 [2, 128], replicated, may hold values from 0.5 to 1.5
- ln_in_bias: float32 [2, 128], replicated, may hold values from -3 to 3
- chain_embed: float32 [2, 128], replicated, may hold values from -4 to 4
- w_ab: bfloat16 [2, 128, 512], replicated, may hold values from -0.5 to 0.5
- w_gate: bfloat16 [2, 128, 128], replicated, may hold values from -0.5 to 0.5
- ln_mid_gain: float32 [2, 128], replicated, may hold values from 0.5 to 1.5
- ln_mid_bias: float32 [2, 128], replicated, may hold values from -3 to 3
- w_out: bfloat16 [2, 128, 128], replicated, may hold values from -0.5 to 0.5
Outputs:
- updated_pair: bfloat16 [384, 384, 128], P(('grp', 'row'))
Inputs may be any that keep to these rules, and one draw needn't show every extreme that they name: `chain_ids`: never falls along the residues; each chain holds 1 to 96 residues and one holds exactly 96.
All inputs are finite; a program needn't handle non-finite values.
Results may differ from a plain program's by a relative error of at most 0.0055.
Values may be sent and summed in bfloat16 or wider, within the bound.
No kernel may reach another device: no remote copies, remote signals or barrier semaphores. Data moves between devices by JAX's collectives and lax.ppermute only.
A program may use at most 64 MiB of HBM per device.

v0:
```python
import jax
import jax.numpy as jnp
from jax import lax
from jax.sharding import PartitionSpec as P

HC = 128


EPS = 1e-05


def norm_last(values, gain, bias):
    mean = jnp.mean(values, axis=-1, keepdims=True)
    centred = values - mean
    var = jnp.mean(centred * centred, axis=-1, keepdims=True)
    return centred * lax.rsqrt(var + EPS) * gain + bias


def norm_first(values, gain, bias):
    mean = jnp.mean(values, axis=0, keepdims=True)
    centred = values - mean
    var = jnp.mean(centred * centred, axis=0, keepdims=True)
    return centred * lax.rsqrt(var + EPS) * gain[:, None, None] + bias[:, None, None]


def products(left, right, incoming):
    if incoming:
        tri = jnp.einsum("xcki,xckj->xcij", left, right, preferred_element_type=jnp.float32)
    else:
        tri = jnp.einsum("xcik,xcjk->xcij", left, right, preferred_element_type=jnp.float32)
    return tri.astype(jnp.bfloat16)


def one_update(state, pair_mask, same_rows, weights, incoming):
    g_in, b_in, embed, w_ab, w_gate, g_mid, b_mid, w_out = weights
    devices = lax.axis_size("row")
    rows = state.shape[0]
    width = state.shape[1]
    normed = norm_last(state.astype(jnp.float32), g_in, b_in) + same_rows[..., None] * embed
    normed = normed.astype(jnp.bfloat16)
    proj = jnp.einsum("rkc,ce->erk", normed, w_ab, preferred_element_type=jnp.float32)
    left = (jax.nn.sigmoid(proj[:HC]) * proj[HC : 2 * HC] * pair_mask[None]).astype(jnp.bfloat16)
    right = (jax.nn.sigmoid(proj[2 * HC : 3 * HC]) * proj[3 * HC :] * pair_mask[None]).astype(
        jnp.bfloat16
    )
    left = left.reshape(devices, HC // devices, rows, width)
    right = right.reshape(devices, HC // devices, rows, width)
    left_cols, right_cols = (
        lax.all_to_all(left, "row", split_axis=0, concat_axis=2, tiled=True),
        lax.all_to_all(right, "row", split_axis=0, concat_axis=2, tiled=True),
    )
    tri = products(left_cols, right_cols, incoming)
    tri_rows = lax.all_to_all(tri, "row", split_axis=2, concat_axis=0, tiled=True)
    tri_rows = tri_rows.reshape(HC, rows, width)
    tri_norm = norm_first(tri_rows.astype(jnp.float32), g_mid, b_mid).astype(jnp.bfloat16)
    branch = jnp.einsum("erj,ed->rjd", tri_norm, w_out, preferred_element_type=jnp.float32)
    gate = jax.nn.sigmoid(
        jnp.einsum("rjc,cd->rjd", normed, w_gate, preferred_element_type=jnp.float32)
    )
    return (state.astype(jnp.float32) + gate * branch).astype(jnp.bfloat16)


def local(
    pair,
    residue_mask,
    chain_ids,
    ln_in_gain,
    ln_in_bias,
    chain_embed,
    w_ab,
    w_gate,
    ln_mid_gain,
    ln_mid_bias,
    w_out,
):
    rows = pair.shape[0]
    start = lax.axis_index("row") * rows
    mask_f = residue_mask.astype(jnp.float32)
    mask_rows = lax.dynamic_slice_in_dim(mask_f, start, rows)
    chain_rows = lax.dynamic_slice_in_dim(chain_ids, start, rows)
    pair_mask = mask_rows[:, None] * mask_f[None, :]
    same_rows = (chain_rows[:, None] == chain_ids[None, :]).astype(jnp.float32)
    state = pair
    for layer in range(2):
        weights = (
            ln_in_gain[layer],
            ln_in_bias[layer],
            chain_embed[layer],
            w_ab[layer],
            w_gate[layer],
            ln_mid_gain[layer],
            ln_mid_bias[layer],
            w_out[layer],
        )
        state = one_update(state, pair_mask, same_rows, weights, layer == 1)
    return state


def solution(mesh):
    in_specs = (
        P(("grp", "row"), None, None),
        P("grp"),
        P("grp"),
        P(),
        P(),
        P(),
        P(),
        P(),
        P(),
        P(),
        P(),
    )
    out_specs = P(("grp", "row"), None, None)
    return jax.shard_map(local, mesh=mesh, in_specs=in_specs, out_specs=out_specs, check_vma=False)
```

profile of v0, /device:TPU:0, one launch (start us, length us, event | category | flops | bytes accessed | tf_op | source)
XLA Modules:
  0.0 243.0 jit_solution(3530721668817418181)
XLA Ops:
  0.0 1.8 copy.85
  2.0 0.3 fusion.9
  2.8 0.6 slice_bitcast_fusion
  3.4 1.6 convolution_bitcast_fusion.1
  5.0 1.5 fusion.32
  6.4 1.4 copy.89
  7.8 2.5 %reshape.171 = bf16[32,4,12,384]{3,1,0,2:T(4,128)(2,1)S(1)} reshape(bf16[128,12,384]{2,0,1:T(8,128)(2,1)} %copy.89) | data formatting | bytes 2359296 | tf_op jit(solution)/shard_map/reshape | solution.py:46
  10.3 1.4 copy.90
  11.7 7.4 %all-to-all-start = ((bf16[32,4,12,384]{3,1,2,0:T(4,128)(2,1)}), bf16[32,4,12,384]{3,1,2,0:T(4,128)(2,1)}, u32[]{:S(2)}, u32[]{:S(2)}) async-start(bf16[32,4,12,384]{3,1,2,0:T(4,128)(2,1)} %copy.90), calls=%async_computation | async-start | bytes 2359296 | tf_op jit(solution)/shard_map/all_to_all | solution.py:49
  19.2 0.7 copy.91
  19.9 1.2 reshape.173
  21.1 1.7 copy.92
  22.8 25.5 %all-to-all-done = bf16[32,4,12,384]{3,1,2,0:T(4,128)(2,1)} async-done(((bf16[32,4,12,384]{3,1,2,0:T(4,128)(2,1)}), bf16[32,4,12,384]{3,1,2,0:T(4,128)(2,1)}, u32[]{:S(2)}, u32[]{:S(2)}) %all-to-all-start) | async-done | bytes 1179680 | tf_op jit(solution)/shard_map/all_to_all | solution.py:49
  48.2 34.1 %all_to_all.78 = bf16[32,4,12,384]{3,1,2,0:T(4,128)(2,1)S(1)} all-to-all(bf16[32,4,12,384]{3,1,2,0:T(4,128)(2,1)S(1)} %copy.92), channel_id=1, replica_groups=mesh['grp'=1,'row'=32] {'row'}, dimensions={0} | all-to-all | bytes 2359296 | tf_op jit(solution)/shard_map/all_to_all | solution.py:50
  82.3 2.2 fusion.52
  84.6 1.9 copy.95
  86.5 2.8 %all-to-all-start.2 = ((bf16[1,4,384,384]{3,1,0,2:T(4,128)(2,1)}), bf16[1,4,384,384]{3,1,0,2:T(4,128)(2,1)S(1)}, u32[]{:S(2)}, u32[]{:S(2)}) async-start(bf16[1,4,384,384]{3,1,0,2:T(4,128)(2,1)} %copy.95), calls=%async_computation.2 | async-start | bytes 2359296 | tf_op jit(solution)/shard_map/all_to_all | solution.py:53
  89.4 0.6 slice_reduce_fusion
  90.3 2.3 fusion.63
  92.6 25.7 %all-to-all-done.2 = bf16[1,4,384,384]{3,1,0,2:T(4,128)(2,1)S(1)} async-done(((bf16[1,4,384,384]{3,1,0,2:T(4,128)(2,1)}), bf16[1,4,384,384]{3,1,0,2:T(4,128)(2,1)S(1)}, u32[]{:S(2)}, u32[]{:S(2)}) %all-to-all-start.2) | async-done | bytes 1179680 | tf_op jit(solution)/shard_map/all_to_all | solution.py:53
  118.3 0.5 fusion.45
  118.8 0.8 fusion.48
  119.6 1.0 fusion.51
  120.6 0.5 copy.96
  121.5 2.7 %convert_reduce_fusion = (f32[12,384]{1,0:T(8,128)S(1)}, bf16[12,384,128]{1,2,0:T(8,128)(2,1)S(1)}) fusion(bf16[128,12,384]{2,0,1:T(8,128)(2,1)S(1)} %convert_element_type.102, bf16[2,128,128]{2,1,0:T(8,128)(2,1)} %param.21, f32[12,384,128]{1,2,0:T(8,128)} %fusion.63, bf16[12,384,128]{1,2,0:T(8,128)(2,1)S(1)} %copy.85), kind=kOutput, calls=%fused_computation.2 | convolution fusion | flops 156298752 | bytes 5949440 | tf_op jit(solution)/shard_map/erj,ed->rjd/dot_general | solution.py:56
  124.2 0.3 fusion.4
  124.7 1.6 convolution_bitcast_fusion
  126.2 1.5 fusion.22
  127.7 1.4 copy.101
  129.1 2.5 %reshape.175 = bf16[32,4,12,384]{3,1,0,2:T(4,128)(2,1)S(1)} reshape(bf16[128,12,384]{2,0,1:T(8,128)(2,1)} %copy.101) | data formatting | bytes 2359296 | tf_op jit(solution)/shard_map/reshape | solution.py:46
  131.6 1.4 copy.102
  133.0 3.6 %all-to-all-start.3 = ((bf16[32,4,12,384]{3,1,2,0:T(4,128)(2,1)}), bf16[32,4,12,384]{3,1,2,0:T(4,128)(2,1)}, u32[]{:S(2)}, u32[]{:S(2)}) async-start(bf16[32,4,12,384]{3,1,2,0:T(4,128)(2,1)} %copy.102), calls=%async_computation.3 | async-start | bytes 2359296 | tf_op jit(solution)/shard_map/all_to_all | solution.py:49
  136.7 0.7 copy.103
  137.4 1.2 reshape.177
  138.6 1.7 copy.104
  140.3 25.5 %all-to-all-done.3 = bf16[32,4,12,384]{3,1,2,0:T(4,128)(2,1)} async-done(((bf16[32,4,12,384]{3,1,2,0:T(4,128)(2,1)}), bf16[32,4,12,384]{3,1,2,0:T(4,128)(2,1)}, u32[]{:S(2)}, u32[]{:S(2)}) %all-to-all-start.3) | async-done | bytes 1179680 | tf_op jit(solution)/shard_map/all_to_all | solution.py:49
  165.7 34.1 %all_to_all.79 = bf16[32,4,12,384]{3,1,2,0:T(4,128)(2,1)S(1)} all-to-all(bf16[32,4,12,384]{3,1,2,0:T(4,128)(2,1)S(1)} %copy.104), channel_id=1, replica_groups=mesh['grp'=1,'row'=32] {'row'}, dimensions={0} | all-to-all | bytes 2359296 | tf_op jit(solution)/shard_map/all_to_all | solution.py:50
  199.9 2.2 fusion.53
  202.2 1.9 copy.107
  204.1 2.9 %all-to-all-start.5 = ((bf16[1,4,384,384]{3,1,0,2:T(4,128)(2,1)}), bf16[1,4,384,384]{3,1,0,2:T(4,128)(2,1)S(1)}, u32[]{:S(2)}, u32[]{:S(2)}) async-start(bf16[1,4,384,384]{3,1,0,2:T(4,128)(2,1)} %copy.107), calls=%async_computation.5 | async-start | bytes 2359296 | tf_op jit(solution)/shard_map/all_to_all | solution.py:53
  207.2 2.3 fusion.66
  209.5 26.3 %all-to-all-done.5 = bf16[1,4,384,384]{3,1,0,2:T(4,128)(2,1)S(1)} async-done(((bf16[1,4,384,384]{3,1,0,2:T(4,128)(2,1)}), bf16[1,4,384,384]{3,1,0,2:T(4,128)(2,1)S(1)}, u32[]{:S(2)}, u32[]{:S(2)}) %all-to-all-start.5) | async-done | bytes 1179680 | tf_op jit(solution)/shard_map/all_to_all | solution.py:53
  235.8 0.5 fusion.37
  236.3 0.8 fusion.40
  237.1 1.0 fusion.43
  238.1 0.5 copy.108
  239.0 2.6 %fusion.15 = bf16[12,384,128]{1,2,0:T(8,128)(2,1)S(1)} fusion(bf16[12,384,128]{1,2,0:T(8,128)(2,1)S(1)} %get-tuple-element.20, f32[12,384,128]{1,2,0:T(8,128)} %fusion.66, bf16[128,12,384]{2,0,1:T(8,128)(2,1)S(1)} %convert_element_type.114, bf16[2,128,128]{2,1,0:T(8,128)(2,1)} %param.21), kind=kOutput, calls=%fused_computation.23 | convolution fusion | flops 155123712 | bytes 5931008 | tf_op jit(solution)/shard_map/erj,ed->rjd/dot_general | solution.py:56
  241.6 1.4 copy.111
  (79 shorter events, 1.7 us)
Async XLA Ops:
  0.0 2.4 copy-start.23
  0.0 2.6 %copy-start.24 = (f32[2,128]{1,0:T(2,128)S(1)}, f32[2,128]{1,0:T(2,128)}, u32[]{:S(2)}) copy-start(f32[2,128]{1,0:T(2,128)} %param.14) | copy-start | bytes 3076
  0.0 2.6 %copy-start.20 = (s32[384]{0:T(512)S(1)}, s32[384]{0:T(512)}, u32[]{:S(2)}) copy-start(s32[384]{0:T(512)} %param.12) | copy-start | bytes 4612
  0.0 2.8 %copy-start.25 = (f32[2,128]{1,0:T(2,128)S(1)}, f32[2,128]{1,0:T(2,128)}, u32[]{:S(2)}) copy-start(f32[2,128]{1,0:T(2,128)} %param.16) | copy-start | bytes 3076
  0.0 2.8 %copy-start.26 = (f32[2,128]{1,0:T(2,128)S(1)}, f32[2,128]{1,0:T(2,128)}, u32[]{:S(2)}) copy-start(f32[2,128]{1,0:T(2,128)} %param.15) | copy-start | bytes 3076
  0.0 3.4 %copy-start.6 = (bf16[2,128,512]{2,1,0:T(8,128)(2,1)S(1)}, bf16[2,128,512]{2,1,0:T(8,128)(2,1)}, u32[]{:S(2)}) copy-start(bf16[2,128,512]{2,1,0:T(8,128)(2,1)} %param.17) | copy-start | bytes 786436
  2.0 1.3 copy-start.4
  2.4 1.0 copy-start.8
  2.6 2.4 copy-start
  2.8 2.2 copy-start.10
  11.7 36.5 %all-to-all-start = ((bf16[32,4,12,384]{3,1,2,0:T(4,128)(2,1)}), bf16[32,4,12,384]{3,1,2,0:T(4,128)(2,1)}, u32[]{:S(2)}, u32[]{:S(2)}) async-start(bf16[32,4,12,384]{3,1,2,0:T(4,128)(2,1)} %copy.90), calls=%async_computation | async-start | bytes 2359296 | tf_op jit(solution)/shard_map/all_to_all | solution.py:49
  84.6 4.8 %copy-start.27 = (f32[2,128]{1,0:T(2,128)S(1)}, f32[2,128]{1,0:T(2,128)}, u32[]{:S(2)}) copy-start(f32[2,128]{1,0:T(2,128)} %param.20) | copy-start | bytes 3076
  84.6 4.8 %copy-start.28 = (f32[2,128]{1,0:T(2,128)S(1)}, f32[2,128]{1,0:T(2,128)}, u32[]{:S(2)}) copy-start(f32[2,128]{1,0:T(2,128)} %param.19) | copy-start | bytes 3076
  84.6 5.6 %copy-start.1 = (f32[12,384]{1,0:T(8,128)S(1)}, f32[12,384]{1,0:T(8,128)}, u32[]{:S(2)}) copy-start(f32[12,384]{1,0:T(8,128)} %copy-done) | copy-start | bytes 55300
  84.6 5.6 %copy-start.5 = (f32[12,384]{1,0:T(8,128)S(1)}, f32[12,384]{1,0:T(8,128)}, u32[]{:S(2)}) copy-start(f32[12,384]{1,0:T(8,128)} %copy-done.4) | copy-start | bytes 55300
  84.6 5.6 %copy-start.9 = (f32[12,384]{1,0:T(8,128)S(1)}, f32[12,384]{1,0:T(8,128)}, u32[]{:S(2)}) copy-start(f32[12,384]{1,0:T(8,128)} %copy-done.8) | copy-start | bytes 55300
  84.6 5.6 %copy-start.16 = (bf16[2,128,128]{2,1,0:T(8,128)(2,1)S(1)}, bf16[2,128,128]{2,1,0:T(8,128)(2,1)}, u32[]{:S(2)}) copy-start(bf16[2,128,128]{2,1,0:T(8,128)(2,1)} %param.18) | copy-start | bytes 196612
  86.5 31.7 %all-to-all-start.2 = ((bf16[1,4,384,384]{3,1,0,2:T(4,128)(2,1)}), bf16[1,4,384,384]{3,1,0,2:T(4,128)(2,1)S(1)}, u32[]{:S(2)}, u32[]{:S(2)}) async-start(bf16[1,4,384,384]{3,1,0,2:T(4,128)(2,1)} %copy.95), calls=%async_computation.2 | async-start | bytes 2359296 | tf_op jit(solution)/shard_map/all_to_all | solution.py:53
  121.4 3.2 %copy-start.2 = (f32[12,384]{1,0:T(8,128)S(1)}, f32[12,384]{1,0:T(8,128)}, u32[]{:S(2)}) copy-start(f32[12,384]{1,0:T(8,128)} %copy-done) | copy-start | bytes 55300
  121.4 3.2 %copy-start.7 = (bf16[2,128,512]{2,1,0:T(8,128)(2,1)S(1)}, bf16[2,128,512]{2,1,0:T(8,128)(2,1)}, u32[]{:S(2)}) copy-start(bf16[2,128,512]{2,1,0:T(8,128)(2,1)} %param.17) | copy-start | bytes 786436
  121.5 3.2 %copy-start.18 = (f32[128]{0:T(128)S(1)}, f32[128]{0:T(128)}, u32[]{:S(2)}) copy-start(f32[128]{0:T(128)} %get-tuple-element.17) | copy-start | bytes 1540
  121.5 3.2 %copy-start.19 = (f32[128]{0:T(128)S(1)}, f32[128]{0:T(128)}, u32[]{:S(2)}) copy-start(f32[128]{0:T(128)} %get-tuple-element.22) | copy-start | bytes 1540
  124.2 2.0 copy-start.12
  124.6 1.6 copy-start.14
  124.6 1.6 copy-start.11
  133.0 32.7 %all-to-all-start.3 = ((bf16[32,4,12,384]{3,1,2,0:T(4,128)(2,1)}), bf16[32,4,12,384]{3,1,2,0:T(4,128)(2,1)}, u32[]{:S(2)}, u32[]{:S(2)}) async-start(bf16[32,4,12,384]{3,1,2,0:T(4,128)(2,1)} %copy.102), calls=%async_computation.3 | async-start | bytes 2359296 | tf_op jit(solution)/shard_map/all_to_all | solution.py:49
  202.1 4.9 %copy-start.22 = (f32[128]{0:T(128)S(1)}, f32[128]{0:T(128)}, u32[]{:S(2)}) copy-start(f32[128]{0:T(128)} %get-tuple-element.7) | copy-start | bytes 1540
  202.1 5.0 %copy-start.21 = (f32[128]{0:T(128)S(1)}, f32[128]{0:T(128)}, u32[]{:S(2)}) copy-start(f32[128]{0:T(128)} %get-tuple-element.24) | copy-start | bytes 1540
  202.1 5.1 %copy-start.3 = (f32[12,384]{1,0:T(8,128)S(1)}, f32[12,384]{1,0:T(8,128)}, u32[]{:S(2)}) copy-start(f32[12,384]{1,0:T(8,128)} %copy-done) | copy-start | bytes 55300
  202.1 5.1 %copy-start.13 = (f32[12,384]{1,0:T(8,128)S(1)}, f32[12,384]{1,0:T(8,128)}, u32[]{:S(2)}) copy-start(f32[12,384]{1,0:T(8,128)} %copy-done.12) | copy-start | bytes 55300
  202.1 5.1 %copy-start.15 = (f32[12,384]{1,0:T(8,128)S(1)}, f32[12,384]{1,0:T(8,128)}, u32[]{:S(2)}) copy-start(f32[12,384]{1,0:T(8,128)} %copy-done.14) | copy-start | bytes 55300
  202.1 5.1 %copy-start.17 = (bf16[2,128,128]{2,1,0:T(8,128)(2,1)S(1)}, bf16[2,128,128]{2,1,0:T(8,128)(2,1)}, u32[]{:S(2)}) copy-start(bf16[2,128,128]{2,1,0:T(8,128)(2,1)} %param.18) | copy-start | bytes 196612
  204.1 31.7 %all-to-all-start.5 = ((bf16[1,4,384,384]{3,1,0,2:T(4,128)(2,1)}), bf16[1,4,384,384]{3,1,0,2:T(4,128)(2,1)S(1)}, u32[]{:S(2)}, u32[]{:S(2)}) async-start(bf16[1,4,384,384]{3,1,0,2:T(4,128)(2,1)} %copy.107), calls=%async_computation.5 | async-start | bytes 2359296 | tf_op jit(solution)/shard_map/all_to_all | solution.py:53
where the time goes:
time: 244 us; the launch traced here: 243 us
  waiting for transfers between devices  103 us (42%)
  blocking collectives  68.2 us (28%)
  local copies, waits for them, and re-layouts  28.4 us (12%)
  matrix products  17.5 us (7%)
  starting transfers between devices  16.8 us (7%)
  other arithmetic  8.61 us (4%)
    all_to_all x2, blocking collectives, one_update(): lax.all_to_all(right, 'row', split_axis=0, concat_axis=2, tiled=True)  68.2 us
    all_to_all x2, waiting for transfers between devices, one_update(): lax.all_to_all(tri, 'row', split_axis=2, concat_axis=0, tiled=True)  51.9 us
    all_to_all x2, waiting for transfers between devices, one_update(): lax.all_to_all(left, 'row', split_axis=0, concat_axis=2, tiled=True)  50.9 us
    all_to_all x2, starting transfers between devices, one_update(): lax.all_to_all(left, 'row', split_axis=0, concat_axis=2, tiled=True)  11 us
    reshape x4, local copies, waits for them, and re-layouts, one_update(): left = left.reshape(devices, HC // devices, rows, width)  7.81 us
    all_to_all x2, starting transfers between devices, one_update(): lax.all_to_all(tri, 'row', split_axis=2, concat_axis=0, tiled=True)  5.71 us
    reshape x4, local copies, waits for them, and re-layouts, one_update(): right = right.reshape(devices, HC // devices, rows, width)  5.68 us
    dot_general x2, matrix products, one_update(): jnp.einsum('erj,ed->rjd', tri_norm, w_out, preferred_element_type=jnp.flo...  5.3 us
  transfers between devices with their start and end apart: 4, of which 4 were waited for; matrix products, arithmetic and copies ran while one was open for 5% of the time, Pallas kernels for 0%

commit v1 on v0

v1 whole, which is shorter than its diff:
```python
import functools

import jax
import jax.numpy as jnp
from jax import lax
from jax.experimental import pallas as pl
from jax.experimental.pallas import tpu as pltpu
from jax.sharding import PartitionSpec as P

C = 128
HC = 128
EPS = 1e-05
F32 = jnp.float32
BF16 = jnp.bfloat16
VMEM_LIMIT = 48 * 1024 * 1024

WHOLE = pl.BlockSpec(memory_space=pltpu.VMEM)
SCALARS = pl.BlockSpec(memory_space=pltpu.SMEM)


def blocks(width):
    return [(j, slice(j * 128, (j + 1) * 128)) for j in range(width // 128)]


def column(vector_ref, layer, width):
    square = jnp.broadcast_to(vector_ref[layer : layer + 1, :], (C, C)).T
    return jnp.concatenate([square] * (width // C), axis=1)


def norm_channels(values, gain, bias):
    mean = jnp.sum(values, axis=0, keepdims=True) * (1.0 / C)
    centred = values - mean
    var = jnp.sum(centred * centred, axis=0, keepdims=True) * (1.0 / C)
    return centred * lax.rsqrt(var + EPS) * gain + bias


def norm_input(x_t, chain_row, chain_ref, gain, bias, embed):
    same = (chain_ref[...] == chain_row).astype(F32)
    return (norm_channels(x_t, gain, bias) + same * embed).astype(BF16)


def project_row(r, normed, mask_row, mask_ref, w_t, slabs):
    rows = slabs.shape[1] // (2 * HC)
    proj = jnp.dot(w_t[...], normed, preferred_element_type=F32)
    mask = mask_ref[...] * mask_row
    for side in range(2):
        p = proj[2 * side * HC : (2 * side + 2) * HC]
        value = jax.nn.sigmoid(p[:HC]) * p[HC:] * mask
        for j, columns in blocks(value.shape[1]):
            slabs[j, pl.ds(side * HC * rows + r, HC, stride=rows), :] = value[:, columns]


def write_slabs(slabs, out):
    devices, depth, width = out.shape
    half = depth // 2
    for side in range(2):
        for d in range(devices):
            start = (side * devices + d) * half
            for j, columns in blocks(width):
                out[d, side * half : (side + 1) * half, columns] = slabs[j, start : start + half, :].astype(BF16)


def first_kernel(
    mask_rows, chain_rows, x, mask, chain, gain, bias, embed, w_ab, out, x_t, w_t, g, b, e, slabs
):
    rows, width, _ = x.shape
    w_t[...] = w_ab[0].astype(F32).T.astype(BF16)
    g[...] = column(gain, 0, width)
    b[...] = column(bias, 0, width)
    e[...] = column(embed, 0, width)
    eye = (
        lax.broadcasted_iota(jnp.int32, (C, C), 0) == lax.broadcasted_iota(jnp.int32, (C, C), 1)
    ).astype(BF16)

    def step(r, carry):
        turned = lax.dot_general(
            eye, x[r], (((1,), (1,)), ((), ())), preferred_element_type=F32
        )
        x_t[r] = turned.astype(BF16)
        normed = norm_input(turned, chain_rows[r], chain, g[...], b[...], e[...])
        project_row(r, normed, mask_rows[r], mask, w_t, slabs)
        return carry

    lax.fori_loop(0, rows, step, 0)
    write_slabs(slabs, out)


def gate_kernel(layer, chain_rows, x_t, chain, gain, bias, embed, w_gate, out, w_t, g, b, e):
    rows, _, width = x_t.shape
    w_t[...] = w_gate[layer].astype(F32).T.astype(BF16)
    g[...] = column(gain, layer, width)
    b[...] = column(bias, layer, width)
    e[...] = column(embed, layer, width)

    def step(r, carry):
        normed = norm_input(x_t[r].astype(F32), chain_rows[r], chain, g[...], b[...], e[...])
        out[r] = jax.nn.sigmoid(jnp.dot(w_t[...], normed, preferred_element_type=F32))
        return carry

    lax.fori_loop(0, rows, step, 0)


def products_kernel(incoming, rows, recv, out, wide, square, turned):
    devices, depth, width = recv.shape
    channels = depth // (2 * rows)
    widen(recv, wide)

    def gathered(side, c, where):
        for j, _ in blocks(width):
            for r in range(rows):
                start = (side * channels + c) * rows + r
                where[j, pl.ds(r, devices, stride=rows), :] = wide[j, pl.ds(start, devices, stride=depth), :]
        return jnp.concatenate([where[j].astype(BF16) for j, _ in blocks(width)], axis=1)

    for c in range(channels):
        left = gathered(0, c, square)
        right = gathered(1, c, square)
        dims = (((0,), (0,)), ((), ())) if incoming else (((1,), (1,)), ((), ()))
        product = lax.dot_general(left, right, dims, preferred_element_type=F32)
        for j, columns in blocks(width):
            square[j] = product[:, columns]
            for r in range(rows):
                turned[j, pl.ds(c * rows + r, devices, stride=channels * rows), :] = square[
                    j, pl.ds(r, devices, stride=rows), :
                ]
    for s in range(devices):
        for j, columns in blocks(width):
            out[s, :, columns] = turned[j, s * channels * rows : (s + 1) * channels * rows, :].astype(BF16)


def finish_row(r, tri, gate, x_t, g, b, w_t):
    rows = tri.shape[1] // HC
    values = jnp.concatenate([tri[j, pl.ds(r, HC, stride=rows), :] for j in range(tri.shape[0])], axis=1)
    normed = norm_channels(values, g[...], b[...]).astype(BF16)
    branch = jnp.dot(w_t[...], normed, preferred_element_type=F32)
    return (x_t[r].astype(F32) + gate[r] * branch).astype(BF16)


def widen(recv, wide):
    devices, depth, width = recv.shape
    for s in range(devices):
        for j, columns in blocks(width):
            wide[j, s * depth : (s + 1) * depth, :] = recv[s, :, columns].astype(F32)


def middle_kernel(
    mask_rows, chain_rows, recv, gate, x_t, mask, chain, gain, bias, embed, w_ab, mid_gain, mid_bias, w_out,
    out, new_t, w_t, g, b, e, slabs, w_out_t, mg, mb, tri,
):
    rows, _, width = x_t.shape
    w_t[...] = w_ab[1].astype(F32).T.astype(BF16)
    g[...] = column(gain, 1, width)
    b[...] = column(bias, 1, width)
    e[...] = column(embed, 1, width)
    w_out_t[...] = w_out[0].astype(F32).T.astype(BF16)
    mg[...] = column(mid_gain, 0, width)
    mb[...] = column(mid_bias, 0, width)
    widen(recv, tri)

    def step(r, carry):
        state = finish_row(r, tri, gate, x_t, mg, mb, w_out_t)
        new_t[r] = state
        normed = norm_input(state.astype(F32), chain_rows[r], chain, g[...], b[...], e[...])
        project_row(r, normed, mask_rows[r], mask, w_t, slabs)
        return carry

    lax.fori_loop(0, rows, step, 0)
    write_slabs(slabs, out)


def last_kernel(recv, gate, x_t, mid_gain, mid_bias, w_out, out, w_out_t, mg, mb, tri):
    rows, _, width = x_t.shape
    w_out_t[...] = w_out[1].astype(F32).T.astype(BF16)
    mg[...] = column(mid_gain, 1, width)
    mb[...] = column(mid_bias, 1, width)
    widen(recv, tri)

    def step(r, carry):
        out[r] = finish_row(r, tri, gate, x_t, mg, mb, w_out_t).astype(F32).T.astype(BF16)
        return carry

    lax.fori_loop(0, rows, step, 0)


def call(kernel, outs, scratch, scalars, arrays, flops):
    size = sum(a.size * a.dtype.itemsize for a in list(arrays) + list(outs))
    return pl.pallas_call(
        kernel,
        out_shape=outs,
        in_specs=[SCALARS] * len(scalars) + [WHOLE] * len(arrays),
        out_specs=[WHOLE] * len(outs),
        scratch_shapes=[pltpu.VMEM(shape, dtype) for shape, dtype in scratch],
        compiler_params=pltpu.CompilerParams(vmem_limit_bytes=VMEM_LIMIT),
        cost_estimate=pl.CostEstimate(flops=flops, bytes_accessed=size, transcendentals=0),
    )(*scalars, *arrays)


def local(
    pair, residue_mask, chain_ids, ln_in_gain, ln_in_bias, chain_embed, w_ab, w_gate, ln_mid_gain, ln_mid_bias, w_out
):
    rows, width, _ = pair.shape
    devices = lax.axis_size("row")
    channels = HC // devices
    start = lax.axis_index("row") * rows
    mask = residue_mask.astype(F32)
    mask_rows = lax.dynamic_slice_in_dim(mask, start, rows)
    chain_rows = lax.dynamic_slice_in_dim(chain_ids, start, rows)
    mask = mask[None, :]
    chain = chain_ids[None, :]

    sent = jax.ShapeDtypeStruct((devices, 2 * channels * rows, width), BF16)
    back = jax.ShapeDtypeStruct((devices, channels * rows, width), BF16)
    state_t = jax.ShapeDtypeStruct((rows, C, width), BF16)
    gate_t = jax.ShapeDtypeStruct((rows, C, width), F32)
    vector = ((C, width), F32)
    square = ((C, C), BF16)
    head = [((4 * HC, C), BF16), vector, vector, vector, ((width // 128, 2 * HC * rows, 128), F32)]
    tail = [square, vector, vector, ((width // 128, HC * rows, 128), F32)]
    pairs = rows * width
    norms = (ln_in_gain, ln_in_bias, chain_embed)
    mids = (ln_mid_gain, ln_mid_bias, w_out)

    def exchange(slabs):
        return lax.all_to_all(slabs, "row", split_axis=0, concat_axis=0, tiled=True)

    def gates(layer, state):
        return call(
            functools.partial(gate_kernel, layer), [gate_t], [square, vector, vector, vector], (chain_rows,),
            (state, chain, *norms, w_gate), 2 * pairs * C * C,
        )[0]

    def products(recv, incoming):
        return call(
            functools.partial(products_kernel, incoming, rows), [back],
            [((width // 128, depth, 128), F32) for depth in (2 * HC * rows, width, HC * rows)], (),
            (recv,), 2 * channels * width**3,
        )[0]

    slabs, x_t = call(
        first_kernel, [sent, state_t], head, (mask_rows, chain_rows), (pair, mask, chain, *norms, w_ab),
        2 * pairs * C * 5 * HC,
    )
    recv = exchange(slabs)
    gate = gates(0, x_t)
    tri = exchange(products(recv, False))
    slabs, x_t = call(
        middle_kernel, [sent, state_t], head + tail, (mask_rows, chain_rows),
        (tri, gate, x_t, mask, chain, *norms, w_ab, *mids), 2 * pairs * C * 5 * HC,
    )
    recv = exchange(slabs)
    gate = gates(1, x_t)
    tri = exchange(products(recv, True))
    return call(
        last_kernel, [jax.ShapeDtypeStruct(pair.shape, BF16)], tail, (), (tri, gate, x_t, *mids), 2 * pairs * C * C
    )[0]


def solution(mesh):
    in_specs = (P(("grp", "row"), None, None), P("grp"), P("grp")) + (P(),) * 8
    out_specs = P(("grp", "row"), None, None)
    return jax.shard_map(local, mesh=mesh, in_specs=in_specs, out_specs=out_specs, check_vma=False)
```

time: 244 us -> 237 us (0.971)
  waiting for transfers between devices: 103 us -> 47.5 us
  blocking collectives: 68.2 us -> 122 us
  Pallas kernels: 0 us -> 43.4 us
  matrix products: 17.5 us -> 0 us
  local copies, waits for them, and re-layouts: 28.4 us -> 16 us
  starting transfers between devices: 16.8 us -> 6.19 us
  other arithmetic: 8.61 us -> 0.68 us
    all_to_all x4 -> x2, waiting for transfers between devices: 103 us -> 47.5 us  [exchange(): return lax.all_to_all(slabs, 'row', split_axis=0, concat_axis=0, tiled=True)]
    all_to_all x2, blocking collectives: 68.2 us -> 122 us  [exchange(): return lax.all_to_all(slabs, 'row', split_axis=0, concat_axis=0, tiled=True)]
    pallas_call x0 -> x7, Pallas kernels: none -> 43.4 us  [call(): pl.pallas_call(kernel, out_shape=outs, in_specs=[SCALARS] * len(scalars)...]
    dot_general x8 -> x0, matrix products: 17.5 us -> none  [the longest x2 5.3 us: one_update(): jnp.einsum('erj,ed->rjd', tri_norm, w_out, preferred_element_type=jnp.flo...]
    reshape x8 -> x0, local copies, waits for them, and re-layouts: 13.5 us -> none  [the longest x4 7.81 us: one_update(): left = left.reshape(devices, HC // devices, rows, width)]
    unnamed x59 -> x50, local copies, waits for them, and re-layouts: 1.91 us -> 14.5 us
    convert_element_type x11 -> x0, local copies, waits for them, and re-layouts: 11.2 us -> none  [the longest x2 3.85 us: products(): return tri.astype(jnp.bfloat16)]
    all_to_all x4 -> x2, starting transfers between devices: 16.8 us -> 6.19 us  [exchange(): return lax.all_to_all(slabs, 'row', split_axis=0, concat_axis=0, tiled=True)]
  transfers between devices with their start and end apart: 4 -> 2, of which waited for: 4 -> 2; matrix products, arithmetic and copies ran while one was open for 5% -> 0% of each run, Pallas kernels for 0% -> 3%
where the time goes in v1:
time: 237 us; the launch traced here: 236 us
  blocking collectives  122 us (51%)
  waiting for transfers between devices  47.5 us (20%)
  Pallas kernels  43.4 us (18%)
  local copies, waits for them, and re-layouts  16 us (7%)
  starting transfers between devices  6.19 us (3%)
    all_to_all x2, blocking collectives, exchange(): return lax.all_to_all(slabs, 'row', split_axis=0, concat_axis=0, tiled=True)  122 us
    all_to_all x2, waiting for transfers between devices, exchange(): return lax.all_to_all(slabs, 'row', split_axis=0, concat_axis=0, tiled=True)  47.5 us
    pallas_call x7, Pallas kernels, call(): pl.pallas_call(kernel, out_shape=outs, in_specs=[SCALARS] * len(scalars)...  43.4 us
    unnamed x50, local copies, waits for them, and re-layouts  14.5 us
    all_to_all x2, starting transfers between devices, exchange(): return lax.all_to_all(slabs, 'row', split_axis=0, concat_axis=0, tiled=True)  6.19 us
  transfers between devices with their start and end apart: 2, of which 2 were waited for; matrix products, arithmetic and copies ran while one was open for 0% of the time, Pallas kernels for 3%

profile of v1, /device:TPU:0, one launch (start us, length us, event | category | flops | bytes accessed | tf_op | source)
XLA Modules:
  0.0 235.9 jit_solution(14079885198579701088)
XLA Ops:
  0.0 0.7 broadcast_in_dim.7.chain
  0.7 0.8 dynamic_slice.7.chain_rows
  1.4 0.0 copy-start.15
  1.4 0.7 convert_element_type.3
  2.1 0.1 dynamic_slice.6.mask_rows
  2.2 0.0 copy-start.22
  2.2 0.0 copy-start.5
  2.2 0.9 copy-done.5
  3.2 0.0 copy-start.7
  3.2 0.7 copy-done.7
  3.8 0.7 copy-done.9
  4.5 0.7 copy-done.11
  5.2 1.3 copy-done.24
  6.5 7.1 %shard_map.109 = (bf16[32,96,384]{2,1,0:T(8,128)(2,1)S(1)}, bf16[12,128,384]{2,1,0:T(8,128)(2,1)S(1)}) custom-call(f32[12]{0:T(128)S(1)} %dynamic_slice.6.mask_rows, s32[12]{0:T(128)S(1)} %dynamic_slice.7.chain_rows, bf16[12,384,128]{2,1,0:T(8,128)(2,1)S(1)} %copy-done.24, f32[1,384]{1,0:T(1,128)S(1)} %broadcast_in_dim.6.mask, ...), custom_call_target="tpu_custom_call" | custom-call | flops 754974720 | bytes 4986880 | tf_op jit(solution)/shard_map/pallas_call | solution.py:187
  13.6 0.0 copy-done.22
  13.6 0.0 copy-done.13
  13.6 62.8 %all_to_all.20.recv = bf16[32,96,384]{2,1,0:T(8,128)(2,1)S(1)} all-to-all(bf16[32,96,384]{2,1,0:T(8,128)(2,1)S(1)} %get-tuple-element.9), channel_id=1, replica_groups=mesh['grp'=1,'row'=32] {'row'}, dimensions={0} | all-to-all | bytes 4718592 | tf_op jit(solution)/shard_map/all_to_all | solution.py:224
  76.4 5.8 %shard_map.110 = bf16[32,48,384]{2,1,0:T(8,128)(2,1)} custom-call(bf16[32,96,384]{2,1,0:T(8,128)(2,1)S(1)} %all_to_all.20.recv), custom_call_target="tpu_custom_call" | custom-call | flops 452984832 | bytes 3538944 | tf_op jit(solution)/shard_map/pallas_call | solution.py:187
  82.2 2.8 %all-to-all-start.1 = ((bf16[32,48,384]{2,1,0:T(8,128)(2,1)}), bf16[32,48,384]{2,1,0:T(8,128)(2,1)S(1)}, u32[]{:S(2)}, u32[]{:S(2)}) async-start(bf16[32,48,384]{2,1,0:T(8,128)(2,1)} %shard_map.110), calls=%async_computation.1 | async-start | bytes 2359296 | tf_op jit(solution)/shard_map/all_to_all | solution.py:224
  85.0 0.0 copy-done.15
  85.0 0.0 copy-done.1
  85.0 0.0 copy-done.8
  85.0 0.0 copy-done.10
  85.0 0.0 copy-done.12
  85.1 3.8 %shard_map.111.gate = f32[12,128,384]{2,1,0:T(8,128)S(1)} custom-call(s32[12]{0:T(128)S(1)} %dynamic_slice.7.chain_rows, bf16[12,128,384]{2,1,0:T(8,128)(2,1)S(1)} %get-tuple-element.10.x_t, s32[1,384]{1,0:T(1,128)S(1)} %broadcast_in_dim.7.chain, f32[2,128]{1,0:T(2,128)S(1)} %copy-done.8, f32[2,128]{1,0:T(2,128)S(1)} %copy-done.10, f32[2,128]{1,0:T(2,128)S(1)} %copy-done.12, ...), custom_call_target="tpu_custom_call" | custom-call | flops 150994944 | bytes 3609088 | tf_op jit(solution)/shard_map/pallas_call | solution.py:187
  88.9 0.0 copy-start
  88.9 1.4 copy-done
  90.3 23.7 %all-to-all-done.1.recv = bf16[32,48,384]{2,1,0:T(8,128)(2,1)S(1)} async-done(((bf16[32,48,384]{2,1,0:T(8,128)(2,1)}), bf16[32,48,384]{2,1,0:T(8,128)(2,1)S(1)}, u32[]{:S(2)}, u32[]{:S(2)}) %all-to-all-start.1) | async-done | bytes 1179680 | tf_op jit(solution)/shard_map/all_to_all | solution.py:224
  114.1 0.8 copy-done.3
  114.9 0.9 copy-done.6
  115.8 0.7 copy-done.14
  116.5 0.6 copy-done.16
  117.2 0.7 copy-done.18
  117.8 0.7 copy-done.20
  118.5 0.7 copy-done.23
  119.2 10.6 %shard_map.112 = (bf16[32,96,384]{2,1,0:T(8,128)(2,1)}, bf16[12,128,384]{2,1,0:T(8,128)(2,1)S(1)}) custom-call(f32[12]{0:T(128)S(1)} %copy-done.23, s32[12]{0:T(128)S(1)} %copy-done.16, bf16[32,48,384]{2,1,0:T(8,128)(2,1)S(1)} %all-to-all-done.1.recv, f32[12,128,384]{2,1,0:T(8,128)} %copy-done, bf16[12,128,384]{2,1,0:T(8,128)(2,1)S(1)} %get-tuple-element.10.x_t, ...), custom_call_target="tpu_custom_call" | custom-call | flops 754974720 | bytes 8593408 | tf_op jit(solution)/shard_map/pallas_call | solution.py:187
  129.8 59.3 %all_to_all.21.recv = bf16[32,96,384]{2,1,0:T(8,128)(2,1)S(1)} all-to-all(bf16[32,96,384]{2,1,0:T(8,128)(2,1)} %get-tuple-element.11), channel_id=1, replica_groups=mesh['grp'=1,'row'=32] {'row'}, dimensions={0} | all-to-all | bytes 4718592 | tf_op jit(solution)/shard_map/all_to_all | solution.py:224
  189.1 5.8 %shard_map.113 = bf16[32,48,384]{2,1,0:T(8,128)(2,1)} custom-call(bf16[32,96,384]{2,1,0:T(8,128)(2,1)S(1)} %all_to_all.21.recv), custom_call_target="tpu_custom_call" | custom-call | flops 452984832 | bytes 3538944 | tf_op jit(solution)/shard_map/pallas_call | solution.py:187
  194.9 3.4 %all-to-all-start.3 = ((bf16[32,48,384]{2,1,0:T(8,128)(2,1)}), bf16[32,48,384]{2,1,0:T(8,128)(2,1)}, u32[]{:S(2)}, u32[]{:S(2)}) async-start(bf16[32,48,384]{2,1,0:T(8,128)(2,1)} %shard_map.113), calls=%async_computation.3 | async-start | bytes 2359296 | tf_op jit(solution)/shard_map/all_to_all | solution.py:224
  198.2 0.0 copy-start.2
  198.3 0.8 copy-done.2
  199.1 0.6 copy-done.17
  199.7 3.8 %shard_map.114.gate = f32[12,128,384]{2,1,0:T(8,128)S(1)} custom-call(s32[12]{0:T(128)S(1)} %copy-done.17, bf16[12,128,384]{2,1,0:T(8,128)(2,1)S(1)} %get-tuple-element.12.x_t, s32[1,384]{1,0:T(1,128)S(1)} %broadcast_in_dim.7.chain, f32[2,128]{1,0:T(2,128)S(1)} %copy-done.8, f32[2,128]{1,0:T(2,128)S(1)} %copy-done.10, f32[2,128]{1,0:T(2,128)S(1)} %copy-done.12, ...), custom_call_target="tpu_custom_call" | custom-call | flops 150994944 | bytes 3609088 | tf_op jit(solution)/shard_map/pallas_call | solution.py:187
  203.5 23.7 %all-to-all-done.3.recv = bf16[32,48,384]{2,1,0:T(8,128)(2,1)} async-done(((bf16[32,48,384]{2,1,0:T(8,128)(2,1)}), bf16[32,48,384]{2,1,0:T(8,128)(2,1)}, u32[]{:S(2)}, u32[]{:S(2)}) %all-to-all-start.3) | async-done | bytes 1179680 | tf_op jit(solution)/shard_map/all_to_all | solution.py:224
  227.3 0.8 copy-done.4
  228.1 0.7 copy-done.19
  228.8 0.7 copy-done.21
  229.5 6.4 %shard_map.115 = bf16[12,384,128]{2,1,0:T(8,128)(2,1)} custom-call(bf16[32,48,384]{2,1,0:T(8,128)(2,1)} %all-to-all-done.3.recv, f32[12,128,384]{2,1,0:T(8,128)S(1)} %shard_map.114.gate, bf16[12,128,384]{2,1,0:T(8,128)(2,1)S(1)} %get-tuple-element.12.x_t, f32[2,128]{1,0:T(2,128)S(1)} %copy-done.19, f32[2,128]{1,0:T(2,128)S(1)} %copy-done.21, ...), custom_call_target="tpu_custom_call" | custom-call | flops 150994944 | bytes 5965824 | tf_op jit(solution)/shard_map/pallas_call | solution.py:187
  (20 shorter events, 0.0 us)
Async XLA Ops:
  1.4 83.6 %copy-start.15 = (s32[12]{0:T(128)}, s32[12]{0:T(128)S(1)}, u32[]{:S(2)}) copy-start(s32[12]{0:T(128)S(1)} %dynamic_slice.7.chain_rows) | copy-start | bytes 148
  2.2 11.4 %copy-start.22 = (f32[12]{0:T(128)}, f32[12]{0:T(128)S(1)}, u32[]{:S(2)}) copy-start(f32[12]{0:T(128)S(1)} %dynamic_slice.6.mask_rows) | copy-start | bytes 148
  2.2 0.9 copy-start.5
  3.2 0.7 copy-start.7
  3.8 0.7 copy-start.9
  4.5 0.7 copy-start.11
  5.2 1.3 copy-start.24
  6.5 7.1 %copy-start.13 = (f32[1,384]{1,0:T(1,128)}, f32[1,384]{1,0:T(1,128)S(1)}, u32[]{:S(2)}) copy-start(f32[1,384]{1,0:T(1,128)S(1)} %broadcast_in_dim.6.mask) | copy-start | bytes 4612
  82.2 2.8 %copy-start.1 = (bf16[2,128,128]{2,1,0:T(8,128)(2,1)S(1)}, bf16[2,128,128]{2,1,0:T(8,128)(2,1)}, u32[]{:S(2)}) copy-start(bf16[2,128,128]{2,1,0:T(8,128)(2,1)} %w_gate.3) | copy-start | bytes 196612
  82.2 2.8 %copy-start.8 = (f32[2,128]{1,0:T(2,128)S(1)}, f32[2,128]{1,0:T(2,128)}, u32[]{:S(2)}) copy-start(f32[2,128]{1,0:T(2,128)} %gain.7) | copy-start | bytes 3076
  82.2 2.9 %copy-start.10 = (f32[2,128]{1,0:T(2,128)S(1)}, f32[2,128]{1,0:T(2,128)}, u32[]{:S(2)}) copy-start(f32[2,128]{1,0:T(2,128)} %bias.7) | copy-start | bytes 3076
  82.2 2.9 %copy-start.12 = (f32[2,128]{1,0:T(2,128)S(1)}, f32[2,128]{1,0:T(2,128)}, u32[]{:S(2)}) copy-start(f32[2,128]{1,0:T(2,128)} %embed.7) | copy-start | bytes 3076
  82.2 31.9 %all-to-all-start.1 = ((bf16[32,48,384]{2,1,0:T(8,128)(2,1)}), bf16[32,48,384]{2,1,0:T(8,128)(2,1)S(1)}, u32[]{:S(2)}, u32[]{:S(2)}) async-start(bf16[32,48,384]{2,1,0:T(8,128)(2,1)} %shard_map.110), calls=%async_computation.1 | async-start | bytes 2359296 | tf_op jit(solution)/shard_map/all_to_all | solution.py:224
  88.9 1.4 copy-start
  114.1 0.8 copy-start.3
  114.9 0.9 copy-start.6
  115.8 0.7 copy-start.14
  116.5 0.6 copy-start.16
  117.2 0.7 copy-start.18
  117.8 0.7 copy-start.20
  118.5 0.7 copy-start.23
  194.9 32.4 %all-to-all-start.3 = ((bf16[32,48,384]{2,1,0:T(8,128)(2,1)}), bf16[32,48,384]{2,1,0:T(8,128)(2,1)}, u32[]{:S(2)}, u32[]{:S(2)}) async-start(bf16[32,48,384]{2,1,0:T(8,128)(2,1)} %shard_map.113), calls=%async_computation.3 | async-start | bytes 2359296 | tf_op jit(solution)/shard_map/all_to_all | solution.py:224
  198.2 0.8 copy-start.2
  199.1 0.6 copy-start.17
  227.3 0.8 copy-start.4
  228.1 0.7 copy-start.19
  228.8 0.7 copy-start.21

commit v2 on v1

v2 whole, which is shorter than its diff:
```python
import functools

import jax
import jax.numpy as jnp
from jax import lax
from jax.experimental import pallas as pl
from jax.experimental.pallas import tpu as pltpu
from jax.sharding import PartitionSpec as P

C = 128
HC = 128
EPS = 1e-05
F32 = jnp.float32
BF16 = jnp.bfloat16
VMEM_LIMIT = 32 * 1024 * 1024
GROUP = 2

WHOLE = pl.BlockSpec(memory_space=pltpu.VMEM)
SCALARS = pl.BlockSpec(memory_space=pltpu.SMEM)
ANYWHERE = pl.BlockSpec(memory_space=pl.ANY)


def blocks(width):
    return [(j, slice(j * 128, (j + 1) * 128)) for j in range(width // 128)]


def column(vector_ref, layer):
    return jnp.broadcast_to(vector_ref[layer : layer + 1, :], (C, C)).T


def turn(ref):
    return ref[...].astype(F32).T.astype(BF16)


def norm_channels(values, gain, bias):
    mean = jnp.sum(values, axis=0, keepdims=True) * (1.0 / C)
    centred = values - mean
    var = jnp.sum(centred * centred, axis=0, keepdims=True) * (1.0 / C)
    return centred * lax.rsqrt(var + EPS) * gain + bias


def norm_input(values, same, g, b, e):
    return (norm_channels(values, g[...], b[...]) + same * e[...]).astype(BF16)


def same_chain(chain_ids, chain, place, columns):
    return (chain[:, columns] == chain_ids[place]).astype(F32)


def project(first, normed, masks, mask, w_t, slabs):
    rows = slabs.shape[1] // (2 * HC)
    width = slabs.shape[0] * 128
    proj = jnp.dot(w_t[...], normed, preferred_element_type=F32)
    for k, mask_row in enumerate(masks):
        for side in range(2):
            for j, columns in blocks(width):
                p = proj[2 * side * HC : (2 * side + 2) * HC, k * width + j * 128 : k * width + (j + 1) * 128]
                value = jax.nn.sigmoid(p[:HC]) * p[HC:] * (mask[:, columns] * mask_row)
                slabs[j, pl.ds(side * HC * rows + first + k, HC, stride=rows), :] = value


def write_slabs(slabs, out):
    devices, depth, width = out.shape
    half = depth // 2
    for side in range(2):
        for d in range(devices):
            start = (side * devices + d) * half
            for j, columns in blocks(width):
                out[d, side * half : (side + 1) * half, columns] = slabs[j, start : start + half, :].astype(BF16)


def widen(recv, wide):
    devices, depth, width = recv.shape
    for s in range(devices):
        for j, columns in blocks(width):
            wide[j, s * depth : (s + 1) * depth, :] = recv[s, :, columns].astype(F32)


def fetch(pairs, sems):
    copies = [pltpu.make_async_copy(src, dst, sems.at[i]) for i, (src, dst) in enumerate(pairs)]
    for copy in copies:
        copy.start()
    return copies


def groups(rows):
    return [range(i, min(i + GROUP, rows)) for i in range(0, rows, GROUP)]


def overlapped(rows, prepare, consume):
    todo = groups(rows)
    ready = prepare(todo[0])
    for i, group in enumerate(todo):
        current = ready
        if i + 1 < len(todo):
            ready = prepare(todo[i + 1])
        consume(group, current)


def first_kernel(
    residue_mask, chain_ids, marks, x_in, gain, bias, embed, w_ab, out, x_t,
    x, w, vectors, ids, w_t, g, b, e, slabs, sems, x_sems,
):
    rows, width, _ = x.shape
    start = lax.axis_index("row") * rows
    smalls = fetch(
        [(gain, vectors.at[0]), (bias, vectors.at[1]), (embed, vectors.at[2]), (marks, ids), (w_ab.at[0], w)], sems
    )
    larges = fetch([(x_in.at[pl.ds(r[0], len(r))], x.at[pl.ds(r[0], len(r))]) for r in groups(rows)], x_sems)
    for copy in smalls:
        copy.wait()
    w_t[...] = turn(w)
    g[...] = column(vectors.at[0], 0)
    b[...] = column(vectors.at[1], 0)
    e[...] = column(vectors.at[2], 0)
    mask = ids[0:1, :].astype(F32)
    chain = ids[1:2, :]

    def prepare(group):
        larges[group[0] // GROUP].wait()
        parts = []
        for r in group:
            for _, columns in blocks(width):
                values = x[r, columns, :].astype(F32).T
                x_t[r, :, columns] = values.astype(BF16)
                parts.append(norm_input(values, same_chain(chain_ids, chain, start + r, columns), g, b, e))
        return jnp.concatenate(parts, axis=1)

    def consume(group, normed):
        project(group[0], normed, [residue_mask[start + r].astype(F32) for r in group], mask, w_t, slabs)

    overlapped(rows, prepare, consume)
    write_slabs(slabs, out)


def gate_kernel(layer, chain_ids, marks, x_t, gain, bias, embed, w_gate, out, w, vectors, ids, w_t, g, b, e, sems):
    rows, _, width = x_t.shape
    start = lax.axis_index("row") * rows
    smalls = fetch(
        [(gain, vectors.at[0]), (bias, vectors.at[1]), (embed, vectors.at[2]), (marks, ids), (w_gate.at[layer], w)],
        sems,
    )
    for copy in smalls:
        copy.wait()
    w_t[...] = turn(w)
    g[...] = column(vectors.at[0], layer)
    b[...] = column(vectors.at[1], layer)
    e[...] = column(vectors.at[2], layer)
    chain = ids[1:2, :]

    def prepare(group):
        return jnp.concatenate(
            [
                norm_input(x_t[r, :, columns].astype(F32), same_chain(chain_ids, chain, start + r, columns), g, b, e)
                for r in group
                for _, columns in blocks(width)
            ],
            axis=1,
        )

    def consume(group, normed):
        gates = jax.nn.sigmoid(jnp.dot(w_t[...], normed, preferred_element_type=F32))
        for k, r in enumerate(group):
            out[r] = gates[:, k * width : (k + 1) * width]

    overlapped(rows, prepare, consume)


def products_kernel(incoming, rows, recv, out, wide, natural, turned):
    devices, depth, width = recv.shape
    channels = depth // (2 * rows)
    widen(recv, wide)

    def rows_of(side, c, r, j):
        return wide[j, pl.ds((side * channels + c) * rows + r, devices, stride=depth), :]

    def by_row(side, c):
        return jnp.concatenate(
            [
                jnp.concatenate([rows_of(side, c, r, j).astype(BF16) for r in range(rows)], axis=0)
                for j, _ in blocks(width)
            ],
            axis=1,
        )

    def put(c, r, j, values):
        turned[j, pl.ds(c * rows + r, devices, stride=channels * rows), :] = values

    for c in range(channels):
        left = by_row(0, c)
        if incoming:
            right = by_row(1, c)
            product = lax.dot_general(left, right, (((0,), (0,)), ((), ())), preferred_element_type=F32)
            for j, columns in blocks(width):
                natural[c, j] = product[:, columns]
                for r in range(rows):
                    put(c, r, j, natural[c, j, pl.ds(r, devices, stride=rows), :])
        else:
            for j, _ in blocks(width):
                for r in range(rows):
                    natural[c, j, pl.ds(r, devices, stride=rows), :] = rows_of(1, c, r, j)
            right = jnp.concatenate([natural[c, j].astype(BF16) for j, _ in blocks(width)], axis=1)
            product = lax.dot_general(left, right, (((1,), (1,)), ((), ())), preferred_element_type=F32)
            for j, columns in blocks(width):
                for r in range(rows):
                    put(c, r, j, product[r * devices : (r + 1) * devices, columns])
    for s in range(devices):
        for j, columns in blocks(width):
            out[s, :, columns] = turned[j, s * channels * rows : (s + 1) * channels * rows, :].astype(BF16)


def finish(group, width, tri, gate, x_t, g, b, w_t):
    rows = tri.shape[1] // HC
    normed = jnp.concatenate(
        [
            norm_channels(tri[j, pl.ds(r, HC, stride=rows), :], g[...], b[...]).astype(BF16)
            for r in group
            for j, _ in blocks(width)
        ],
        axis=1,
    )
    branch = jnp.dot(w_t[...], normed, preferred_element_type=F32)
    return {
        (r, j): (
            x_t[r, :, columns].astype(F32)
            + gate[r, :, columns] * branch[:, k * width + j * 128 : k * width + (j + 1) * 128]
        ).astype(BF16)
        for k, r in enumerate(group)
        for j, columns in blocks(width)
    }


def middle_kernel(
    residue_mask, chain_ids, recv, gate, x_t, marks, gain, bias, embed, w_ab, mid_gain, mid_bias, w_out, out, new_t,
    w, vectors, ids, w_t, g, b, e, slabs, w_mid, w_out_t, mg, mb, tri, sems,
):
    rows, _, width = x_t.shape
    start = lax.axis_index("row") * rows
    smalls = fetch(
        [
            (gain, vectors.at[0]), (bias, vectors.at[1]), (embed, vectors.at[2]), (marks, ids), (w_ab.at[1], w),
            (mid_gain, vectors.at[3]), (mid_bias, vectors.at[4]), (w_out.at[0], w_mid),
        ],
        sems,
    )
    widen(recv, tri)
    for copy in smalls:
        copy.wait()
    w_t[...] = turn(w)
    g[...] = column(vectors.at[0], 1)
    b[...] = column(vectors.at[1], 1)
    e[...] = column(vectors.at[2], 1)
    w_out_t[...] = turn(w_mid)
    mg[...] = column(vectors.at[3], 0)
    mb[...] = column(vectors.at[4], 0)
    mask = ids[0:1, :].astype(F32)
    chain = ids[1:2, :]

    def prepare(group):
        states = finish(group, width, tri, gate, x_t, mg, mb, w_out_t)
        parts = []
        for r in group:
            for j, columns in blocks(width):
                new_t[r, :, columns] = states[r, j]
                same = same_chain(chain_ids, chain, start + r, columns)
                parts.append(norm_input(states[r, j].astype(F32), same, g, b, e))
        return jnp.concatenate(parts, axis=1)

    def consume(group, normed):
        project(group[0], normed, [residue_mask[start + r].astype(F32) for r in group], mask, w_t, slabs)

    overlapped(rows, prepare, consume)
    write_slabs(slabs, out)


def last_kernel(recv, gate, x_t, mid_gain, mid_bias, w_out, out, vectors, w_mid, w_out_t, mg, mb, tri, sems):
    rows, _, width = x_t.shape
    smalls = fetch([(mid_gain, vectors.at[0]), (mid_bias, vectors.at[1]), (w_out.at[1], w_mid)], sems)
    widen(recv, tri)
    for copy in smalls:
        copy.wait()
    w_out_t[...] = turn(w_mid)
    mg[...] = column(vectors.at[0], 1)
    mb[...] = column(vectors.at[1], 1)
    for group in groups(rows):
        for (r, j), state in finish(group, width, tri, gate, x_t, mg, mb, w_out_t).items():
            out[r, j * 128 : (j + 1) * 128, :] = state.astype(F32).T.astype(BF16)


def call(kernel, outs, scratch, scalars, arrays, anywhere, flops):
    size = sum(a.size * a.dtype.itemsize for a in list(arrays) + list(outs))
    return pl.pallas_call(
        kernel,
        out_shape=outs,
        in_specs=[SCALARS] * len(scalars) + [WHOLE] * len(arrays) + [ANYWHERE] * len(anywhere),
        out_specs=[WHOLE] * len(outs),
        scratch_shapes=scratch,
        compiler_params=pltpu.CompilerParams(vmem_limit_bytes=VMEM_LIMIT),
        cost_estimate=pl.CostEstimate(flops=flops, bytes_accessed=size, transcendentals=0),
    )(*scalars, *arrays, *anywhere)


def local(
    pair, residue_mask, chain_ids, ln_in_gain, ln_in_bias, chain_embed, w_ab, w_gate, ln_mid_gain, ln_mid_bias, w_out
):
    rows, width, _ = pair.shape
    devices = lax.axis_size("row")
    channels = HC // devices
    cols = width // 128
    marks = jnp.stack([residue_mask, chain_ids])

    sent = jax.ShapeDtypeStruct((devices, 2 * channels * rows, width), BF16)
    back = jax.ShapeDtypeStruct((devices, channels * rows, width), BF16)
    state_t = jax.ShapeDtypeStruct((rows, C, width), BF16)
    gate_t = jax.ShapeDtypeStruct((rows, C, width), F32)
    vector = pltpu.VMEM((C, 128), F32)
    square = pltpu.VMEM((C, C), BF16)
    ids = pltpu.VMEM((2, width), jnp.int32)

    def vectors(n):
        return pltpu.VMEM((n, 2, C), F32)

    head = [
        pltpu.VMEM((4 * HC, C), BF16), vector, vector, vector, pltpu.VMEM((cols, 2 * HC * rows, 128), F32),
    ]
    w_raw = pltpu.VMEM((C, 4 * HC), BF16)
    tri_wide = pltpu.VMEM((cols, HC * rows, 128), F32)
    pairs = rows * width
    norms = (ln_in_gain, ln_in_bias, chain_embed)
    mids = (ln_mid_gain, ln_mid_bias, w_out)

    def sems(n):
        return pltpu.SemaphoreType.DMA((n,))

    def exchange(slabs):
        return lax.all_to_all(slabs, "row", split_axis=0, concat_axis=0, tiled=True)

    def gates(layer, state):
        def kernel(chain_ids, x_t, marks, *rest):
            gate_kernel(layer, chain_ids, marks, x_t, *rest)

        return call(
            kernel, [gate_t], [square, vectors(3), ids, square, vector, vector, vector, sems(5)], (chain_ids,),
            (state,), (marks, *norms, w_gate), 2 * pairs * C * C,
        )[0]

    def products(recv, incoming):
        return call(
            functools.partial(products_kernel, incoming, rows), [back],
            [
                pltpu.VMEM((cols, 2 * HC * rows, 128), F32),
                pltpu.VMEM((channels, cols, width, 128), F32),
                pltpu.VMEM((cols, HC * rows, 128), F32),
            ],
            (), (recv,), (), 2 * channels * width**3,
        )[0]

    slabs, x_t = call(
        first_kernel, [sent, state_t],
        [pltpu.VMEM(pair.shape, BF16), w_raw, vectors(3), ids, *head, sems(5), sems(len(groups(rows)))],
        (residue_mask, chain_ids), (), (marks, pair, *norms, w_ab), 2 * pairs * C * 5 * HC,
    )
    recv = exchange(slabs)
    gate = gates(0, x_t)
    tri = exchange(products(recv, False))
    slabs, x_t = call(
        middle_kernel, [sent, state_t],
        [w_raw, vectors(5), ids, *head, square, square, vector, vector, tri_wide, sems(8)],
        (residue_mask, chain_ids), (tri, gate, x_t), (marks, *norms, w_ab, *mids), 2 * pairs * C * 5 * HC,
    )
    recv = exchange(slabs)
    gate = gates(1, x_t)
    tri = exchange(products(recv, True))
    return call(
        last_kernel, [jax.ShapeDtypeStruct(pair.shape, BF16)],
        [vectors(2), square, square, vector, vector, tri_wide, sems(3)], (), (tri, gate, x_t), mids,
        2 * pairs * C * C,
    )[0]


def solution(mesh):
    in_specs = (P(("grp", "row"), None, None), P("grp"), P("grp")) + (P(),) * 8
    out_specs = P(("grp", "row"), None, None)
    return jax.shard_map(local, mesh=mesh, in_specs=in_specs, out_specs=out_specs, check_vma=False)
```

time: 237 us -> 229 us (0.966)
  Pallas kernels: 43.4 us -> 30 us
  waiting for transfers between devices: 47.5 us -> 50.4 us
    pallas_call x7, Pallas kernels: 43.4 us -> 30 us  [call(): pl.pallas_call(kernel, out_shape=outs, in_specs=[SCALARS] * len(scalars)...]
    all_to_all x2, waiting for transfers between devices: 47.5 us -> 50.4 us  [exchange(): return lax.all_to_all(slabs, 'row', split_axis=0, concat_axis=0, tiled=True)]
  transfers between devices with their start and end apart: 2 -> 2, of which waited for: 2 -> 2; matrix products, arithmetic and copies ran while one was open for 0% -> 0% of each run, Pallas kernels for 3% -> 2%
where the time goes in v2:
time: 229 us; the launch traced here: 228 us
  blocking collectives  122 us (53%)
  waiting for transfers between devices  50.4 us (22%)
  Pallas kernels  30 us (13%)
  local copies, waits for them, and re-layouts  18 us (8%)
  starting transfers between devices  7.3 us (3%)
    all_to_all x2, blocking collectives, exchange(): return lax.all_to_all(slabs, 'row', split_axis=0, concat_axis=0, tiled=True)  122 us
    all_to_all x2, waiting for transfers between devices, exchange(): return lax.all_to_all(slabs, 'row', split_axis=0, concat_axis=0, tiled=True)  50.4 us
    pallas_call x7, Pallas kernels, call(): pl.pallas_call(kernel, out_shape=outs, in_specs=[SCALARS] * len(scalars)...  30 us
    unnamed x50, local copies, waits for them, and re-layouts  16.6 us
    all_to_all x2, starting transfers between devices, exchange(): return lax.all_to_all(slabs, 'row', split_axis=0, concat_axis=0, tiled=True)  7.3 us
  transfers between devices with their start and end apart: 2, of which 2 were waited for; matrix products, arithmetic and copies ran while one was open for 0% of the time, Pallas kernels for 2%

profile of v2, /device:TPU:0, one launch (start us, length us, event | category | flops | bytes accessed | tf_op | source)
XLA Modules:
  0.0 227.9 jit_solution(3025263850897021221)
XLA Ops:
  0.0 0.7 stack.9
  0.7 0.7 stack.10
  1.4 0.0 copy-start.6
  1.4 0.9 copy-done.6
  2.3 0.0 copy-start.8
  2.3 0.7 copy-done.8
  3.0 0.0 copy-start.10
  3.0 0.7 copy-done.10
  3.7 0.0 copy-start.12
  3.7 0.7 copy-done.12
  4.4 0.0 copy-start.14
  4.4 0.7 copy-done.14
  5.1 0.7 copy-done.18
  5.7 1.3 copy-done.24
  7.0 5.8 %shard_map.109 = (bf16[32,96,384]{2,1,0:T(8,128)(2,1)S(1)}, bf16[12,128,384]{2,1,0:T(8,128)(2,1)S(1)}) custom-call(s32[384]{0:T(512)S(1)} %copy-done.18, s32[384]{0:T(512)S(1)} %copy-done.8, s32[2,384]{1,0:T(2,128)S(1)} %pad_add_fusion.marks, bf16[12,384,128]{2,1,0:T(8,128)(2,1)S(1)} %copy-done.24, f32[2,128]{1,0:T(2,128)S(1)} %copy-done.10, ...), custom_call_target="tpu_custom_call" | custom-call | flops 754974720 | bytes 3538944 | tf_op jit(solution)/shard_map/pallas_call | solution.py:292
  12.8 0.0 copy-start
  12.8 62.8 %all_to_all.20.recv = bf16[32,96,384]{2,1,0:T(8,128)(2,1)S(1)} all-to-all(bf16[32,96,384]{2,1,0:T(8,128)(2,1)S(1)} %get-tuple-element.9), channel_id=1, replica_groups=mesh['grp'=1,'row'=32] {'row'}, dimensions={0} | all-to-all | bytes 4718592 | tf_op jit(solution)/shard_map/all_to_all | solution.py:336
  75.6 5.4 %shard_map.110 = bf16[32,48,384]{2,1,0:T(8,128)(2,1)} custom-call(bf16[32,96,384]{2,1,0:T(8,128)(2,1)S(1)} %all_to_all.20.recv), custom_call_target="tpu_custom_call" | custom-call | flops 452984832 | bytes 3538944 | tf_op jit(solution)/shard_map/pallas_call | solution.py:292
  81.1 3.7 %all-to-all-start.1 = ((bf16[32,48,384]{2,1,0:T(8,128)(2,1)}), bf16[32,48,384]{2,1,0:T(8,128)(2,1)}, u32[]{:S(2)}, u32[]{:S(2)}) async-start(bf16[32,48,384]{2,1,0:T(8,128)(2,1)} %shard_map.110), calls=%async_computation.1 | async-start | bytes 2359296 | tf_op jit(solution)/shard_map/all_to_all | solution.py:336
  84.8 0.0 copy-done
  84.8 0.0 copy-done.9
  84.8 0.0 copy-done.11
  84.8 0.0 copy-done.13
  84.8 0.0 copy-start.2
  84.9 0.8 copy-done.2
  85.7 0.7 copy-done.15
  86.4 2.1 shard_map.111.gate
  88.4 25.2 %all-to-all-done.1.recv = bf16[32,48,384]{2,1,0:T(8,128)(2,1)} async-done(((bf16[32,48,384]{2,1,0:T(8,128)(2,1)}), bf16[32,48,384]{2,1,0:T(8,128)(2,1)}, u32[]{:S(2)}, u32[]{:S(2)}) %all-to-all-start.1) | async-done | bytes 1179680 | tf_op jit(solution)/shard_map/all_to_all | solution.py:336
  113.7 1.3 copy-done.1
  114.9 0.8 copy-done.4
  115.8 0.9 copy-done.7
  116.7 0.7 copy-done.16
  117.4 0.7 copy-done.19
  118.1 0.7 copy-done.20
  118.8 0.7 copy-done.22
  119.4 5.5 %shard_map.112 = (bf16[32,96,384]{2,1,0:T(8,128)(2,1)S(1)}, bf16[12,128,384]{2,1,0:T(8,128)(2,1)S(1)}) custom-call(s32[384]{0:T(512)S(1)} %copy-done.19, s32[384]{0:T(512)S(1)} %copy-done.9, bf16[32,48,384]{2,1,0:T(8,128)(2,1)} %all-to-all-done.1.recv, f32[12,128,384]{2,1,0:T(8,128)S(1)} %shard_map.111.gate, bf16[12,128,384]{2,1,0:T(8,128)(2,1)S(1)} %copy-done.1, ...), custom_call_target="tpu_custom_call" | custom-call | flops 754974720 | bytes 8257536 | tf_op jit(solution)/shard_map/pallas_call | solution.py:292
  124.9 59.1 %all_to_all.21.recv = bf16[32,96,384]{2,1,0:T(8,128)(2,1)S(1)} all-to-all(bf16[32,96,384]{2,1,0:T(8,128)(2,1)S(1)} %get-tuple-element.11), channel_id=1, replica_groups=mesh['grp'=1,'row'=32] {'row'}, dimensions={0} | all-to-all | bytes 4718592 | tf_op jit(solution)/shard_map/all_to_all | solution.py:336
  184.0 5.3 %shard_map.113 = bf16[32,48,384]{2,1,0:T(8,128)(2,1)} custom-call(bf16[32,96,384]{2,1,0:T(8,128)(2,1)S(1)} %all_to_all.21.recv), custom_call_target="tpu_custom_call" | custom-call | flops 452984832 | bytes 3538944 | tf_op jit(solution)/shard_map/pallas_call | solution.py:292
  189.2 3.6 %all-to-all-start.3 = ((bf16[32,48,384]{2,1,0:T(8,128)(2,1)}), bf16[32,48,384]{2,1,0:T(8,128)(2,1)}, u32[]{:S(2)}, u32[]{:S(2)}) async-start(bf16[32,48,384]{2,1,0:T(8,128)(2,1)} %shard_map.113), calls=%async_computation.3 | async-start | bytes 2359296 | tf_op jit(solution)/shard_map/all_to_all | solution.py:336
  192.9 0.0 copy-start.3
  192.9 0.8 copy-done.3
  193.7 0.7 copy-done.17
  194.4 2.1 shard_map.114.gate
  196.5 25.2 %all-to-all-done.3.recv = bf16[32,48,384]{2,1,0:T(8,128)(2,1)} async-done(((bf16[32,48,384]{2,1,0:T(8,128)(2,1)}), bf16[32,48,384]{2,1,0:T(8,128)(2,1)}, u32[]{:S(2)}, u32[]{:S(2)}) %all-to-all-start.3) | async-done | bytes 1179680 | tf_op jit(solution)/shard_map/all_to_all | solution.py:336
  221.7 0.8 copy-done.5
  222.5 0.7 copy-done.21
  223.2 0.7 copy-done.23
  223.9 3.9 %shard_map.115 = bf16[12,384,128]{2,1,0:T(8,128)(2,1)} custom-call(bf16[32,48,384]{2,1,0:T(8,128)(2,1)} %all-to-all-done.3.recv, f32[12,128,384]{2,1,0:T(8,128)S(1)} %shard_map.114.gate, bf16[12,128,384]{2,1,0:T(8,128)(2,1)S(1)} %get-tuple-element.12.x_t, f32[2,128]{1,0:T(2,128)S(1)} %copy-done.21, f32[2,128]{1,0:T(2,128)S(1)} %copy-done.23, ...), custom_call_target="tpu_custom_call" | custom-call | flops 150994944 | bytes 5898240 | tf_op jit(solution)/shard_map/pallas_call | solution.py:292
  (18 shorter events, 0.0 us)
Async XLA Ops:
  1.4 1.0 copy-start.6
  2.3 0.7 copy-start.8
  3.0 0.7 copy-start.10
  3.7 0.7 copy-start.12
  4.4 0.7 copy-start.14
  5.1 0.7 copy-start.18
  5.7 1.3 copy-start.24
  12.8 72.0 %copy-start = (bf16[12,128,384]{2,1,0:T(8,128)(2,1)}, bf16[12,128,384]{2,1,0:T(8,128)(2,1)S(1)}, u32[]{:S(2)}) copy-start(bf16[12,128,384]{2,1,0:T(8,128)(2,1)S(1)} %get-tuple-element.10.x_t) | copy-start | bytes 3538948
  81.1 3.7 %copy-start.9 = (s32[384]{0:T(512)S(1)}, s32[384]{0:T(512)}, u32[]{:S(2)}) copy-start(s32[384]{0:T(512)} %chain_ids.7) | copy-start | bytes 4612
  81.1 3.7 %copy-start.11 = (f32[2,128]{1,0:T(2,128)S(1)}, f32[2,128]{1,0:T(2,128)}, u32[]{:S(2)}) copy-start(f32[2,128]{1,0:T(2,128)} %rest_0_.3) | copy-start | bytes 3076
  81.1 3.7 %copy-start.13 = (f32[2,128]{1,0:T(2,128)S(1)}, f32[2,128]{1,0:T(2,128)}, u32[]{:S(2)}) copy-start(f32[2,128]{1,0:T(2,128)} %rest_1_.3) | copy-start | bytes 3076
  81.1 32.6 %all-to-all-start.1 = ((bf16[32,48,384]{2,1,0:T(8,128)(2,1)}), bf16[32,48,384]{2,1,0:T(8,128)(2,1)}, u32[]{:S(2)}, u32[]{:S(2)}) async-start(bf16[32,48,384]{2,1,0:T(8,128)(2,1)} %shard_map.110), calls=%async_computation.1 | async-start | bytes 2359296 | tf_op jit(solution)/shard_map/all_to_all | solution.py:336
  84.8 0.8 copy-start.2
  85.7 0.7 copy-start.15
  113.7 1.3 copy-start.1
  114.9 0.8 copy-start.4
  115.8 0.9 copy-start.7
  116.7 0.7 copy-start.16
  117.4 0.7 copy-start.19
  118.1 0.7 copy-start.20
  118.8 0.7 copy-start.22
  189.2 32.4 %all-to-all-start.3 = ((bf16[32,48,384]{2,1,0:T(8,128)(2,1)}), bf16[32,48,384]{2,1,0:T(8,128)(2,1)}, u32[]{:S(2)}, u32[]{:S(2)}) async-start(bf16[32,48,384]{2,1,0:T(8,128)(2,1)} %shard_map.113), calls=%async_computation.3 | async-start | bytes 2359296 | tf_op jit(solution)/shard_map/all_to_all | solution.py:336
  192.9 0.8 copy-start.3
  193.7 0.7 copy-start.17
  221.7 0.8 copy-start.5
  222.5 0.7 copy-start.21
  223.2 0.7 copy-start.23

commit v3 on v2

v3 whole, which is shorter than its diff:
```python
import functools

import jax
import jax.numpy as jnp
from jax import lax
from jax.experimental import pallas as pl
from jax.experimental.pallas import tpu as pltpu
from jax.sharding import PartitionSpec as P

C = 128
HC = 128
EPS = 1e-05
F32 = jnp.float32
BF16 = jnp.bfloat16
VMEM_LIMIT = 32 * 1024 * 1024
FIRST_VMEM_LIMIT = 60 * 1024 * 1024
GROUP = 2

WHOLE = pl.BlockSpec(memory_space=pltpu.VMEM)
ANYWHERE = pl.BlockSpec(memory_space=pl.ANY)


def blocks(width):
    return [(j, slice(j * 128, (j + 1) * 128)) for j in range(width // 128)]


def column(vector_ref, layer):
    return jnp.broadcast_to(vector_ref[layer : layer + 1, :], (C, C)).T


def turn(ref):
    return ref[...].astype(F32).T.astype(BF16)


def norm_channels(values, gain, bias):
    mean = jnp.sum(values, axis=0, keepdims=True) * (1.0 / C)
    centred = values - mean
    var = jnp.sum(centred * centred, axis=0, keepdims=True) * (1.0 / C)
    return centred * lax.rsqrt(var + EPS) * gain + bias


def norm_input(values, same, g, b, e):
    return (norm_channels(values, g, b) + same * e).astype(BF16)


def same_chain(marks, row_marks, r, columns):
    return (marks[1:2, columns] == row_marks[1, r : r + 1, :]).astype(F32)


def project(group, normed, marks, row_marks, w_t, slabs):
    rows = slabs.shape[1] // (2 * HC)
    width = slabs.shape[0] * 128
    proj = jnp.dot(w_t, normed, preferred_element_type=F32)
    for k, r in enumerate(group):
        for j, columns in blocks(width):
            mask = marks[0:1, columns] * row_marks[0, r : r + 1, :]
            for side in range(2):
                p = proj[2 * side * HC : (2 * side + 2) * HC, k * width + j * 128 : k * width + (j + 1) * 128]
                value = jax.nn.sigmoid(p[:HC]) * p[HC:] * mask
                slabs[j, pl.ds(side * HC * rows + r, HC, stride=rows), :] = value


def write_slabs(slabs, out):
    devices, depth, width = out.shape
    half = depth // 2
    for side in range(2):
        for d in range(devices):
            start = (side * devices + d) * half
            for j, columns in blocks(width):
                out[d, side * half : (side + 1) * half, columns] = slabs[j, start : start + half, :].astype(BF16)


def widen(recv, wide):
    devices, depth, width = recv.shape
    for s in range(devices):
        for j, columns in blocks(width):
            wide[j, s * depth : (s + 1) * depth, :] = recv[s, :, columns].astype(F32)


def fetch(pairs, sems):
    copies = [pltpu.make_async_copy(src, dst, sems.at[i]) for i, (src, dst) in enumerate(pairs)]
    for copy in copies:
        copy.start()
    return copies


def groups(rows):
    return [range(i, min(i + GROUP, rows)) for i in range(0, rows, GROUP)]


def overlapped(rows, prepare, consume):
    todo = groups(rows)
    ready = prepare(todo[0])
    for i, group in enumerate(todo):
        current = ready
        if i + 1 < len(todo):
            ready = prepare(todo[i + 1])
        consume(group, current)


def first_kernel(
    residue_mask, chain_ids, x_in, gain, bias, embed, w_ab, out, x_t, marks, row_marks,
    x, w, vectors, mask_ids, chain, w_t, g, b, e, slabs, sems, x_sems,
):
    rows, width, _ = x.shape
    smalls = fetch(
        [
            (residue_mask, mask_ids), (chain_ids, chain), (gain, vectors.at[0]), (bias, vectors.at[1]),
            (embed, vectors.at[2]), (w_ab.at[0], w),
        ],
        sems,
    )
    larges = fetch([(x_in.at[pl.ds(r[0], len(r))], x.at[pl.ds(r[0], len(r))]) for r in groups(rows)], x_sems)
    for copy in smalls:
        copy.wait()
    w_t[...] = turn(w)
    g[...] = column(vectors.at[0], 0)
    b[...] = column(vectors.at[1], 0)
    e[...] = column(vectors.at[2], 0)
    shape = (row_marks.shape[1], width)
    start = lax.axis_index("row") * rows
    own = lax.broadcasted_iota(jnp.int32, shape, 1) == lax.broadcasted_iota(jnp.int32, shape, 0) + start
    for i, ref in enumerate((mask_ids, chain)):
        values = ref[...].astype(F32).reshape(1, width)
        marks[i : i + 1, :] = values
        picked = jnp.sum(jnp.where(own, values, 0.0), axis=1, keepdims=True)
        row_marks[i] = jnp.broadcast_to(picked, row_marks.shape[1:])

    def prepare(group):
        larges[group[0] // GROUP].wait()
        parts = []
        for r in group:
            for _, columns in blocks(width):
                values = x[r, columns, :].astype(F32).T
                x_t[r, :, columns] = values.astype(BF16)
                same = same_chain(marks, row_marks, r, columns)
                parts.append(norm_input(values, same, g[...], b[...], e[...]))
        return jnp.concatenate(parts, axis=1)

    def consume(group, normed):
        project(group, normed, marks, row_marks, w_t[...], slabs)

    overlapped(rows, prepare, consume)
    write_slabs(slabs, out)


def write_gates(x_t, marks, row_marks, g, b, e, w_t, out):
    rows, _, width = x_t.shape

    def prepare(group):
        return jnp.concatenate(
            [
                norm_input(x_t[r, :, columns].astype(F32), same_chain(marks, row_marks, r, columns), g, b, e)
                for r in group
                for _, columns in blocks(width)
            ],
            axis=1,
        )

    def consume(group, normed):
        gates = jax.nn.sigmoid(jnp.dot(w_t, normed, preferred_element_type=F32))
        for k, r in enumerate(group):
            out[r] = gates[:, k * width : (k + 1) * width]

    overlapped(rows, prepare, consume)


W_AB, W_OUT, W_GATE = slice(0, 4 * HC), [slice(4 * HC, 5 * HC), slice(5 * HC, 6 * HC)], slice(6 * HC, 7 * HC)
GAIN, BIAS, EMBED, MID_GAIN, MID_BIAS = 0, 1, 2, [3, 5], [4, 6]


def gate_kernel(
    x_t, marks, row_marks, gain, bias, embed, w_gate, w_ab, mid_gain, mid_bias, w_out, out, weights, columns_out,
    vectors, w_square, w_wide, sems,
):
    copies = fetch(
        [
            (gain, vectors.at[0]), (bias, vectors.at[1]), (embed, vectors.at[2]), (mid_gain, vectors.at[3]),
            (mid_bias, vectors.at[4]), (w_gate, w_square.at[0]), (w_out, w_square.at[1]), (w_ab.at[1], w_wide),
        ],
        sems,
    )
    for copy in copies:
        copy.wait()
    weights[W_AB, :] = turn(w_wide)
    weights[W_GATE, :] = turn(w_square.at[0, 1])
    for layer in range(2):
        weights[W_OUT[layer], :] = turn(w_square.at[1, layer])
        columns_out[MID_GAIN[layer]] = column(vectors.at[3], layer)
        columns_out[MID_BIAS[layer]] = column(vectors.at[4], layer)
    for i in (GAIN, BIAS, EMBED):
        columns_out[i] = column(vectors.at[i], 1)
    first = [column(vectors.at[i], 0) for i in (GAIN, BIAS, EMBED)]
    write_gates(x_t, marks, row_marks, *first, turn(w_square.at[0, 0]), out)


def second_gate_kernel(x_t, marks, row_marks, weights, columns, out):
    write_gates(x_t, marks, row_marks, columns[GAIN], columns[BIAS], columns[EMBED], weights[W_GATE, :], out)


def products_kernel(incoming, rows, recv, out, wide, natural, turned):
    devices, depth, width = recv.shape
    channels = depth // (2 * rows)
    widen(recv, wide)

    def rows_of(side, c, r, j):
        return wide[j, pl.ds((side * channels + c) * rows + r, devices, stride=depth), :]

    def by_row(side, c):
        return jnp.concatenate(
            [
                jnp.concatenate([rows_of(side, c, r, j).astype(BF16) for r in range(rows)], axis=0)
                for j, _ in blocks(width)
            ],
            axis=1,
        )

    def put(c, r, j, values):
        turned[j, pl.ds(c * rows + r, devices, stride=channels * rows), :] = values

    for c in range(channels):
        left = by_row(0, c)
        if incoming:
            right = by_row(1, c)
            product = lax.dot_general(left, right, (((0,), (0,)), ((), ())), preferred_element_type=F32)
            for j, columns in blocks(width):
                natural[c, j] = product[:, columns]
                for r in range(rows):
                    put(c, r, j, natural[c, j, pl.ds(r, devices, stride=rows), :])
        else:
            for j, _ in blocks(width):
                for r in range(rows):
                    natural[c, j, pl.ds(r, devices, stride=rows), :] = rows_of(1, c, r, j)
            right = jnp.concatenate([natural[c, j].astype(BF16) for j, _ in blocks(width)], axis=1)
            product = lax.dot_general(left, right, (((1,), (1,)), ((), ())), preferred_element_type=F32)
            for j, columns in blocks(width):
                for r in range(rows):
                    put(c, r, j, product[r * devices : (r + 1) * devices, columns])
    for s in range(devices):
        for j, columns in blocks(width):
            out[s, :, columns] = turned[j, s * channels * rows : (s + 1) * channels * rows, :].astype(BF16)


def finish(layer, group, width, tri, gate, x_t, weights, vectors):
    rows = tri.shape[1] // HC
    gain, bias = vectors[MID_GAIN[layer]], vectors[MID_BIAS[layer]]
    normed = jnp.concatenate(
        [
            norm_channels(tri[j, pl.ds(r, HC, stride=rows), :], gain, bias).astype(BF16)
            for r in group
            for j, _ in blocks(width)
        ],
        axis=1,
    )
    branch = jnp.dot(weights[W_OUT[layer], :], normed, preferred_element_type=F32)
    return {
        (r, j): (
            x_t[r, :, columns].astype(F32)
            + gate[r, :, columns] * branch[:, k * width + j * 128 : k * width + (j + 1) * 128]
        ).astype(BF16)
        for k, r in enumerate(group)
        for j, columns in blocks(width)
    }


def middle_kernel(recv, gate, x_t, marks, row_marks, weights, vectors, out, new_t, slabs, tri):
    rows, _, width = x_t.shape
    widen(recv, tri)

    def prepare(group):
        states = finish(0, group, width, tri, gate, x_t, weights, vectors)
        parts = []
        for r in group:
            for j, columns in blocks(width):
                new_t[r, :, columns] = states[r, j]
                same = same_chain(marks, row_marks, r, columns)
                parts.append(
                    norm_input(states[r, j].astype(F32), same, vectors[GAIN], vectors[BIAS], vectors[EMBED])
                )
        return jnp.concatenate(parts, axis=1)

    def consume(group, normed):
        project(group, normed, marks, row_marks, weights[W_AB, :], slabs)

    overlapped(rows, prepare, consume)
    write_slabs(slabs, out)


def last_kernel(recv, gate, x_t, weights, vectors, out, tri):
    rows, _, width = x_t.shape
    widen(recv, tri)
    for group in groups(rows):
        for (r, j), state in finish(1, group, width, tri, gate, x_t, weights, vectors).items():
            out[r, j * 128 : (j + 1) * 128, :] = state.astype(F32).T.astype(BF16)


def call(kernel, outs, scratch, arrays, anywhere, flops, limit=VMEM_LIMIT):
    size = sum(a.size * a.dtype.itemsize for a in list(arrays) + list(outs))
    return pl.pallas_call(
        kernel,
        out_shape=outs,
        in_specs=[WHOLE] * len(arrays) + [ANYWHERE] * len(anywhere),
        out_specs=[WHOLE] * len(outs),
        scratch_shapes=scratch,
        compiler_params=pltpu.CompilerParams(vmem_limit_bytes=limit),
        cost_estimate=pl.CostEstimate(flops=flops, bytes_accessed=size, transcendentals=0),
    )(*arrays, *anywhere)


def local(
    pair, residue_mask, chain_ids, ln_in_gain, ln_in_bias, chain_embed, w_ab, w_gate, ln_mid_gain, ln_mid_bias, w_out
):
    rows, width, _ = pair.shape
    devices = lax.axis_size("row")
    channels = HC // devices
    cols = width // 128
    pairs = rows * width

    sent = jax.ShapeDtypeStruct((devices, 2 * channels * rows, width), BF16)
    back = jax.ShapeDtypeStruct((devices, channels * rows, width), BF16)
    state_t = jax.ShapeDtypeStruct((rows, C, width), BF16)
    gate_t = jax.ShapeDtypeStruct((rows, C, width), F32)
    mark = jax.ShapeDtypeStruct((2, width), F32)
    row_mark = jax.ShapeDtypeStruct((2, (rows + 7) // 8 * 8, 128), F32)
    turned = jax.ShapeDtypeStruct((7 * HC, C), BF16)
    columns = jax.ShapeDtypeStruct((7, C, 128), F32)

    vector = pltpu.VMEM((C, 128), F32)
    ids = pltpu.VMEM((width,), jnp.int32)
    w_wide = pltpu.VMEM((C, 4 * HC), BF16)
    slabs_wide = pltpu.VMEM((cols, 2 * HC * rows, 128), F32)
    tri_wide = pltpu.VMEM((cols, HC * rows, 128), F32)
    norms = (ln_in_gain, ln_in_bias, chain_embed)

    def sems(n):
        return pltpu.SemaphoreType.DMA((n,))

    def exchange(slabs):
        return lax.all_to_all(slabs, "row", split_axis=0, concat_axis=0, tiled=True)

    def products(recv, incoming):
        return call(
            functools.partial(products_kernel, incoming, rows), [back],
            [slabs_wide, pltpu.VMEM((channels, cols, width, 128), F32), tri_wide], (recv,), (),
            2 * channels * width**3,
        )[0]

    slabs, x_t, marks, row_marks = call(
        first_kernel, [sent, state_t, mark, row_mark],
        [
            pltpu.VMEM(pair.shape, BF16), w_wide, pltpu.VMEM((3, 2, C), F32), ids, ids, pltpu.VMEM((4 * HC, C), BF16),
            vector, vector, vector, slabs_wide, sems(6), sems(len(groups(rows))),
        ],
        (), (residue_mask, chain_ids, pair, *norms, w_ab), 2 * pairs * C * 4 * HC, FIRST_VMEM_LIMIT,
    )
    recv = exchange(slabs)
    gate, weights, vectors = call(
        gate_kernel, [gate_t, turned, columns],
        [pltpu.VMEM((5, 2, C), F32), pltpu.VMEM((2, 2, C, C), BF16), w_wide, sems(8)],
        (x_t, marks, row_marks), (*norms, w_gate, w_ab, ln_mid_gain, ln_mid_bias, w_out), 2 * pairs * C * C,
    )
    tri = exchange(products(recv, False))
    slabs, x_t = call(
        middle_kernel, [sent, state_t], [slabs_wide, tri_wide],
        (tri, gate, x_t, marks, row_marks, weights, vectors), (), 2 * pairs * C * 5 * HC,
    )
    recv = exchange(slabs)
    gate = call(
        second_gate_kernel, [gate_t], [], (x_t, marks, row_marks, weights, vectors), (), 2 * pairs * C * C
    )[0]
    tri = exchange(products(recv, True))
    return call(
        last_kernel, [jax.ShapeDtypeStruct(pair.shape, BF16)], [tri_wide], (tri, gate, x_t, weights, vectors), (),
        2 * pairs * C * C,
    )[0]


def solution(mesh):
    in_specs = (P(("grp", "row"), None, None), P("grp"), P("grp")) + (P(),) * 8
    out_specs = P(("grp", "row"), None, None)
    return jax.shard_map(local, mesh=mesh, in_specs=in_specs, out_specs=out_specs, check_vma=False)
```

time: 229 us -> 215 us (0.939)
  local copies, waits for them, and re-layouts: 18 us -> 10.3 us
  Pallas kernels: 30 us -> 26.6 us
    unnamed x50 -> x46, local copies, waits for them, and re-layouts: 16.6 us -> 10.3 us
    pallas_call x7, Pallas kernels: 30 us -> 26.6 us  [call(): pl.pallas_call(kernel, out_shape=outs, in_specs=[WHOLE] * len(arrays) + [...]
where the time goes in v3:
time: 215 us; the launch traced here: 214 us
  blocking collectives  122 us (57%)
  waiting for transfers between devices  48.9 us (23%)
  Pallas kernels  26.6 us (12%)
  local copies, waits for them, and re-layouts  10.3 us (5%)
  starting transfers between devices  5.86 us (3%)
    all_to_all x2, blocking collectives, exchange(): return lax.all_to_all(slabs, 'row', split_axis=0, concat_axis=0, tiled=True)  122 us
    all_to_all x2, waiting for transfers between devices, exchange(): return lax.all_to_all(slabs, 'row', split_axis=0, concat_axis=0, tiled=True)  48.9 us
    pallas_call x7, Pallas kernels, call(): pl.pallas_call(kernel, out_shape=outs, in_specs=[WHOLE] * len(arrays) + [...  26.6 us
    unnamed x46, local copies, waits for them, and re-layouts  10.3 us
    all_to_all x2, starting transfers between devices, exchange(): return lax.all_to_all(slabs, 'row', split_axis=0, concat_axis=0, tiled=True)  5.86 us
  transfers between devices with their start and end apart: 2, of which 2 were waited for; matrix products, arithmetic and copies ran while one was open for 0% of the time, Pallas kernels for 2%

profile of v3, /device:TPU:0, one launch (start us, length us, event | category | flops | bytes accessed | tf_op | source)
XLA Modules:
  0.0 214.0 jit_solution(17253871529330352307)
XLA Ops:
  0.0 6.3 %shard_map.109 = (bf16[32,96,384]{2,1,0:T(8,128)(2,1)}, bf16[12,128,384]{2,1,0:T(8,128)(2,1)}, f32[2,384]{1,0:T(2,128)}, f32[2,16,128]{2,1,0:T(8,128)}) custom-call(s32[384]{0:T(512)} %residue_mask.1, s32[384]{0:T(512)} %chain_ids.1, bf16[12,384,128]{2,1,0:T(8,128)(2,1)} %x_in.1, f32[2,128]{1,0:T(2,128)} %gain.3, f32[2,128]{1,0:T(2,128)} %bias.3, ...), custom_call_target="tpu_custom_call" | custom-call | flops 603979776 | bytes 3558400 | tf_op jit(solution)/shard_map/pallas_call | solution.py:299
  6.4 63.0 %all_to_all.20.recv = bf16[32,96,384]{2,1,0:T(8,128)(2,1)S(1)} all-to-all(bf16[32,96,384]{2,1,0:T(8,128)(2,1)} %get-tuple-element.14), channel_id=1, replica_groups=mesh['grp'=1,'row'=32] {'row'}, dimensions={0} | all-to-all | bytes 4718592 | tf_op jit(solution)/shard_map/all_to_all | solution.py:339
  69.4 5.4 %shard_map.110 = bf16[32,48,384]{2,1,0:T(8,128)(2,1)} custom-call(bf16[32,96,384]{2,1,0:T(8,128)(2,1)S(1)} %all_to_all.20.recv), custom_call_target="tpu_custom_call" | custom-call | flops 452984832 | bytes 3538944 | tf_op jit(solution)/shard_map/pallas_call | solution.py:299
  74.8 0.0 copy-start.3
  74.8 0.0 copy-start.12
  74.8 0.0 copy-start.15
  74.9 0.0 copy-start.16
  74.9 0.0 copy-start.18
  74.9 0.0 copy-start.19
  74.9 0.0 copy-start.20
  74.9 0.0 copy-start.21
  74.9 0.0 copy-start.22
  74.9 3.0 %all-to-all-start.1 = ((bf16[32,48,384]{2,1,0:T(8,128)(2,1)}), bf16[32,48,384]{2,1,0:T(8,128)(2,1)S(1)}, u32[]{:S(2)}, u32[]{:S(2)}) async-start(bf16[32,48,384]{2,1,0:T(8,128)(2,1)} %shard_map.110), calls=%async_computation.1 | async-start | bytes 2359296 | tf_op jit(solution)/shard_map/all_to_all | solution.py:339
  77.9 0.0 copy-done.3
  77.9 0.0 copy-done.12
  77.9 0.0 copy-done.13
  77.9 0.0 copy-done.14
  78.0 0.0 copy-done.15
  78.0 0.0 copy-done.16
  78.0 0.0 copy-done.18
  78.0 0.0 copy-done.19
  78.0 0.0 copy-done.20
  78.0 0.0 copy-done.21
  78.0 0.0 copy-done.22
  78.0 1.9 shard_map.111
  79.9 0.0 copy-start.7
  80.0 1.4 copy-done.7
  81.4 25.4 %all-to-all-done.1.recv = bf16[32,48,384]{2,1,0:T(8,128)(2,1)S(1)} async-done(((bf16[32,48,384]{2,1,0:T(8,128)(2,1)}), bf16[32,48,384]{2,1,0:T(8,128)(2,1)S(1)}, u32[]{:S(2)}, u32[]{:S(2)}) %all-to-all-start.1) | async-done | bytes 1179680 | tf_op jit(solution)/shard_map/all_to_all | solution.py:339
  106.8 1.7 copy-done.8
  108.5 3.7 %shard_map.112 = (bf16[32,96,384]{2,1,0:T(8,128)(2,1)S(1)}, bf16[12,128,384]{2,1,0:T(8,128)(2,1)S(1)}) custom-call(bf16[32,48,384]{2,1,0:T(8,128)(2,1)S(1)} %all-to-all-done.1.recv, f32[12,128,384]{2,1,0:T(8,128)S(1)} %copy-done.8, bf16[12,128,384]{2,1,0:T(8,128)(2,1)S(1)} %copy-done.3, f32[2,384]{1,0:T(2,128)S(1)} %copy-done.16, ...), custom_call_target="tpu_custom_call" | custom-call | flops 754974720 | bytes 8965120 | tf_op jit(solution)/shard_map/pallas_call | solution.py:299
  112.2 0.0 copy-done.4
  112.2 0.0 copy-done.9
  112.2 0.0 copy-start
  112.2 59.1 %all_to_all.21.recv = bf16[32,96,384]{2,1,0:T(8,128)(2,1)S(1)} all-to-all(bf16[32,96,384]{2,1,0:T(8,128)(2,1)S(1)} %get-tuple-element.21), channel_id=1, replica_groups=mesh['grp'=1,'row'=32] {'row'}, dimensions={0} | all-to-all | bytes 4718592 | tf_op jit(solution)/shard_map/all_to_all | solution.py:339
  171.3 0.0 copy-done
  171.3 5.3 %shard_map.113 = bf16[32,48,384]{2,1,0:T(8,128)(2,1)} custom-call(bf16[32,96,384]{2,1,0:T(8,128)(2,1)S(1)} %all_to_all.21.recv), custom_call_target="tpu_custom_call" | custom-call | flops 452984832 | bytes 3538944 | tf_op jit(solution)/shard_map/pallas_call | solution.py:299
  176.6 2.9 %all-to-all-start.3 = ((bf16[32,48,384]{2,1,0:T(8,128)(2,1)}), bf16[32,48,384]{2,1,0:T(8,128)(2,1)S(1)}, u32[]{:S(2)}, u32[]{:S(2)}) async-start(bf16[32,48,384]{2,1,0:T(8,128)(2,1)} %shard_map.113), calls=%async_computation.3 | async-start | bytes 2359296 | tf_op jit(solution)/shard_map/all_to_all | solution.py:339
  179.4 0.0 copy-start.1
  179.4 1.3 copy-done.1
  180.7 1.0 copy-done.5
  181.7 0.9 copy-done.10
  182.7 0.7 copy-done.17
  183.3 1.5 shard_map.114.gate
  184.8 23.5 %all-to-all-done.3.recv = bf16[32,48,384]{2,1,0:T(8,128)(2,1)S(1)} async-done(((bf16[32,48,384]{2,1,0:T(8,128)(2,1)}), bf16[32,48,384]{2,1,0:T(8,128)(2,1)S(1)}, u32[]{:S(2)}, u32[]{:S(2)}) %all-to-all-start.3) | async-done | bytes 1179680 | tf_op jit(solution)/shard_map/all_to_all | solution.py:339
  208.3 1.3 copy-done.2
  209.5 1.0 copy-done.6
  210.6 0.9 copy-done.11
  211.5 2.5 %shard_map.115 = bf16[12,384,128]{2,1,0:T(8,128)(2,1)} custom-call(bf16[32,48,384]{2,1,0:T(8,128)(2,1)S(1)} %all-to-all-done.3.recv, f32[12,128,384]{2,1,0:T(8,128)S(1)} %shard_map.114.gate, bf16[12,128,384]{2,1,0:T(8,128)(2,1)S(1)} %copy-done.2, bf16[896,128]{1,0:T(8,128)(2,1)S(1)} %copy-done.11, f32[7,128,128]{2,1,0:T(8,128)S(1)} %copy-done.6), custom_call_target="tpu_custom_call" | custom-call | flops 150994944 | bytes 6586368 | tf_op jit(solution)/shard_map/pallas_call | solution.py:299
  (11 shorter events, 0.0 us)
Async XLA Ops:
  74.8 3.1 %copy-start.3 = (bf16[12,128,384]{2,1,0:T(8,128)(2,1)S(1)}, bf16[12,128,384]{2,1,0:T(8,128)(2,1)}, u32[]{:S(2)}) copy-start(bf16[12,128,384]{2,1,0:T(8,128)(2,1)} %get-tuple-element.15.x_t) | copy-start | bytes 3538948
  74.8 3.1 %copy-start.12 = (bf16[2,128,512]{2,1,0:T(8,128)(2,1)S(1)}, bf16[2,128,512]{2,1,0:T(8,128)(2,1)}, u32[]{:S(2)}) copy-start(bf16[2,128,512]{2,1,0:T(8,128)(2,1)} %w_ab.3) | copy-start | bytes 786436
  74.8 3.1 %copy-start.13 = (f32[2,16,128]{2,1,0:T(8,128)S(1)}, f32[2,16,128]{2,1,0:T(8,128)}, u32[]{:S(2)}) copy-start(f32[2,16,128]{2,1,0:T(8,128)} %get-tuple-element.17.row_marks) | copy-start | bytes 49156
  74.8 3.1 %copy-start.14 = (bf16[2,128,128]{2,1,0:T(8,128)(2,1)S(1)}, bf16[2,128,128]{2,1,0:T(8,128)(2,1)}, u32[]{:S(2)}) copy-start(bf16[2,128,128]{2,1,0:T(8,128)(2,1)} %w_gate.1) | copy-start | bytes 196612
  74.8 3.1 %copy-start.15 = (bf16[2,128,128]{2,1,0:T(8,128)(2,1)S(1)}, bf16[2,128,128]{2,1,0:T(8,128)(2,1)}, u32[]{:S(2)}) copy-start(bf16[2,128,128]{2,1,0:T(8,128)(2,1)} %w_out.1) | copy-start | bytes 196612
  74.9 3.1 %copy-start.16 = (f32[2,384]{1,0:T(2,128)S(1)}, f32[2,384]{1,0:T(2,128)}, u32[]{:S(2)}) copy-start(f32[2,384]{1,0:T(2,128)} %get-tuple-element.16.marks) | copy-start | bytes 9220
  74.9 3.1 %copy-start.18 = (f32[2,128]{1,0:T(2,128)S(1)}, f32[2,128]{1,0:T(2,128)}, u32[]{:S(2)}) copy-start(f32[2,128]{1,0:T(2,128)} %gain.3) | copy-start | bytes 3076
  74.9 3.1 %copy-start.19 = (f32[2,128]{1,0:T(2,128)S(1)}, f32[2,128]{1,0:T(2,128)}, u32[]{:S(2)}) copy-start(f32[2,128]{1,0:T(2,128)} %bias.3) | copy-start | bytes 3076
  74.9 3.1 %copy-start.20 = (f32[2,128]{1,0:T(2,128)S(1)}, f32[2,128]{1,0:T(2,128)}, u32[]{:S(2)}) copy-start(f32[2,128]{1,0:T(2,128)} %embed.3) | copy-start | bytes 3076
  74.9 3.1 %copy-start.21 = (f32[2,128]{1,0:T(2,128)S(1)}, f32[2,128]{1,0:T(2,128)}, u32[]{:S(2)}) copy-start(f32[2,128]{1,0:T(2,128)} %mid_gain.1) | copy-start | bytes 3076
  74.9 3.1 %copy-start.22 = (f32[2,128]{1,0:T(2,128)S(1)}, f32[2,128]{1,0:T(2,128)}, u32[]{:S(2)}) copy-start(f32[2,128]{1,0:T(2,128)} %mid_bias.1) | copy-start | bytes 3076
  74.9 31.9 %all-to-all-start.1 = ((bf16[32,48,384]{2,1,0:T(8,128)(2,1)}), bf16[32,48,384]{2,1,0:T(8,128)(2,1)S(1)}, u32[]{:S(2)}, u32[]{:S(2)}) async-start(bf16[32,48,384]{2,1,0:T(8,128)(2,1)} %shard_map.110), calls=%async_computation.1 | async-start | bytes 2359296 | tf_op jit(solution)/shard_map/all_to_all | solution.py:339
  79.9 1.4 copy-start.7
  81.4 30.8 %copy-start.4 = (f32[7,128,128]{2,1,0:T(8,128)}, f32[7,128,128]{2,1,0:T(8,128)S(1)}, u32[]{:S(2)}) copy-start(f32[7,128,128]{2,1,0:T(8,128)S(1)} %get-tuple-element.20.vectors.columns) | copy-start | bytes 1376260
  81.4 30.8 %copy-start.9 = (bf16[896,128]{1,0:T(8,128)(2,1)}, bf16[896,128]{1,0:T(8,128)(2,1)S(1)}, u32[]{:S(2)}) copy-start(bf16[896,128]{1,0:T(8,128)(2,1)S(1)} %get-tuple-element.19.weights) | copy-start | bytes 688132
  106.8 1.7 copy-start.8
  112.2 59.1 %copy-start = (bf16[12,128,384]{2,1,0:T(8,128)(2,1)}, bf16[12,128,384]{2,1,0:T(8,128)(2,1)S(1)}, u32[]{:S(2)}) copy-start(bf16[12,128,384]{2,1,0:T(8,128)(2,1)S(1)} %get-tuple-element.22.x_t) | copy-start | bytes 3538948
  176.6 31.7 %all-to-all-start.3 = ((bf16[32,48,384]{2,1,0:T(8,128)(2,1)}), bf16[32,48,384]{2,1,0:T(8,128)(2,1)S(1)}, u32[]{:S(2)}, u32[]{:S(2)}) async-start(bf16[32,48,384]{2,1,0:T(8,128)(2,1)} %shard_map.113), calls=%async_computation.3 | async-start | bytes 2359296 | tf_op jit(solution)/shard_map/all_to_all | solution.py:339
  179.4 1.3 copy-start.1
  180.7 1.0 copy-start.5
  181.7 0.9 copy-start.10
  182.7 0.7 copy-start.17
  208.3 1.3 copy-start.2
  209.5 1.0 copy-start.6
  210.6 0.9 copy-start.11

commit v4 on v3

--- a/solution.py
+++ b/solution.py
@@ -13,6 +13,7 @@
 F32 = jnp.float32
 BF16 = jnp.bfloat16
 VMEM_LIMIT = 32 * 1024 * 1024
+PRODUCTS_VMEM_LIMIT = 48 * 1024 * 1024
 FIRST_VMEM_LIMIT = 60 * 1024 * 1024
 GROUP = 2
 
@@ -70,6 +71,22 @@
                 out[d, side * half : (side + 1) * half, columns] = slabs[j, start : start + half, :].astype(BF16)
 
 
+def write_crossing(slabs, out, own):
+    devices, depth, width = out.shape
+    half = devices // 2
+    me = lax.axis_index("row")
+    side_rows = half * depth
+    for d in range(devices):
+        side = jnp.where(me // half == d // half, 0, side_rows)
+        start = pl.multiple_of(side + d % half * depth, 8)
+        for j, columns in blocks(width):
+            out[d, :, columns] = slabs[j, pl.ds(start, depth), :].astype(BF16)
+    for o, ref in enumerate(own):
+        start = pl.multiple_of(side_rows + (me % half ^ o) * depth, 8)
+        for j, columns in blocks(width):
+            ref[:, columns] = slabs[j, pl.ds(start, depth), :].astype(BF16)
+
+
 def widen(recv, wide):
     devices, depth, width = recv.shape
     for s in range(devices):
@@ -98,10 +115,9 @@
         consume(group, current)
 
 
-def first_kernel(
-    residue_mask, chain_ids, x_in, gain, bias, embed, w_ab, out, x_t, marks, row_marks,
-    x, w, vectors, mask_ids, chain, w_t, g, b, e, slabs, sems, x_sems,
-):
+def first_kernel(residue_mask, chain_ids, x_in, gain, bias, embed, w_ab, *refs):
+    own = refs[:-16]
+    out, x_t, marks, row_marks, x, w, vectors, mask_ids, chain, w_t, g, b, e, slabs, sems, x_sems = refs[-16:]
     rows, width, _ = x.shape
     smalls = fetch(
         [
@@ -119,11 +135,11 @@
     e[...] = column(vectors.at[2], 0)
     shape = (row_marks.shape[1], width)
     start = lax.axis_index("row") * rows
-    own = lax.broadcasted_iota(jnp.int32, shape, 1) == lax.broadcasted_iota(jnp.int32, shape, 0) + start
+    at_row = lax.broadcasted_iota(jnp.int32, shape, 1) == lax.broadcasted_iota(jnp.int32, shape, 0) + start
     for i, ref in enumerate((mask_ids, chain)):
         values = ref[...].astype(F32).reshape(1, width)
         marks[i : i + 1, :] = values
-        picked = jnp.sum(jnp.where(own, values, 0.0), axis=1, keepdims=True)
+        picked = jnp.sum(jnp.where(at_row, values, 0.0), axis=1, keepdims=True)
         row_marks[i] = jnp.broadcast_to(picked, row_marks.shape[1:])
 
     def prepare(group):
@@ -141,7 +157,7 @@
         project(group, normed, marks, row_marks, w_t[...], slabs)
 
     overlapped(rows, prepare, consume)
-    write_slabs(slabs, out)
+    write_crossing(slabs, out, own)
 
 
 def write_gates(x_t, marks, row_marks, g, b, e, w_t, out):
@@ -198,44 +214,73 @@
     write_gates(x_t, marks, row_marks, columns[GAIN], columns[BIAS], columns[EMBED], weights[W_GATE, :], out)
 
 
-def products_kernel(incoming, rows, recv, out, wide, natural, turned):
+def first_products_kernel(rows, recv, *refs):
+    own, (out, left_wide, right_wide, natural, turned) = refs[:-5], refs[-5:]
+    devices, depth, width = recv.shape
+    half = devices // 2
+    channels = depth // rows
+    me = lax.axis_index("row")
+    mine = me // half * half
+    other = half - mine
+    for q in range(half):
+        to_other = pl.multiple_of((other + q) * depth, 8)
+        to_own = pl.multiple_of((mine + (me % half ^ q)) * depth, 8)
+        for j, columns in blocks(width):
+            left_wide[j, q * depth : (q + 1) * depth, :] = recv[mine + q, :, columns].astype(F32)
+            right_wide[j, pl.ds(to_other, depth), :] = recv[other + q, :, columns].astype(F32)
+            right_wide[j, pl.ds(to_own, depth), :] = own[q][:, columns].astype(F32)
+    for c in range(channels):
+        left, right = [], []
+        for j, _ in blocks(width):
+            pieces = [left_wide[j, pl.ds(c * rows + r, half, stride=depth), :].astype(BF16) for r in range(rows)]
+            left.append(jnp.concatenate(pieces, axis=0))
+            for r in range(rows):
+                natural[c, j, pl.ds(r, devices, stride=rows), :] = right_wide[
+                    j, pl.ds(c * rows + r, devices, stride=depth), :
+                ]
+            right.append(natural[c, j].astype(BF16))
+        product = lax.dot_general(
+            jnp.concatenate(left, axis=1), jnp.concatenate(right, axis=1), (((1,), (1,)), ((), ())),
+            preferred_element_type=F32,
+        )
+        for j, columns in blocks(width):
+            for r in range(rows):
+                turned[j, pl.ds(c * rows + r, half, stride=depth), :] = product[r * half : (r + 1) * half, columns]
+    for q in range(half):
+        for j, columns in blocks(width):
+            out[q, :, columns] = turned[j, q * depth : (q + 1) * depth, :].astype(BF16)
+
+
+def second_products_kernel(rows, recv, out, wide, natural, turned):
     devices, depth, width = recv.shape
     channels = depth // (2 * rows)
     widen(recv, wide)
 
-    def rows_of(side, c, r, j):
-        return wide[j, pl.ds((side * channels + c) * rows + r, devices, stride=depth), :]
-
     def by_row(side, c):
         return jnp.concatenate(
             [
-                jnp.concatenate([rows_of(side, c, r, j).astype(BF16) for r in range(rows)], axis=0)
+                jnp.concatenate(
+                    [
+                        wide[j, pl.ds((side * channels + c) * rows + r, devices, stride=depth), :].astype(BF16)
+                        for r in range(rows)
+                    ],
+                    axis=0,
+                )
                 for j, _ in blocks(width)
             ],
             axis=1,
         )
 
-    def put(c, r, j, values):
-        turned[j, pl.ds(c * rows + r, devices, stride=channels * rows), :] = values
-
     for c in range(channels):
-        left = by_row(0, c)
-        if incoming:
-            right = by_row(1, c)
-            product = lax.dot_general(left, right, (((0,), (0,)), ((), ())), preferred_element_type=F32)
-            for j, columns in blocks(width):
-                natural[c, j] = product[:, columns]
-                for r in range(rows):
-                    put(c, r, j, natural[c, j, pl.ds(r, devices, stride=rows), :])
-        else:
-            for j, _ in blocks(width):
-                for r in range(rows):
-                    natural[c, j, pl.ds(r, devices, stride=rows), :] = rows_of(1, c, r, j)
-            right = jnp.concatenate([natural[c, j].astype(BF16) for j, _ in blocks(width)], axis=1)
-            product = lax.dot_general(left, right, (((1,), (1,)), ((), ())), preferred_element_type=F32)
-            for j, columns in blocks(width):
-                for r in range(rows):
-                    put(c, r, j, product[r * devices : (r + 1) * devices, columns])
+        product = lax.dot_general(
+            by_row(0, c), by_row(1, c), (((0,), (0,)), ((), ())), preferred_element_type=F32
+        )
+        for j, columns in blocks(width):
+            natural[c, j] = product[:, columns]
+            for r in range(rows):
+                turned[j, pl.ds(c * rows + r, devices, stride=channels * rows), :] = natural[
+                    c, j, pl.ds(r, devices, stride=rows), :
+                ]
     for s in range(devices):
         for j, columns in blocks(width):
             out[s, :, columns] = turned[j, s * channels * rows : (s + 1) * channels * rows, :].astype(BF16)
@@ -312,12 +357,15 @@
 ):
     rows, width, _ = pair.shape
     devices = lax.axis_size("row")
+    half = devices // 2
     channels = HC // devices
     cols = width // 128
     pairs = rows * width
 
     sent = jax.ShapeDtypeStruct((devices, 2 * channels * rows, width), BF16)
     back = jax.ShapeDtypeStruct((devices, channels * rows, width), BF16)
+    own_back = jax.ShapeDtypeStruct((half, 2 * channels * rows, width), BF16)
+    own_slab = jax.ShapeDtypeStruct((2 * channels * rows, width), BF16)
     state_t = jax.ShapeDtypeStruct((rows, C, width), BF16)
     gate_t = jax.ShapeDtypeStruct((rows, C, width), F32)
     mark = jax.ShapeDtypeStruct((2, width), F32)
@@ -335,18 +383,14 @@
     def sems(n):
         return pltpu.SemaphoreType.DMA((n,))
 
-    def exchange(slabs):
-        return lax.all_to_all(slabs, "row", split_axis=0, concat_axis=0, tiled=True)
-
-    def products(recv, incoming):
-        return call(
-            functools.partial(products_kernel, incoming, rows), [back],
-            [slabs_wide, pltpu.VMEM((channels, cols, width, 128), F32), tri_wide], (recv,), (),
-            2 * channels * width**3,
-        )[0]
-
-    slabs, x_t, marks, row_marks = call(
-        first_kernel, [sent, state_t, mark, row_mark],
+    def exchange(slabs, groups=None):
+        return lax.all_to_all(
+            slabs, "row", split_axis=0, concat_axis=0, tiled=True, axis_index_groups=groups
+        )
+
+    halves = [list(range(h * half, (h + 1) * half)) for h in range(2)]
+    *own, slabs, x_t, marks, row_marks = call(
+        first_kernel, [own_slab] * half + [sent, state_t, mark, row_mark],
         [
             pltpu.VMEM(pair.shape, BF16), w_wide, pltpu.VMEM((3, 2, C), F32), ids, ids, pltpu.VMEM((4 * HC, C), BF16),
             vector, vector, vector, slabs_wide, sems(6), sems(len(groups(rows))),
@@ -354,12 +398,20 @@
         (), (residue_mask, chain_ids, pair, *norms, w_ab), 2 * pairs * C * 4 * HC, FIRST_VMEM_LIMIT,
     )
     recv = exchange(slabs)
+    own = [own[0]] + [lax.ppermute(own[o], "row", [(i, i ^ o) for i in range(devices)]) for o in range(1, half)]
     gate, weights, vectors = call(
         gate_kernel, [gate_t, turned, columns],
         [pltpu.VMEM((5, 2, C), F32), pltpu.VMEM((2, 2, C, C), BF16), w_wide, sems(8)],
         (x_t, marks, row_marks), (*norms, w_gate, w_ab, ln_mid_gain, ln_mid_bias, w_out), 2 * pairs * C * C,
     )
-    tri = exchange(products(recv, False))
+    products = call(
+        functools.partial(first_products_kernel, rows), [own_back],
+        [
+            tri_wide, slabs_wide, pltpu.VMEM((2 * channels, cols, width, 128), F32), tri_wide,
+        ],
+        (recv, *own), (), 2 * channels * width**3, PRODUCTS_VMEM_LIMIT,
+    )[0]
+    tri = exchange(products, halves)
     slabs, x_t = call(
         middle_kernel, [sent, state_t], [slabs_wide, tri_wide],
         (tri, gate, x_t, marks, row_marks, weights, vectors), (), 2 * pairs * C * 5 * HC,
@@ -368,7 +420,11 @@
     gate = call(
         second_gate_kernel, [gate_t], [], (x_t, marks, row_marks, weights, vectors), (), 2 * pairs * C * C
     )[0]
-    tri = exchange(products(recv, True))
+    products = call(
+        functools.partial(second_products_kernel, rows), [back],
+        [slabs_wide, pltpu.VMEM((channels, cols, width, 128), F32), tri_wide], (recv,), (), 2 * channels * width**3,
+    )[0]
+    tri = exchange(products)
     return call(
         last_kernel, [jax.ShapeDtypeStruct(pair.shape, BF16)], [tri_wide], (tri, gate, x_t, weights, vectors), (),
         2 * pairs * C * C,

time: 215 us -> 209 us (0.972)
  blocking collectives: 122 us -> 60.6 us
  starting transfers between devices: 5.86 us -> 34 us
  waiting for transfers between devices: 48.9 us -> 73.2 us
  Pallas kernels: 26.6 us -> 29.4 us
    all_to_all x2 -> x1, blocking collectives: 122 us -> 60.6 us  [exchange(): lax.all_to_all(slabs, 'row', split_axis=0, concat_axis=0, tiled=True, axi...]
    ppermute x0 -> x15, waiting for transfers between devices: none -> 35.5 us  [local(): lax.ppermute(own[o], 'row', [(i, i ^ o) for i in range(devices)])]
    ppermute x0 -> x15, starting transfers between devices: none -> 19.3 us  [local(): lax.ppermute(own[o], 'row', [(i, i ^ o) for i in range(devices)])]
    all_to_all x2 -> x3, waiting for transfers between devices: 48.9 us -> 37.8 us  [exchange(): lax.all_to_all(slabs, 'row', split_axis=0, concat_axis=0, tiled=True, axi...]
    all_to_all x2 -> x3, starting transfers between devices: 5.86 us -> 14.7 us  [exchange(): lax.all_to_all(slabs, 'row', split_axis=0, concat_axis=0, tiled=True, axi...]
    pallas_call x7, Pallas kernels: 26.6 us -> 29.4 us  [call(): pl.pallas_call(kernel, out_shape=outs, in_specs=[WHOLE] * len(arrays) + [...]
    unnamed x46 -> x68, local copies, waits for them, and re-layouts: 10.3 us -> 10.3 us
  transfers between devices with their start and end apart: 2 -> 18, of which waited for: 2 -> 10; matrix products, arithmetic and copies ran while one was open for 0% -> 0% of each run, Pallas kernels for 2% -> 2%
where the time goes in v4:
time: 209 us; the launch traced here: 208 us
  waiting for transfers between devices  73.2 us (35%)
  blocking collectives  60.6 us (29%)
  starting transfers between devices  34 us (16%)
  Pallas kernels  29.4 us (14%)
  local copies, waits for them, and re-layouts  10.3 us (5%)
    all_to_all x1, blocking collectives, exchange(): lax.all_to_all(slabs, 'row', split_axis=0, concat_axis=0, tiled=True, axi...  60.6 us
    all_to_all x3, waiting for transfers between devices, exchange(): lax.all_to_all(slabs, 'row', split_axis=0, concat_axis=0, tiled=True, axi...  37.8 us
    ppermute x15, waiting for transfers between devices, local(): lax.ppermute(own[o], 'row', [(i, i ^ o) for i in range(devices)])  35.5 us
    pallas_call x7, Pallas kernels, call(): pl.pallas_call(kernel, out_shape=outs, in_specs=[WHOLE] * len(arrays) + [...  29.4 us
    ppermute x15, starting transfers between devices, local(): lax.ppermute(own[o], 'row', [(i, i ^ o) for i in range(devices)])  19.3 us
    all_to_all x3, starting transfers between devices, exchange(): lax.all_to_all(slabs, 'row', split_axis=0, concat_axis=0, tiled=True, axi...  14.7 us
    unnamed x68, local copies, waits for them, and re-layouts  10.3 us
  transfers between devices with their start and end apart: 18, of which 10 were waited for; matrix products, arithmetic and copies ran while one was open for 0% of the time, Pallas kernels for 2%

profile of v4, /device:TPU:0, one launch (start us, length us, event | category | flops | bytes accessed | tf_op | source)
XLA Modules:
  0.0 207.9 jit_solution(10881561763928300825)
XLA Ops:
  0.0 6.6 %shard_map.109 = (bf16[96,384]{1,0:T(8,128)(2,1)}, bf16[96,384]{1,0:T(8,128)(2,1)}, bf16[96,384]{1,0:T(8,128)(2,1)}, bf16[96,384]{1,0:T(8,128)(2,1)}, bf16[96,38...) custom-call(s32[384]{0:T(512)} %residue_mask.1, ...), custom_call_target="tpu_custom_call" | custom-call | flops 603979776 | bytes 4738048 | tf_op jit(solution)/shard_map/pallas_call | solution.py:344
  6.7 7.3 %all-to-all-start = ((bf16[32,96,384]{2,1,0:T(8,128)(2,1)}), bf16[32,96,384]{2,1,0:T(8,128)(2,1)S(1)}, u32[]{:S(2)}, u32[]{:S(2)}) async-start(bf16[32,96,384]{2,1,0:T(8,128)(2,1)} %get-tuple-element.30), calls=%async_computation | async-start | bytes 4718592 | tf_op jit(solution)/shard_map/all_to_all | solution.py:387
  14.0 0.3 collective-permute-start
  14.4 1.7 collective-permute-start.1
  16.0 0.0 collective-permute-start.2
  16.1 1.7 collective-permute-start.3
  17.7 0.1 collective-permute-start.4
  17.9 2.6 %collective-permute-start.5 = (bf16[96,384]{1,0:T(8,128)(2,1)S(1)}, bf16[96,384]{1,0:T(8,128)(2,1)S(1)}, u32[]{:S(2)}, u32[]{:S(2)}) collective-permute-start(bf16[96,384]{1,0:T(8,128)(2,1)S(1)} %copy-done.28), channel_id=1, source_target_pairs={{0,6},{1,7},{2,4},{3,5},{4,2},{5,3},{6,0},{7,1},{8,14},{9,15},{10,... | collective-permute-start | bytes 221192 | tf_op jit(solution)/shard_map/ppermute | solution.py:401
  20.4 13.1 %collective-permute-done.1.refs_2_ = bf16[96,384]{1,0:T(8,128)(2,1)S(1)} collective-permute-done((bf16[96,384]{1,0:T(8,128)(2,1)S(1)}, bf16[96,384]{1,0:T(8,128)(2,1)S(1)}, u32[]{:S(2)}, u32[]{:S(2)}) %collective-permute-start.1) | collective-permute-done | bytes 73760 | tf_op jit(solution)/shard_map/ppermute | solution.py:401
  33.6 0.6 collective-permute-start.6
  34.2 0.2 collective-permute-done.2.refs_3_
  34.4 0.3 collective-permute-start.7
  34.7 2.3 %collective-permute-start.8 = (bf16[96,384]{1,0:T(8,128)(2,1)S(1)}, bf16[96,384]{1,0:T(8,128)(2,1)S(1)}, u32[]{:S(2)}, u32[]{:S(2)}) collective-permute-start(bf16[96,384]{1,0:T(8,128)(2,1)S(1)} %copy-done.25), channel_id=1, source_target_pairs={{0,9},{1,8},{2,11},{3,10},{4,13},{5,12},{6,15},{7,14},{8,1},{9,0},... | collective-permute-start | bytes 221192 | tf_op jit(solution)/shard_map/ppermute | solution.py:401
  37.0 3.3 %collective-permute-start.9 = (bf16[96,384]{1,0:T(8,128)(2,1)S(1)}, bf16[96,384]{1,0:T(8,128)(2,1)S(1)}, u32[]{:S(2)}, u32[]{:S(2)}) collective-permute-start(bf16[96,384]{1,0:T(8,128)(2,1)S(1)} %copy-done.24), channel_id=1, source_target_pairs={{0,10},{1,11},{2,8},{3,9},{4,14},{5,15},{6,12},{7,13},{8,2},{9,3},... | collective-permute-start | bytes 221192 | tf_op jit(solution)/shard_map/ppermute | solution.py:401
  40.2 3.8 %collective-permute-done.5.refs_6_ = bf16[96,384]{1,0:T(8,128)(2,1)S(1)} collective-permute-done((bf16[96,384]{1,0:T(8,128)(2,1)S(1)}, bf16[96,384]{1,0:T(8,128)(2,1)S(1)}, u32[]{:S(2)}, u32[]{:S(2)}) %collective-permute-start.5) | collective-permute-done | bytes 73760 | tf_op jit(solution)/shard_map/ppermute | solution.py:401
  44.1 0.8 collective-permute-done.6.refs_7_
  44.9 10.3 %collective-permute-done.7.refs_8_ = bf16[96,384]{1,0:T(8,128)(2,1)S(1)} collective-permute-done((bf16[96,384]{1,0:T(8,128)(2,1)S(1)}, bf16[96,384]{1,0:T(8,128)(2,1)S(1)}, u32[]{:S(2)}, u32[]{:S(2)}) %collective-permute-start.7) | collective-permute-done | bytes 73760 | tf_op jit(solution)/shard_map/ppermute | solution.py:401
  55.2 2.0 collective-permute-start.12
  57.2 2.8 %collective-permute-start.13 = (bf16[96,384]{1,0:T(8,128)(2,1)}, bf16[96,384]{1,0:T(8,128)(2,1)S(1)}, u32[]{:S(2)}, u32[]{:S(2)}) collective-permute-start(bf16[96,384]{1,0:T(8,128)(2,1)} %get-tuple-element.45), channel_id=1, source_target_pairs={{0,14},{1,15},{2,12},{3,13},{4,10},{5,11},{6,8},{7,9},{8,6},{9,7},... | collective-permute-start | bytes 221192 | tf_op jit(solution)/shard_map/ppermute | solution.py:401
  60.1 1.7 collective-permute-start.14
  61.7 1.5 collective-permute-done.12.refs_13_
  63.2 2.9 %collective-permute-done.13.refs_14_ = bf16[96,384]{1,0:T(8,128)(2,1)S(1)} collective-permute-done((bf16[96,384]{1,0:T(8,128)(2,1)}, bf16[96,384]{1,0:T(8,128)(2,1)S(1)}, u32[]{:S(2)}, u32[]{:S(2)}) %collective-permute-start.13) | collective-permute-done | bytes 73760 | tf_op jit(solution)/shard_map/ppermute | solution.py:401
  66.1 2.7 %collective-permute-done.14.refs_15_ = bf16[96,384]{1,0:T(8,128)(2,1)S(1)} collective-permute-done((bf16[96,384]{1,0:T(8,128)(2,1)}, bf16[96,384]{1,0:T(8,128)(2,1)S(1)}, u32[]{:S(2)}, u32[]{:S(2)}) %collective-permute-start.14) | collective-permute-done | bytes 73760 | tf_op jit(solution)/shard_map/ppermute | solution.py:401
  68.8 8.0 %shard_map.110 = bf16[16,96,384]{2,1,0:T(8,128)(2,1)} custom-call(bf16[32,96,384]{2,1,0:T(8,128)(2,1)S(1)} %all-to-all-done.recv, bf16[96,384]{1,0:T(8,128)(2,1)S(1)} %copy-done.14, bf16[96,384]{1,0:T(8,128)(2,1)S(1)} %collective-permute-done.refs_1_, bf16[96,384]{1,0:T(8,128)(2,1)S(1)} %collective-permute-done.1.refs_2_, ...), custom_call_target="tpu_custom_call" | custom-call | flops 452984832 | bytes 4718592 | tf_op jit(solution)/shard_map/pallas_call | solution.py:344
  76.8 0.0 copy-start.16
  76.8 0.0 copy-start.19
  76.9 0.0 copy-start.20
  76.9 0.0 copy-start.22
  76.9 0.0 copy-start.23
  76.9 4.5 %all-to-all-start.1 = ((bf16[16,96,384]{2,1,0:T(8,128)(2,1)}), bf16[16,96,384]{2,1,0:T(8,128)(2,1)S(1)}, u32[]{:S(2)}, u32[]{:S(2)}) async-start(bf16[16,96,384]{2,1,0:T(8,128)(2,1)} %shard_map.110), calls=%async_computation.1 | async-start | bytes 2359296 | tf_op jit(solution)/shard_map/all_to_all | solution.py:387
  81.5 1.9 shard_map.111
  83.5 1.4 copy-done.7
  84.9 14.3 %all-to-all-done.1.recv = bf16[16,96,384]{2,1,0:T(8,128)(2,1)S(1)} async-done(((bf16[16,96,384]{2,1,0:T(8,128)(2,1)}), bf16[16,96,384]{2,1,0:T(8,128)(2,1)S(1)}, u32[]{:S(2)}, u32[]{:S(2)}) %all-to-all-start.1) | async-done | bytes 1179680 | tf_op jit(solution)/shard_map/all_to_all | solution.py:387
  99.2 1.7 copy-done.8
  100.8 3.8 %shard_map.112 = (bf16[32,96,384]{2,1,0:T(8,128)(2,1)S(1)}, bf16[12,128,384]{2,1,0:T(8,128)(2,1)S(1)}) custom-call(bf16[16,96,384]{2,1,0:T(8,128)(2,1)S(1)} %all-to-all-done.1.recv, f32[12,128,384]{2,1,0:T(8,128)S(1)} %copy-done.8, bf16[12,128,384]{2,1,0:T(8,128)(2,1)S(1)} %copy-done.3, f32[2,384]{1,0:T(2,128)S(1)} %copy-done.17, ...), custom_call_target="tpu_custom_call" | custom-call | flops 754974720 | bytes 8965120 | tf_op jit(solution)/shard_map/pallas_call | solution.py:344
  104.6 60.6 %all_to_all.20.recv = bf16[32,96,384]{2,1,0:T(8,128)(2,1)S(1)} all-to-all(bf16[32,96,384]{2,1,0:T(8,128)(2,1)S(1)} %get-tuple-element.53), channel_id=1, replica_groups=mesh['grp'=1,'row'=32] {'row'}, dimensions={0} | all-to-all | bytes 4718592 | tf_op jit(solution)/shard_map/all_to_all | solution.py:387
  165.2 5.3 %shard_map.113 = bf16[32,48,384]{2,1,0:T(8,128)(2,1)} custom-call(bf16[32,96,384]{2,1,0:T(8,128)(2,1)S(1)} %all_to_all.20.recv), custom_call_target="tpu_custom_call" | custom-call | flops 452984832 | bytes 3538944 | tf_op jit(solution)/shard_map/pallas_call | solution.py:344
  170.5 2.9 %all-to-all-start.3 = ((bf16[32,48,384]{2,1,0:T(8,128)(2,1)}), bf16[32,48,384]{2,1,0:T(8,128)(2,1)S(1)}, u32[]{:S(2)}, u32[]{:S(2)}) async-start(bf16[32,48,384]{2,1,0:T(8,128)(2,1)} %shard_map.113), calls=%async_computation.3 | async-start | bytes 2359296 | tf_op jit(solution)/shard_map/all_to_all | solution.py:387
  173.4 1.3 copy-done.1
  174.6 1.0 copy-done.5
  175.6 0.9 copy-done.10
  176.6 0.7 copy-done.18
  177.2 1.5 shard_map.114.gate
  178.7 23.5 %all-to-all-done.3.recv = bf16[32,48,384]{2,1,0:T(8,128)(2,1)S(1)} async-done(((bf16[32,48,384]{2,1,0:T(8,128)(2,1)}), bf16[32,48,384]{2,1,0:T(8,128)(2,1)S(1)}, u32[]{:S(2)}, u32[]{:S(2)}) %all-to-all-start.3) | async-done | bytes 1179680 | tf_op jit(solution)/shard_map/all_to_all | solution.py:387
  202.2 1.3 copy-done.2
  203.5 1.0 copy-done.6
  204.5 0.9 copy-done.11
  205.4 2.5 %shard_map.115 = bf16[12,384,128]{2,1,0:T(8,128)(2,1)} custom-call(bf16[32,48,384]{2,1,0:T(8,128)(2,1)S(1)} %all-to-all-done.3.recv, f32[12,128,384]{2,1,0:T(8,128)S(1)} %shard_map.114.gate, bf16[12,128,384]{2,1,0:T(8,128)(2,1)S(1)} %copy-done.2, bf16[896,128]{1,0:T(8,128)(2,1)S(1)} %copy-done.11, f32[7,128,128]{2,1,0:T(8,128)S(1)} %copy-done.6), custom_call_target="tpu_custom_call" | custom-call | flops 150994944 | bytes 6586368 | tf_op jit(solution)/shard_map/pallas_call | solution.py:344
  (64 shorter events, 0.1 us)
Async XLA Ops:
  6.6 7.4 %copy-start.33 = (bf16[96,384]{1,0:T(8,128)(2,1)S(1)}, bf16[96,384]{1,0:T(8,128)(2,1)}, u32[]{:S(2)}) copy-start(bf16[96,384]{1,0:T(8,128)(2,1)} %get-tuple-element.32) | copy-start | bytes 221188
  6.6 7.7 %copy-start.32 = (bf16[96,384]{1,0:T(8,128)(2,1)S(1)}, bf16[96,384]{1,0:T(8,128)(2,1)}, u32[]{:S(2)}) copy-start(bf16[96,384]{1,0:T(8,128)(2,1)} %get-tuple-element.33) | copy-start | bytes 221188
  6.6 9.4 %copy-start.31 = (bf16[96,384]{1,0:T(8,128)(2,1)S(1)}, bf16[96,384]{1,0:T(8,128)(2,1)}, u32[]{:S(2)}) copy-start(bf16[96,384]{1,0:T(8,128)(2,1)} %get-tuple-element.34) | copy-start | bytes 221188
  6.6 9.4 %copy-start.30 = (bf16[96,384]{1,0:T(8,128)(2,1)S(1)}, bf16[96,384]{1,0:T(8,128)(2,1)}, u32[]{:S(2)}) copy-start(bf16[96,384]{1,0:T(8,128)(2,1)} %get-tuple-element.35) | copy-start | bytes 221188
  6.6 11.1 %copy-start.29 = (bf16[96,384]{1,0:T(8,128)(2,1)S(1)}, bf16[96,384]{1,0:T(8,128)(2,1)}, u32[]{:S(2)}) copy-start(bf16[96,384]{1,0:T(8,128)(2,1)} %get-tuple-element.36) | copy-start | bytes 221188
  6.6 11.2 %copy-start.28 = (bf16[96,384]{1,0:T(8,128)(2,1)S(1)}, bf16[96,384]{1,0:T(8,128)(2,1)}, u32[]{:S(2)}) copy-start(bf16[96,384]{1,0:T(8,128)(2,1)} %get-tuple-element.37) | copy-start | bytes 221188
  6.7 26.9 %copy-start.27 = (bf16[96,384]{1,0:T(8,128)(2,1)S(1)}, bf16[96,384]{1,0:T(8,128)(2,1)}, u32[]{:S(2)}) copy-start(bf16[96,384]{1,0:T(8,128)(2,1)} %get-tuple-element.38) | copy-start | bytes 221188
  6.7 27.7 %copy-start.26 = (bf16[96,384]{1,0:T(8,128)(2,1)S(1)}, bf16[96,384]{1,0:T(8,128)(2,1)}, u32[]{:S(2)}) copy-start(bf16[96,384]{1,0:T(8,128)(2,1)} %get-tuple-element.39) | copy-start | bytes 221188
  6.7 28.0 %copy-start.25 = (bf16[96,384]{1,0:T(8,128)(2,1)S(1)}, bf16[96,384]{1,0:T(8,128)(2,1)}, u32[]{:S(2)}) copy-start(bf16[96,384]{1,0:T(8,128)(2,1)} %get-tuple-element.40) | copy-start | bytes 221188
  6.7 30.3 %copy-start.24 = (bf16[96,384]{1,0:T(8,128)(2,1)S(1)}, bf16[96,384]{1,0:T(8,128)(2,1)}, u32[]{:S(2)}) copy-start(bf16[96,384]{1,0:T(8,128)(2,1)} %get-tuple-element.41) | copy-start | bytes 221188
  6.7 62.1 %copy-start.14 = (bf16[96,384]{1,0:T(8,128)(2,1)S(1)}, bf16[96,384]{1,0:T(8,128)(2,1)}, u32[]{:S(2)}) copy-start(bf16[96,384]{1,0:T(8,128)(2,1)} %get-tuple-element.31.refs_0_) | copy-start | bytes 221188
  6.7 62.1 %all-to-all-start = ((bf16[32,96,384]{2,1,0:T(8,128)(2,1)}), bf16[32,96,384]{2,1,0:T(8,128)(2,1)S(1)}, u32[]{:S(2)}, u32[]{:S(2)}) async-start(bf16[32,96,384]{2,1,0:T(8,128)(2,1)} %get-tuple-element.30), calls=%async_computation | async-start | bytes 4718592 | tf_op jit(solution)/shard_map/all_to_all | solution.py:387
  14.0 3.8 %collective-permute-start = (bf16[96,384]{1,0:T(8,128)(2,1)S(1)}, bf16[96,384]{1,0:T(8,128)(2,1)S(1)}, u32[]{:S(2)}, u32[]{:S(2)}) collective-permute-start(bf16[96,384]{1,0:T(8,128)(2,1)S(1)} %copy-done.33), channel_id=1, source_target_pairs={{0,1},{1,0},{2,3},{3,2},{4,5},{5,4},{6,7},{7,6},{8,9},{9,8},{10,11... | collective-permute-start | bytes 221192 | tf_op jit(solution)/shard_map/ppermute | solution.py:401
  14.4 19.2 %collective-permute-start.1 = (bf16[96,384]{1,0:T(8,128)(2,1)S(1)}, bf16[96,384]{1,0:T(8,128)(2,1)S(1)}, u32[]{:S(2)}, u32[]{:S(2)}) collective-permute-start(bf16[96,384]{1,0:T(8,128)(2,1)S(1)} %copy-done.32), channel_id=1, source_target_pairs={{0,2},{1,3},{2,0},{3,1},{4,6},{5,7},{6,4},{7,5},{8,10},{9,11},{10,... | collective-permute-start | bytes 221192 | tf_op jit(solution)/shard_map/ppermute | solution.py:401
  16.0 18.4 %collective-permute-start.2 = (bf16[96,384]{1,0:T(8,128)(2,1)S(1)}, bf16[96,384]{1,0:T(8,128)(2,1)S(1)}, u32[]{:S(2)}, u32[]{:S(2)}) collective-permute-start(bf16[96,384]{1,0:T(8,128)(2,1)S(1)} %copy-done.31), channel_id=1, source_target_pairs={{0,3},{1,2},{2,1},{3,0},{4,7},{5,6},{6,5},{7,4},{8,11},{9,10},{10,... | collective-permute-start | bytes 221192 | tf_op jit(solution)/shard_map/ppermute | solution.py:401
  16.1 18.6 %collective-permute-start.3 = (bf16[96,384]{1,0:T(8,128)(2,1)S(1)}, bf16[96,384]{1,0:T(8,128)(2,1)S(1)}, u32[]{:S(2)}, u32[]{:S(2)}) collective-permute-start(bf16[96,384]{1,0:T(8,128)(2,1)S(1)} %copy-done.30), channel_id=1, source_target_pairs={{0,4},{1,5},{2,6},{3,7},{4,0},{5,1},{6,2},{7,3},{8,12},{9,13},{10,... | collective-permute-start | bytes 221192 | tf_op jit(solution)/shard_map/ppermute | solution.py:401
  17.7 19.2 %collective-permute-start.4 = (bf16[96,384]{1,0:T(8,128)(2,1)S(1)}, bf16[96,384]{1,0:T(8,128)(2,1)S(1)}, u32[]{:S(2)}, u32[]{:S(2)}) collective-permute-start(bf16[96,384]{1,0:T(8,128)(2,1)S(1)} %copy-done.29), channel_id=1, source_target_pairs={{0,5},{1,4},{2,7},{3,6},{4,1},{5,0},{6,3},{7,2},{8,13},{9,12},{10,... | collective-permute-start | bytes 221192 | tf_op jit(solution)/shard_map/ppermute | solution.py:401
  17.9 26.2 %collective-permute-start.5 = (bf16[96,384]{1,0:T(8,128)(2,1)S(1)}, bf16[96,384]{1,0:T(8,128)(2,1)S(1)}, u32[]{:S(2)}, u32[]{:S(2)}) collective-permute-start(bf16[96,384]{1,0:T(8,128)(2,1)S(1)} %copy-done.28), channel_id=1, source_target_pairs={{0,6},{1,7},{2,4},{3,5},{4,2},{5,3},{6,0},{7,1},{8,14},{9,15},{10,... | collective-permute-start | bytes 221192 | tf_op jit(solution)/shard_map/ppermute | solution.py:401
  33.6 11.3 %collective-permute-start.6 = (bf16[96,384]{1,0:T(8,128)(2,1)S(1)}, bf16[96,384]{1,0:T(8,128)(2,1)S(1)}, u32[]{:S(2)}, u32[]{:S(2)}) collective-permute-start(bf16[96,384]{1,0:T(8,128)(2,1)S(1)} %copy-done.27), channel_id=1, source_target_pairs={{0,7},{1,6},{2,5},{3,4},{4,3},{5,2},{6,1},{7,0},{8,15},{9,14},{10,... | collective-permute-start | bytes 221192 | tf_op jit(solution)/shard_map/ppermute | solution.py:401
  34.4 20.8 %collective-permute-start.7 = (bf16[96,384]{1,0:T(8,128)(2,1)S(1)}, bf16[96,384]{1,0:T(8,128)(2,1)S(1)}, u32[]{:S(2)}, u32[]{:S(2)}) collective-permute-start(bf16[96,384]{1,0:T(8,128)(2,1)S(1)} %copy-done.26), channel_id=1, source_target_pairs={{0,8},{1,9},{2,10},{3,11},{4,12},{5,13},{6,14},{7,15},{8,0},{9,1},... | collective-permute-start | bytes 221192 | tf_op jit(solution)/shard_map/ppermute | solution.py:401
  34.7 22.6 %collective-permute-start.8 = (bf16[96,384]{1,0:T(8,128)(2,1)S(1)}, bf16[96,384]{1,0:T(8,128)(2,1)S(1)}, u32[]{:S(2)}, u32[]{:S(2)}) collective-permute-start(bf16[96,384]{1,0:T(8,128)(2,1)S(1)} %copy-done.25), channel_id=1, source_target_pairs={{0,9},{1,8},{2,11},{3,10},{4,13},{5,12},{6,15},{7,14},{8,1},{9,0},... | collective-permute-start | bytes 221192 | tf_op jit(solution)/shard_map/ppermute | solution.py:401
  37.0 23.1 %collective-permute-start.9 = (bf16[96,384]{1,0:T(8,128)(2,1)S(1)}, bf16[96,384]{1,0:T(8,128)(2,1)S(1)}, u32[]{:S(2)}, u32[]{:S(2)}) collective-permute-start(bf16[96,384]{1,0:T(8,128)(2,1)S(1)} %copy-done.24), channel_id=1, source_target_pairs={{0,10},{1,11},{2,8},{3,9},{4,14},{5,15},{6,12},{7,13},{8,2},{9,3},... | collective-permute-start | bytes 221192 | tf_op jit(solution)/shard_map/ppermute | solution.py:401
  44.1 17.7 %collective-permute-start.10 = (bf16[96,384]{1,0:T(8,128)(2,1)}, bf16[96,384]{1,0:T(8,128)(2,1)S(1)}, u32[]{:S(2)}, u32[]{:S(2)}) collective-permute-start(bf16[96,384]{1,0:T(8,128)(2,1)} %get-tuple-element.42), channel_id=1, source_target_pairs={{0,11},{1,10},{2,9},{3,8},{4,15},{5,14},{6,13},{7,12},{8,3},{9,2},... | collective-permute-start | bytes 221192 | tf_op jit(solution)/shard_map/ppermute | solution.py:401
  44.9 16.9 %collective-permute-start.11 = (bf16[96,384]{1,0:T(8,128)(2,1)}, bf16[96,384]{1,0:T(8,128)(2,1)S(1)}, u32[]{:S(2)}, u32[]{:S(2)}) collective-permute-start(bf16[96,384]{1,0:T(8,128)(2,1)} %get-tuple-element.43), channel_id=1, source_target_pairs={{0,12},{1,13},{2,14},{3,15},{4,8},{5,9},{6,10},{7,11},{8,4},{9,5},... | collective-permute-start | bytes 221192 | tf_op jit(solution)/shard_map/ppermute | solution.py:401
  55.2 8.0 %collective-permute-start.12 = (bf16[96,384]{1,0:T(8,128)(2,1)}, bf16[96,384]{1,0:T(8,128)(2,1)S(1)}, u32[]{:S(2)}, u32[]{:S(2)}) collective-permute-start(bf16[96,384]{1,0:T(8,128)(2,1)} %get-tuple-element.44), channel_id=1, source_target_pairs={{0,13},{1,12},{2,15},{3,14},{4,9},{5,8},{6,11},{7,10},{8,5},{9,4},... | collective-permute-start | bytes 221192 | tf_op jit(solution)/shard_map/ppermute | solution.py:401
  57.2 8.9 %collective-permute-start.13 = (bf16[96,384]{1,0:T(8,128)(2,1)}, bf16[96,384]{1,0:T(8,128)(2,1)S(1)}, u32[]{:S(2)}, u32[]{:S(2)}) collective-permute-start(bf16[96,384]{1,0:T(8,128)(2,1)} %get-tuple-element.45), channel_id=1, source_target_pairs={{0,14},{1,15},{2,12},{3,13},{4,10},{5,11},{6,8},{7,9},{8,6},{9,7},... | collective-permute-start | bytes 221192 | tf_op jit(solution)/shard_map/ppermute | solution.py:401
  60.1 8.8 %collective-permute-start.14 = (bf16[96,384]{1,0:T(8,128)(2,1)}, bf16[96,384]{1,0:T(8,128)(2,1)S(1)}, u32[]{:S(2)}, u32[]{:S(2)}) collective-permute-start(bf16[96,384]{1,0:T(8,128)(2,1)} %get-tuple-element.46), channel_id=1, source_target_pairs={{0,15},{1,14},{2,13},{3,12},{4,11},{5,10},{6,9},{7,8},{8,7},{9,6},... | collective-permute-start | bytes 221192 | tf_op jit(solution)/shard_map/ppermute | solution.py:401
  76.8 4.6 %copy-start.3 = (bf16[12,128,384]{2,1,0:T(8,128)(2,1)S(1)}, bf16[12,128,384]{2,1,0:T(8,128)(2,1)}, u32[]{:S(2)}) copy-start(bf16[12,128,384]{2,1,0:T(8,128)(2,1)} %get-tuple-element.47.x_t) | copy-start | bytes 3538948
  76.8 4.6 %copy-start.12 = (bf16[2,128,512]{2,1,0:T(8,128)(2,1)S(1)}, bf16[2,128,512]{2,1,0:T(8,128)(2,1)}, u32[]{:S(2)}) copy-start(bf16[2,128,512]{2,1,0:T(8,128)(2,1)} %w_ab.3) | copy-start | bytes 786436
  76.8 4.6 %copy-start.13 = (f32[2,16,128]{2,1,0:T(8,128)S(1)}, f32[2,16,128]{2,1,0:T(8,128)}, u32[]{:S(2)}) copy-start(f32[2,16,128]{2,1,0:T(8,128)} %get-tuple-element.49.row_marks) | copy-start | bytes 49156
  76.8 4.6 %copy-start.15 = (bf16[2,128,128]{2,1,0:T(8,128)(2,1)S(1)}, bf16[2,128,128]{2,1,0:T(8,128)(2,1)}, u32[]{:S(2)}) copy-start(bf16[2,128,128]{2,1,0:T(8,128)(2,1)} %w_gate.1) | copy-start | bytes 196612
  76.8 4.6 %copy-start.16 = (bf16[2,128,128]{2,1,0:T(8,128)(2,1)S(1)}, bf16[2,128,128]{2,1,0:T(8,128)(2,1)}, u32[]{:S(2)}) copy-start(bf16[2,128,128]{2,1,0:T(8,128)(2,1)} %w_out.1) | copy-start | bytes 196612
  76.8 4.6 %copy-start.17 = (f32[2,384]{1,0:T(2,128)S(1)}, f32[2,384]{1,0:T(2,128)}, u32[]{:S(2)}) copy-start(f32[2,384]{1,0:T(2,128)} %get-tuple-element.48.marks) | copy-start | bytes 9220
  76.8 4.6 %copy-start.19 = (f32[2,128]{1,0:T(2,128)S(1)}, f32[2,128]{1,0:T(2,128)}, u32[]{:S(2)}) copy-start(f32[2,128]{1,0:T(2,128)} %gain.3) | copy-start | bytes 3076
  76.9 4.6 %copy-start.20 = (f32[2,128]{1,0:T(2,128)S(1)}, f32[2,128]{1,0:T(2,128)}, u32[]{:S(2)}) copy-start(f32[2,128]{1,0:T(2,128)} %bias.3) | copy-start | bytes 3076
  76.9 4.6 %copy-start.21 = (f32[2,128]{1,0:T(2,128)S(1)}, f32[2,128]{1,0:T(2,128)}, u32[]{:S(2)}) copy-start(f32[2,128]{1,0:T(2,128)} %embed.3) | copy-start | bytes 3076
  76.9 4.6 %copy-start.22 = (f32[2,128]{1,0:T(2,128)S(1)}, f32[2,128]{1,0:T(2,128)}, u32[]{:S(2)}) copy-start(f32[2,128]{1,0:T(2,128)} %mid_gain.1) | copy-start | bytes 3076
  76.9 4.6 %copy-start.23 = (f32[2,128]{1,0:T(2,128)S(1)}, f32[2,128]{1,0:T(2,128)}, u32[]{:S(2)}) copy-start(f32[2,128]{1,0:T(2,128)} %mid_bias.1) | copy-start | bytes 3076
  76.9 22.3 %all-to-all-start.1 = ((bf16[16,96,384]{2,1,0:T(8,128)(2,1)}), bf16[16,96,384]{2,1,0:T(8,128)(2,1)S(1)}, u32[]{:S(2)}, u32[]{:S(2)}) async-start(bf16[16,96,384]{2,1,0:T(8,128)(2,1)} %shard_map.110), calls=%async_computation.1 | async-start | bytes 2359296 | tf_op jit(solution)/shard_map/all_to_all | solution.py:387
  83.4 1.4 copy-start.7
  84.8 19.8 %copy-start.4 = (f32[7,128,128]{2,1,0:T(8,128)}, f32[7,128,128]{2,1,0:T(8,128)S(1)}, u32[]{:S(2)}) copy-start(f32[7,128,128]{2,1,0:T(8,128)S(1)} %get-tuple-element.52.vectors.columns) | copy-start | bytes 1376260
  84.8 19.8 %copy-start.9 = (bf16[896,128]{1,0:T(8,128)(2,1)}, bf16[896,128]{1,0:T(8,128)(2,1)S(1)}, u32[]{:S(2)}) copy-start(bf16[896,128]{1,0:T(8,128)(2,1)S(1)} %get-tuple-element.51.weights) | copy-start | bytes 688132
  99.2 1.7 copy-start.8
  104.6 60.6 %copy-start = (bf16[12,128,384]{2,1,0:T(8,128)(2,1)}, bf16[12,128,384]{2,1,0:T(8,128)(2,1)S(1)}, u32[]{:S(2)}) copy-start(bf16[12,128,384]{2,1,0:T(8,128)(2,1)S(1)} %get-tuple-element.54.x_t) | copy-start | bytes 3538948
  170.5 31.7 %all-to-all-start.3 = ((bf16[32,48,384]{2,1,0:T(8,128)(2,1)}), bf16[32,48,384]{2,1,0:T(8,128)(2,1)S(1)}, u32[]{:S(2)}, u32[]{:S(2)}) async-start(bf16[32,48,384]{2,1,0:T(8,128)(2,1)} %shard_map.113), calls=%async_computation.3 | async-start | bytes 2359296 | tf_op jit(solution)/shard_map/all_to_all | solution.py:387
  173.3 1.3 copy-start.1
  174.6 1.0 copy-start.5
  202.2 1.3 copy-start.2
  (4 other events, 3.6 us)

commit v5 on v4

--- a/solution.py
+++ b/solution.py
@@ -71,20 +71,30 @@
                 out[d, side * half : (side + 1) * half, columns] = slabs[j, start : start + half, :].astype(BF16)
 
 
-def write_crossing(slabs, out, own):
-    devices, depth, width = out.shape
-    half = devices // 2
+def write_crossing(slabs, left, right, out, own, sems):
+    half, depth, width = left.shape
     me = lax.axis_index("row")
-    side_rows = half * depth
-    for d in range(devices):
-        side = jnp.where(me // half == d // half, 0, side_rows)
-        start = pl.multiple_of(side + d % half * depth, 8)
-        for j, columns in blocks(width):
-            out[d, :, columns] = slabs[j, pl.ds(start, depth), :].astype(BF16)
-    for o, ref in enumerate(own):
-        start = pl.multiple_of(side_rows + (me % half ^ o) * depth, 8)
-        for j, columns in blocks(width):
-            ref[:, columns] = slabs[j, pl.ds(start, depth), :].astype(BF16)
+    mine = me // half * half
+    copies = []
+
+    def send(src, dst):
+        copies.append(pltpu.make_async_copy(src, dst, sems.at[len(copies)]))
+        copies[-1].start()
+
+    parts = [slice(q, min(q + half // 4, half)) for q in range(0, half, half // 4)]
+    for side, ref, first in ((1, right, half - mine), (0, left, mine)):
+        for part in parts:
+            for q in range(part.start, part.stop):
+                start = (side * half + q) * depth
+                for j, columns in blocks(width):
+                    ref[q, :, columns] = slabs[j, start : start + depth, :].astype(BF16)
+            size = part.stop - part.start
+            send(ref.at[pl.ds(part.start, size)], out.at[pl.ds(first + part.start, size)])
+        if side == 1:
+            for o, dst in enumerate(own):
+                send(ref.at[me % half ^ o], dst)
+    for copy in copies:
+        copy.wait()
 
 
 def widen(recv, wide):
@@ -116,8 +126,8 @@
 
 
 def first_kernel(residue_mask, chain_ids, x_in, gain, bias, embed, w_ab, *refs):
-    own = refs[:-16]
-    out, x_t, marks, row_marks, x, w, vectors, mask_ids, chain, w_t, g, b, e, slabs, sems, x_sems = refs[-16:]
+    own, (out, x_out, marks, row_marks) = refs[:-20], refs[-20:-16]
+    x, x_t, w, vectors, mask_ids, chain, w_t, g, b, e, slabs, left, right, sems, x_sems, out_sems = refs[-16:]
     rows, width, _ = x.shape
     smalls = fetch(
         [
@@ -153,11 +163,18 @@
                 parts.append(norm_input(values, same, g[...], b[...], e[...]))
         return jnp.concatenate(parts, axis=1)
 
+    turned = []
+
     def consume(group, normed):
+        part = pl.ds(group[0], len(group))
+        turned.append(pltpu.make_async_copy(x_t.at[part], x_out.at[part], x_sems.at[group[0] // GROUP]))
+        turned[-1].start()
         project(group, normed, marks, row_marks, w_t[...], slabs)
 
     overlapped(rows, prepare, consume)
-    write_crossing(slabs, out, own)
+    write_crossing(slabs, left, right, out, own, out_sems)
+    for copy in turned:
+        copy.wait()
 
 
 def write_gates(x_t, marks, row_marks, g, b, e, w_t, out):
@@ -215,20 +232,31 @@
 
 
 def first_products_kernel(rows, recv, *refs):
-    own, (out, left_wide, right_wide, natural, turned) = refs[:-5], refs[-5:]
+    own, (out, own_recv, left_wide, right_wide, natural, turned, sems) = refs[:-7], refs[-7:]
     devices, depth, width = recv.shape
     half = devices // 2
     channels = depth // rows
     me = lax.axis_index("row")
     mine = me // half * half
     other = half - mine
-    for q in range(half):
-        to_other = pl.multiple_of((other + q) * depth, 8)
-        to_own = pl.multiple_of((mine + (me % half ^ q)) * depth, 8)
-        for j, columns in blocks(width):
-            left_wide[j, q * depth : (q + 1) * depth, :] = recv[mine + q, :, columns].astype(F32)
-            right_wide[j, pl.ds(to_other, depth), :] = recv[other + q, :, columns].astype(F32)
-            right_wide[j, pl.ds(to_own, depth), :] = own[q][:, columns].astype(F32)
+    copies = fetch([(src, own_recv.at[me % half ^ o]) for o, src in enumerate(own)], sems)
+
+    def widen_part(wide, first, ref, start):
+        def step(i, carry):
+            for k in range(4):
+                q = i * 4 + k
+                place = pl.multiple_of((first + q) * depth, 8)
+                for j, columns in blocks(width):
+                    wide[j, pl.ds(place, depth), :] = ref[start + q, :, columns].astype(F32)
+            return carry
+
+        lax.fori_loop(0, half // 4, step, 0)
+
+    widen_part(left_wide, 0, recv, mine)
+    widen_part(right_wide, other, recv, other)
+    for copy in copies:
+        copy.wait()
+    widen_part(right_wide, mine, own_recv, 0)
     for c in range(channels):
         left, right = [], []
         for j, _ in blocks(width):
@@ -286,9 +314,8 @@
             out[s, :, columns] = turned[j, s * channels * rows : (s + 1) * channels * rows, :].astype(BF16)
 
 
-def finish(layer, group, width, tri, gate, x_t, weights, vectors):
+def finish(group, width, tri, gate, x_t, w_t, gain, bias):
     rows = tri.shape[1] // HC
-    gain, bias = vectors[MID_GAIN[layer]], vectors[MID_BIAS[layer]]
     normed = jnp.concatenate(
         [
             norm_channels(tri[j, pl.ds(r, HC, stride=rows), :], gain, bias).astype(BF16)
@@ -297,7 +324,7 @@
         ],
         axis=1,
     )
-    branch = jnp.dot(weights[W_OUT[layer], :], normed, preferred_element_type=F32)
+    branch = jnp.dot(w_t, normed, preferred_element_type=F32)
     return {
         (r, j): (
             x_t[r, :, columns].astype(F32)
@@ -313,7 +340,8 @@
     widen(recv, tri)
 
     def prepare(group):
-        states = finish(0, group, width, tri, gate, x_t, weights, vectors)
+        mid = (vectors[MID_GAIN[0]], vectors[MID_BIAS[0]])
+        states = finish(group, width, tri, gate, x_t, weights[W_OUT[0], :], *mid)
         parts = []
         for r in group:
             for j, columns in blocks(width):
@@ -331,21 +359,46 @@
     write_slabs(slabs, out)
 
 
-def last_kernel(recv, gate, x_t, weights, vectors, out, tri):
+def last_kernel(recv_in, gate_in, x_in, weights_in, vectors_in, out, recv, gate, x_t, weights, vectors, tri, result, sems):
     rows, _, width = x_t.shape
-    widen(recv, tri)
-    for group in groups(rows):
-        for (r, j), state in finish(1, group, width, tri, gate, x_t, weights, vectors).items():
-            out[r, j * 128 : (j + 1) * 128, :] = state.astype(F32).T.astype(BF16)
-
-
-def call(kernel, outs, scratch, arrays, anywhere, flops, limit=VMEM_LIMIT):
+    devices, depth, _ = recv.shape
+    parts = [pl.ds(d, devices // 4) for d in range(0, devices, devices // 4)]
+    todo = groups(rows)
+    pairs = [(recv_in.at[part], recv.at[part]) for part in parts]
+    pairs.append((weights_in.at[W_OUT[1]], weights))
+    pairs += [(vectors_in.at[i], vectors.at[k]) for k, i in enumerate((MID_GAIN[1], MID_BIAS[1]))]
+    for group in todo:
+        part = pl.ds(group[0], len(group))
+        pairs += [(gate_in.at[part], gate.at[part]), (x_in.at[part], x_t.at[part])]
+    copies = fetch(pairs, sems)
+    for k, part in enumerate(parts):
+        copies[k].wait()
+        for d in range(part.start, part.start + part.size):
+            for j, columns in blocks(width):
+                tri[j, d * depth : (d + 1) * depth, :] = recv[d, :, columns].astype(F32)
+    for copy in copies[4:7]:
+        copy.wait()
+    done = []
+    for k, group in enumerate(todo):
+        for copy in copies[7 + 2 * k : 9 + 2 * k]:
+            copy.wait()
+        states = finish(group, width, tri, gate, x_t, weights[...], vectors[0], vectors[1])
+        for (r, j), state in states.items():
+            result[r, j * 128 : (j + 1) * 128, :] = state.astype(F32).T.astype(BF16)
+        part = pl.ds(group[0], len(group))
+        done.append(pltpu.make_async_copy(result.at[part], out.at[part], sems.at[k]))
+        done[-1].start()
+    for copy in done:
+        copy.wait()
+
+
+def call(kernel, outs, scratch, arrays, anywhere, flops, limit=VMEM_LIMIT, far=0):
     size = sum(a.size * a.dtype.itemsize for a in list(arrays) + list(outs))
     return pl.pallas_call(
         kernel,
         out_shape=outs,
         in_specs=[WHOLE] * len(arrays) + [ANYWHERE] * len(anywhere),
-        out_specs=[WHOLE] * len(outs),
+        out_specs=[ANYWHERE] * far + [WHOLE] * (len(outs) - far),
         scratch_shapes=scratch,
         compiler_params=pltpu.CompilerParams(vmem_limit_bytes=limit),
         cost_estimate=pl.CostEstimate(flops=flops, bytes_accessed=size, transcendentals=0),
@@ -392,10 +445,11 @@
     *own, slabs, x_t, marks, row_marks = call(
         first_kernel, [own_slab] * half + [sent, state_t, mark, row_mark],
         [
-            pltpu.VMEM(pair.shape, BF16), w_wide, pltpu.VMEM((3, 2, C), F32), ids, ids, pltpu.VMEM((4 * HC, C), BF16),
-            vector, vector, vector, slabs_wide, sems(6), sems(len(groups(rows))),
-        ],
-        (), (residue_mask, chain_ids, pair, *norms, w_ab), 2 * pairs * C * 4 * HC, FIRST_VMEM_LIMIT,
+            pltpu.VMEM(pair.shape, BF16), pltpu.VMEM(state_t.shape, BF16), w_wide, pltpu.VMEM((3, 2, C), F32), ids, ids,
+            pltpu.VMEM((4 * HC, C), BF16), vector, vector, vector, slabs_wide, pltpu.VMEM(own_back.shape, BF16),
+            pltpu.VMEM(own_back.shape, BF16), sems(6), sems(len(groups(rows))), sems(8 + half),
+        ],
+        (), (residue_mask, chain_ids, pair, *norms, w_ab), 2 * pairs * C * 4 * HC, FIRST_VMEM_LIMIT, half + 2,
     )
     recv = exchange(slabs)
     own = [own[0]] + [lax.ppermute(own[o], "row", [(i, i ^ o) for i in range(devices)]) for o in range(1, half)]
@@ -407,9 +461,10 @@
     products = call(
         functools.partial(first_products_kernel, rows), [own_back],
         [
-            tri_wide, slabs_wide, pltpu.VMEM((2 * channels, cols, width, 128), F32), tri_wide,
-        ],
-        (recv, *own), (), 2 * channels * width**3, PRODUCTS_VMEM_LIMIT,
+            pltpu.VMEM(own_back.shape, BF16), tri_wide, slabs_wide, pltpu.VMEM((2 * channels, cols, width, 128), F32),
+            tri_wide, sems(half),
+        ],
+        (recv,), own, 2 * channels * width**3, PRODUCTS_VMEM_LIMIT,
     )[0]
     tri = exchange(products, halves)
     slabs, x_t = call(
@@ -426,8 +481,13 @@
     )[0]
     tri = exchange(products)
     return call(
-        last_kernel, [jax.ShapeDtypeStruct(pair.shape, BF16)], [tri_wide], (tri, gate, x_t, weights, vectors), (),
-        2 * pairs * C * C,
+        last_kernel, [jax.ShapeDtypeStruct(pair.shape, BF16)],
+        [
+            pltpu.VMEM(back.shape, BF16), pltpu.VMEM(gate_t.shape, F32), pltpu.VMEM(state_t.shape, BF16),
+            pltpu.VMEM((HC, C), BF16), pltpu.VMEM((2, C, 128), F32), tri_wide, pltpu.VMEM(pair.shape, BF16),
+            sems(7 + 2 * len(groups(rows))),
+        ],
+        (), (tri, gate, x_t, weights, vectors), 2 * pairs * C * C, FIRST_VMEM_LIMIT, 1,
     )[0]
 
 

time: 209 us -> 214 us (1.024)
  Pallas kernels: 29.4 us -> 34.1 us
    pallas_call x7, Pallas kernels: 29.4 us -> 34.1 us  [call(): pl.pallas_call(kernel, out_shape=outs, in_specs=[WHOLE] * len(arrays) + [...]
    unnamed x68 -> x70, local copies, waits for them, and re-layouts: 10.3 us -> 9.71 us
where the time goes in v5:
time: 214 us; the launch traced here: 213 us
  waiting for transfers between devices  74.3 us (35%)
  blocking collectives  60.6 us (28%)
  Pallas kernels  34.1 us (16%)
  starting transfers between devices  34.1 us (16%)
  local copies, waits for them, and re-layouts  9.71 us (5%)
    all_to_all x1, blocking collectives, exchange(): lax.all_to_all(slabs, 'row', split_axis=0, concat_axis=0, tiled=True, axi...  60.6 us
    all_to_all x3, waiting for transfers between devices, exchange(): lax.all_to_all(slabs, 'row', split_axis=0, concat_axis=0, tiled=True, axi...  38.9 us
    ppermute x15, waiting for transfers between devices, local(): lax.ppermute(own[o], 'row', [(i, i ^ o) for i in range(devices)])  35.5 us
    pallas_call x7, Pallas kernels, call(): pl.pallas_call(kernel, out_shape=outs, in_specs=[WHOLE] * len(arrays) + [...  34.1 us
    ppermute x15, starting transfers between devices, local(): lax.ppermute(own[o], 'row', [(i, i ^ o) for i in range(devices)])  19.3 us
    all_to_all x3, starting transfers between devices, exchange(): lax.all_to_all(slabs, 'row', split_axis=0, concat_axis=0, tiled=True, axi...  14.8 us
    unnamed x70, local copies, waits for them, and re-layouts  9.71 us
  transfers between devices with their start and end apart: 18, of which 10 were waited for; matrix products, arithmetic and copies ran while one was open for 0% of the time, Pallas kernels for 2%

profile of v5, /device:TPU:0, one launch (start us, length us, event | category | flops | bytes accessed | tf_op | source)
XLA Modules:
  0.0 213.4 jit_solution(4373443881908471453)
XLA Ops:
  0.0 7.4 %shard_map.109 = (bf16[96,384]{1,0:T(8,128)(2,1)}, bf16[96,384]{1,0:T(8,128)(2,1)}, bf16[96,384]{1,0:T(8,128)(2,1)}, bf16[96,384]{1,0:T(8,128)(2,1)}, bf16[96,38...) custom-call(s32[384]{0:T(512)} %residue_mask.1, ...), custom_call_target="tpu_custom_call" | custom-call | flops 603979776 | bytes 4738048 | tf_op jit(solution)/shard_map/pallas_call | solution.py:397
  7.6 7.3 %all-to-all-start = ((bf16[32,96,384]{2,1,0:T(8,128)(2,1)}), bf16[32,96,384]{2,1,0:T(8,128)(2,1)S(1)}, u32[]{:S(2)}, u32[]{:S(2)}) async-start(bf16[32,96,384]{2,1,0:T(8,128)(2,1)} %get-tuple-element.30), calls=%async_computation | async-start | bytes 4718592 | tf_op jit(solution)/shard_map/all_to_all | solution.py:440
  14.9 0.3 collective-permute-start
  15.2 1.7 collective-permute-start.1
  16.9 0.0 collective-permute-start.2
  16.9 1.7 collective-permute-start.3
  18.6 0.1 collective-permute-start.4
  18.7 2.6 %collective-permute-start.5 = (bf16[96,384]{1,0:T(8,128)(2,1)S(1)}, bf16[96,384]{1,0:T(8,128)(2,1)S(1)}, u32[]{:S(2)}, u32[]{:S(2)}) collective-permute-start(bf16[96,384]{1,0:T(8,128)(2,1)S(1)} %copy-done.29), channel_id=1, source_target_pairs={{0,6},{1,7},{2,4},{3,5},{4,2},{5,3},{6,0},{7,1},{8,14},{9,15},{10,... | collective-permute-start | bytes 221192 | tf_op jit(solution)/shard_map/ppermute | solution.py:455
  21.3 13.1 %collective-permute-done.1.refs_2_ = bf16[96,384]{1,0:T(8,128)(2,1)S(1)} collective-permute-done((bf16[96,384]{1,0:T(8,128)(2,1)S(1)}, bf16[96,384]{1,0:T(8,128)(2,1)S(1)}, u32[]{:S(2)}, u32[]{:S(2)}) %collective-permute-start.1) | collective-permute-done | bytes 73760 | tf_op jit(solution)/shard_map/ppermute | solution.py:455
  34.4 0.6 collective-permute-start.6
  35.0 0.2 collective-permute-done.2.refs_3_
  35.3 0.3 collective-permute-start.7
  35.5 2.3 %collective-permute-start.8 = (bf16[96,384]{1,0:T(8,128)(2,1)S(1)}, bf16[96,384]{1,0:T(8,128)(2,1)S(1)}, u32[]{:S(2)}, u32[]{:S(2)}) collective-permute-start(bf16[96,384]{1,0:T(8,128)(2,1)S(1)} %copy-done.26), channel_id=1, source_target_pairs={{0,9},{1,8},{2,11},{3,10},{4,13},{5,12},{6,15},{7,14},{8,1},{9,0},... | collective-permute-start | bytes 221192 | tf_op jit(solution)/shard_map/ppermute | solution.py:455
  37.8 3.3 %collective-permute-start.9 = (bf16[96,384]{1,0:T(8,128)(2,1)S(1)}, bf16[96,384]{1,0:T(8,128)(2,1)S(1)}, u32[]{:S(2)}, u32[]{:S(2)}) collective-permute-start(bf16[96,384]{1,0:T(8,128)(2,1)S(1)} %copy-done.25), channel_id=1, source_target_pairs={{0,10},{1,11},{2,8},{3,9},{4,14},{5,15},{6,12},{7,13},{8,2},{9,3},... | collective-permute-start | bytes 221192 | tf_op jit(solution)/shard_map/ppermute | solution.py:455
  41.1 3.8 %collective-permute-done.5.refs_6_ = bf16[96,384]{1,0:T(8,128)(2,1)S(1)} collective-permute-done((bf16[96,384]{1,0:T(8,128)(2,1)S(1)}, bf16[96,384]{1,0:T(8,128)(2,1)S(1)}, u32[]{:S(2)}, u32[]{:S(2)}) %collective-permute-start.5) | collective-permute-done | bytes 73760 | tf_op jit(solution)/shard_map/ppermute | solution.py:455
  44.9 0.8 collective-permute-done.6.refs_7_
  45.7 10.3 %collective-permute-done.7.refs_8_ = bf16[96,384]{1,0:T(8,128)(2,1)S(1)} collective-permute-done((bf16[96,384]{1,0:T(8,128)(2,1)S(1)}, bf16[96,384]{1,0:T(8,128)(2,1)S(1)}, u32[]{:S(2)}, u32[]{:S(2)}) %collective-permute-start.7) | collective-permute-done | bytes 73760 | tf_op jit(solution)/shard_map/ppermute | solution.py:455
  56.1 2.0 collective-permute-start.12
  58.1 2.8 %collective-permute-start.13 = (bf16[96,384]{1,0:T(8,128)(2,1)}, bf16[96,384]{1,0:T(8,128)(2,1)S(1)}, u32[]{:S(2)}, u32[]{:S(2)}) collective-permute-start(bf16[96,384]{1,0:T(8,128)(2,1)} %get-tuple-element.45), channel_id=1, source_target_pairs={{0,14},{1,15},{2,12},{3,13},{4,10},{5,11},{6,8},{7,9},{8,6},{9,7},... | collective-permute-start | bytes 221192 | tf_op jit(solution)/shard_map/ppermute | solution.py:455
  60.9 1.7 collective-permute-start.14
  62.6 1.5 collective-permute-done.12.refs_13_
  64.1 2.9 %collective-permute-done.13.refs_14_ = bf16[96,384]{1,0:T(8,128)(2,1)S(1)} collective-permute-done((bf16[96,384]{1,0:T(8,128)(2,1)}, bf16[96,384]{1,0:T(8,128)(2,1)S(1)}, u32[]{:S(2)}, u32[]{:S(2)}) %collective-permute-start.13) | collective-permute-done | bytes 73760 | tf_op jit(solution)/shard_map/ppermute | solution.py:455
  67.0 2.7 %collective-permute-done.14.refs_15_ = bf16[96,384]{1,0:T(8,128)(2,1)S(1)} collective-permute-done((bf16[96,384]{1,0:T(8,128)(2,1)}, bf16[96,384]{1,0:T(8,128)(2,1)S(1)}, u32[]{:S(2)}, u32[]{:S(2)}) %collective-permute-start.14) | collective-permute-done | bytes 73760 | tf_op jit(solution)/shard_map/ppermute | solution.py:455
  69.7 9.8 %shard_map.110 = bf16[16,96,384]{2,1,0:T(8,128)(2,1)} custom-call(bf16[32,96,384]{2,1,0:T(8,128)(2,1)S(1)} %all-to-all-done.recv, bf16[96,384]{1,0:T(8,128)(2,1)S(1)} %copy-done.13, bf16[96,384]{1,0:T(8,128)(2,1)S(1)} %collective-permute-done.refs_1_, bf16[96,384]{1,0:T(8,128)(2,1)S(1)} %collective-permute-done.1.refs_2_, ...), custom_call_target="tpu_custom_call" | custom-call | flops 452984832 | bytes 3538944 | tf_op jit(solution)/shard_map/pallas_call | solution.py:397
  79.5 0.0 copy-start.2
  79.5 0.0 copy-start.15
  79.5 0.0 copy-start.19
  79.6 0.0 copy-start.22
  79.6 0.0 copy-start.23
  79.6 4.5 %all-to-all-start.1 = ((bf16[16,96,384]{2,1,0:T(8,128)(2,1)}), bf16[16,96,384]{2,1,0:T(8,128)(2,1)S(1)}, u32[]{:S(2)}, u32[]{:S(2)}) async-start(bf16[16,96,384]{2,1,0:T(8,128)(2,1)} %shard_map.110), calls=%async_computation.1 | async-start | bytes 2359296 | tf_op jit(solution)/shard_map/all_to_all | solution.py:440
  84.2 1.9 shard_map.111
  86.1 0.8 copy-done.3
  86.9 1.4 copy-done.6
  88.3 0.7 copy-done.8
  89.0 12.9 %all-to-all-done.1.recv = bf16[16,96,384]{2,1,0:T(8,128)(2,1)S(1)} async-done(((bf16[16,96,384]{2,1,0:T(8,128)(2,1)}), bf16[16,96,384]{2,1,0:T(8,128)(2,1)S(1)}, u32[]{:S(2)}, u32[]{:S(2)}) %all-to-all-start.1) | async-done | bytes 1179680 | tf_op jit(solution)/shard_map/all_to_all | solution.py:440
  101.9 1.0 copy-done.4
  102.9 1.7 copy-done.7
  104.5 0.9 copy-done.9
  105.5 0.7 copy-done.17
  106.2 3.8 %shard_map.112 = (bf16[32,96,384]{2,1,0:T(8,128)(2,1)S(1)}, bf16[12,128,384]{2,1,0:T(8,128)(2,1)S(1)}) custom-call(bf16[16,96,384]{2,1,0:T(8,128)(2,1)S(1)} %all-to-all-done.1.recv, f32[12,128,384]{2,1,0:T(8,128)S(1)} %copy-done.7, bf16[12,128,384]{2,1,0:T(8,128)(2,1)S(1)} %copy-done.2, f32[2,384]{1,0:T(2,128)S(1)} %copy-done.17, ...), custom_call_target="tpu_custom_call" | custom-call | flops 754974720 | bytes 8965120 | tf_op jit(solution)/shard_map/pallas_call | solution.py:397
  110.0 60.6 %all_to_all.20.recv = bf16[32,96,384]{2,1,0:T(8,128)(2,1)S(1)} all-to-all(bf16[32,96,384]{2,1,0:T(8,128)(2,1)S(1)} %get-tuple-element.53), channel_id=1, replica_groups=mesh['grp'=1,'row'=32] {'row'}, dimensions={0} | all-to-all | bytes 4718592 | tf_op jit(solution)/shard_map/all_to_all | solution.py:440
  170.6 5.3 %shard_map.113 = bf16[32,48,384]{2,1,0:T(8,128)(2,1)} custom-call(bf16[32,96,384]{2,1,0:T(8,128)(2,1)S(1)} %all_to_all.20.recv), custom_call_target="tpu_custom_call" | custom-call | flops 452984832 | bytes 3538944 | tf_op jit(solution)/shard_map/pallas_call | solution.py:397
  175.8 3.0 %all-to-all-start.3 = ((bf16[32,48,384]{2,1,0:T(8,128)(2,1)}), bf16[32,48,384]{2,1,0:T(8,128)(2,1)S(1)}, u32[]{:S(2)}, u32[]{:S(2)}) async-start(bf16[32,48,384]{2,1,0:T(8,128)(2,1)} %shard_map.113), calls=%async_computation.3 | async-start | bytes 2359296 | tf_op jit(solution)/shard_map/all_to_all | solution.py:440
  178.9 1.4 shard_map.114.gate_in
  180.3 1.4 copy-done
  181.7 26.0 %all-to-all-done.3.recv_in = bf16[32,48,384]{2,1,0:T(8,128)(2,1)S(1)} async-done(((bf16[32,48,384]{2,1,0:T(8,128)(2,1)}), bf16[32,48,384]{2,1,0:T(8,128)(2,1)S(1)}, u32[]{:S(2)}, u32[]{:S(2)}) %all-to-all-start.3) | async-done | bytes 1179680 | tf_op jit(solution)/shard_map/all_to_all | solution.py:440
  207.7 1.0 copy-done.24
  208.7 4.6 %shard_map.115 = bf16[12,384,128]{2,1,0:T(8,128)(2,1)} custom-call(bf16[32,48,384]{2,1,0:T(8,128)(2,1)} %copy-done.24, f32[12,128,384]{2,1,0:T(8,128)} %copy-done, bf16[12,128,384]{2,1,0:T(8,128)(2,1)} %copy-done.1, bf16[896,128]{1,0:T(8,128)(2,1)} %copy-done.8, f32[7,128,128]{2,1,0:T(8,128)} %copy-done.3), custom_call_target="tpu_custom_call" | custom-call | flops 150994944 | bytes 1179648 | tf_op jit(solution)/shard_map/pallas_call | solution.py:397
  (66 shorter events, 0.1 us)
Async XLA Ops:
  7.4 7.4 %copy-start.34 = (bf16[96,384]{1,0:T(8,128)(2,1)S(1)}, bf16[96,384]{1,0:T(8,128)(2,1)}, u32[]{:S(2)}) copy-start(bf16[96,384]{1,0:T(8,128)(2,1)} %get-tuple-element.32) | copy-start | bytes 221188
  7.5 7.8 %copy-start.33 = (bf16[96,384]{1,0:T(8,128)(2,1)S(1)}, bf16[96,384]{1,0:T(8,128)(2,1)}, u32[]{:S(2)}) copy-start(bf16[96,384]{1,0:T(8,128)(2,1)} %get-tuple-element.33) | copy-start | bytes 221188
  7.5 9.4 %copy-start.32 = (bf16[96,384]{1,0:T(8,128)(2,1)S(1)}, bf16[96,384]{1,0:T(8,128)(2,1)}, u32[]{:S(2)}) copy-start(bf16[96,384]{1,0:T(8,128)(2,1)} %get-tuple-element.34) | copy-start | bytes 221188
  7.5 9.4 %copy-start.31 = (bf16[96,384]{1,0:T(8,128)(2,1)S(1)}, bf16[96,384]{1,0:T(8,128)(2,1)}, u32[]{:S(2)}) copy-start(bf16[96,384]{1,0:T(8,128)(2,1)} %get-tuple-element.35) | copy-start | bytes 221188
  7.5 11.1 %copy-start.30 = (bf16[96,384]{1,0:T(8,128)(2,1)S(1)}, bf16[96,384]{1,0:T(8,128)(2,1)}, u32[]{:S(2)}) copy-start(bf16[96,384]{1,0:T(8,128)(2,1)} %get-tuple-element.36) | copy-start | bytes 221188
  7.5 11.2 %copy-start.29 = (bf16[96,384]{1,0:T(8,128)(2,1)S(1)}, bf16[96,384]{1,0:T(8,128)(2,1)}, u32[]{:S(2)}) copy-start(bf16[96,384]{1,0:T(8,128)(2,1)} %get-tuple-element.37) | copy-start | bytes 221188
  7.5 26.9 %copy-start.28 = (bf16[96,384]{1,0:T(8,128)(2,1)S(1)}, bf16[96,384]{1,0:T(8,128)(2,1)}, u32[]{:S(2)}) copy-start(bf16[96,384]{1,0:T(8,128)(2,1)} %get-tuple-element.38) | copy-start | bytes 221188
  7.5 27.7 %copy-start.27 = (bf16[96,384]{1,0:T(8,128)(2,1)S(1)}, bf16[96,384]{1,0:T(8,128)(2,1)}, u32[]{:S(2)}) copy-start(bf16[96,384]{1,0:T(8,128)(2,1)} %get-tuple-element.39) | copy-start | bytes 221188
  7.5 28.0 %copy-start.26 = (bf16[96,384]{1,0:T(8,128)(2,1)S(1)}, bf16[96,384]{1,0:T(8,128)(2,1)}, u32[]{:S(2)}) copy-start(bf16[96,384]{1,0:T(8,128)(2,1)} %get-tuple-element.40) | copy-start | bytes 221188
  7.5 30.3 %copy-start.25 = (bf16[96,384]{1,0:T(8,128)(2,1)S(1)}, bf16[96,384]{1,0:T(8,128)(2,1)}, u32[]{:S(2)}) copy-start(bf16[96,384]{1,0:T(8,128)(2,1)} %get-tuple-element.41) | copy-start | bytes 221188
  7.5 62.2 %copy-start.13 = (bf16[96,384]{1,0:T(8,128)(2,1)S(1)}, bf16[96,384]{1,0:T(8,128)(2,1)}, u32[]{:S(2)}) copy-start(bf16[96,384]{1,0:T(8,128)(2,1)} %get-tuple-element.31.refs_0_) | copy-start | bytes 221188
  7.6 62.1 %all-to-all-start = ((bf16[32,96,384]{2,1,0:T(8,128)(2,1)}), bf16[32,96,384]{2,1,0:T(8,128)(2,1)S(1)}, u32[]{:S(2)}, u32[]{:S(2)}) async-start(bf16[32,96,384]{2,1,0:T(8,128)(2,1)} %get-tuple-element.30), calls=%async_computation | async-start | bytes 4718592 | tf_op jit(solution)/shard_map/all_to_all | solution.py:440
  14.9 3.8 %collective-permute-start = (bf16[96,384]{1,0:T(8,128)(2,1)S(1)}, bf16[96,384]{1,0:T(8,128)(2,1)S(1)}, u32[]{:S(2)}, u32[]{:S(2)}) collective-permute-start(bf16[96,384]{1,0:T(8,128)(2,1)S(1)} %copy-done.34), channel_id=1, source_target_pairs={{0,1},{1,0},{2,3},{3,2},{4,5},{5,4},{6,7},{7,6},{8,9},{9,8},{10,11... | collective-permute-start | bytes 221192 | tf_op jit(solution)/shard_map/ppermute | solution.py:455
  15.2 19.2 %collective-permute-start.1 = (bf16[96,384]{1,0:T(8,128)(2,1)S(1)}, bf16[96,384]{1,0:T(8,128)(2,1)S(1)}, u32[]{:S(2)}, u32[]{:S(2)}) collective-permute-start(bf16[96,384]{1,0:T(8,128)(2,1)S(1)} %copy-done.33), channel_id=1, source_target_pairs={{0,2},{1,3},{2,0},{3,1},{4,6},{5,7},{6,4},{7,5},{8,10},{9,11},{10,... | collective-permute-start | bytes 221192 | tf_op jit(solution)/shard_map/ppermute | solution.py:455
  16.9 18.4 %collective-permute-start.2 = (bf16[96,384]{1,0:T(8,128)(2,1)S(1)}, bf16[96,384]{1,0:T(8,128)(2,1)S(1)}, u32[]{:S(2)}, u32[]{:S(2)}) collective-permute-start(bf16[96,384]{1,0:T(8,128)(2,1)S(1)} %copy-done.32), channel_id=1, source_target_pairs={{0,3},{1,2},{2,1},{3,0},{4,7},{5,6},{6,5},{7,4},{8,11},{9,10},{10,... | collective-permute-start | bytes 221192 | tf_op jit(solution)/shard_map/ppermute | solution.py:455
  16.9 18.6 %collective-permute-start.3 = (bf16[96,384]{1,0:T(8,128)(2,1)S(1)}, bf16[96,384]{1,0:T(8,128)(2,1)S(1)}, u32[]{:S(2)}, u32[]{:S(2)}) collective-permute-start(bf16[96,384]{1,0:T(8,128)(2,1)S(1)} %copy-done.31), channel_id=1, source_target_pairs={{0,4},{1,5},{2,6},{3,7},{4,0},{5,1},{6,2},{7,3},{8,12},{9,13},{10,... | collective-permute-start | bytes 221192 | tf_op jit(solution)/shard_map/ppermute | solution.py:455
  18.6 19.2 %collective-permute-start.4 = (bf16[96,384]{1,0:T(8,128)(2,1)S(1)}, bf16[96,384]{1,0:T(8,128)(2,1)S(1)}, u32[]{:S(2)}, u32[]{:S(2)}) collective-permute-start(bf16[96,384]{1,0:T(8,128)(2,1)S(1)} %copy-done.30), channel_id=1, source_target_pairs={{0,5},{1,4},{2,7},{3,6},{4,1},{5,0},{6,3},{7,2},{8,13},{9,12},{10,... | collective-permute-start | bytes 221192 | tf_op jit(solution)/shard_map/ppermute | solution.py:455
  18.7 26.2 %collective-permute-start.5 = (bf16[96,384]{1,0:T(8,128)(2,1)S(1)}, bf16[96,384]{1,0:T(8,128)(2,1)S(1)}, u32[]{:S(2)}, u32[]{:S(2)}) collective-permute-start(bf16[96,384]{1,0:T(8,128)(2,1)S(1)} %copy-done.29), channel_id=1, source_target_pairs={{0,6},{1,7},{2,4},{3,5},{4,2},{5,3},{6,0},{7,1},{8,14},{9,15},{10,... | collective-permute-start | bytes 221192 | tf_op jit(solution)/shard_map/ppermute | solution.py:455
  34.4 11.3 %collective-permute-start.6 = (bf16[96,384]{1,0:T(8,128)(2,1)S(1)}, bf16[96,384]{1,0:T(8,128)(2,1)S(1)}, u32[]{:S(2)}, u32[]{:S(2)}) collective-permute-start(bf16[96,384]{1,0:T(8,128)(2,1)S(1)} %copy-done.28), channel_id=1, source_target_pairs={{0,7},{1,6},{2,5},{3,4},{4,3},{5,2},{6,1},{7,0},{8,15},{9,14},{10,... | collective-permute-start | bytes 221192 | tf_op jit(solution)/shard_map/ppermute | solution.py:455
  35.3 20.8 %collective-permute-start.7 = (bf16[96,384]{1,0:T(8,128)(2,1)S(1)}, bf16[96,384]{1,0:T(8,128)(2,1)S(1)}, u32[]{:S(2)}, u32[]{:S(2)}) collective-permute-start(bf16[96,384]{1,0:T(8,128)(2,1)S(1)} %copy-done.27), channel_id=1, source_target_pairs={{0,8},{1,9},{2,10},{3,11},{4,12},{5,13},{6,14},{7,15},{8,0},{9,1},... | collective-permute-start | bytes 221192 | tf_op jit(solution)/shard_map/ppermute | solution.py:455
  35.5 22.6 %collective-permute-start.8 = (bf16[96,384]{1,0:T(8,128)(2,1)S(1)}, bf16[96,384]{1,0:T(8,128)(2,1)S(1)}, u32[]{:S(2)}, u32[]{:S(2)}) collective-permute-start(bf16[96,384]{1,0:T(8,128)(2,1)S(1)} %copy-done.26), channel_id=1, source_target_pairs={{0,9},{1,8},{2,11},{3,10},{4,13},{5,12},{6,15},{7,14},{8,1},{9,0},... | collective-permute-start | bytes 221192 | tf_op jit(solution)/shard_map/ppermute | solution.py:455
  37.8 23.1 %collective-permute-start.9 = (bf16[96,384]{1,0:T(8,128)(2,1)S(1)}, bf16[96,384]{1,0:T(8,128)(2,1)S(1)}, u32[]{:S(2)}, u32[]{:S(2)}) collective-permute-start(bf16[96,384]{1,0:T(8,128)(2,1)S(1)} %copy-done.25), channel_id=1, source_target_pairs={{0,10},{1,11},{2,8},{3,9},{4,14},{5,15},{6,12},{7,13},{8,2},{9,3},... | collective-permute-start | bytes 221192 | tf_op jit(solution)/shard_map/ppermute | solution.py:455
  44.9 17.7 %collective-permute-start.10 = (bf16[96,384]{1,0:T(8,128)(2,1)}, bf16[96,384]{1,0:T(8,128)(2,1)S(1)}, u32[]{:S(2)}, u32[]{:S(2)}) collective-permute-start(bf16[96,384]{1,0:T(8,128)(2,1)} %get-tuple-element.42), channel_id=1, source_target_pairs={{0,11},{1,10},{2,9},{3,8},{4,15},{5,14},{6,13},{7,12},{8,3},{9,2},... | collective-permute-start | bytes 221192 | tf_op jit(solution)/shard_map/ppermute | solution.py:455
  45.7 16.9 %collective-permute-start.11 = (bf16[96,384]{1,0:T(8,128)(2,1)}, bf16[96,384]{1,0:T(8,128)(2,1)S(1)}, u32[]{:S(2)}, u32[]{:S(2)}) collective-permute-start(bf16[96,384]{1,0:T(8,128)(2,1)} %get-tuple-element.43), channel_id=1, source_target_pairs={{0,12},{1,13},{2,14},{3,15},{4,8},{5,9},{6,10},{7,11},{8,4},{9,5},... | collective-permute-start | bytes 221192 | tf_op jit(solution)/shard_map/ppermute | solution.py:455
  56.1 8.0 %collective-permute-start.12 = (bf16[96,384]{1,0:T(8,128)(2,1)}, bf16[96,384]{1,0:T(8,128)(2,1)S(1)}, u32[]{:S(2)}, u32[]{:S(2)}) collective-permute-start(bf16[96,384]{1,0:T(8,128)(2,1)} %get-tuple-element.44), channel_id=1, source_target_pairs={{0,13},{1,12},{2,15},{3,14},{4,9},{5,8},{6,11},{7,10},{8,5},{9,4},... | collective-permute-start | bytes 221192 | tf_op jit(solution)/shard_map/ppermute | solution.py:455
  58.1 8.9 %collective-permute-start.13 = (bf16[96,384]{1,0:T(8,128)(2,1)}, bf16[96,384]{1,0:T(8,128)(2,1)S(1)}, u32[]{:S(2)}, u32[]{:S(2)}) collective-permute-start(bf16[96,384]{1,0:T(8,128)(2,1)} %get-tuple-element.45), channel_id=1, source_target_pairs={{0,14},{1,15},{2,12},{3,13},{4,10},{5,11},{6,8},{7,9},{8,6},{9,7},... | collective-permute-start | bytes 221192 | tf_op jit(solution)/shard_map/ppermute | solution.py:455
  60.9 8.8 %collective-permute-start.14 = (bf16[96,384]{1,0:T(8,128)(2,1)}, bf16[96,384]{1,0:T(8,128)(2,1)S(1)}, u32[]{:S(2)}, u32[]{:S(2)}) collective-permute-start(bf16[96,384]{1,0:T(8,128)(2,1)} %get-tuple-element.46), channel_id=1, source_target_pairs={{0,15},{1,14},{2,13},{3,12},{4,11},{5,10},{6,9},{7,8},{8,7},{9,6},... | collective-permute-start | bytes 221192 | tf_op jit(solution)/shard_map/ppermute | solution.py:455
  79.5 4.6 %copy-start.2 = (bf16[12,128,384]{2,1,0:T(8,128)(2,1)S(1)}, bf16[12,128,384]{2,1,0:T(8,128)(2,1)}, u32[]{:S(2)}) copy-start(bf16[12,128,384]{2,1,0:T(8,128)(2,1)} %get-tuple-element.47.x_t) | copy-start | bytes 3538948
  79.5 4.6 %copy-start.11 = (bf16[2,128,512]{2,1,0:T(8,128)(2,1)S(1)}, bf16[2,128,512]{2,1,0:T(8,128)(2,1)}, u32[]{:S(2)}) copy-start(bf16[2,128,512]{2,1,0:T(8,128)(2,1)} %w_ab.3) | copy-start | bytes 786436
  79.5 4.6 %copy-start.12 = (f32[2,16,128]{2,1,0:T(8,128)S(1)}, f32[2,16,128]{2,1,0:T(8,128)}, u32[]{:S(2)}) copy-start(f32[2,16,128]{2,1,0:T(8,128)} %get-tuple-element.49.row_marks) | copy-start | bytes 49156
  79.5 4.6 %copy-start.14 = (bf16[2,128,128]{2,1,0:T(8,128)(2,1)S(1)}, bf16[2,128,128]{2,1,0:T(8,128)(2,1)}, u32[]{:S(2)}) copy-start(bf16[2,128,128]{2,1,0:T(8,128)(2,1)} %w_gate.1) | copy-start | bytes 196612
  79.5 4.6 %copy-start.15 = (bf16[2,128,128]{2,1,0:T(8,128)(2,1)S(1)}, bf16[2,128,128]{2,1,0:T(8,128)(2,1)}, u32[]{:S(2)}) copy-start(bf16[2,128,128]{2,1,0:T(8,128)(2,1)} %w_out.1) | copy-start | bytes 196612
  79.5 4.6 %copy-start.16 = (f32[2,384]{1,0:T(2,128)S(1)}, f32[2,384]{1,0:T(2,128)}, u32[]{:S(2)}) copy-start(f32[2,384]{1,0:T(2,128)} %get-tuple-element.48.marks) | copy-start | bytes 9220
  79.5 4.6 %copy-start.19 = (f32[2,128]{1,0:T(2,128)S(1)}, f32[2,128]{1,0:T(2,128)}, u32[]{:S(2)}) copy-start(f32[2,128]{1,0:T(2,128)} %gain.3) | copy-start | bytes 3076
  79.5 4.6 %copy-start.20 = (f32[2,128]{1,0:T(2,128)S(1)}, f32[2,128]{1,0:T(2,128)}, u32[]{:S(2)}) copy-start(f32[2,128]{1,0:T(2,128)} %bias.3) | copy-start | bytes 3076
  79.6 4.6 %copy-start.21 = (f32[2,128]{1,0:T(2,128)S(1)}, f32[2,128]{1,0:T(2,128)}, u32[]{:S(2)}) copy-start(f32[2,128]{1,0:T(2,128)} %embed.3) | copy-start | bytes 3076
  79.6 4.6 %copy-start.22 = (f32[2,128]{1,0:T(2,128)S(1)}, f32[2,128]{1,0:T(2,128)}, u32[]{:S(2)}) copy-start(f32[2,128]{1,0:T(2,128)} %mid_gain.1) | copy-start | bytes 3076
  79.6 4.6 %copy-start.23 = (f32[2,128]{1,0:T(2,128)S(1)}, f32[2,128]{1,0:T(2,128)}, u32[]{:S(2)}) copy-start(f32[2,128]{1,0:T(2,128)} %mid_bias.1) | copy-start | bytes 3076
  79.6 22.3 %all-to-all-start.1 = ((bf16[16,96,384]{2,1,0:T(8,128)(2,1)}), bf16[16,96,384]{2,1,0:T(8,128)(2,1)S(1)}, u32[]{:S(2)}, u32[]{:S(2)}) async-start(bf16[16,96,384]{2,1,0:T(8,128)(2,1)} %shard_map.110), calls=%async_computation.1 | async-start | bytes 2359296 | tf_op jit(solution)/shard_map/all_to_all | solution.py:440
  86.9 1.4 copy-start.6
  102.9 1.7 copy-start.7
  110.0 68.9 %copy-start.1 = (bf16[12,128,384]{2,1,0:T(8,128)(2,1)}, bf16[12,128,384]{2,1,0:T(8,128)(2,1)S(1)}, u32[]{:S(2)}) copy-start(bf16[12,128,384]{2,1,0:T(8,128)(2,1)S(1)} %get-tuple-element.54.x_t.x_in) | copy-start | bytes 3538948
  175.8 3.0 %copy-start.5 = (f32[7,128,128]{2,1,0:T(8,128)S(1)}, f32[7,128,128]{2,1,0:T(8,128)}, u32[]{:S(2)}) copy-start(f32[7,128,128]{2,1,0:T(8,128)} %copy-done.3) | copy-start | bytes 1376260
  175.8 3.0 %copy-start.10 = (bf16[896,128]{1,0:T(8,128)(2,1)S(1)}, bf16[896,128]{1,0:T(8,128)(2,1)}, u32[]{:S(2)}) copy-start(bf16[896,128]{1,0:T(8,128)(2,1)} %copy-done.8) | copy-start | bytes 688132
  175.8 3.1 %copy-start.18 = (f32[2,384]{1,0:T(2,128)S(1)}, f32[2,384]{1,0:T(2,128)}, u32[]{:S(2)}) copy-start(f32[2,384]{1,0:T(2,128)} %get-tuple-element.48.marks) | copy-start | bytes 9220
  175.8 31.8 %all-to-all-start.3 = ((bf16[32,48,384]{2,1,0:T(8,128)(2,1)}), bf16[32,48,384]{2,1,0:T(8,128)(2,1)S(1)}, u32[]{:S(2)}, u32[]{:S(2)}) async-start(bf16[32,48,384]{2,1,0:T(8,128)(2,1)} %shard_map.113), calls=%async_computation.3 | async-start | bytes 2359296 | tf_op jit(solution)/shard_map/all_to_all | solution.py:440
  180.3 1.4 copy-start
  207.7 1.0 copy-start.24
  (5 other events, 4.1 us)

commit v6 on v4

--- a/solution.py
+++ b/solution.py
@@ -87,11 +87,15 @@
             ref[:, columns] = slabs[j, pl.ds(start, depth), :].astype(BF16)
 
 
-def widen(recv, wide):
+def spread(depth):
+    return depth + 4 if depth % 8 == 0 else depth
+
+
+def widen(recv, wide, pitch):
     devices, depth, width = recv.shape
     for s in range(devices):
         for j, columns in blocks(width):
-            wide[j, s * depth : (s + 1) * depth, :] = recv[s, :, columns].astype(F32)
+            wide[j, s * pitch : s * pitch + depth, :] = recv[s, :, columns].astype(F32)
 
 
 def fetch(pairs, sems):
@@ -222,21 +226,22 @@
     me = lax.axis_index("row")
     mine = me // half * half
     other = half - mine
+    pitch = spread(depth)
     for q in range(half):
-        to_other = pl.multiple_of((other + q) * depth, 8)
-        to_own = pl.multiple_of((mine + (me % half ^ q)) * depth, 8)
-        for j, columns in blocks(width):
-            left_wide[j, q * depth : (q + 1) * depth, :] = recv[mine + q, :, columns].astype(F32)
+        to_other = (other + q) * pitch
+        to_own = (mine + (me % half ^ q)) * pitch
+        for j, columns in blocks(width):
+            left_wide[j, q * pitch : q * pitch + depth, :] = recv[mine + q, :, columns].astype(F32)
             right_wide[j, pl.ds(to_other, depth), :] = recv[other + q, :, columns].astype(F32)
             right_wide[j, pl.ds(to_own, depth), :] = own[q][:, columns].astype(F32)
     for c in range(channels):
         left, right = [], []
         for j, _ in blocks(width):
-            pieces = [left_wide[j, pl.ds(c * rows + r, half, stride=depth), :].astype(BF16) for r in range(rows)]
+            pieces = [left_wide[j, pl.ds(c * rows + r, half, stride=pitch), :].astype(BF16) for r in range(rows)]
             left.append(jnp.concatenate(pieces, axis=0))
             for r in range(rows):
                 natural[c, j, pl.ds(r, devices, stride=rows), :] = right_wide[
-                    j, pl.ds(c * rows + r, devices, stride=depth), :
+                    j, pl.ds(c * rows + r, devices, stride=pitch), :
                 ]
             right.append(natural[c, j].astype(BF16))
         product = lax.dot_general(
@@ -245,23 +250,24 @@
         )
         for j, columns in blocks(width):
             for r in range(rows):
-                turned[j, pl.ds(c * rows + r, half, stride=depth), :] = product[r * half : (r + 1) * half, columns]
+                turned[j, pl.ds(c * rows + r, half, stride=pitch), :] = product[r * half : (r + 1) * half, columns]
     for q in range(half):
         for j, columns in blocks(width):
-            out[q, :, columns] = turned[j, q * depth : (q + 1) * depth, :].astype(BF16)
+            out[q, :, columns] = turned[j, q * pitch : q * pitch + depth, :].astype(BF16)
 
 
 def second_products_kernel(rows, recv, out, wide, natural, turned):
     devices, depth, width = recv.shape
     channels = depth // (2 * rows)
-    widen(recv, wide)
+    pitch, out_pitch = spread(depth), spread(channels * rows)
+    widen(recv, wide, pitch)
 
     def by_row(side, c):
         return jnp.concatenate(
             [
                 jnp.concatenate(
                     [
-                        wide[j, pl.ds((side * channels + c) * rows + r, devices, stride=depth), :].astype(BF16)
+                        wide[j, pl.ds((side * channels + c) * rows + r, devices, stride=pitch), :].astype(BF16)
                         for r in range(rows)
                     ],
                     axis=0,
@@ -278,12 +284,12 @@
         for j, columns in blocks(width):
             natural[c, j] = product[:, columns]
             for r in range(rows):
-                turned[j, pl.ds(c * rows + r, devices, stride=channels * rows), :] = natural[
+                turned[j, pl.ds(c * rows + r, devices, stride=out_pitch), :] = natural[
                     c, j, pl.ds(r, devices, stride=rows), :
                 ]
     for s in range(devices):
         for j, columns in blocks(width):
-            out[s, :, columns] = turned[j, s * channels * rows : (s + 1) * channels * rows, :].astype(BF16)
+            out[s, :, columns] = turned[j, s * out_pitch : s * out_pitch + channels * rows, :].astype(BF16)
 
 
 def finish(layer, group, width, tri, gate, x_t, weights, vectors):
@@ -310,7 +316,7 @@
 
 def middle_kernel(recv, gate, x_t, marks, row_marks, weights, vectors, out, new_t, slabs, tri):
     rows, _, width = x_t.shape
-    widen(recv, tri)
+    widen(recv, tri, recv.shape[1])
 
     def prepare(group):
         states = finish(0, group, width, tri, gate, x_t, weights, vectors)
@@ -333,7 +339,7 @@
 
 def last_kernel(recv, gate, x_t, weights, vectors, out, tri):
     rows, _, width = x_t.shape
-    widen(recv, tri)
+    widen(recv, tri, recv.shape[1])
     for group in groups(rows):
         for (r, j), state in finish(1, group, width, tri, gate, x_t, weights, vectors).items():
             out[r, j * 128 : (j + 1) * 128, :] = state.astype(F32).T.astype(BF16)
@@ -377,6 +383,9 @@
     ids = pltpu.VMEM((width,), jnp.int32)
     w_wide = pltpu.VMEM((C, 4 * HC), BF16)
     slabs_wide = pltpu.VMEM((cols, 2 * HC * rows, 128), F32)
+    own_spread = pltpu.VMEM((cols, half * spread(2 * channels * rows), 128), F32)
+    all_spread = pltpu.VMEM((cols, devices * spread(2 * channels * rows), 128), F32)
+    back_spread = pltpu.VMEM((cols, devices * spread(channels * rows), 128), F32)
     tri_wide = pltpu.VMEM((cols, HC * rows, 128), F32)
     norms = (ln_in_gain, ln_in_bias, chain_embed)
 
@@ -407,7 +416,7 @@
     products = call(
         functools.partial(first_products_kernel, rows), [own_back],
         [
-            tri_wide, slabs_wide, pltpu.VMEM((2 * channels, cols, width, 128), F32), tri_wide,
+            own_spread, all_spread, pltpu.VMEM((2 * channels, cols, width, 128), F32), own_spread,
         ],
         (recv, *own), (), 2 * channels * width**3, PRODUCTS_VMEM_LIMIT,
     )[0]
@@ -422,7 +431,7 @@
     )[0]
     products = call(
         functools.partial(second_products_kernel, rows), [back],
-        [slabs_wide, pltpu.VMEM((channels, cols, width, 128), F32), tri_wide], (recv,), (), 2 * channels * width**3,
+        [all_spread, pltpu.VMEM((channels, cols, width, 128), F32), back_spread], (recv,), (), 2 * channels * width**3,
     )[0]
     tri = exchange(products)
     return call(

time: 209 us -> 200 us (0.957)
  Pallas kernels: 29.4 us -> 21.2 us
    pallas_call x7, Pallas kernels: 29.4 us -> 21.2 us  [call(): pl.pallas_call(kernel, out_shape=outs, in_specs=[WHOLE] * len(arrays) + [...]
where the time goes in v6:
time: 200 us
  waiting for transfers between devices  73.5 us (37%)
  blocking collectives  60.6 us (30%)
  starting transfers between devices  33.8 us (17%)
  Pallas kernels  21.2 us (11%)
  local copies, waits for them, and re-layouts  10.3 us (5%)
    all_to_all x1, blocking collectives, exchange(): lax.all_to_all(slabs, 'row', split_axis=0, concat_axis=0, tiled=True, axi...  60.6 us
    all_to_all x3, waiting for transfers between devices, exchange(): lax.all_to_all(slabs, 'row', split_axis=0, concat_axis=0, tiled=True, axi...  38 us
    ppermute x15, waiting for transfers between devices, local(): lax.ppermute(own[o], 'row', [(i, i ^ o) for i in range(devices)])  35.5 us
    pallas_call x7, Pallas kernels, call(): pl.pallas_call(kernel, out_shape=outs, in_specs=[WHOLE] * len(arrays) + [...  21.2 us
    ppermute x15, starting transfers between devices, local(): lax.ppermute(own[o], 'row', [(i, i ^ o) for i in range(devices)])  19.3 us
    all_to_all x3, starting transfers between devices, exchange(): lax.all_to_all(slabs, 'row', split_axis=0, concat_axis=0, tiled=True, axi...  14.5 us
    unnamed x68, local copies, waits for them, and re-layouts  10.3 us
  transfers between devices with their start and end apart: 18, of which 10 were waited for; matrix products, arithmetic and copies ran while one was open for 0% of the time, Pallas kernels for 2%

profile of v6, /device:TPU:0, one launch (start us, length us, event | category | flops | bytes accessed | tf_op | source)
XLA Modules:
  0.0 199.7 jit_solution(13493687654379248255)
XLA Ops:
  0.0 6.6 %shard_map.109 = (bf16[96,384]{1,0:T(8,128)(2,1)}, bf16[96,384]{1,0:T(8,128)(2,1)}, bf16[96,384]{1,0:T(8,128)(2,1)}, bf16[96,384]{1,0:T(8,128)(2,1)}, bf16[96,38...) custom-call(s32[384]{0:T(512)} %residue_mask.1, ...), custom_call_target="tpu_custom_call" | custom-call | flops 603979776 | bytes 4738048 | tf_op jit(solution)/shard_map/pallas_call | solution.py:350
  6.7 7.3 %all-to-all-start = ((bf16[32,96,384]{2,1,0:T(8,128)(2,1)}), bf16[32,96,384]{2,1,0:T(8,128)(2,1)S(1)}, u32[]{:S(2)}, u32[]{:S(2)}) async-start(bf16[32,96,384]{2,1,0:T(8,128)(2,1)} %get-tuple-element.30), calls=%async_computation | async-start | bytes 4718592 | tf_op jit(solution)/shard_map/all_to_all | solution.py:396
  14.0 0.3 collective-permute-start
  14.4 1.7 collective-permute-start.1
  16.0 0.0 collective-permute-start.2
  16.1 1.7 collective-permute-start.3
  17.7 0.1 collective-permute-start.4
  17.9 2.6 %collective-permute-start.5 = (bf16[96,384]{1,0:T(8,128)(2,1)S(1)}, bf16[96,384]{1,0:T(8,128)(2,1)S(1)}, u32[]{:S(2)}, u32[]{:S(2)}) collective-permute-start(bf16[96,384]{1,0:T(8,128)(2,1)S(1)} %copy-done.28), channel_id=1, source_target_pairs={{0,6},{1,7},{2,4},{3,5},{4,2},{5,3},{6,0},{7,1},{8,14},{9,15},{10,... | collective-permute-start | bytes 221192 | tf_op jit(solution)/shard_map/ppermute | solution.py:410
  20.4 13.1 %collective-permute-done.1.refs_2_ = bf16[96,384]{1,0:T(8,128)(2,1)S(1)} collective-permute-done((bf16[96,384]{1,0:T(8,128)(2,1)S(1)}, bf16[96,384]{1,0:T(8,128)(2,1)S(1)}, u32[]{:S(2)}, u32[]{:S(2)}) %collective-permute-start.1) | collective-permute-done | bytes 73760 | tf_op jit(solution)/shard_map/ppermute | solution.py:410
  33.6 0.6 collective-permute-start.6
  34.2 0.2 collective-permute-done.2.refs_3_
  34.4 0.3 collective-permute-start.7
  34.7 2.3 %collective-permute-start.8 = (bf16[96,384]{1,0:T(8,128)(2,1)S(1)}, bf16[96,384]{1,0:T(8,128)(2,1)S(1)}, u32[]{:S(2)}, u32[]{:S(2)}) collective-permute-start(bf16[96,384]{1,0:T(8,128)(2,1)S(1)} %copy-done.25), channel_id=1, source_target_pairs={{0,9},{1,8},{2,11},{3,10},{4,13},{5,12},{6,15},{7,14},{8,1},{9,0},... | collective-permute-start | bytes 221192 | tf_op jit(solution)/shard_map/ppermute | solution.py:410
  37.0 3.3 %collective-permute-start.9 = (bf16[96,384]{1,0:T(8,128)(2,1)S(1)}, bf16[96,384]{1,0:T(8,128)(2,1)S(1)}, u32[]{:S(2)}, u32[]{:S(2)}) collective-permute-start(bf16[96,384]{1,0:T(8,128)(2,1)S(1)} %copy-done.24), channel_id=1, source_target_pairs={{0,10},{1,11},{2,8},{3,9},{4,14},{5,15},{6,12},{7,13},{8,2},{9,3},... | collective-permute-start | bytes 221192 | tf_op jit(solution)/shard_map/ppermute | solution.py:410
  40.2 3.8 %collective-permute-done.5.refs_6_ = bf16[96,384]{1,0:T(8,128)(2,1)S(1)} collective-permute-done((bf16[96,384]{1,0:T(8,128)(2,1)S(1)}, bf16[96,384]{1,0:T(8,128)(2,1)S(1)}, u32[]{:S(2)}, u32[]{:S(2)}) %collective-permute-start.5) | collective-permute-done | bytes 73760 | tf_op jit(solution)/shard_map/ppermute | solution.py:410
  44.1 0.8 collective-permute-done.6.refs_7_
  44.9 10.3 %collective-permute-done.7.refs_8_ = bf16[96,384]{1,0:T(8,128)(2,1)S(1)} collective-permute-done((bf16[96,384]{1,0:T(8,128)(2,1)S(1)}, bf16[96,384]{1,0:T(8,128)(2,1)S(1)}, u32[]{:S(2)}, u32[]{:S(2)}) %collective-permute-start.7) | collective-permute-done | bytes 73760 | tf_op jit(solution)/shard_map/ppermute | solution.py:410
  55.2 2.0 %collective-permute-start.12 = (bf16[96,384]{1,0:T(8,128)(2,1)}, bf16[96,384]{1,0:T(8,128)(2,1)S(1)}, u32[]{:S(2)}, u32[]{:S(2)}) collective-permute-start(bf16[96,384]{1,0:T(8,128)(2,1)} %get-tuple-element.44), channel_id=1, source_target_pairs={{0,13},{1,12},{2,15},{3,14},{4,9},{5,8},{6,11},{7,10},{8,5},{9,4},... | collective-permute-start | bytes 221192 | tf_op jit(solution)/shard_map/ppermute | solution.py:410
  57.2 2.8 %collective-permute-start.13 = (bf16[96,384]{1,0:T(8,128)(2,1)}, bf16[96,384]{1,0:T(8,128)(2,1)S(1)}, u32[]{:S(2)}, u32[]{:S(2)}) collective-permute-start(bf16[96,384]{1,0:T(8,128)(2,1)} %get-tuple-element.45), channel_id=1, source_target_pairs={{0,14},{1,15},{2,12},{3,13},{4,10},{5,11},{6,8},{7,9},{8,6},{9,7},... | collective-permute-start | bytes 221192 | tf_op jit(solution)/shard_map/ppermute | solution.py:410
  60.1 1.7 collective-permute-start.14
  61.7 1.5 collective-permute-done.12.refs_13_
  63.2 2.9 %collective-permute-done.13.refs_14_ = bf16[96,384]{1,0:T(8,128)(2,1)S(1)} collective-permute-done((bf16[96,384]{1,0:T(8,128)(2,1)}, bf16[96,384]{1,0:T(8,128)(2,1)S(1)}, u32[]{:S(2)}, u32[]{:S(2)}) %collective-permute-start.13) | collective-permute-done | bytes 73760 | tf_op jit(solution)/shard_map/ppermute | solution.py:410
  66.1 2.7 %collective-permute-done.14.refs_15_ = bf16[96,384]{1,0:T(8,128)(2,1)S(1)} collective-permute-done((bf16[96,384]{1,0:T(8,128)(2,1)}, bf16[96,384]{1,0:T(8,128)(2,1)S(1)}, u32[]{:S(2)}, u32[]{:S(2)}) %collective-permute-start.14) | collective-permute-done | bytes 73760 | tf_op jit(solution)/shard_map/ppermute | solution.py:410
  68.8 2.7 %shard_map.110 = bf16[16,96,384]{2,1,0:T(8,128)(2,1)} custom-call(bf16[32,96,384]{2,1,0:T(8,128)(2,1)S(1)} %all-to-all-done.recv, bf16[96,384]{1,0:T(8,128)(2,1)S(1)} %copy-done.14, bf16[96,384]{1,0:T(8,128)(2,1)S(1)} %collective-permute-done.refs_1_, bf16[96,384]{1,0:T(8,128)(2,1)S(1)} %collective-permute-done.1.refs_2_, ...), custom_call_target="tpu_custom_call" | custom-call | flops 452984832 | bytes 4718592 | tf_op jit(solution)/shard_map/pallas_call | solution.py:350
  71.5 0.0 copy-start.16
  71.6 0.0 copy-start.19
  71.6 0.0 copy-start.20
  71.6 0.0 copy-start.21
  71.6 0.0 copy-start.22
  71.6 4.5 %all-to-all-start.1 = ((bf16[16,96,384]{2,1,0:T(8,128)(2,1)}), bf16[16,96,384]{2,1,0:T(8,128)(2,1)S(1)}, u32[]{:S(2)}, u32[]{:S(2)}) async-start(bf16[16,96,384]{2,1,0:T(8,128)(2,1)} %shard_map.110), calls=%async_computation.1 | async-start | bytes 2359296 | tf_op jit(solution)/shard_map/all_to_all | solution.py:396
  76.3 1.9 shard_map.111
  78.2 1.4 copy-done.7
  79.6 14.3 %all-to-all-done.1.recv = bf16[16,96,384]{2,1,0:T(8,128)(2,1)S(1)} async-done(((bf16[16,96,384]{2,1,0:T(8,128)(2,1)}), bf16[16,96,384]{2,1,0:T(8,128)(2,1)S(1)}, u32[]{:S(2)}, u32[]{:S(2)}) %all-to-all-start.1) | async-done | bytes 1179680 | tf_op jit(solution)/shard_map/all_to_all | solution.py:396
  93.9 1.7 copy-done.8
  95.6 3.8 %shard_map.112 = (bf16[32,96,384]{2,1,0:T(8,128)(2,1)S(1)}, bf16[12,128,384]{2,1,0:T(8,128)(2,1)S(1)}) custom-call(bf16[16,96,384]{2,1,0:T(8,128)(2,1)S(1)} %all-to-all-done.1.recv, f32[12,128,384]{2,1,0:T(8,128)S(1)} %copy-done.8, bf16[12,128,384]{2,1,0:T(8,128)(2,1)S(1)} %copy-done.3, f32[2,384]{1,0:T(2,128)S(1)} %copy-done.17, ...), custom_call_target="tpu_custom_call" | custom-call | flops 754974720 | bytes 8965120 | tf_op jit(solution)/shard_map/pallas_call | solution.py:350
  99.4 60.6 %all_to_all.20.recv = bf16[32,96,384]{2,1,0:T(8,128)(2,1)S(1)} all-to-all(bf16[32,96,384]{2,1,0:T(8,128)(2,1)S(1)} %get-tuple-element.53), channel_id=1, replica_groups=mesh['grp'=1,'row'=32] {'row'}, dimensions={0} | all-to-all | bytes 4718592 | tf_op jit(solution)/shard_map/all_to_all | solution.py:396
  159.9 2.3 %shard_map.113 = bf16[32,48,384]{2,1,0:T(8,128)(2,1)} custom-call(bf16[32,96,384]{2,1,0:T(8,128)(2,1)S(1)} %all_to_all.20.recv), custom_call_target="tpu_custom_call" | custom-call | flops 452984832 | bytes 3538944 | tf_op jit(solution)/shard_map/pallas_call | solution.py:350
  162.3 2.7 %all-to-all-start.3 = ((bf16[32,48,384]{2,1,0:T(8,128)(2,1)}), bf16[32,48,384]{2,1,0:T(8,128)(2,1)S(1)}, u32[]{:S(2)}, u32[]{:S(2)}) async-start(bf16[32,48,384]{2,1,0:T(8,128)(2,1)} %shard_map.113), calls=%async_computation.3 | async-start | bytes 2359296 | tf_op jit(solution)/shard_map/all_to_all | solution.py:396
  164.9 1.3 copy-done.1
  166.2 1.0 copy-done.5
  167.2 0.9 copy-done.10
  168.2 0.7 copy-done.18
  168.8 1.5 shard_map.114.gate
  170.3 23.7 %all-to-all-done.3.recv = bf16[32,48,384]{2,1,0:T(8,128)(2,1)S(1)} async-done(((bf16[32,48,384]{2,1,0:T(8,128)(2,1)}), bf16[32,48,384]{2,1,0:T(8,128)(2,1)S(1)}, u32[]{:S(2)}, u32[]{:S(2)}) %all-to-all-start.3) | async-done | bytes 1179680 | tf_op jit(solution)/shard_map/all_to_all | solution.py:396
  194.0 1.3 copy-done.2
  195.2 1.0 copy-done.6
  196.3 0.9 copy-done.11
  197.2 2.5 %shard_map.115 = bf16[12,384,128]{2,1,0:T(8,128)(2,1)} custom-call(bf16[32,48,384]{2,1,0:T(8,128)(2,1)S(1)} %all-to-all-done.3.recv, f32[12,128,384]{2,1,0:T(8,128)S(1)} %shard_map.114.gate, bf16[12,128,384]{2,1,0:T(8,128)(2,1)S(1)} %copy-done.2, bf16[896,128]{1,0:T(8,128)(2,1)S(1)} %copy-done.11, f32[7,128,128]{2,1,0:T(8,128)S(1)} %copy-done.6), custom_call_target="tpu_custom_call" | custom-call | flops 150994944 | bytes 6586368 | tf_op jit(solution)/shard_map/pallas_call | solution.py:350
  (64 shorter events, 0.1 us)
Async XLA Ops:
  6.6 7.4 %copy-start.33 = (bf16[96,384]{1,0:T(8,128)(2,1)S(1)}, bf16[96,384]{1,0:T(8,128)(2,1)}, u32[]{:S(2)}) copy-start(bf16[96,384]{1,0:T(8,128)(2,1)} %get-tuple-element.32) | copy-start | bytes 221188
  6.6 7.7 %copy-start.32 = (bf16[96,384]{1,0:T(8,128)(2,1)S(1)}, bf16[96,384]{1,0:T(8,128)(2,1)}, u32[]{:S(2)}) copy-start(bf16[96,384]{1,0:T(8,128)(2,1)} %get-tuple-element.33) | copy-start | bytes 221188
  6.6 9.4 %copy-start.31 = (bf16[96,384]{1,0:T(8,128)(2,1)S(1)}, bf16[96,384]{1,0:T(8,128)(2,1)}, u32[]{:S(2)}) copy-start(bf16[96,384]{1,0:T(8,128)(2,1)} %get-tuple-element.34) | copy-start | bytes 221188
  6.6 9.4 %copy-start.30 = (bf16[96,384]{1,0:T(8,128)(2,1)S(1)}, bf16[96,384]{1,0:T(8,128)(2,1)}, u32[]{:S(2)}) copy-start(bf16[96,384]{1,0:T(8,128)(2,1)} %get-tuple-element.35) | copy-start | bytes 221188
  6.6 11.1 %copy-start.29 = (bf16[96,384]{1,0:T(8,128)(2,1)S(1)}, bf16[96,384]{1,0:T(8,128)(2,1)}, u32[]{:S(2)}) copy-start(bf16[96,384]{1,0:T(8,128)(2,1)} %get-tuple-element.36) | copy-start | bytes 221188
  6.6 11.2 %copy-start.28 = (bf16[96,384]{1,0:T(8,128)(2,1)S(1)}, bf16[96,384]{1,0:T(8,128)(2,1)}, u32[]{:S(2)}) copy-start(bf16[96,384]{1,0:T(8,128)(2,1)} %get-tuple-element.37) | copy-start | bytes 221188
  6.7 26.9 %copy-start.27 = (bf16[96,384]{1,0:T(8,128)(2,1)S(1)}, bf16[96,384]{1,0:T(8,128)(2,1)}, u32[]{:S(2)}) copy-start(bf16[96,384]{1,0:T(8,128)(2,1)} %get-tuple-element.38) | copy-start | bytes 221188
  6.7 27.7 %copy-start.26 = (bf16[96,384]{1,0:T(8,128)(2,1)S(1)}, bf16[96,384]{1,0:T(8,128)(2,1)}, u32[]{:S(2)}) copy-start(bf16[96,384]{1,0:T(8,128)(2,1)} %get-tuple-element.39) | copy-start | bytes 221188
  6.7 28.0 %copy-start.25 = (bf16[96,384]{1,0:T(8,128)(2,1)S(1)}, bf16[96,384]{1,0:T(8,128)(2,1)}, u32[]{:S(2)}) copy-start(bf16[96,384]{1,0:T(8,128)(2,1)} %get-tuple-element.40) | copy-start | bytes 221188
  6.7 30.3 %copy-start.24 = (bf16[96,384]{1,0:T(8,128)(2,1)S(1)}, bf16[96,384]{1,0:T(8,128)(2,1)}, u32[]{:S(2)}) copy-start(bf16[96,384]{1,0:T(8,128)(2,1)} %get-tuple-element.41) | copy-start | bytes 221188
  6.7 62.1 %copy-start.14 = (bf16[96,384]{1,0:T(8,128)(2,1)S(1)}, bf16[96,384]{1,0:T(8,128)(2,1)}, u32[]{:S(2)}) copy-start(bf16[96,384]{1,0:T(8,128)(2,1)} %get-tuple-element.31.refs_0_) | copy-start | bytes 221188
  6.7 62.1 %all-to-all-start = ((bf16[32,96,384]{2,1,0:T(8,128)(2,1)}), bf16[32,96,384]{2,1,0:T(8,128)(2,1)S(1)}, u32[]{:S(2)}, u32[]{:S(2)}) async-start(bf16[32,96,384]{2,1,0:T(8,128)(2,1)} %get-tuple-element.30), calls=%async_computation | async-start | bytes 4718592 | tf_op jit(solution)/shard_map/all_to_all | solution.py:396
  14.0 3.8 %collective-permute-start = (bf16[96,384]{1,0:T(8,128)(2,1)S(1)}, bf16[96,384]{1,0:T(8,128)(2,1)S(1)}, u32[]{:S(2)}, u32[]{:S(2)}) collective-permute-start(bf16[96,384]{1,0:T(8,128)(2,1)S(1)} %copy-done.33), channel_id=1, source_target_pairs={{0,1},{1,0},{2,3},{3,2},{4,5},{5,4},{6,7},{7,6},{8,9},{9,8},{10,11... | collective-permute-start | bytes 221192 | tf_op jit(solution)/shard_map/ppermute | solution.py:410
  14.4 19.2 %collective-permute-start.1 = (bf16[96,384]{1,0:T(8,128)(2,1)S(1)}, bf16[96,384]{1,0:T(8,128)(2,1)S(1)}, u32[]{:S(2)}, u32[]{:S(2)}) collective-permute-start(bf16[96,384]{1,0:T(8,128)(2,1)S(1)} %copy-done.32), channel_id=1, source_target_pairs={{0,2},{1,3},{2,0},{3,1},{4,6},{5,7},{6,4},{7,5},{8,10},{9,11},{10,... | collective-permute-start | bytes 221192 | tf_op jit(solution)/shard_map/ppermute | solution.py:410
  16.0 18.4 %collective-permute-start.2 = (bf16[96,384]{1,0:T(8,128)(2,1)S(1)}, bf16[96,384]{1,0:T(8,128)(2,1)S(1)}, u32[]{:S(2)}, u32[]{:S(2)}) collective-permute-start(bf16[96,384]{1,0:T(8,128)(2,1)S(1)} %copy-done.31), channel_id=1, source_target_pairs={{0,3},{1,2},{2,1},{3,0},{4,7},{5,6},{6,5},{7,4},{8,11},{9,10},{10,... | collective-permute-start | bytes 221192 | tf_op jit(solution)/shard_map/ppermute | solution.py:410
  16.1 18.6 %collective-permute-start.3 = (bf16[96,384]{1,0:T(8,128)(2,1)S(1)}, bf16[96,384]{1,0:T(8,128)(2,1)S(1)}, u32[]{:S(2)}, u32[]{:S(2)}) collective-permute-start(bf16[96,384]{1,0:T(8,128)(2,1)S(1)} %copy-done.30), channel_id=1, source_target_pairs={{0,4},{1,5},{2,6},{3,7},{4,0},{5,1},{6,2},{7,3},{8,12},{9,13},{10,... | collective-permute-start | bytes 221192 | tf_op jit(solution)/shard_map/ppermute | solution.py:410
  17.7 19.2 %collective-permute-start.4 = (bf16[96,384]{1,0:T(8,128)(2,1)S(1)}, bf16[96,384]{1,0:T(8,128)(2,1)S(1)}, u32[]{:S(2)}, u32[]{:S(2)}) collective-permute-start(bf16[96,384]{1,0:T(8,128)(2,1)S(1)} %copy-done.29), channel_id=1, source_target_pairs={{0,5},{1,4},{2,7},{3,6},{4,1},{5,0},{6,3},{7,2},{8,13},{9,12},{10,... | collective-permute-start | bytes 221192 | tf_op jit(solution)/shard_map/ppermute | solution.py:410
  17.9 26.2 %collective-permute-start.5 = (bf16[96,384]{1,0:T(8,128)(2,1)S(1)}, bf16[96,384]{1,0:T(8,128)(2,1)S(1)}, u32[]{:S(2)}, u32[]{:S(2)}) collective-permute-start(bf16[96,384]{1,0:T(8,128)(2,1)S(1)} %copy-done.28), channel_id=1, source_target_pairs={{0,6},{1,7},{2,4},{3,5},{4,2},{5,3},{6,0},{7,1},{8,14},{9,15},{10,... | collective-permute-start | bytes 221192 | tf_op jit(solution)/shard_map/ppermute | solution.py:410
  33.6 11.3 %collective-permute-start.6 = (bf16[96,384]{1,0:T(8,128)(2,1)S(1)}, bf16[96,384]{1,0:T(8,128)(2,1)S(1)}, u32[]{:S(2)}, u32[]{:S(2)}) collective-permute-start(bf16[96,384]{1,0:T(8,128)(2,1)S(1)} %copy-done.27), channel_id=1, source_target_pairs={{0,7},{1,6},{2,5},{3,4},{4,3},{5,2},{6,1},{7,0},{8,15},{9,14},{10,... | collective-permute-start | bytes 221192 | tf_op jit(solution)/shard_map/ppermute | solution.py:410
  34.4 20.8 %collective-permute-start.7 = (bf16[96,384]{1,0:T(8,128)(2,1)S(1)}, bf16[96,384]{1,0:T(8,128)(2,1)S(1)}, u32[]{:S(2)}, u32[]{:S(2)}) collective-permute-start(bf16[96,384]{1,0:T(8,128)(2,1)S(1)} %copy-done.26), channel_id=1, source_target_pairs={{0,8},{1,9},{2,10},{3,11},{4,12},{5,13},{6,14},{7,15},{8,0},{9,1},... | collective-permute-start | bytes 221192 | tf_op jit(solution)/shard_map/ppermute | solution.py:410
  34.7 22.6 %collective-permute-start.8 = (bf16[96,384]{1,0:T(8,128)(2,1)S(1)}, bf16[96,384]{1,0:T(8,128)(2,1)S(1)}, u32[]{:S(2)}, u32[]{:S(2)}) collective-permute-start(bf16[96,384]{1,0:T(8,128)(2,1)S(1)} %copy-done.25), channel_id=1, source_target_pairs={{0,9},{1,8},{2,11},{3,10},{4,13},{5,12},{6,15},{7,14},{8,1},{9,0},... | collective-permute-start | bytes 221192 | tf_op jit(solution)/shard_map/ppermute | solution.py:410
  37.0 23.1 %collective-permute-start.9 = (bf16[96,384]{1,0:T(8,128)(2,1)S(1)}, bf16[96,384]{1,0:T(8,128)(2,1)S(1)}, u32[]{:S(2)}, u32[]{:S(2)}) collective-permute-start(bf16[96,384]{1,0:T(8,128)(2,1)S(1)} %copy-done.24), channel_id=1, source_target_pairs={{0,10},{1,11},{2,8},{3,9},{4,14},{5,15},{6,12},{7,13},{8,2},{9,3},... | collective-permute-start | bytes 221192 | tf_op jit(solution)/shard_map/ppermute | solution.py:410
  44.1 17.7 %collective-permute-start.10 = (bf16[96,384]{1,0:T(8,128)(2,1)}, bf16[96,384]{1,0:T(8,128)(2,1)S(1)}, u32[]{:S(2)}, u32[]{:S(2)}) collective-permute-start(bf16[96,384]{1,0:T(8,128)(2,1)} %get-tuple-element.42), channel_id=1, source_target_pairs={{0,11},{1,10},{2,9},{3,8},{4,15},{5,14},{6,13},{7,12},{8,3},{9,2},... | collective-permute-start | bytes 221192 | tf_op jit(solution)/shard_map/ppermute | solution.py:410
  44.9 16.9 %collective-permute-start.11 = (bf16[96,384]{1,0:T(8,128)(2,1)}, bf16[96,384]{1,0:T(8,128)(2,1)S(1)}, u32[]{:S(2)}, u32[]{:S(2)}) collective-permute-start(bf16[96,384]{1,0:T(8,128)(2,1)} %get-tuple-element.43), channel_id=1, source_target_pairs={{0,12},{1,13},{2,14},{3,15},{4,8},{5,9},{6,10},{7,11},{8,4},{9,5},... | collective-permute-start | bytes 221192 | tf_op jit(solution)/shard_map/ppermute | solution.py:410
  55.2 8.0 %collective-permute-start.12 = (bf16[96,384]{1,0:T(8,128)(2,1)}, bf16[96,384]{1,0:T(8,128)(2,1)S(1)}, u32[]{:S(2)}, u32[]{:S(2)}) collective-permute-start(bf16[96,384]{1,0:T(8,128)(2,1)} %get-tuple-element.44), channel_id=1, source_target_pairs={{0,13},{1,12},{2,15},{3,14},{4,9},{5,8},{6,11},{7,10},{8,5},{9,4},... | collective-permute-start | bytes 221192 | tf_op jit(solution)/shard_map/ppermute | solution.py:410
  57.2 8.9 %collective-permute-start.13 = (bf16[96,384]{1,0:T(8,128)(2,1)}, bf16[96,384]{1,0:T(8,128)(2,1)S(1)}, u32[]{:S(2)}, u32[]{:S(2)}) collective-permute-start(bf16[96,384]{1,0:T(8,128)(2,1)} %get-tuple-element.45), channel_id=1, source_target_pairs={{0,14},{1,15},{2,12},{3,13},{4,10},{5,11},{6,8},{7,9},{8,6},{9,7},... | collective-permute-start | bytes 221192 | tf_op jit(solution)/shard_map/ppermute | solution.py:410
  60.1 8.8 %collective-permute-start.14 = (bf16[96,384]{1,0:T(8,128)(2,1)}, bf16[96,384]{1,0:T(8,128)(2,1)S(1)}, u32[]{:S(2)}, u32[]{:S(2)}) collective-permute-start(bf16[96,384]{1,0:T(8,128)(2,1)} %get-tuple-element.46), channel_id=1, source_target_pairs={{0,15},{1,14},{2,13},{3,12},{4,11},{5,10},{6,9},{7,8},{8,7},{9,6},... | collective-permute-start | bytes 221192 | tf_op jit(solution)/shard_map/ppermute | solution.py:410
  71.5 4.6 %copy-start.3 = (bf16[12,128,384]{2,1,0:T(8,128)(2,1)S(1)}, bf16[12,128,384]{2,1,0:T(8,128)(2,1)}, u32[]{:S(2)}) copy-start(bf16[12,128,384]{2,1,0:T(8,128)(2,1)} %get-tuple-element.47.x_t) | copy-start | bytes 3538948
  71.5 4.6 %copy-start.12 = (bf16[2,128,512]{2,1,0:T(8,128)(2,1)S(1)}, bf16[2,128,512]{2,1,0:T(8,128)(2,1)}, u32[]{:S(2)}) copy-start(bf16[2,128,512]{2,1,0:T(8,128)(2,1)} %w_ab.3) | copy-start | bytes 786436
  71.5 4.6 %copy-start.13 = (f32[2,16,128]{2,1,0:T(8,128)S(1)}, f32[2,16,128]{2,1,0:T(8,128)}, u32[]{:S(2)}) copy-start(f32[2,16,128]{2,1,0:T(8,128)} %get-tuple-element.49.row_marks) | copy-start | bytes 49156
  71.5 4.6 %copy-start.15 = (bf16[2,128,128]{2,1,0:T(8,128)(2,1)S(1)}, bf16[2,128,128]{2,1,0:T(8,128)(2,1)}, u32[]{:S(2)}) copy-start(bf16[2,128,128]{2,1,0:T(8,128)(2,1)} %w_gate.1) | copy-start | bytes 196612
  71.5 4.6 %copy-start.16 = (bf16[2,128,128]{2,1,0:T(8,128)(2,1)S(1)}, bf16[2,128,128]{2,1,0:T(8,128)(2,1)}, u32[]{:S(2)}) copy-start(bf16[2,128,128]{2,1,0:T(8,128)(2,1)} %w_out.1) | copy-start | bytes 196612
  71.6 4.6 %copy-start.17 = (f32[2,384]{1,0:T(2,128)S(1)}, f32[2,384]{1,0:T(2,128)}, u32[]{:S(2)}) copy-start(f32[2,384]{1,0:T(2,128)} %get-tuple-element.48.marks) | copy-start | bytes 9220
  71.6 4.6 %copy-start.19 = (f32[2,128]{1,0:T(2,128)S(1)}, f32[2,128]{1,0:T(2,128)}, u32[]{:S(2)}) copy-start(f32[2,128]{1,0:T(2,128)} %gain.3) | copy-start | bytes 3076
  71.6 4.6 %copy-start.20 = (f32[2,128]{1,0:T(2,128)S(1)}, f32[2,128]{1,0:T(2,128)}, u32[]{:S(2)}) copy-start(f32[2,128]{1,0:T(2,128)} %bias.3) | copy-start | bytes 3076
  71.6 4.6 %copy-start.21 = (f32[2,128]{1,0:T(2,128)S(1)}, f32[2,128]{1,0:T(2,128)}, u32[]{:S(2)}) copy-start(f32[2,128]{1,0:T(2,128)} %embed.3) | copy-start | bytes 3076
  71.6 4.6 %copy-start.22 = (f32[2,128]{1,0:T(2,128)S(1)}, f32[2,128]{1,0:T(2,128)}, u32[]{:S(2)}) copy-start(f32[2,128]{1,0:T(2,128)} %mid_gain.1) | copy-start | bytes 3076
  71.6 4.6 %copy-start.23 = (f32[2,128]{1,0:T(2,128)S(1)}, f32[2,128]{1,0:T(2,128)}, u32[]{:S(2)}) copy-start(f32[2,128]{1,0:T(2,128)} %mid_bias.1) | copy-start | bytes 3076
  71.6 22.3 %all-to-all-start.1 = ((bf16[16,96,384]{2,1,0:T(8,128)(2,1)}), bf16[16,96,384]{2,1,0:T(8,128)(2,1)S(1)}, u32[]{:S(2)}, u32[]{:S(2)}) async-start(bf16[16,96,384]{2,1,0:T(8,128)(2,1)} %shard_map.110), calls=%async_computation.1 | async-start | bytes 2359296 | tf_op jit(solution)/shard_map/all_to_all | solution.py:396
  78.2 1.4 copy-start.7
  79.6 19.8 %copy-start.4 = (f32[7,128,128]{2,1,0:T(8,128)}, f32[7,128,128]{2,1,0:T(8,128)S(1)}, u32[]{:S(2)}) copy-start(f32[7,128,128]{2,1,0:T(8,128)S(1)} %get-tuple-element.52.vectors.columns) | copy-start | bytes 1376260
  79.6 19.8 %copy-start.9 = (bf16[896,128]{1,0:T(8,128)(2,1)}, bf16[896,128]{1,0:T(8,128)(2,1)S(1)}, u32[]{:S(2)}) copy-start(bf16[896,128]{1,0:T(8,128)(2,1)S(1)} %get-tuple-element.51.weights) | copy-start | bytes 688132
  93.9 1.7 copy-start.8
  99.4 60.6 %copy-start = (bf16[12,128,384]{2,1,0:T(8,128)(2,1)}, bf16[12,128,384]{2,1,0:T(8,128)(2,1)S(1)}, u32[]{:S(2)}) copy-start(bf16[12,128,384]{2,1,0:T(8,128)(2,1)S(1)} %get-tuple-element.54.x_t) | copy-start | bytes 3538948
  162.3 31.7 %all-to-all-start.3 = ((bf16[32,48,384]{2,1,0:T(8,128)(2,1)}), bf16[32,48,384]{2,1,0:T(8,128)(2,1)S(1)}, u32[]{:S(2)}, u32[]{:S(2)}) async-start(bf16[32,48,384]{2,1,0:T(8,128)(2,1)} %shard_map.113), calls=%async_computation.3 | async-start | bytes 2359296 | tf_op jit(solution)/shard_map/all_to_all | solution.py:396
  164.9 1.3 copy-start.1
  166.2 1.0 copy-start.5
  194.0 1.3 copy-start.2
  (4 other events, 3.6 us)

commit v7 on v6

--- a/solution.py
+++ b/solution.py
@@ -71,16 +71,27 @@
                 out[d, side * half : (side + 1) * half, columns] = slabs[j, start : start + half, :].astype(BF16)
 
 
+def over(count, body):
+    if count <= 16:
+        for i in range(count):
+            body(i)
+    else:
+        lax.fori_loop(0, count, lambda i, carry: (body(i), carry)[1], 0)
+
+
 def write_crossing(slabs, out, own):
     devices, depth, width = out.shape
     half = devices // 2
     me = lax.axis_index("row")
+    mine = me // half * half
     side_rows = half * depth
-    for d in range(devices):
-        side = jnp.where(me // half == d // half, 0, side_rows)
-        start = pl.multiple_of(side + d % half * depth, 8)
-        for j, columns in blocks(width):
-            out[d, :, columns] = slabs[j, pl.ds(start, depth), :].astype(BF16)
+
+    def slab(q):
+        for first, side in ((mine, 0), (half - mine, side_rows)):
+            for j, columns in blocks(width):
+                out[first + q, :, columns] = slabs[j, pl.ds(side + q * depth, depth), :].astype(BF16)
+
+    over(half, slab)
     for o, ref in enumerate(own):
         start = pl.multiple_of(side_rows + (me % half ^ o) * depth, 8)
         for j, columns in blocks(width):
@@ -180,7 +191,7 @@
     def consume(group, normed):
         gates = jax.nn.sigmoid(jnp.dot(w_t, normed, preferred_element_type=F32))
         for k, r in enumerate(group):
-            out[r] = gates[:, k * width : (k + 1) * width]
+            out[r] = gates[:, k * width : (k + 1) * width].astype(BF16)
 
     overlapped(rows, prepare, consume)
 
@@ -227,13 +238,16 @@
     mine = me // half * half
     other = half - mine
     pitch = spread(depth)
-    for q in range(half):
-        to_other = (other + q) * pitch
-        to_own = (mine + (me % half ^ q)) * pitch
-        for j, columns in blocks(width):
-            left_wide[j, q * pitch : q * pitch + depth, :] = recv[mine + q, :, columns].astype(F32)
-            right_wide[j, pl.ds(to_other, depth), :] = recv[other + q, :, columns].astype(F32)
-            right_wide[j, pl.ds(to_own, depth), :] = own[q][:, columns].astype(F32)
+
+    def slab(q):
+        for j, columns in blocks(width):
+            left_wide[j, pl.ds(q * pitch, depth), :] = recv[mine + q, :, columns].astype(F32)
+            right_wide[j, pl.ds((other + q) * pitch, depth), :] = recv[other + q, :, columns].astype(F32)
+
+    over(half, slab)
+    for o, ref in enumerate(own):
+        for j, columns in blocks(width):
+            right_wide[j, pl.ds((mine + (me % half ^ o)) * pitch, depth), :] = ref[:, columns].astype(F32)
     for c in range(channels):
         left, right = [], []
         for j, _ in blocks(width):
@@ -307,7 +321,7 @@
     return {
         (r, j): (
             x_t[r, :, columns].astype(F32)
-            + gate[r, :, columns] * branch[:, k * width + j * 128 : k * width + (j + 1) * 128]
+            + gate[r, :, columns].astype(F32) * branch[:, k * width + j * 128 : k * width + (j + 1) * 128]
         ).astype(BF16)
         for k, r in enumerate(group)
         for j, columns in blocks(width)
@@ -373,7 +387,7 @@
     own_back = jax.ShapeDtypeStruct((half, 2 * channels * rows, width), BF16)
     own_slab = jax.ShapeDtypeStruct((2 * channels * rows, width), BF16)
     state_t = jax.ShapeDtypeStruct((rows, C, width), BF16)
-    gate_t = jax.ShapeDtypeStruct((rows, C, width), F32)
+    gate_t = jax.ShapeDtypeStruct((rows, C, width), BF16)
     mark = jax.ShapeDtypeStruct((2, width), F32)
     row_mark = jax.ShapeDtypeStruct((2, (rows + 7) // 8 * 8, 128), F32)
     turned = jax.ShapeDtypeStruct((7 * HC, C), BF16)
@@ -436,7 +450,7 @@
     tri = exchange(products)
     return call(
         last_kernel, [jax.ShapeDtypeStruct(pair.shape, BF16)], [tri_wide], (tri, gate, x_t, weights, vectors), (),
-        2 * pairs * C * C,
+        2 * pairs * C * C, FIRST_VMEM_LIMIT,
     )[0]
 
 

time: 200 us -> 203 us (1.015)
  Pallas kernels: 21.2 us -> 23.5 us
    pallas_call x7, Pallas kernels: 21.2 us -> 23.5 us  [call(): pl.pallas_call(kernel, out_shape=outs, in_specs=[WHOLE] * len(arrays) + [...]
    unnamed x68 -> x70, local copies, waits for them, and re-layouts: 10.3 us -> 8.58 us
where the time goes in v7:
time: 203 us; the launch traced here: 202 us
  waiting for transfers between devices  75.2 us (37%)
  blocking collectives  60.6 us (30%)
  starting transfers between devices  33.9 us (17%)
  Pallas kernels  23.5 us (12%)
  local copies, waits for them, and re-layouts  8.58 us (4%)
    all_to_all x1, blocking collectives, exchange(): lax.all_to_all(slabs, 'row', split_axis=0, concat_axis=0, tiled=True, axi...  60.6 us
    all_to_all x3, waiting for transfers between devices, exchange(): lax.all_to_all(slabs, 'row', split_axis=0, concat_axis=0, tiled=True, axi...  39.7 us
    ppermute x15, waiting for transfers between devices, local(): lax.ppermute(own[o], 'row', [(i, i ^ o) for i in range(devices)])  35.5 us
    pallas_call x7, Pallas kernels, call(): pl.pallas_call(kernel, out_shape=outs, in_specs=[WHOLE] * len(arrays) + [...  23.5 us
    ppermute x15, starting transfers between devices, local(): lax.ppermute(own[o], 'row', [(i, i ^ o) for i in range(devices)])  19.3 us
    all_to_all x3, starting transfers between devices, exchange(): lax.all_to_all(slabs, 'row', split_axis=0, concat_axis=0, tiled=True, axi...  14.6 us
    unnamed x70, local copies, waits for them, and re-layouts  8.58 us
  transfers between devices with their start and end apart: 18, of which 10 were waited for; matrix products, arithmetic and copies ran while one was open for 0% of the time, Pallas kernels for 2%

profile of v7, /device:TPU:0, one launch (start us, length us, event | category | flops | bytes accessed | tf_op | source)
XLA Modules:
  0.0 202.2 jit_solution(15928514072579106610)
XLA Ops:
  0.0 6.6 %shard_map.109 = (bf16[96,384]{1,0:T(8,128)(2,1)}, bf16[96,384]{1,0:T(8,128)(2,1)}, bf16[96,384]{1,0:T(8,128)(2,1)}, bf16[96,384]{1,0:T(8,128)(2,1)}, bf16[96,38...) custom-call(s32[384]{0:T(512)} %residue_mask.1, ...), custom_call_target="tpu_custom_call" | custom-call | flops 603979776 | bytes 4738048 | tf_op jit(solution)/shard_map/pallas_call | solution.py:364
  6.7 7.3 %all-to-all-start = ((bf16[32,96,384]{2,1,0:T(8,128)(2,1)}), bf16[32,96,384]{2,1,0:T(8,128)(2,1)S(1)}, u32[]{:S(2)}, u32[]{:S(2)}) async-start(bf16[32,96,384]{2,1,0:T(8,128)(2,1)} %get-tuple-element.30), calls=%async_computation | async-start | bytes 4718592 | tf_op jit(solution)/shard_map/all_to_all | solution.py:410
  14.0 0.3 collective-permute-start
  14.4 1.7 collective-permute-start.1
  16.0 0.0 collective-permute-start.2
  16.1 1.7 collective-permute-start.3
  17.7 0.1 collective-permute-start.4
  17.9 2.6 %collective-permute-start.5 = (bf16[96,384]{1,0:T(8,128)(2,1)S(1)}, bf16[96,384]{1,0:T(8,128)(2,1)S(1)}, u32[]{:S(2)}, u32[]{:S(2)}) collective-permute-start(bf16[96,384]{1,0:T(8,128)(2,1)S(1)} %copy-done.29), channel_id=1, source_target_pairs={{0,6},{1,7},{2,4},{3,5},{4,2},{5,3},{6,0},{7,1},{8,14},{9,15},{10,... | collective-permute-start | bytes 221192 | tf_op jit(solution)/shard_map/ppermute | solution.py:424
  20.4 13.1 %collective-permute-done.1.refs_2_ = bf16[96,384]{1,0:T(8,128)(2,1)S(1)} collective-permute-done((bf16[96,384]{1,0:T(8,128)(2,1)S(1)}, bf16[96,384]{1,0:T(8,128)(2,1)S(1)}, u32[]{:S(2)}, u32[]{:S(2)}) %collective-permute-start.1) | collective-permute-done | bytes 73760 | tf_op jit(solution)/shard_map/ppermute | solution.py:424
  33.6 0.6 collective-permute-start.6
  34.2 0.2 collective-permute-done.2.refs_3_
  34.4 0.3 collective-permute-start.7
  34.7 2.3 %collective-permute-start.8 = (bf16[96,384]{1,0:T(8,128)(2,1)S(1)}, bf16[96,384]{1,0:T(8,128)(2,1)S(1)}, u32[]{:S(2)}, u32[]{:S(2)}) collective-permute-start(bf16[96,384]{1,0:T(8,128)(2,1)S(1)} %copy-done.26), channel_id=1, source_target_pairs={{0,9},{1,8},{2,11},{3,10},{4,13},{5,12},{6,15},{7,14},{8,1},{9,0},... | collective-permute-start | bytes 221192 | tf_op jit(solution)/shard_map/ppermute | solution.py:424
  37.0 3.3 %collective-permute-start.9 = (bf16[96,384]{1,0:T(8,128)(2,1)S(1)}, bf16[96,384]{1,0:T(8,128)(2,1)S(1)}, u32[]{:S(2)}, u32[]{:S(2)}) collective-permute-start(bf16[96,384]{1,0:T(8,128)(2,1)S(1)} %copy-done.25), channel_id=1, source_target_pairs={{0,10},{1,11},{2,8},{3,9},{4,14},{5,15},{6,12},{7,13},{8,2},{9,3},... | collective-permute-start | bytes 221192 | tf_op jit(solution)/shard_map/ppermute | solution.py:424
  40.2 3.8 %collective-permute-done.5.refs_6_ = bf16[96,384]{1,0:T(8,128)(2,1)S(1)} collective-permute-done((bf16[96,384]{1,0:T(8,128)(2,1)S(1)}, bf16[96,384]{1,0:T(8,128)(2,1)S(1)}, u32[]{:S(2)}, u32[]{:S(2)}) %collective-permute-start.5) | collective-permute-done | bytes 73760 | tf_op jit(solution)/shard_map/ppermute | solution.py:424
  44.1 0.8 collective-permute-done.6.refs_7_
  44.9 10.3 %collective-permute-done.7.refs_8_ = bf16[96,384]{1,0:T(8,128)(2,1)S(1)} collective-permute-done((bf16[96,384]{1,0:T(8,128)(2,1)S(1)}, bf16[96,384]{1,0:T(8,128)(2,1)S(1)}, u32[]{:S(2)}, u32[]{:S(2)}) %collective-permute-start.7) | collective-permute-done | bytes 73760 | tf_op jit(solution)/shard_map/ppermute | solution.py:424
  55.2 2.0 collective-permute-start.12
  57.2 2.8 %collective-permute-start.13 = (bf16[96,384]{1,0:T(8,128)(2,1)}, bf16[96,384]{1,0:T(8,128)(2,1)S(1)}, u32[]{:S(2)}, u32[]{:S(2)}) collective-permute-start(bf16[96,384]{1,0:T(8,128)(2,1)} %get-tuple-element.45), channel_id=1, source_target_pairs={{0,14},{1,15},{2,12},{3,13},{4,10},{5,11},{6,8},{7,9},{8,6},{9,7},... | collective-permute-start | bytes 221192 | tf_op jit(solution)/shard_map/ppermute | solution.py:424
  60.1 1.7 collective-permute-start.14
  61.7 1.5 collective-permute-done.12.refs_13_
  63.2 2.9 %collective-permute-done.13.refs_14_ = bf16[96,384]{1,0:T(8,128)(2,1)S(1)} collective-permute-done((bf16[96,384]{1,0:T(8,128)(2,1)}, bf16[96,384]{1,0:T(8,128)(2,1)S(1)}, u32[]{:S(2)}, u32[]{:S(2)}) %collective-permute-start.13) | collective-permute-done | bytes 73760 | tf_op jit(solution)/shard_map/ppermute | solution.py:424
  66.1 2.7 %collective-permute-done.14.refs_15_ = bf16[96,384]{1,0:T(8,128)(2,1)S(1)} collective-permute-done((bf16[96,384]{1,0:T(8,128)(2,1)}, bf16[96,384]{1,0:T(8,128)(2,1)S(1)}, u32[]{:S(2)}, u32[]{:S(2)}) %collective-permute-start.14) | collective-permute-done | bytes 73760 | tf_op jit(solution)/shard_map/ppermute | solution.py:424
  68.8 2.7 %shard_map.110 = bf16[16,96,384]{2,1,0:T(8,128)(2,1)} custom-call(bf16[32,96,384]{2,1,0:T(8,128)(2,1)S(1)} %all-to-all-done.recv, bf16[96,384]{1,0:T(8,128)(2,1)S(1)} %copy-done.13, bf16[96,384]{1,0:T(8,128)(2,1)S(1)} %collective-permute-done.refs_1_, bf16[96,384]{1,0:T(8,128)(2,1)S(1)} %collective-permute-done.1.refs_2_, ...), custom_call_target="tpu_custom_call" | custom-call | flops 452984832 | bytes 4718592 | tf_op jit(solution)/shard_map/pallas_call | solution.py:364
  71.5 0.0 copy-start.15
  71.6 0.0 copy-start.19
  71.6 0.0 copy-start.20
  71.6 0.0 copy-start.21
  71.6 0.0 copy-start.23
  71.6 4.5 %all-to-all-start.1 = ((bf16[16,96,384]{2,1,0:T(8,128)(2,1)}), bf16[16,96,384]{2,1,0:T(8,128)(2,1)S(1)}, u32[]{:S(2)}, u32[]{:S(2)}) async-start(bf16[16,96,384]{2,1,0:T(8,128)(2,1)} %shard_map.110), calls=%async_computation.1 | async-start | bytes 2359296 | tf_op jit(solution)/shard_map/all_to_all | solution.py:410
  76.3 1.9 shard_map.111
  78.2 0.8 copy-done.3
  79.0 0.7 copy-done.6
  79.7 1.0 copy-done.9
  80.7 13.2 %all-to-all-done.1.recv = bf16[16,96,384]{2,1,0:T(8,128)(2,1)S(1)} async-done(((bf16[16,96,384]{2,1,0:T(8,128)(2,1)}), bf16[16,96,384]{2,1,0:T(8,128)(2,1)S(1)}, u32[]{:S(2)}, u32[]{:S(2)}) %all-to-all-start.1) | async-done | bytes 1179680 | tf_op jit(solution)/shard_map/all_to_all | solution.py:410
  93.9 1.0 copy-done.4
  94.9 0.9 copy-done.7
  95.9 1.3 copy-done.10
  97.1 0.7 copy-done.17
  97.8 3.9 %shard_map.112 = (bf16[32,96,384]{2,1,0:T(8,128)(2,1)S(1)}, bf16[12,128,384]{2,1,0:T(8,128)(2,1)S(1)}) custom-call(bf16[16,96,384]{2,1,0:T(8,128)(2,1)S(1)} %all-to-all-done.1.recv, bf16[12,128,384]{2,1,0:T(8,128)(2,1)S(1)} %copy-done.10, bf16[12,128,384]{2,1,0:T(8,128)(2,1)S(1)} %copy-done.2, f32[2,384]{1,0:T(2,128)S(1)} %copy-done.17, ...), custom_call_target="tpu_custom_call" | custom-call | flops 754974720 | bytes 7785472 | tf_op jit(solution)/shard_map/pallas_call | solution.py:364
  101.7 60.6 %all_to_all.20.recv = bf16[32,96,384]{2,1,0:T(8,128)(2,1)S(1)} all-to-all(bf16[32,96,384]{2,1,0:T(8,128)(2,1)S(1)} %get-tuple-element.53), channel_id=1, replica_groups=mesh['grp'=1,'row'=32] {'row'}, dimensions={0} | all-to-all | bytes 4718592 | tf_op jit(solution)/shard_map/all_to_all | solution.py:410
  162.2 2.3 %shard_map.113 = bf16[32,48,384]{2,1,0:T(8,128)(2,1)} custom-call(bf16[32,96,384]{2,1,0:T(8,128)(2,1)S(1)} %all_to_all.20.recv), custom_call_target="tpu_custom_call" | custom-call | flops 452984832 | bytes 3538944 | tf_op jit(solution)/shard_map/pallas_call | solution.py:364
  164.6 2.8 %all-to-all-start.3 = ((bf16[32,48,384]{2,1,0:T(8,128)(2,1)}), bf16[32,48,384]{2,1,0:T(8,128)(2,1)S(1)}, u32[]{:S(2)}, u32[]{:S(2)}) async-start(bf16[32,48,384]{2,1,0:T(8,128)(2,1)} %shard_map.113), calls=%async_computation.3 | async-start | bytes 2359296 | tf_op jit(solution)/shard_map/all_to_all | solution.py:410
  167.4 1.4 shard_map.114.gate
  168.9 1.0 copy-done.1
  169.9 26.5 %all-to-all-done.3.recv = bf16[32,48,384]{2,1,0:T(8,128)(2,1)S(1)} async-done(((bf16[32,48,384]{2,1,0:T(8,128)(2,1)}), bf16[32,48,384]{2,1,0:T(8,128)(2,1)S(1)}, u32[]{:S(2)}, u32[]{:S(2)}) %all-to-all-start.3) | async-done | bytes 1179680 | tf_op jit(solution)/shard_map/all_to_all | solution.py:410
  196.4 1.0 copy-done.24
  197.5 4.7 %shard_map.115 = bf16[12,384,128]{2,1,0:T(8,128)(2,1)} custom-call(bf16[32,48,384]{2,1,0:T(8,128)(2,1)} %copy-done.24, bf16[12,128,384]{2,1,0:T(8,128)(2,1)} %copy-done.1, bf16[12,128,384]{2,1,0:T(8,128)(2,1)} %copy-done, bf16[896,128]{1,0:T(8,128)(2,1)} %copy-done.6, f32[7,128,128]{2,1,0:T(8,128)} %copy-done.3), custom_call_target="tpu_custom_call" | custom-call | flops 150994944 | bytes 5406720 | tf_op jit(solution)/shard_map/pallas_call | solution.py:364
  (66 shorter events, 0.1 us)
Async XLA Ops:
  6.6 7.4 %copy-start.34 = (bf16[96,384]{1,0:T(8,128)(2,1)S(1)}, bf16[96,384]{1,0:T(8,128)(2,1)}, u32[]{:S(2)}) copy-start(bf16[96,384]{1,0:T(8,128)(2,1)} %get-tuple-element.32) | copy-start | bytes 221188
  6.6 7.7 %copy-start.33 = (bf16[96,384]{1,0:T(8,128)(2,1)S(1)}, bf16[96,384]{1,0:T(8,128)(2,1)}, u32[]{:S(2)}) copy-start(bf16[96,384]{1,0:T(8,128)(2,1)} %get-tuple-element.33) | copy-start | bytes 221188
  6.6 9.4 %copy-start.32 = (bf16[96,384]{1,0:T(8,128)(2,1)S(1)}, bf16[96,384]{1,0:T(8,128)(2,1)}, u32[]{:S(2)}) copy-start(bf16[96,384]{1,0:T(8,128)(2,1)} %get-tuple-element.34) | copy-start | bytes 221188
  6.6 9.4 %copy-start.31 = (bf16[96,384]{1,0:T(8,128)(2,1)S(1)}, bf16[96,384]{1,0:T(8,128)(2,1)}, u32[]{:S(2)}) copy-start(bf16[96,384]{1,0:T(8,128)(2,1)} %get-tuple-element.35) | copy-start | bytes 221188
  6.6 11.1 %copy-start.30 = (bf16[96,384]{1,0:T(8,128)(2,1)S(1)}, bf16[96,384]{1,0:T(8,128)(2,1)}, u32[]{:S(2)}) copy-start(bf16[96,384]{1,0:T(8,128)(2,1)} %get-tuple-element.36) | copy-start | bytes 221188
  6.6 11.2 %copy-start.29 = (bf16[96,384]{1,0:T(8,128)(2,1)S(1)}, bf16[96,384]{1,0:T(8,128)(2,1)}, u32[]{:S(2)}) copy-start(bf16[96,384]{1,0:T(8,128)(2,1)} %get-tuple-element.37) | copy-start | bytes 221188
  6.7 26.9 %copy-start.28 = (bf16[96,384]{1,0:T(8,128)(2,1)S(1)}, bf16[96,384]{1,0:T(8,128)(2,1)}, u32[]{:S(2)}) copy-start(bf16[96,384]{1,0:T(8,128)(2,1)} %get-tuple-element.38) | copy-start | bytes 221188
  6.7 27.7 %copy-start.27 = (bf16[96,384]{1,0:T(8,128)(2,1)S(1)}, bf16[96,384]{1,0:T(8,128)(2,1)}, u32[]{:S(2)}) copy-start(bf16[96,384]{1,0:T(8,128)(2,1)} %get-tuple-element.39) | copy-start | bytes 221188
  6.7 28.0 %copy-start.26 = (bf16[96,384]{1,0:T(8,128)(2,1)S(1)}, bf16[96,384]{1,0:T(8,128)(2,1)}, u32[]{:S(2)}) copy-start(bf16[96,384]{1,0:T(8,128)(2,1)} %get-tuple-element.40) | copy-start | bytes 221188
  6.7 30.3 %copy-start.25 = (bf16[96,384]{1,0:T(8,128)(2,1)S(1)}, bf16[96,384]{1,0:T(8,128)(2,1)}, u32[]{:S(2)}) copy-start(bf16[96,384]{1,0:T(8,128)(2,1)} %get-tuple-element.41) | copy-start | bytes 221188
  6.7 62.1 %copy-start.13 = (bf16[96,384]{1,0:T(8,128)(2,1)S(1)}, bf16[96,384]{1,0:T(8,128)(2,1)}, u32[]{:S(2)}) copy-start(bf16[96,384]{1,0:T(8,128)(2,1)} %get-tuple-element.31.refs_0_) | copy-start | bytes 221188
  6.7 62.1 %all-to-all-start = ((bf16[32,96,384]{2,1,0:T(8,128)(2,1)}), bf16[32,96,384]{2,1,0:T(8,128)(2,1)S(1)}, u32[]{:S(2)}, u32[]{:S(2)}) async-start(bf16[32,96,384]{2,1,0:T(8,128)(2,1)} %get-tuple-element.30), calls=%async_computation | async-start | bytes 4718592 | tf_op jit(solution)/shard_map/all_to_all | solution.py:410
  14.0 3.8 %collective-permute-start = (bf16[96,384]{1,0:T(8,128)(2,1)S(1)}, bf16[96,384]{1,0:T(8,128)(2,1)S(1)}, u32[]{:S(2)}, u32[]{:S(2)}) collective-permute-start(bf16[96,384]{1,0:T(8,128)(2,1)S(1)} %copy-done.34), channel_id=1, source_target_pairs={{0,1},{1,0},{2,3},{3,2},{4,5},{5,4},{6,7},{7,6},{8,9},{9,8},{10,11... | collective-permute-start | bytes 221192 | tf_op jit(solution)/shard_map/ppermute | solution.py:424
  14.4 19.2 %collective-permute-start.1 = (bf16[96,384]{1,0:T(8,128)(2,1)S(1)}, bf16[96,384]{1,0:T(8,128)(2,1)S(1)}, u32[]{:S(2)}, u32[]{:S(2)}) collective-permute-start(bf16[96,384]{1,0:T(8,128)(2,1)S(1)} %copy-done.33), channel_id=1, source_target_pairs={{0,2},{1,3},{2,0},{3,1},{4,6},{5,7},{6,4},{7,5},{8,10},{9,11},{10,... | collective-permute-start | bytes 221192 | tf_op jit(solution)/shard_map/ppermute | solution.py:424
  16.0 18.4 %collective-permute-start.2 = (bf16[96,384]{1,0:T(8,128)(2,1)S(1)}, bf16[96,384]{1,0:T(8,128)(2,1)S(1)}, u32[]{:S(2)}, u32[]{:S(2)}) collective-permute-start(bf16[96,384]{1,0:T(8,128)(2,1)S(1)} %copy-done.32), channel_id=1, source_target_pairs={{0,3},{1,2},{2,1},{3,0},{4,7},{5,6},{6,5},{7,4},{8,11},{9,10},{10,... | collective-permute-start | bytes 221192 | tf_op jit(solution)/shard_map/ppermute | solution.py:424
  16.1 18.6 %collective-permute-start.3 = (bf16[96,384]{1,0:T(8,128)(2,1)S(1)}, bf16[96,384]{1,0:T(8,128)(2,1)S(1)}, u32[]{:S(2)}, u32[]{:S(2)}) collective-permute-start(bf16[96,384]{1,0:T(8,128)(2,1)S(1)} %copy-done.31), channel_id=1, source_target_pairs={{0,4},{1,5},{2,6},{3,7},{4,0},{5,1},{6,2},{7,3},{8,12},{9,13},{10,... | collective-permute-start | bytes 221192 | tf_op jit(solution)/shard_map/ppermute | solution.py:424
  17.7 19.2 %collective-permute-start.4 = (bf16[96,384]{1,0:T(8,128)(2,1)S(1)}, bf16[96,384]{1,0:T(8,128)(2,1)S(1)}, u32[]{:S(2)}, u32[]{:S(2)}) collective-permute-start(bf16[96,384]{1,0:T(8,128)(2,1)S(1)} %copy-done.30), channel_id=1, source_target_pairs={{0,5},{1,4},{2,7},{3,6},{4,1},{5,0},{6,3},{7,2},{8,13},{9,12},{10,... | collective-permute-start | bytes 221192 | tf_op jit(solution)/shard_map/ppermute | solution.py:424
  17.9 26.2 %collective-permute-start.5 = (bf16[96,384]{1,0:T(8,128)(2,1)S(1)}, bf16[96,384]{1,0:T(8,128)(2,1)S(1)}, u32[]{:S(2)}, u32[]{:S(2)}) collective-permute-start(bf16[96,384]{1,0:T(8,128)(2,1)S(1)} %copy-done.29), channel_id=1, source_target_pairs={{0,6},{1,7},{2,4},{3,5},{4,2},{5,3},{6,0},{7,1},{8,14},{9,15},{10,... | collective-permute-start | bytes 221192 | tf_op jit(solution)/shard_map/ppermute | solution.py:424
  33.6 11.3 %collective-permute-start.6 = (bf16[96,384]{1,0:T(8,128)(2,1)S(1)}, bf16[96,384]{1,0:T(8,128)(2,1)S(1)}, u32[]{:S(2)}, u32[]{:S(2)}) collective-permute-start(bf16[96,384]{1,0:T(8,128)(2,1)S(1)} %copy-done.28), channel_id=1, source_target_pairs={{0,7},{1,6},{2,5},{3,4},{4,3},{5,2},{6,1},{7,0},{8,15},{9,14},{10,... | collective-permute-start | bytes 221192 | tf_op jit(solution)/shard_map/ppermute | solution.py:424
  34.4 20.8 %collective-permute-start.7 = (bf16[96,384]{1,0:T(8,128)(2,1)S(1)}, bf16[96,384]{1,0:T(8,128)(2,1)S(1)}, u32[]{:S(2)}, u32[]{:S(2)}) collective-permute-start(bf16[96,384]{1,0:T(8,128)(2,1)S(1)} %copy-done.27), channel_id=1, source_target_pairs={{0,8},{1,9},{2,10},{3,11},{4,12},{5,13},{6,14},{7,15},{8,0},{9,1},... | collective-permute-start | bytes 221192 | tf_op jit(solution)/shard_map/ppermute | solution.py:424
  34.7 22.6 %collective-permute-start.8 = (bf16[96,384]{1,0:T(8,128)(2,1)S(1)}, bf16[96,384]{1,0:T(8,128)(2,1)S(1)}, u32[]{:S(2)}, u32[]{:S(2)}) collective-permute-start(bf16[96,384]{1,0:T(8,128)(2,1)S(1)} %copy-done.26), channel_id=1, source_target_pairs={{0,9},{1,8},{2,11},{3,10},{4,13},{5,12},{6,15},{7,14},{8,1},{9,0},... | collective-permute-start | bytes 221192 | tf_op jit(solution)/shard_map/ppermute | solution.py:424
  37.0 23.1 %collective-permute-start.9 = (bf16[96,384]{1,0:T(8,128)(2,1)S(1)}, bf16[96,384]{1,0:T(8,128)(2,1)S(1)}, u32[]{:S(2)}, u32[]{:S(2)}) collective-permute-start(bf16[96,384]{1,0:T(8,128)(2,1)S(1)} %copy-done.25), channel_id=1, source_target_pairs={{0,10},{1,11},{2,8},{3,9},{4,14},{5,15},{6,12},{7,13},{8,2},{9,3},... | collective-permute-start | bytes 221192 | tf_op jit(solution)/shard_map/ppermute | solution.py:424
  44.1 17.7 %collective-permute-start.10 = (bf16[96,384]{1,0:T(8,128)(2,1)}, bf16[96,384]{1,0:T(8,128)(2,1)S(1)}, u32[]{:S(2)}, u32[]{:S(2)}) collective-permute-start(bf16[96,384]{1,0:T(8,128)(2,1)} %get-tuple-element.42), channel_id=1, source_target_pairs={{0,11},{1,10},{2,9},{3,8},{4,15},{5,14},{6,13},{7,12},{8,3},{9,2},... | collective-permute-start | bytes 221192 | tf_op jit(solution)/shard_map/ppermute | solution.py:424
  44.9 16.9 %collective-permute-start.11 = (bf16[96,384]{1,0:T(8,128)(2,1)}, bf16[96,384]{1,0:T(8,128)(2,1)S(1)}, u32[]{:S(2)}, u32[]{:S(2)}) collective-permute-start(bf16[96,384]{1,0:T(8,128)(2,1)} %get-tuple-element.43), channel_id=1, source_target_pairs={{0,12},{1,13},{2,14},{3,15},{4,8},{5,9},{6,10},{7,11},{8,4},{9,5},... | collective-permute-start | bytes 221192 | tf_op jit(solution)/shard_map/ppermute | solution.py:424
  55.2 8.0 %collective-permute-start.12 = (bf16[96,384]{1,0:T(8,128)(2,1)}, bf16[96,384]{1,0:T(8,128)(2,1)S(1)}, u32[]{:S(2)}, u32[]{:S(2)}) collective-permute-start(bf16[96,384]{1,0:T(8,128)(2,1)} %get-tuple-element.44), channel_id=1, source_target_pairs={{0,13},{1,12},{2,15},{3,14},{4,9},{5,8},{6,11},{7,10},{8,5},{9,4},... | collective-permute-start | bytes 221192 | tf_op jit(solution)/shard_map/ppermute | solution.py:424
  57.2 8.9 %collective-permute-start.13 = (bf16[96,384]{1,0:T(8,128)(2,1)}, bf16[96,384]{1,0:T(8,128)(2,1)S(1)}, u32[]{:S(2)}, u32[]{:S(2)}) collective-permute-start(bf16[96,384]{1,0:T(8,128)(2,1)} %get-tuple-element.45), channel_id=1, source_target_pairs={{0,14},{1,15},{2,12},{3,13},{4,10},{5,11},{6,8},{7,9},{8,6},{9,7},... | collective-permute-start | bytes 221192 | tf_op jit(solution)/shard_map/ppermute | solution.py:424
  60.1 8.8 %collective-permute-start.14 = (bf16[96,384]{1,0:T(8,128)(2,1)}, bf16[96,384]{1,0:T(8,128)(2,1)S(1)}, u32[]{:S(2)}, u32[]{:S(2)}) collective-permute-start(bf16[96,384]{1,0:T(8,128)(2,1)} %get-tuple-element.46), channel_id=1, source_target_pairs={{0,15},{1,14},{2,13},{3,12},{4,11},{5,10},{6,9},{7,8},{8,7},{9,6},... | collective-permute-start | bytes 221192 | tf_op jit(solution)/shard_map/ppermute | solution.py:424
  71.5 4.6 %copy-start.2 = (bf16[12,128,384]{2,1,0:T(8,128)(2,1)S(1)}, bf16[12,128,384]{2,1,0:T(8,128)(2,1)}, u32[]{:S(2)}) copy-start(bf16[12,128,384]{2,1,0:T(8,128)(2,1)} %get-tuple-element.47.x_t) | copy-start | bytes 3538948
  71.5 4.6 %copy-start.11 = (bf16[2,128,512]{2,1,0:T(8,128)(2,1)S(1)}, bf16[2,128,512]{2,1,0:T(8,128)(2,1)}, u32[]{:S(2)}) copy-start(bf16[2,128,512]{2,1,0:T(8,128)(2,1)} %w_ab.3) | copy-start | bytes 786436
  71.5 4.6 %copy-start.12 = (f32[2,16,128]{2,1,0:T(8,128)S(1)}, f32[2,16,128]{2,1,0:T(8,128)}, u32[]{:S(2)}) copy-start(f32[2,16,128]{2,1,0:T(8,128)} %get-tuple-element.49.row_marks) | copy-start | bytes 49156
  71.5 4.6 %copy-start.14 = (bf16[2,128,128]{2,1,0:T(8,128)(2,1)S(1)}, bf16[2,128,128]{2,1,0:T(8,128)(2,1)}, u32[]{:S(2)}) copy-start(bf16[2,128,128]{2,1,0:T(8,128)(2,1)} %w_gate.1) | copy-start | bytes 196612
  71.5 4.6 %copy-start.15 = (bf16[2,128,128]{2,1,0:T(8,128)(2,1)S(1)}, bf16[2,128,128]{2,1,0:T(8,128)(2,1)}, u32[]{:S(2)}) copy-start(bf16[2,128,128]{2,1,0:T(8,128)(2,1)} %w_out.1) | copy-start | bytes 196612
  71.6 4.6 %copy-start.16 = (f32[2,384]{1,0:T(2,128)S(1)}, f32[2,384]{1,0:T(2,128)}, u32[]{:S(2)}) copy-start(f32[2,384]{1,0:T(2,128)} %get-tuple-element.48.marks) | copy-start | bytes 9220
  71.6 4.6 %copy-start.19 = (f32[2,128]{1,0:T(2,128)S(1)}, f32[2,128]{1,0:T(2,128)}, u32[]{:S(2)}) copy-start(f32[2,128]{1,0:T(2,128)} %gain.3) | copy-start | bytes 3076
  71.6 4.6 %copy-start.20 = (f32[2,128]{1,0:T(2,128)S(1)}, f32[2,128]{1,0:T(2,128)}, u32[]{:S(2)}) copy-start(f32[2,128]{1,0:T(2,128)} %bias.3) | copy-start | bytes 3076
  71.6 4.6 %copy-start.21 = (f32[2,128]{1,0:T(2,128)S(1)}, f32[2,128]{1,0:T(2,128)}, u32[]{:S(2)}) copy-start(f32[2,128]{1,0:T(2,128)} %embed.3) | copy-start | bytes 3076
  71.6 4.6 %copy-start.22 = (f32[2,128]{1,0:T(2,128)S(1)}, f32[2,128]{1,0:T(2,128)}, u32[]{:S(2)}) copy-start(f32[2,128]{1,0:T(2,128)} %mid_gain.1) | copy-start | bytes 3076
  71.6 4.6 %copy-start.23 = (f32[2,128]{1,0:T(2,128)S(1)}, f32[2,128]{1,0:T(2,128)}, u32[]{:S(2)}) copy-start(f32[2,128]{1,0:T(2,128)} %mid_bias.1) | copy-start | bytes 3076
  71.6 22.3 %all-to-all-start.1 = ((bf16[16,96,384]{2,1,0:T(8,128)(2,1)}), bf16[16,96,384]{2,1,0:T(8,128)(2,1)S(1)}, u32[]{:S(2)}, u32[]{:S(2)}) async-start(bf16[16,96,384]{2,1,0:T(8,128)(2,1)} %shard_map.110), calls=%async_computation.1 | async-start | bytes 2359296 | tf_op jit(solution)/shard_map/all_to_all | solution.py:410
  93.9 1.0 copy-start.4
  95.9 1.3 copy-start.10
  101.7 65.7 %copy-start = (bf16[12,128,384]{2,1,0:T(8,128)(2,1)}, bf16[12,128,384]{2,1,0:T(8,128)(2,1)S(1)}, u32[]{:S(2)}) copy-start(bf16[12,128,384]{2,1,0:T(8,128)(2,1)S(1)} %get-tuple-element.54.x_t) | copy-start | bytes 3538948
  164.6 2.8 %copy-start.5 = (f32[7,128,128]{2,1,0:T(8,128)S(1)}, f32[7,128,128]{2,1,0:T(8,128)}, u32[]{:S(2)}) copy-start(f32[7,128,128]{2,1,0:T(8,128)} %copy-done.3) | copy-start | bytes 1376260
  164.6 2.8 %copy-start.8 = (bf16[896,128]{1,0:T(8,128)(2,1)S(1)}, bf16[896,128]{1,0:T(8,128)(2,1)}, u32[]{:S(2)}) copy-start(bf16[896,128]{1,0:T(8,128)(2,1)} %copy-done.6) | copy-start | bytes 688132
  164.6 2.8 %copy-start.18 = (f32[2,384]{1,0:T(2,128)S(1)}, f32[2,384]{1,0:T(2,128)}, u32[]{:S(2)}) copy-start(f32[2,384]{1,0:T(2,128)} %get-tuple-element.48.marks) | copy-start | bytes 9220
  164.6 31.8 %all-to-all-start.3 = ((bf16[32,48,384]{2,1,0:T(8,128)(2,1)}), bf16[32,48,384]{2,1,0:T(8,128)(2,1)S(1)}, u32[]{:S(2)}, u32[]{:S(2)}) async-start(bf16[32,48,384]{2,1,0:T(8,128)(2,1)} %shard_map.113), calls=%async_computation.3 | async-start | bytes 2359296 | tf_op jit(solution)/shard_map/all_to_all | solution.py:410
  168.9 1.0 copy-start.1
  196.4 1.0 copy-start.24
  (5 other events, 4.1 us)

commit v8 on v7

--- a/solution.py
+++ b/solution.py
@@ -48,27 +48,15 @@
     return (marks[1:2, columns] == row_marks[1, r : r + 1, :]).astype(F32)
 
 
-def project(group, normed, marks, row_marks, w_t, slabs):
-    rows = slabs.shape[1] // (2 * HC)
-    width = slabs.shape[0] * 128
+def project(group, normed, marks, row_marks, w_t, put):
+    width = marks.shape[1]
     proj = jnp.dot(w_t, normed, preferred_element_type=F32)
     for k, r in enumerate(group):
         for j, columns in blocks(width):
             mask = marks[0:1, columns] * row_marks[0, r : r + 1, :]
             for side in range(2):
                 p = proj[2 * side * HC : (2 * side + 2) * HC, k * width + j * 128 : k * width + (j + 1) * 128]
-                value = jax.nn.sigmoid(p[:HC]) * p[HC:] * mask
-                slabs[j, pl.ds(side * HC * rows + r, HC, stride=rows), :] = value
-
-
-def write_slabs(slabs, out):
-    devices, depth, width = out.shape
-    half = depth // 2
-    for side in range(2):
-        for d in range(devices):
-            start = (side * devices + d) * half
-            for j, columns in blocks(width):
-                out[d, side * half : (side + 1) * half, columns] = slabs[j, start : start + half, :].astype(BF16)
+                put(side, r, j, jax.nn.sigmoid(p[:HC]) * p[HC:] * mask)
 
 
 def over(count, body):
@@ -168,8 +156,11 @@
                 parts.append(norm_input(values, same, g[...], b[...], e[...]))
         return jnp.concatenate(parts, axis=1)
 
+    def put(side, r, j, values):
+        slabs[j, pl.ds(side * HC * rows + r, HC, stride=rows), :] = values
+
     def consume(group, normed):
-        project(group, normed, marks, row_marks, w_t[...], slabs)
+        project(group, normed, marks, row_marks, w_t[...], put)
 
     overlapped(rows, prepare, consume)
     write_crossing(slabs, out, own)
@@ -191,7 +182,7 @@
     def consume(group, normed):
         gates = jax.nn.sigmoid(jnp.dot(w_t, normed, preferred_element_type=F32))
         for k, r in enumerate(group):
-            out[r] = gates[:, k * width : (k + 1) * width].astype(BF16)
+            out[r] = gates[:, k * width : (k + 1) * width]
 
     overlapped(rows, prepare, consume)
 
@@ -270,48 +261,56 @@
             out[q, :, columns] = turned[j, q * pitch : q * pitch + depth, :].astype(BF16)
 
 
-def second_products_kernel(rows, recv, out, wide, natural, turned):
+def split_channels(devices):
+    once = 3 * HC // (4 * devices)
+    return HC // (devices // 2) - 2 * once, once
+
+
+def second_products_kernel(rows, recv, *refs):
+    own, (out, wide, own_wide, natural, turned) = refs[:-5], refs[-5:]
     devices, depth, width = recv.shape
-    channels = depth // (2 * rows)
-    pitch, out_pitch = spread(depth), spread(channels * rows)
+    half = devices // 2
+    twice, once = split_channels(devices)
+    own_depth = own[0].shape[0]
+    pitch, own_pitch, out_pitch = spread(depth), spread(own_depth), spread((twice + once) * rows)
     widen(recv, wide, pitch)
-
-    def by_row(side, c):
+    for o, ref in enumerate(own):
+        for j, columns in blocks(width):
+            own_wide[j, o * own_pitch : o * own_pitch + own_depth, :] = ref[:, columns].astype(F32)
+
+    def by_row(ref, start, count, stride):
         return jnp.concatenate(
             [
                 jnp.concatenate(
-                    [
-                        wide[j, pl.ds((side * channels + c) * rows + r, devices, stride=pitch), :].astype(BF16)
-                        for r in range(rows)
-                    ],
-                    axis=0,
+                    [ref[j, pl.ds(start + r, count, stride=stride), :].astype(BF16) for r in range(rows)], axis=0
                 )
                 for j, _ in blocks(width)
             ],
             axis=1,
         )
 
-    for c in range(channels):
-        product = lax.dot_general(
-            by_row(0, c), by_row(1, c), (((0,), (0,)), ((), ())), preferred_element_type=F32
-        )
-        for j, columns in blocks(width):
-            natural[c, j] = product[:, columns]
+    for t in range(twice + once):
+        if t < twice:
+            left, right = (by_row(own_wide, (side * twice + t) * rows, half, own_pitch) for side in range(2))
+        else:
+            left, right = (by_row(wide, (side * once + t - twice) * rows, devices, pitch) for side in range(2))
+        product = lax.dot_general(left, right, (((0,), (0,)), ((), ())), preferred_element_type=F32)
+        for j, columns in blocks(width):
+            natural[t, j] = product[:, columns]
             for r in range(rows):
-                turned[j, pl.ds(c * rows + r, devices, stride=out_pitch), :] = natural[
-                    c, j, pl.ds(r, devices, stride=rows), :
+                turned[j, pl.ds(t * rows + r, devices, stride=out_pitch), :] = natural[
+                    t, j, pl.ds(r, devices, stride=rows), :
                 ]
     for s in range(devices):
         for j, columns in blocks(width):
-            out[s, :, columns] = turned[j, s * out_pitch : s * out_pitch + channels * rows, :].astype(BF16)
-
-
-def finish(layer, group, width, tri, gate, x_t, weights, vectors):
-    rows = tri.shape[1] // HC
+            out[s, :, columns] = turned[j, s * out_pitch : s * out_pitch + out.shape[1], :].astype(BF16)
+
+
+def finish(layer, group, width, values, gate, x_t, weights, vectors):
     gain, bias = vectors[MID_GAIN[layer]], vectors[MID_BIAS[layer]]
     normed = jnp.concatenate(
         [
-            norm_channels(tri[j, pl.ds(r, HC, stride=rows), :], gain, bias).astype(BF16)
+            norm_channels(values(r, j), gain, bias).astype(BF16)
             for r in group
             for j, _ in blocks(width)
         ],
@@ -321,19 +320,28 @@
     return {
         (r, j): (
             x_t[r, :, columns].astype(F32)
-            + gate[r, :, columns].astype(F32) * branch[:, k * width + j * 128 : k * width + (j + 1) * 128]
+            + gate[r, :, columns] * branch[:, k * width + j * 128 : k * width + (j + 1) * 128]
         ).astype(BF16)
         for k, r in enumerate(group)
         for j, columns in blocks(width)
     }
 
 
-def middle_kernel(recv, gate, x_t, marks, row_marks, weights, vectors, out, new_t, slabs, tri):
+def middle_kernel(recv, gate, x_t, marks, row_marks, weights, vectors, *refs):
+    own, (out, new_t, slabs, own_slabs, tri) = refs[:-5], refs[-5:]
     rows, _, width = x_t.shape
+    devices, depth, _ = out.shape
+    half = devices // 2
+    twice, once = split_channels(devices)
+    own_depth = own[0].shape[0]
+    pitch, own_pitch = spread(depth), spread(own_depth)
     widen(recv, tri, recv.shape[1])
 
+    def values(r, j):
+        return tri[j, pl.ds(r, HC, stride=rows), :]
+
     def prepare(group):
-        states = finish(0, group, width, tri, gate, x_t, weights, vectors)
+        states = finish(0, group, width, values, gate, x_t, weights, vectors)
         parts = []
         for r in group:
             for j, columns in blocks(width):
@@ -344,18 +352,45 @@
                 )
         return jnp.concatenate(parts, axis=1)
 
+    def put(side, r, j, value):
+        for ch in range(twice):
+            own_slabs[j, pl.ds((side * twice + ch) * rows + r, half, stride=own_pitch), :] = value[
+                ch * half : (ch + 1) * half
+            ]
+        for ch in range(once):
+            start = twice * half + ch * devices
+            slabs[j, pl.ds((side * once + ch) * rows + r, devices, stride=pitch), :] = value[start : start + devices]
+
     def consume(group, normed):
-        project(group, normed, marks, row_marks, weights[W_AB, :], slabs)
+        project(group, normed, marks, row_marks, weights[W_AB, :], put)
 
     overlapped(rows, prepare, consume)
-    write_slabs(slabs, out)
+    for d in range(devices):
+        for j, columns in blocks(width):
+            out[d, :, columns] = slabs[j, d * pitch : d * pitch + depth, :].astype(BF16)
+    place = lax.axis_index("row") % half
+    for o, ref in enumerate(own):
+        for j, columns in blocks(width):
+            ref[:, columns] = own_slabs[j, pl.ds((place ^ o) * own_pitch, own_depth), :].astype(BF16)
 
 
 def last_kernel(recv, gate, x_t, weights, vectors, out, tri):
     rows, _, width = x_t.shape
-    widen(recv, tri, recv.shape[1])
+    devices, depth, _ = recv.shape
+    half = devices // 2
+    twice, once = split_channels(devices)
+    pitch = spread(depth)
+    widen(recv, tri, pitch)
+
+    def values(r, j):
+        def part(first, count, t):
+            return tri[j, pl.ds(first * pitch + t * rows + r, count, stride=pitch), :]
+
+        sums = [part(0, half, t) + part(half, half, t) for t in range(twice)]
+        return jnp.concatenate(sums + [part(0, devices, twice + t) for t in range(once)], axis=0)
+
     for group in groups(rows):
-        for (r, j), state in finish(1, group, width, tri, gate, x_t, weights, vectors).items():
+        for (r, j), state in finish(1, group, width, values, gate, x_t, weights, vectors).items():
             out[r, j * 128 : (j + 1) * 128, :] = state.astype(F32).T.astype(BF16)
 
 
@@ -383,11 +418,14 @@
     pairs = rows * width
 
     sent = jax.ShapeDtypeStruct((devices, 2 * channels * rows, width), BF16)
-    back = jax.ShapeDtypeStruct((devices, channels * rows, width), BF16)
+    twice, once = split_channels(devices)
+    sent_once = jax.ShapeDtypeStruct((devices, 2 * once * rows, width), BF16)
+    sent_twice = jax.ShapeDtypeStruct((2 * twice * rows, width), BF16)
+    back = jax.ShapeDtypeStruct((devices, (twice + once) * rows, width), BF16)
     own_back = jax.ShapeDtypeStruct((half, 2 * channels * rows, width), BF16)
     own_slab = jax.ShapeDtypeStruct((2 * channels * rows, width), BF16)
     state_t = jax.ShapeDtypeStruct((rows, C, width), BF16)
-    gate_t = jax.ShapeDtypeStruct((rows, C, width), BF16)
+    gate_t = jax.ShapeDtypeStruct((rows, C, width), F32)
     mark = jax.ShapeDtypeStruct((2, width), F32)
     row_mark = jax.ShapeDtypeStruct((2, (rows + 7) // 8 * 8, 128), F32)
     turned = jax.ShapeDtypeStruct((7 * HC, C), BF16)
@@ -399,7 +437,9 @@
     slabs_wide = pltpu.VMEM((cols, 2 * HC * rows, 128), F32)
     own_spread = pltpu.VMEM((cols, half * spread(2 * channels * rows), 128), F32)
     all_spread = pltpu.VMEM((cols, devices * spread(2 * channels * rows), 128), F32)
-    back_spread = pltpu.VMEM((cols, devices * spread(channels * rows), 128), F32)
+    once_spread = pltpu.VMEM((cols, devices * spread(2 * once * rows), 128), F32)
+    twice_spread = pltpu.VMEM((cols, half * spread(2 * twice * rows), 128), F32)
+    back_spread = pltpu.VMEM((cols, devices * spread((twice + once) * rows), 128), F32)
     tri_wide = pltpu.VMEM((cols, HC * rows, 128), F32)
     norms = (ln_in_gain, ln_in_bias, chain_embed)
 
@@ -410,6 +450,11 @@
         return lax.all_to_all(
             slabs, "row", split_axis=0, concat_axis=0, tiled=True, axis_index_groups=groups
         )
+
+    def exchange_own(slabs):
+        return slabs[:1] + [
+            lax.ppermute(slabs[o], "row", [(i, i ^ o) for i in range(devices)]) for o in range(1, half)
+        ]
 
     halves = [list(range(h * half, (h + 1) * half)) for h in range(2)]
     *own, slabs, x_t, marks, row_marks = call(
@@ -421,7 +466,7 @@
         (), (residue_mask, chain_ids, pair, *norms, w_ab), 2 * pairs * C * 4 * HC, FIRST_VMEM_LIMIT,
     )
     recv = exchange(slabs)
-    own = [own[0]] + [lax.ppermute(own[o], "row", [(i, i ^ o) for i in range(devices)]) for o in range(1, half)]
+    own = exchange_own(own)
     gate, weights, vectors = call(
         gate_kernel, [gate_t, turned, columns],
         [pltpu.VMEM((5, 2, C), F32), pltpu.VMEM((2, 2, C, C), BF16), w_wide, sems(8)],
@@ -435,22 +480,24 @@
         (recv, *own), (), 2 * channels * width**3, PRODUCTS_VMEM_LIMIT,
     )[0]
     tri = exchange(products, halves)
-    slabs, x_t = call(
-        middle_kernel, [sent, state_t], [slabs_wide, tri_wide],
+    *own, slabs, x_t = call(
+        middle_kernel, [sent_twice] * half + [sent_once, state_t], [once_spread, twice_spread, tri_wide],
         (tri, gate, x_t, marks, row_marks, weights, vectors), (), 2 * pairs * C * 5 * HC,
     )
     recv = exchange(slabs)
+    own = exchange_own(own)
     gate = call(
         second_gate_kernel, [gate_t], [], (x_t, marks, row_marks, weights, vectors), (), 2 * pairs * C * C
     )[0]
     products = call(
         functools.partial(second_products_kernel, rows), [back],
-        [all_spread, pltpu.VMEM((channels, cols, width, 128), F32), back_spread], (recv,), (), 2 * channels * width**3,
+        [once_spread, twice_spread, pltpu.VMEM((twice + once, cols, width, 128), F32), back_spread],
+        (recv, *own), (), 2 * channels * width**3,
     )[0]
     tri = exchange(products)
     return call(
-        last_kernel, [jax.ShapeDtypeStruct(pair.shape, BF16)], [tri_wide], (tri, gate, x_t, weights, vectors), (),
-        2 * pairs * C * C, FIRST_VMEM_LIMIT,
+        last_kernel, [jax.ShapeDtypeStruct(pair.shape, BF16)], [back_spread], (tri, gate, x_t, weights, vectors), (),
+        2 * pairs * C * C,
     )[0]
 
 

time: 203 us -> 210 us (1.034)
  blocking collectives: 60.6 us -> 0 us
  waiting for transfers between devices: 75.2 us -> 106 us
  starting transfers between devices: 33.9 us -> 59 us
  local copies, waits for them, and re-layouts: 8.58 us -> 20.4 us
    all_to_all x1 -> x0, blocking collectives: 60.6 us -> none  [exchange(): lax.all_to_all(slabs, 'row', split_axis=0, concat_axis=0, tiled=True, axi...]
    ppermute x15 -> x30, waiting for transfers between devices: 35.5 us -> 58.5 us  [exchange_own(): lax.ppermute(slabs[o], 'row', [(i, i ^ o) for i in range(devices)])]
    ppermute x15 -> x30, starting transfers between devices: 19.3 us -> 36.9 us  [exchange_own(): lax.ppermute(slabs[o], 'row', [(i, i ^ o) for i in range(devices)])]
    unnamed x70 -> x116, local copies, waits for them, and re-layouts: 8.58 us -> 20.4 us
    all_to_all x3 -> x4, waiting for transfers between devices: 39.7 us -> 47.6 us  [exchange(): lax.all_to_all(slabs, 'row', split_axis=0, concat_axis=0, tiled=True, axi...]
    all_to_all x3 -> x4, starting transfers between devices: 14.6 us -> 22.1 us  [exchange(): lax.all_to_all(slabs, 'row', split_axis=0, concat_axis=0, tiled=True, axi...]
  transfers between devices with their start and end apart: 18 -> 34, of which waited for: 10 -> 16; matrix products, arithmetic and copies ran while one was open for 0% -> 0% of each run, Pallas kernels for 2% -> 2%
where the time goes in v8:
time: 210 us
  waiting for transfers between devices  106 us (50%)
  starting transfers between devices  59 us (28%)
  Pallas kernels  23.5 us (11%)
  local copies, waits for them, and re-layouts  20.4 us (10%)
    ppermute x30, waiting for transfers between devices, exchange_own(): lax.ppermute(slabs[o], 'row', [(i, i ^ o) for i in range(devices)])  58.5 us
    all_to_all x4, waiting for transfers between devices, exchange(): lax.all_to_all(slabs, 'row', split_axis=0, concat_axis=0, tiled=True, axi...  47.6 us
    ppermute x30, starting transfers between devices, exchange_own(): lax.ppermute(slabs[o], 'row', [(i, i ^ o) for i in range(devices)])  36.9 us
    pallas_call x7, Pallas kernels, call(): pl.pallas_call(kernel, out_shape=outs, in_specs=[WHOLE] * len(arrays) + [...  23.5 us
    all_to_all x4, starting transfers between devices, exchange(): lax.all_to_all(slabs, 'row', split_axis=0, concat_axis=0, tiled=True, axi...  22.1 us
    unnamed x116, local copies, waits for them, and re-layouts  20.4 us
  transfers between devices with their start and end apart: 34, of which 16 were waited for; matrix products, arithmetic and copies ran while one was open for 0% of the time, Pallas kernels for 2%

profile of v8, /device:TPU:0, one launch (start us, length us, event | category | flops | bytes accessed | tf_op | source)
XLA Modules:
  0.0 209.5 jit_solution(2832408272926082198)
XLA Ops:
  0.0 6.6 %shard_map.109 = (bf16[96,384]{1,0:T(8,128)(2,1)}, bf16[96,384]{1,0:T(8,128)(2,1)}, bf16[96,384]{1,0:T(8,128)(2,1)}, bf16[96,384]{1,0:T(8,128)(2,1)}, bf16[96,38...) custom-call(s32[384]{0:T(512)} %residue_mask.1, ...), custom_call_target="tpu_custom_call" | custom-call | flops 603979776 | bytes 4738048 | tf_op jit(solution)/shard_map/pallas_call | solution.py:399
  6.7 7.3 %all-to-all-start = ((bf16[32,96,384]{2,1,0:T(8,128)(2,1)}), bf16[32,96,384]{2,1,0:T(8,128)(2,1)S(1)}, u32[]{:S(2)}, u32[]{:S(2)}) async-start(bf16[32,96,384]{2,1,0:T(8,128)(2,1)} %get-tuple-element.46), calls=%async_computation | async-start | bytes 4718592 | tf_op jit(solution)/shard_map/all_to_all | solution.py:450
  14.3 1.7 collective-permute-start.1
  16.0 1.7 collective-permute-start.3
  17.9 2.6 %collective-permute-start.5 = (bf16[96,384]{1,0:T(8,128)(2,1)S(1)}, bf16[96,384]{1,0:T(8,128)(2,1)S(1)}, u32[]{:S(2)}, u32[]{:S(2)}) collective-permute-start(bf16[96,384]{1,0:T(8,128)(2,1)S(1)} %copy-done.52), channel_id=1, source_target_pairs={{0,6},{1,7},{2,4},{3,5},{4,2},{5,3},{6,0},{7,1},{8,14},{9,15},{10,... | collective-permute-start | bytes 221192 | tf_op jit(solution)/shard_map/ppermute | solution.py:456
  20.4 13.1 %collective-permute-done.1.refs_2_ = bf16[96,384]{1,0:T(8,128)(2,1)S(1)} collective-permute-done((bf16[96,384]{1,0:T(8,128)(2,1)S(1)}, bf16[96,384]{1,0:T(8,128)(2,1)S(1)}, u32[]{:S(2)}, u32[]{:S(2)}) %collective-permute-start.1) | collective-permute-done | bytes 73760 | tf_op jit(solution)/shard_map/ppermute | solution.py:456
  34.7 2.3 %collective-permute-start.8 = (bf16[96,384]{1,0:T(8,128)(2,1)S(1)}, bf16[96,384]{1,0:T(8,128)(2,1)S(1)}, u32[]{:S(2)}, u32[]{:S(2)}) collective-permute-start(bf16[96,384]{1,0:T(8,128)(2,1)S(1)} %copy-done.49), channel_id=1, source_target_pairs={{0,9},{1,8},{2,11},{3,10},{4,13},{5,12},{6,15},{7,14},{8,1},{9,0},... | collective-permute-start | bytes 221192 | tf_op jit(solution)/shard_map/ppermute | solution.py:456
  36.9 3.3 %collective-permute-start.9 = (bf16[96,384]{1,0:T(8,128)(2,1)S(1)}, bf16[96,384]{1,0:T(8,128)(2,1)S(1)}, u32[]{:S(2)}, u32[]{:S(2)}) collective-permute-start(bf16[96,384]{1,0:T(8,128)(2,1)S(1)} %copy-done.48), channel_id=1, source_target_pairs={{0,10},{1,11},{2,8},{3,9},{4,14},{5,15},{6,12},{7,13},{8,2},{9,3},... | collective-permute-start | bytes 221192 | tf_op jit(solution)/shard_map/ppermute | solution.py:456
  40.2 3.8 %collective-permute-done.5.refs_6_ = bf16[96,384]{1,0:T(8,128)(2,1)S(1)} collective-permute-done((bf16[96,384]{1,0:T(8,128)(2,1)S(1)}, bf16[96,384]{1,0:T(8,128)(2,1)S(1)}, u32[]{:S(2)}, u32[]{:S(2)}) %collective-permute-start.5) | collective-permute-done | bytes 73760 | tf_op jit(solution)/shard_map/ppermute | solution.py:456
  44.9 10.3 %collective-permute-done.7.refs_8_ = bf16[96,384]{1,0:T(8,128)(2,1)S(1)} collective-permute-done((bf16[96,384]{1,0:T(8,128)(2,1)S(1)}, bf16[96,384]{1,0:T(8,128)(2,1)S(1)}, u32[]{:S(2)}, u32[]{:S(2)}) %collective-permute-start.7) | collective-permute-done | bytes 73760 | tf_op jit(solution)/shard_map/ppermute | solution.py:456
  55.2 2.0 collective-permute-start.12
  57.2 2.8 %collective-permute-start.13 = (bf16[96,384]{1,0:T(8,128)(2,1)}, bf16[96,384]{1,0:T(8,128)(2,1)S(1)}, u32[]{:S(2)}, u32[]{:S(2)}) collective-permute-start(bf16[96,384]{1,0:T(8,128)(2,1)} %get-tuple-element.61), channel_id=1, source_target_pairs={{0,14},{1,15},{2,12},{3,13},{4,10},{5,11},{6,8},{7,9},{8,6},{9,7},... | collective-permute-start | bytes 221192 | tf_op jit(solution)/shard_map/ppermute | solution.py:456
  60.0 1.7 collective-permute-start.14
  61.7 1.5 collective-permute-done.12.refs_13_
  63.2 2.9 %collective-permute-done.13.refs_14_ = bf16[96,384]{1,0:T(8,128)(2,1)S(1)} collective-permute-done((bf16[96,384]{1,0:T(8,128)(2,1)}, bf16[96,384]{1,0:T(8,128)(2,1)S(1)}, u32[]{:S(2)}, u32[]{:S(2)}) %collective-permute-start.13) | collective-permute-done | bytes 73760 | tf_op jit(solution)/shard_map/ppermute | solution.py:456
  66.1 2.7 %collective-permute-done.14.refs_15_ = bf16[96,384]{1,0:T(8,128)(2,1)S(1)} collective-permute-done((bf16[96,384]{1,0:T(8,128)(2,1)}, bf16[96,384]{1,0:T(8,128)(2,1)S(1)}, u32[]{:S(2)}, u32[]{:S(2)}) %collective-permute-start.14) | collective-permute-done | bytes 73760 | tf_op jit(solution)/shard_map/ppermute | solution.py:456
  68.8 2.7 %shard_map.110 = bf16[16,96,384]{2,1,0:T(8,128)(2,1)} custom-call(bf16[32,96,384]{2,1,0:T(8,128)(2,1)S(1)} %all-to-all-done.recv, bf16[96,384]{1,0:T(8,128)(2,1)S(1)} %copy-done.14, bf16[96,384]{1,0:T(8,128)(2,1)S(1)} %collective-permute-done.refs_1_, bf16[96,384]{1,0:T(8,128)(2,1)S(1)} %collective-permute-done.1.refs_2_, ...), custom_call_target="tpu_custom_call" | custom-call | flops 452984832 | bytes 4718592 | tf_op jit(solution)/shard_map/pallas_call | solution.py:399
  71.6 4.5 %all-to-all-start.1 = ((bf16[16,96,384]{2,1,0:T(8,128)(2,1)}), bf16[16,96,384]{2,1,0:T(8,128)(2,1)S(1)}, u32[]{:S(2)}, u32[]{:S(2)}) async-start(bf16[16,96,384]{2,1,0:T(8,128)(2,1)} %shard_map.110), calls=%async_computation.1 | async-start | bytes 2359296 | tf_op jit(solution)/shard_map/all_to_all | solution.py:450
  76.2 1.9 shard_map.111
  78.9 1.4 copy-done.5
  81.0 12.9 %all-to-all-done.1.recv = bf16[16,96,384]{2,1,0:T(8,128)(2,1)S(1)} async-done(((bf16[16,96,384]{2,1,0:T(8,128)(2,1)}), bf16[16,96,384]{2,1,0:T(8,128)(2,1)S(1)}, u32[]{:S(2)}, u32[]{:S(2)}) %all-to-all-start.1) | async-done | bytes 1179680 | tf_op jit(solution)/shard_map/all_to_all | solution.py:450
  93.9 1.0 copy-done.2
  94.9 1.7 copy-done.6
  98.2 4.4 %shard_map.112 = (bf16[48,384]{1,0:T(8,128)(2,1)S(1)}, bf16[48,384]{1,0:T(8,128)(2,1)S(1)}, bf16[48,384]{1,0:T(8,128)(2,1)S(1)}, bf16[48,384]{1,0:T(8,128)(2,1)S...) custom-call(bf16[16,96,384]{2,1,0:T(8,128)(2,1)S(1)} %all-to-all-don, ...), custom_call_target="tpu_custom_call" | custom-call | flops 754974720 | bytes 8965120 | tf_op jit(solution)/shard_map/pallas_call | solution.py:399
  102.5 1.2 copy-done.11
  111.1 5.1 %all-to-all-start.2 = ((bf16[32,72,384]{2,1,0:T(8,128)(2,1)}), bf16[32,72,384]{2,1,0:T(8,128)(2,1)S(1)}, u32[]{:S(2)}, u32[]{:S(2)}) async-start(bf16[32,72,384]{2,1,0:T(8,128)(2,1)} %copy-done.11), calls=%async_computation.2 | async-start | bytes 3538944 | tf_op jit(solution)/shard_map/all_to_all | solution.py:450
  116.5 1.7 collective-permute-start.16
  118.2 1.7 collective-permute-start.18
  120.0 2.6 %collective-permute-start.20 = (bf16[48,384]{1,0:T(8,128)(2,1)S(1)}, bf16[48,384]{1,0:T(8,128)(2,1)S(1)}, u32[]{:S(2)}, u32[]{:S(2)}) collective-permute-start(bf16[48,384]{1,0:T(8,128)(2,1)S(1)} %copy-done.37), channel_id=1, source_target_pairs={{0,6},{1,7},{2,4},{3,5},{4,2},{5,3},{6,0},{7,1},{8,14},{9,15},{10,... | collective-permute-start | bytes 110600 | tf_op jit(solution)/shard_map/ppermute | solution.py:456
  122.6 8.7 %collective-permute-done.16.refs_2_ = bf16[48,384]{1,0:T(8,128)(2,1)S(1)} collective-permute-done((bf16[48,384]{1,0:T(8,128)(2,1)S(1)}, bf16[48,384]{1,0:T(8,128)(2,1)S(1)}, u32[]{:S(2)}, u32[]{:S(2)}) %collective-permute-start.16) | collective-permute-done | bytes 36896 | tf_op jit(solution)/shard_map/ppermute | solution.py:456
  131.8 2.7 %collective-permute-start.23 = (bf16[48,384]{1,0:T(8,128)(2,1)S(1)}, bf16[48,384]{1,0:T(8,128)(2,1)S(1)}, u32[]{:S(2)}, u32[]{:S(2)}) collective-permute-start(bf16[48,384]{1,0:T(8,128)(2,1)S(1)} %copy-done.31), channel_id=1, source_target_pairs={{0,9},{1,8},{2,11},{3,10},{4,13},{5,12},{6,15},{7,14},{8,1},{9,0},... | collective-permute-start | bytes 110600 | tf_op jit(solution)/shard_map/ppermute | solution.py:456
  135.1 1.0 collective-permute-start.25
  136.2 1.5 collective-permute-done.21.refs_7_
  137.7 9.5 %collective-permute-done.22.refs_8_ = bf16[48,384]{1,0:T(8,128)(2,1)S(1)} collective-permute-done((bf16[48,384]{1,0:T(8,128)(2,1)S(1)}, bf16[48,384]{1,0:T(8,128)(2,1)S(1)}, u32[]{:S(2)}, u32[]{:S(2)}) %collective-permute-start.22) | collective-permute-done | bytes 36896 | tf_op jit(solution)/shard_map/ppermute | solution.py:456
  147.2 1.6 collective-permute-start.27
  148.8 2.4 %collective-permute-start.28 = (bf16[48,384]{1,0:T(8,128)(2,1)}, bf16[48,384]{1,0:T(8,128)(2,1)S(1)}, u32[]{:S(2)}, u32[]{:S(2)}) collective-permute-start(bf16[48,384]{1,0:T(8,128)(2,1)} %get-tuple-element.84), channel_id=1, source_target_pairs={{0,14},{1,15},{2,12},{3,13},{4,10},{5,11},{6,8},{7,9},{8,6},{9,7},... | collective-permute-start | bytes 110600 | tf_op jit(solution)/shard_map/ppermute | solution.py:456
  151.2 2.4 %collective-permute-start.29 = (bf16[48,384]{1,0:T(8,128)(2,1)}, bf16[48,384]{1,0:T(8,128)(2,1)S(1)}, u32[]{:S(2)}, u32[]{:S(2)}) collective-permute-start(bf16[48,384]{1,0:T(8,128)(2,1)} %copy-done.27), channel_id=1, source_target_pairs={{0,15},{1,14},{2,13},{3,12},{4,11},{5,10},{6,9},{7,8},{8,7},{9,6},... | collective-permute-start | bytes 110600 | tf_op jit(solution)/shard_map/ppermute | solution.py:456
  153.6 1.6 collective-permute-done.28.refs_14_
  155.2 1.7 collective-permute-done.29.refs_15_
  157.0 1.1 all-to-all-done.2.recv
  158.1 2.6 %shard_map.113 = bf16[32,60,384]{2,1,0:T(8,128)(2,1)} custom-call(bf16[32,72,384]{2,1,0:T(8,128)(2,1)S(1)} %all-to-all-done.2.recv, bf16[48,384]{1,0:T(8,128)(2,1)S(1)} %copy-done.18, bf16[48,384]{1,0:T(8,128)(2,1)S(1)} %collective-permute-done.15.refs_1_, bf16[48,384]{1,0:T(8,128)(2,1)S(1)} %collective-permute-done.16.refs_2_, ...), custom_call_target="tpu_custom_call" | custom-call | flops 452984832 | bytes 3833856 | tf_op jit(solution)/shard_map/pallas_call | solution.py:399
  160.7 5.2 %all-to-all-start.3 = ((bf16[32,60,384]{2,1,0:T(8,128)(2,1)}), bf16[32,60,384]{2,1,0:T(8,128)(2,1)}, u32[]{:S(2)}, u32[]{:S(2)}) async-start(bf16[32,60,384]{2,1,0:T(8,128)(2,1)} %shard_map.113), calls=%async_computation.3 | async-start | bytes 3145728 | tf_op jit(solution)/shard_map/all_to_all | solution.py:450
  165.9 1.0 copy-done.3
  166.9 0.9 copy-done.9
  168.5 1.5 shard_map.114.gate
  170.0 33.6 %all-to-all-done.3.recv = bf16[32,60,384]{2,1,0:T(8,128)(2,1)} async-done(((bf16[32,60,384]{2,1,0:T(8,128)(2,1)}), bf16[32,60,384]{2,1,0:T(8,128)(2,1)}, u32[]{:S(2)}, u32[]{:S(2)}) %all-to-all-start.3) | async-done | bytes 1474592 | tf_op jit(solution)/shard_map/all_to_all | solution.py:450
  203.6 1.0 copy-done.4
  205.6 4.0 %shard_map.115 = bf16[12,384,128]{2,1,0:T(8,128)(2,1)} custom-call(bf16[32,60,384]{2,1,0:T(8,128)(2,1)} %all-to-all-done.3.recv, f32[12,128,384]{2,1,0:T(8,128)S(1)} %shard_map.114.gate, bf16[12,128,384]{2,1,0:T(8,128)(2,1)S(1)} %get-tuple-element.86.x_t, bf16[896,128]{1,0:T(8,128)(2,1)S(1)} %copy-done.10, f32[7,128,128]{2,1,0:T(8,128)S(1)} %copy-done.4), custom_call_target="tpu_custom_call" | custom-call | flops 150994944 | bytes 6881280 | tf_op jit(solution)/shard_map/pallas_call | solution.py:399
  (143 shorter events, 16.1 us)
Async XLA Ops:
  6.6 9.4 %copy-start.55 = (bf16[96,384]{1,0:T(8,128)(2,1)S(1)}, bf16[96,384]{1,0:T(8,128)(2,1)}, u32[]{:S(2)}) copy-start(bf16[96,384]{1,0:T(8,128)(2,1)} %get-tuple-element.50) | copy-start | bytes 221188
  6.6 9.4 %copy-start.54 = (bf16[96,384]{1,0:T(8,128)(2,1)S(1)}, bf16[96,384]{1,0:T(8,128)(2,1)}, u32[]{:S(2)}) copy-start(bf16[96,384]{1,0:T(8,128)(2,1)} %get-tuple-element.51) | copy-start | bytes 221188
  6.6 11.1 %copy-start.53 = (bf16[96,384]{1,0:T(8,128)(2,1)S(1)}, bf16[96,384]{1,0:T(8,128)(2,1)}, u32[]{:S(2)}) copy-start(bf16[96,384]{1,0:T(8,128)(2,1)} %get-tuple-element.52) | copy-start | bytes 221188
  6.6 11.2 %copy-start.52 = (bf16[96,384]{1,0:T(8,128)(2,1)S(1)}, bf16[96,384]{1,0:T(8,128)(2,1)}, u32[]{:S(2)}) copy-start(bf16[96,384]{1,0:T(8,128)(2,1)} %get-tuple-element.53) | copy-start | bytes 221188
  6.6 26.9 %copy-start.51 = (bf16[96,384]{1,0:T(8,128)(2,1)S(1)}, bf16[96,384]{1,0:T(8,128)(2,1)}, u32[]{:S(2)}) copy-start(bf16[96,384]{1,0:T(8,128)(2,1)} %get-tuple-element.54) | copy-start | bytes 221188
  6.7 27.7 %copy-start.50 = (bf16[96,384]{1,0:T(8,128)(2,1)S(1)}, bf16[96,384]{1,0:T(8,128)(2,1)}, u32[]{:S(2)}) copy-start(bf16[96,384]{1,0:T(8,128)(2,1)} %get-tuple-element.55) | copy-start | bytes 221188
  6.7 28.0 %copy-start.49 = (bf16[96,384]{1,0:T(8,128)(2,1)S(1)}, bf16[96,384]{1,0:T(8,128)(2,1)}, u32[]{:S(2)}) copy-start(bf16[96,384]{1,0:T(8,128)(2,1)} %get-tuple-element.56) | copy-start | bytes 221188
  6.7 30.3 %copy-start.48 = (bf16[96,384]{1,0:T(8,128)(2,1)S(1)}, bf16[96,384]{1,0:T(8,128)(2,1)}, u32[]{:S(2)}) copy-start(bf16[96,384]{1,0:T(8,128)(2,1)} %get-tuple-element.57) | copy-start | bytes 221188
  6.7 62.1 %copy-start.14 = (bf16[96,384]{1,0:T(8,128)(2,1)S(1)}, bf16[96,384]{1,0:T(8,128)(2,1)}, u32[]{:S(2)}) copy-start(bf16[96,384]{1,0:T(8,128)(2,1)} %get-tuple-element.47.refs_0_) | copy-start | bytes 221188
  6.7 62.1 %all-to-all-start = ((bf16[32,96,384]{2,1,0:T(8,128)(2,1)}), bf16[32,96,384]{2,1,0:T(8,128)(2,1)S(1)}, u32[]{:S(2)}, u32[]{:S(2)}) async-start(bf16[32,96,384]{2,1,0:T(8,128)(2,1)} %get-tuple-element.46), calls=%async_computation | async-start | bytes 4718592 | tf_op jit(solution)/shard_map/all_to_all | solution.py:450
  14.0 3.8 %collective-permute-start = (bf16[96,384]{1,0:T(8,128)(2,1)S(1)}, bf16[96,384]{1,0:T(8,128)(2,1)S(1)}, u32[]{:S(2)}, u32[]{:S(2)}) collective-permute-start(bf16[96,384]{1,0:T(8,128)(2,1)S(1)} %copy-done.57), channel_id=1, source_target_pairs={{0,1},{1,0},{2,3},{3,2},{4,5},{5,4},{6,7},{7,6},{8,9},{9,8},{10,11... | collective-permute-start | bytes 221192 | tf_op jit(solution)/shard_map/ppermute | solution.py:456
  14.3 19.2 %collective-permute-start.1 = (bf16[96,384]{1,0:T(8,128)(2,1)S(1)}, bf16[96,384]{1,0:T(8,128)(2,1)S(1)}, u32[]{:S(2)}, u32[]{:S(2)}) collective-permute-start(bf16[96,384]{1,0:T(8,128)(2,1)S(1)} %copy-done.56), channel_id=1, source_target_pairs={{0,2},{1,3},{2,0},{3,1},{4,6},{5,7},{6,4},{7,5},{8,10},{9,11},{10,... | collective-permute-start | bytes 221192 | tf_op jit(solution)/shard_map/ppermute | solution.py:456
  16.0 18.4 %collective-permute-start.2 = (bf16[96,384]{1,0:T(8,128)(2,1)S(1)}, bf16[96,384]{1,0:T(8,128)(2,1)S(1)}, u32[]{:S(2)}, u32[]{:S(2)}) collective-permute-start(bf16[96,384]{1,0:T(8,128)(2,1)S(1)} %copy-done.55), channel_id=1, source_target_pairs={{0,3},{1,2},{2,1},{3,0},{4,7},{5,6},{6,5},{7,4},{8,11},{9,10},{10,... | collective-permute-start | bytes 221192 | tf_op jit(solution)/shard_map/ppermute | solution.py:456
  16.0 18.6 %collective-permute-start.3 = (bf16[96,384]{1,0:T(8,128)(2,1)S(1)}, bf16[96,384]{1,0:T(8,128)(2,1)S(1)}, u32[]{:S(2)}, u32[]{:S(2)}) collective-permute-start(bf16[96,384]{1,0:T(8,128)(2,1)S(1)} %copy-done.54), channel_id=1, source_target_pairs={{0,4},{1,5},{2,6},{3,7},{4,0},{5,1},{6,2},{7,3},{8,12},{9,13},{10,... | collective-permute-start | bytes 221192 | tf_op jit(solution)/shard_map/ppermute | solution.py:456
  17.7 19.2 %collective-permute-start.4 = (bf16[96,384]{1,0:T(8,128)(2,1)S(1)}, bf16[96,384]{1,0:T(8,128)(2,1)S(1)}, u32[]{:S(2)}, u32[]{:S(2)}) collective-permute-start(bf16[96,384]{1,0:T(8,128)(2,1)S(1)} %copy-done.53), channel_id=1, source_target_pairs={{0,5},{1,4},{2,7},{3,6},{4,1},{5,0},{6,3},{7,2},{8,13},{9,12},{10,... | collective-permute-start | bytes 221192 | tf_op jit(solution)/shard_map/ppermute | solution.py:456
  17.9 26.2 %collective-permute-start.5 = (bf16[96,384]{1,0:T(8,128)(2,1)S(1)}, bf16[96,384]{1,0:T(8,128)(2,1)S(1)}, u32[]{:S(2)}, u32[]{:S(2)}) collective-permute-start(bf16[96,384]{1,0:T(8,128)(2,1)S(1)} %copy-done.52), channel_id=1, source_target_pairs={{0,6},{1,7},{2,4},{3,5},{4,2},{5,3},{6,0},{7,1},{8,14},{9,15},{10,... | collective-permute-start | bytes 221192 | tf_op jit(solution)/shard_map/ppermute | solution.py:456
  33.6 11.3 %collective-permute-start.6 = (bf16[96,384]{1,0:T(8,128)(2,1)S(1)}, bf16[96,384]{1,0:T(8,128)(2,1)S(1)}, u32[]{:S(2)}, u32[]{:S(2)}) collective-permute-start(bf16[96,384]{1,0:T(8,128)(2,1)S(1)} %copy-done.51), channel_id=1, source_target_pairs={{0,7},{1,6},{2,5},{3,4},{4,3},{5,2},{6,1},{7,0},{8,15},{9,14},{10,... | collective-permute-start | bytes 221192 | tf_op jit(solution)/shard_map/ppermute | solution.py:456
  34.4 20.8 %collective-permute-start.7 = (bf16[96,384]{1,0:T(8,128)(2,1)S(1)}, bf16[96,384]{1,0:T(8,128)(2,1)S(1)}, u32[]{:S(2)}, u32[]{:S(2)}) collective-permute-start(bf16[96,384]{1,0:T(8,128)(2,1)S(1)} %copy-done.50), channel_id=1, source_target_pairs={{0,8},{1,9},{2,10},{3,11},{4,12},{5,13},{6,14},{7,15},{8,0},{9,1},... | collective-permute-start | bytes 221192 | tf_op jit(solution)/shard_map/ppermute | solution.py:456
  34.7 22.6 %collective-permute-start.8 = (bf16[96,384]{1,0:T(8,128)(2,1)S(1)}, bf16[96,384]{1,0:T(8,128)(2,1)S(1)}, u32[]{:S(2)}, u32[]{:S(2)}) collective-permute-start(bf16[96,384]{1,0:T(8,128)(2,1)S(1)} %copy-done.49), channel_id=1, source_target_pairs={{0,9},{1,8},{2,11},{3,10},{4,13},{5,12},{6,15},{7,14},{8,1},{9,0},... | collective-permute-start | bytes 221192 | tf_op jit(solution)/shard_map/ppermute | solution.py:456
  36.9 23.1 %collective-permute-start.9 = (bf16[96,384]{1,0:T(8,128)(2,1)S(1)}, bf16[96,384]{1,0:T(8,128)(2,1)S(1)}, u32[]{:S(2)}, u32[]{:S(2)}) collective-permute-start(bf16[96,384]{1,0:T(8,128)(2,1)S(1)} %copy-done.48), channel_id=1, source_target_pairs={{0,10},{1,11},{2,8},{3,9},{4,14},{5,15},{6,12},{7,13},{8,2},{9,3},... | collective-permute-start | bytes 221192 | tf_op jit(solution)/shard_map/ppermute | solution.py:456
  44.0 17.7 %collective-permute-start.10 = (bf16[96,384]{1,0:T(8,128)(2,1)}, bf16[96,384]{1,0:T(8,128)(2,1)S(1)}, u32[]{:S(2)}, u32[]{:S(2)}) collective-permute-start(bf16[96,384]{1,0:T(8,128)(2,1)} %get-tuple-element.58), channel_id=1, source_target_pairs={{0,11},{1,10},{2,9},{3,8},{4,15},{5,14},{6,13},{7,12},{8,3},{9,2},... | collective-permute-start | bytes 221192 | tf_op jit(solution)/shard_map/ppermute | solution.py:456
  44.9 16.9 %collective-permute-start.11 = (bf16[96,384]{1,0:T(8,128)(2,1)}, bf16[96,384]{1,0:T(8,128)(2,1)S(1)}, u32[]{:S(2)}, u32[]{:S(2)}) collective-permute-start(bf16[96,384]{1,0:T(8,128)(2,1)} %get-tuple-element.59), channel_id=1, source_target_pairs={{0,12},{1,13},{2,14},{3,15},{4,8},{5,9},{6,10},{7,11},{8,4},{9,5},... | collective-permute-start | bytes 221192 | tf_op jit(solution)/shard_map/ppermute | solution.py:456
  55.2 8.0 %collective-permute-start.12 = (bf16[96,384]{1,0:T(8,128)(2,1)}, bf16[96,384]{1,0:T(8,128)(2,1)S(1)}, u32[]{:S(2)}, u32[]{:S(2)}) collective-permute-start(bf16[96,384]{1,0:T(8,128)(2,1)} %get-tuple-element.60), channel_id=1, source_target_pairs={{0,13},{1,12},{2,15},{3,14},{4,9},{5,8},{6,11},{7,10},{8,5},{9,4},... | collective-permute-start | bytes 221192 | tf_op jit(solution)/shard_map/ppermute | solution.py:456
  57.2 8.9 %collective-permute-start.13 = (bf16[96,384]{1,0:T(8,128)(2,1)}, bf16[96,384]{1,0:T(8,128)(2,1)S(1)}, u32[]{:S(2)}, u32[]{:S(2)}) collective-permute-start(bf16[96,384]{1,0:T(8,128)(2,1)} %get-tuple-element.61), channel_id=1, source_target_pairs={{0,14},{1,15},{2,12},{3,13},{4,10},{5,11},{6,8},{7,9},{8,6},{9,7},... | collective-permute-start | bytes 221192 | tf_op jit(solution)/shard_map/ppermute | solution.py:456
  60.0 8.8 %collective-permute-start.14 = (bf16[96,384]{1,0:T(8,128)(2,1)}, bf16[96,384]{1,0:T(8,128)(2,1)S(1)}, u32[]{:S(2)}, u32[]{:S(2)}) collective-permute-start(bf16[96,384]{1,0:T(8,128)(2,1)} %get-tuple-element.62), channel_id=1, source_target_pairs={{0,15},{1,14},{2,13},{3,12},{4,11},{5,10},{6,9},{7,8},{8,7},{9,6},... | collective-permute-start | bytes 221192 | tf_op jit(solution)/shard_map/ppermute | solution.py:456
  71.6 22.3 %all-to-all-start.1 = ((bf16[16,96,384]{2,1,0:T(8,128)(2,1)}), bf16[16,96,384]{2,1,0:T(8,128)(2,1)S(1)}, u32[]{:S(2)}, u32[]{:S(2)}) async-start(bf16[16,96,384]{2,1,0:T(8,128)(2,1)} %shard_map.110), calls=%async_computation.1 | async-start | bytes 2359296 | tf_op jit(solution)/shard_map/all_to_all | solution.py:450
  111.1 20.2 %copy-start.35 = (bf16[48,384]{1,0:T(8,128)(2,1)S(1)}, bf16[48,384]{1,0:T(8,128)(2,1)}, u32[]{:S(2)}) copy-start(bf16[48,384]{1,0:T(8,128)(2,1)} %copy-done.34) | copy-start | bytes 110596
  111.1 20.7 %copy-start.33 = (bf16[48,384]{1,0:T(8,128)(2,1)S(1)}, bf16[48,384]{1,0:T(8,128)(2,1)}, u32[]{:S(2)}) copy-start(bf16[48,384]{1,0:T(8,128)(2,1)} %copy-done.32) | copy-start | bytes 110596
  111.1 20.7 %copy-start.31 = (bf16[48,384]{1,0:T(8,128)(2,1)S(1)}, bf16[48,384]{1,0:T(8,128)(2,1)}, u32[]{:S(2)}) copy-start(bf16[48,384]{1,0:T(8,128)(2,1)} %copy-done.30) | copy-start | bytes 110596
  111.1 23.4 %copy-start.29 = (bf16[48,384]{1,0:T(8,128)(2,1)S(1)}, bf16[48,384]{1,0:T(8,128)(2,1)}, u32[]{:S(2)}) copy-start(bf16[48,384]{1,0:T(8,128)(2,1)} %copy-done.28) | copy-start | bytes 110596
  111.1 47.0 %copy-start.18 = (bf16[48,384]{1,0:T(8,128)(2,1)S(1)}, bf16[48,384]{1,0:T(8,128)(2,1)}, u32[]{:S(2)}) copy-start(bf16[48,384]{1,0:T(8,128)(2,1)} %copy-done.17) | copy-start | bytes 110596
  111.1 47.0 %all-to-all-start.2 = ((bf16[32,72,384]{2,1,0:T(8,128)(2,1)}), bf16[32,72,384]{2,1,0:T(8,128)(2,1)S(1)}, u32[]{:S(2)}, u32[]{:S(2)}) async-start(bf16[32,72,384]{2,1,0:T(8,128)(2,1)} %copy-done.11), calls=%async_computation.2 | async-start | bytes 3538944 | tf_op jit(solution)/shard_map/all_to_all | solution.py:450
  116.2 3.8 %collective-permute-start.15 = (bf16[48,384]{1,0:T(8,128)(2,1)S(1)}, bf16[48,384]{1,0:T(8,128)(2,1)S(1)}, u32[]{:S(2)}, u32[]{:S(2)}) collective-permute-start(bf16[48,384]{1,0:T(8,128)(2,1)S(1)} %copy-done.47), channel_id=1, source_target_pairs={{0,1},{1,0},{2,3},{3,2},{4,5},{5,4},{6,7},{7,6},{8,9},{9,8},{10,11... | collective-permute-start | bytes 110600 | tf_op jit(solution)/shard_map/ppermute | solution.py:456
  116.5 14.8 %collective-permute-start.16 = (bf16[48,384]{1,0:T(8,128)(2,1)S(1)}, bf16[48,384]{1,0:T(8,128)(2,1)S(1)}, u32[]{:S(2)}, u32[]{:S(2)}) collective-permute-start(bf16[48,384]{1,0:T(8,128)(2,1)S(1)} %copy-done.45), channel_id=1, source_target_pairs={{0,2},{1,3},{2,0},{3,1},{4,6},{5,7},{6,4},{7,5},{8,10},{9,11},{10,... | collective-permute-start | bytes 110600 | tf_op jit(solution)/shard_map/ppermute | solution.py:456
  118.2 13.6 %collective-permute-start.17 = (bf16[48,384]{1,0:T(8,128)(2,1)S(1)}, bf16[48,384]{1,0:T(8,128)(2,1)S(1)}, u32[]{:S(2)}, u32[]{:S(2)}) collective-permute-start(bf16[48,384]{1,0:T(8,128)(2,1)S(1)} %copy-done.43), channel_id=1, source_target_pairs={{0,3},{1,2},{2,1},{3,0},{4,7},{5,6},{6,5},{7,4},{8,11},{9,10},{10,... | collective-permute-start | bytes 110600 | tf_op jit(solution)/shard_map/ppermute | solution.py:456
  118.2 13.5 %collective-permute-start.18 = (bf16[48,384]{1,0:T(8,128)(2,1)S(1)}, bf16[48,384]{1,0:T(8,128)(2,1)S(1)}, u32[]{:S(2)}, u32[]{:S(2)}) collective-permute-start(bf16[48,384]{1,0:T(8,128)(2,1)S(1)} %copy-done.41), channel_id=1, source_target_pairs={{0,4},{1,5},{2,6},{3,7},{4,0},{5,1},{6,2},{7,3},{8,12},{9,13},{10,... | collective-permute-start | bytes 110600 | tf_op jit(solution)/shard_map/ppermute | solution.py:456
  119.9 14.6 %collective-permute-start.19 = (bf16[48,384]{1,0:T(8,128)(2,1)S(1)}, bf16[48,384]{1,0:T(8,128)(2,1)S(1)}, u32[]{:S(2)}, u32[]{:S(2)}) collective-permute-start(bf16[48,384]{1,0:T(8,128)(2,1)S(1)} %copy-done.39), channel_id=1, source_target_pairs={{0,5},{1,4},{2,7},{3,6},{4,1},{5,0},{6,3},{7,2},{8,13},{9,12},{10,... | collective-permute-start | bytes 110600 | tf_op jit(solution)/shard_map/ppermute | solution.py:456
  120.0 15.1 %collective-permute-start.20 = (bf16[48,384]{1,0:T(8,128)(2,1)S(1)}, bf16[48,384]{1,0:T(8,128)(2,1)S(1)}, u32[]{:S(2)}, u32[]{:S(2)}) collective-permute-start(bf16[48,384]{1,0:T(8,128)(2,1)S(1)} %copy-done.37), channel_id=1, source_target_pairs={{0,6},{1,7},{2,4},{3,5},{4,2},{5,3},{6,0},{7,1},{8,14},{9,15},{10,... | collective-permute-start | bytes 110600 | tf_op jit(solution)/shard_map/ppermute | solution.py:456
  131.3 6.4 %collective-permute-start.21 = (bf16[48,384]{1,0:T(8,128)(2,1)S(1)}, bf16[48,384]{1,0:T(8,128)(2,1)S(1)}, u32[]{:S(2)}, u32[]{:S(2)}) collective-permute-start(bf16[48,384]{1,0:T(8,128)(2,1)S(1)} %copy-done.35), channel_id=1, source_target_pairs={{0,7},{1,6},{2,5},{3,4},{4,3},{5,2},{6,1},{7,0},{8,15},{9,14},{10,... | collective-permute-start | bytes 110600 | tf_op jit(solution)/shard_map/ppermute | solution.py:456
  131.8 15.4 %collective-permute-start.22 = (bf16[48,384]{1,0:T(8,128)(2,1)S(1)}, bf16[48,384]{1,0:T(8,128)(2,1)S(1)}, u32[]{:S(2)}, u32[]{:S(2)}) collective-permute-start(bf16[48,384]{1,0:T(8,128)(2,1)S(1)} %copy-done.33), channel_id=1, source_target_pairs={{0,8},{1,9},{2,10},{3,11},{4,12},{5,13},{6,14},{7,15},{8,0},{9,1},... | collective-permute-start | bytes 110600 | tf_op jit(solution)/shard_map/ppermute | solution.py:456
  131.8 17.0 %collective-permute-start.23 = (bf16[48,384]{1,0:T(8,128)(2,1)S(1)}, bf16[48,384]{1,0:T(8,128)(2,1)S(1)}, u32[]{:S(2)}, u32[]{:S(2)}) collective-permute-start(bf16[48,384]{1,0:T(8,128)(2,1)S(1)} %copy-done.31), channel_id=1, source_target_pairs={{0,9},{1,8},{2,11},{3,10},{4,13},{5,12},{6,15},{7,14},{8,1},{9,0},... | collective-permute-start | bytes 110600 | tf_op jit(solution)/shard_map/ppermute | solution.py:456
  134.5 16.7 %collective-permute-start.24 = (bf16[48,384]{1,0:T(8,128)(2,1)S(1)}, bf16[48,384]{1,0:T(8,128)(2,1)S(1)}, u32[]{:S(2)}, u32[]{:S(2)}) collective-permute-start(bf16[48,384]{1,0:T(8,128)(2,1)S(1)} %copy-done.29), channel_id=1, source_target_pairs={{0,10},{1,11},{2,8},{3,9},{4,14},{5,15},{6,12},{7,13},{8,2},{9,3},... | collective-permute-start | bytes 110600 | tf_op jit(solution)/shard_map/ppermute | solution.py:456
  135.1 18.5 %collective-permute-start.25 = (bf16[48,384]{1,0:T(8,128)(2,1)}, bf16[48,384]{1,0:T(8,128)(2,1)S(1)}, u32[]{:S(2)}, u32[]{:S(2)}) collective-permute-start(bf16[48,384]{1,0:T(8,128)(2,1)} %get-tuple-element.81), channel_id=1, source_target_pairs={{0,11},{1,10},{2,9},{3,8},{4,15},{5,14},{6,13},{7,12},{8,3},{9,2},... | collective-permute-start | bytes 110600 | tf_op jit(solution)/shard_map/ppermute | solution.py:456
  137.7 15.9 %collective-permute-start.26 = (bf16[48,384]{1,0:T(8,128)(2,1)}, bf16[48,384]{1,0:T(8,128)(2,1)S(1)}, u32[]{:S(2)}, u32[]{:S(2)}) collective-permute-start(bf16[48,384]{1,0:T(8,128)(2,1)} %get-tuple-element.82), channel_id=1, source_target_pairs={{0,12},{1,13},{2,14},{3,15},{4,8},{5,9},{6,10},{7,11},{8,4},{9,5},... | collective-permute-start | bytes 110600 | tf_op jit(solution)/shard_map/ppermute | solution.py:456
  147.2 6.4 %collective-permute-start.27 = (bf16[48,384]{1,0:T(8,128)(2,1)}, bf16[48,384]{1,0:T(8,128)(2,1)S(1)}, u32[]{:S(2)}, u32[]{:S(2)}) collective-permute-start(bf16[48,384]{1,0:T(8,128)(2,1)} %get-tuple-element.83), channel_id=1, source_target_pairs={{0,13},{1,12},{2,15},{3,14},{4,9},{5,8},{6,11},{7,10},{8,5},{9,4},... | collective-permute-start | bytes 110600 | tf_op jit(solution)/shard_map/ppermute | solution.py:456
  148.8 6.4 %collective-permute-start.28 = (bf16[48,384]{1,0:T(8,128)(2,1)}, bf16[48,384]{1,0:T(8,128)(2,1)S(1)}, u32[]{:S(2)}, u32[]{:S(2)}) collective-permute-start(bf16[48,384]{1,0:T(8,128)(2,1)} %get-tuple-element.84), channel_id=1, source_target_pairs={{0,14},{1,15},{2,12},{3,13},{4,10},{5,11},{6,8},{7,9},{8,6},{9,7},... | collective-permute-start | bytes 110600 | tf_op jit(solution)/shard_map/ppermute | solution.py:456
  151.2 5.8 %collective-permute-start.29 = (bf16[48,384]{1,0:T(8,128)(2,1)}, bf16[48,384]{1,0:T(8,128)(2,1)S(1)}, u32[]{:S(2)}, u32[]{:S(2)}) collective-permute-start(bf16[48,384]{1,0:T(8,128)(2,1)} %copy-done.27), channel_id=1, source_target_pairs={{0,15},{1,14},{2,13},{3,12},{4,11},{5,10},{6,9},{7,8},{8,7},{9,6},... | collective-permute-start | bytes 110600 | tf_op jit(solution)/shard_map/ppermute | solution.py:456
  160.7 42.9 %all-to-all-start.3 = ((bf16[32,60,384]{2,1,0:T(8,128)(2,1)}), bf16[32,60,384]{2,1,0:T(8,128)(2,1)}, u32[]{:S(2)}, u32[]{:S(2)}) async-start(bf16[32,60,384]{2,1,0:T(8,128)(2,1)} %shard_map.113), calls=%async_computation.3 | async-start | bytes 3145728 | tf_op jit(solution)/shard_map/all_to_all | solution.py:450
  (44 other events, 129.1 us)

commit v9 on v7

--- a/solution.py
+++ b/solution.py
@@ -15,7 +15,7 @@
 VMEM_LIMIT = 32 * 1024 * 1024
 PRODUCTS_VMEM_LIMIT = 48 * 1024 * 1024
 FIRST_VMEM_LIMIT = 60 * 1024 * 1024
-GROUP = 2
+GROUP = 4
 
 WHOLE = pl.BlockSpec(memory_space=pltpu.VMEM)
 ANYWHERE = pl.BlockSpec(memory_space=pl.ANY)
@@ -191,7 +191,7 @@
     def consume(group, normed):
         gates = jax.nn.sigmoid(jnp.dot(w_t, normed, preferred_element_type=F32))
         for k, r in enumerate(group):
-            out[r] = gates[:, k * width : (k + 1) * width].astype(BF16)
+            out[r] = gates[:, k * width : (k + 1) * width]
 
     overlapped(rows, prepare, consume)
 
@@ -225,7 +225,11 @@
     write_gates(x_t, marks, row_marks, *first, turn(w_square.at[0, 0]), out)
 
 
-def second_gate_kernel(x_t, marks, row_marks, weights, columns, out):
+def second_gate_kernel(x_t, marks, row_marks, weights, columns, out, x_out, w_out, columns_out):
+    x_out[...] = x_t[...]
+    w_out[...] = weights[W_OUT[1], :]
+    columns_out[0] = columns[MID_GAIN[1]]
+    columns_out[1] = columns[MID_BIAS[1]]
     write_gates(x_t, marks, row_marks, columns[GAIN], columns[BIAS], columns[EMBED], weights[W_GATE, :], out)
 
 
@@ -306,9 +310,8 @@
             out[s, :, columns] = turned[j, s * out_pitch : s * out_pitch + channels * rows, :].astype(BF16)
 
 
-def finish(layer, group, width, tri, gate, x_t, weights, vectors):
+def finish(group, width, tri, gate, x_t, w_t, gain, bias):
     rows = tri.shape[1] // HC
-    gain, bias = vectors[MID_GAIN[layer]], vectors[MID_BIAS[layer]]
     normed = jnp.concatenate(
         [
             norm_channels(tri[j, pl.ds(r, HC, stride=rows), :], gain, bias).astype(BF16)
@@ -317,11 +320,11 @@
         ],
         axis=1,
     )
-    branch = jnp.dot(weights[W_OUT[layer], :], normed, preferred_element_type=F32)
+    branch = jnp.dot(w_t, normed, preferred_element_type=F32)
     return {
         (r, j): (
             x_t[r, :, columns].astype(F32)
-            + gate[r, :, columns].astype(F32) * branch[:, k * width + j * 128 : k * width + (j + 1) * 128]
+            + gate[r, :, columns] * branch[:, k * width + j * 128 : k * width + (j + 1) * 128]
         ).astype(BF16)
         for k, r in enumerate(group)
         for j, columns in blocks(width)
@@ -333,7 +336,8 @@
     widen(recv, tri, recv.shape[1])
 
     def prepare(group):
-        states = finish(0, group, width, tri, gate, x_t, weights, vectors)
+        mid = (vectors[MID_GAIN[0]], vectors[MID_BIAS[0]])
+        states = finish(group, width, tri, gate, x_t, weights[W_OUT[0], :], *mid)
         parts = []
         for r in group:
             for j, columns in blocks(width):
@@ -351,11 +355,11 @@
     write_slabs(slabs, out)
 
 
-def last_kernel(recv, gate, x_t, weights, vectors, out, tri):
+def last_kernel(recv, gate, x_t, w_t, vectors, out, tri):
     rows, _, width = x_t.shape
     widen(recv, tri, recv.shape[1])
     for group in groups(rows):
-        for (r, j), state in finish(1, group, width, tri, gate, x_t, weights, vectors).items():
+        for (r, j), state in finish(group, width, tri, gate, x_t, w_t[...], vectors[0], vectors[1]).items():
             out[r, j * 128 : (j + 1) * 128, :] = state.astype(F32).T.astype(BF16)
 
 
@@ -387,7 +391,7 @@
     own_back = jax.ShapeDtypeStruct((half, 2 * channels * rows, width), BF16)
     own_slab = jax.ShapeDtypeStruct((2 * channels * rows, width), BF16)
     state_t = jax.ShapeDtypeStruct((rows, C, width), BF16)
-    gate_t = jax.ShapeDtypeStruct((rows, C, width), BF16)
+    gate_t = jax.ShapeDtypeStruct((rows, C, width), F32)
     mark = jax.ShapeDtypeStruct((2, width), F32)
     row_mark = jax.ShapeDtypeStruct((2, (rows + 7) // 8 * 8, 128), F32)
     turned = jax.ShapeDtypeStruct((7 * HC, C), BF16)
@@ -440,9 +444,13 @@
         (tri, gate, x_t, marks, row_marks, weights, vectors), (), 2 * pairs * C * 5 * HC,
     )
     recv = exchange(slabs)
-    gate = call(
-        second_gate_kernel, [gate_t], [], (x_t, marks, row_marks, weights, vectors), (), 2 * pairs * C * C
-    )[0]
+    w_last = jax.ShapeDtypeStruct((HC, C), BF16)
+    columns_last = jax.ShapeDtypeStruct((2, C, 128), F32)
+    gate, x_t, weights, vectors = call(
+        second_gate_kernel, [gate_t, state_t, w_last, columns_last], [], (x_t, marks, row_marks, weights, vectors), (),
+        2 * pairs * C * C,
+    )
+    recv, gate, x_t, weights, vectors = lax.optimization_barrier((recv, gate, x_t, weights, vectors))
     products = call(
         functools.partial(second_products_kernel, rows), [back],
         [all_spread, pltpu.VMEM((channels, cols, width, 128), F32), back_spread], (recv,), (), 2 * channels * width**3,
@@ -450,7 +458,7 @@
     tri = exchange(products)
     return call(
         last_kernel, [jax.ShapeDtypeStruct(pair.shape, BF16)], [tri_wide], (tri, gate, x_t, weights, vectors), (),
-        2 * pairs * C * C, FIRST_VMEM_LIMIT,
+        2 * pairs * C * C,
     )[0]
 
 

time: 203 us -> 200 us (0.985)
  blocking collectives: 60.6 us -> 34.5 us
  waiting for transfers between devices: 75.2 us -> 99 us
  Pallas kernels: 23.5 us -> 19.8 us
  starting transfers between devices: 33.9 us -> 36.1 us
    all_to_all x1, blocking collectives: 60.6 us -> 34.5 us  [exchange(): lax.all_to_all(slabs, 'row', split_axis=0, concat_axis=0, tiled=True, axi...]
    all_to_all x3, waiting for transfers between devices: 39.7 us -> 63.6 us  [exchange(): lax.all_to_all(slabs, 'row', split_axis=0, concat_axis=0, tiled=True, axi...]
    pallas_call x7, Pallas kernels: 23.5 us -> 19.8 us  [call(): pl.pallas_call(kernel, out_shape=outs, in_specs=[WHOLE] * len(arrays) + [...]
    all_to_all x3, starting transfers between devices: 14.6 us -> 16.8 us  [exchange(): lax.all_to_all(slabs, 'row', split_axis=0, concat_axis=0, tiled=True, axi...]
    unnamed x70 -> x62, local copies, waits for them, and re-layouts: 8.58 us -> 9.32 us
where the time goes in v9:
time: 200 us; the launch traced here: 199 us
  waiting for transfers between devices  99 us (50%)
  starting transfers between devices  36.1 us (18%)
  blocking collectives  34.5 us (17%)
  Pallas kernels  19.8 us (10%)
  local copies, waits for them, and re-layouts  9.32 us (5%)
    all_to_all x3, waiting for transfers between devices, exchange(): lax.all_to_all(slabs, 'row', split_axis=0, concat_axis=0, tiled=True, axi...  63.6 us
    ppermute x15, waiting for transfers between devices, local(): lax.ppermute(own[o], 'row', [(i, i ^ o) for i in range(devices)])  35.5 us
    all_to_all x1, blocking collectives, exchange(): lax.all_to_all(slabs, 'row', split_axis=0, concat_axis=0, tiled=True, axi...  34.5 us
    pallas_call x7, Pallas kernels, call(): pl.pallas_call(kernel, out_shape=outs, in_specs=[WHOLE] * len(arrays) + [...  19.8 us
    ppermute x15, starting transfers between devices, local(): lax.ppermute(own[o], 'row', [(i, i ^ o) for i in range(devices)])  19.3 us
    all_to_all x3, starting transfers between devices, exchange(): lax.all_to_all(slabs, 'row', split_axis=0, concat_axis=0, tiled=True, axi...  16.8 us
    unnamed x62, local copies, waits for them, and re-layouts  9.32 us
  transfers between devices with their start and end apart: 18, of which 10 were waited for; matrix products, arithmetic and copies ran while one was open for 0% of the time, Pallas kernels for 2%

profile of v9, /device:TPU:0, one launch (start us, length us, event | category | flops | bytes accessed | tf_op | source)
XLA Modules:
  0.0 199.2 jit_solution(10210665999132535923)
XLA Ops:
  0.0 6.1 %shard_map.109 = (bf16[96,384]{1,0:T(8,128)(2,1)}, bf16[96,384]{1,0:T(8,128)(2,1)}, bf16[96,384]{1,0:T(8,128)(2,1)}, bf16[96,384]{1,0:T(8,128)(2,1)}, bf16[96,38...) custom-call(s32[384]{0:T(512)} %residue_mask.1, ...), custom_call_target="tpu_custom_call" | custom-call | flops 603979776 | bytes 4738048 | tf_op jit(solution)/shard_map/pallas_call | solution.py:368
  6.3 7.3 %all-to-all-start = ((bf16[32,96,384]{2,1,0:T(8,128)(2,1)}), bf16[32,96,384]{2,1,0:T(8,128)(2,1)S(1)}, u32[]{:S(2)}, u32[]{:S(2)}) async-start(bf16[32,96,384]{2,1,0:T(8,128)(2,1)} %get-tuple-element.39), calls=%async_computation | async-start | bytes 4718592 | tf_op jit(solution)/shard_map/all_to_all | solution.py:414
  13.6 0.3 collective-permute-start
  13.9 1.7 collective-permute-start.1
  15.6 0.0 collective-permute-start.2
  15.6 1.7 collective-permute-start.3
  17.3 0.1 collective-permute-start.4
  17.4 2.6 %collective-permute-start.5 = (bf16[96,384]{1,0:T(8,128)(2,1)S(1)}, bf16[96,384]{1,0:T(8,128)(2,1)S(1)}, u32[]{:S(2)}, u32[]{:S(2)}) collective-permute-start(bf16[96,384]{1,0:T(8,128)(2,1)S(1)} %copy-done.25), channel_id=1, source_target_pairs={{0,6},{1,7},{2,4},{3,5},{4,2},{5,3},{6,0},{7,1},{8,14},{9,15},{10,... | collective-permute-start | bytes 221192 | tf_op jit(solution)/shard_map/ppermute | solution.py:428
  20.0 13.1 %collective-permute-done.1.refs_2_ = bf16[96,384]{1,0:T(8,128)(2,1)S(1)} collective-permute-done((bf16[96,384]{1,0:T(8,128)(2,1)S(1)}, bf16[96,384]{1,0:T(8,128)(2,1)S(1)}, u32[]{:S(2)}, u32[]{:S(2)}) %collective-permute-start.1) | collective-permute-done | bytes 73760 | tf_op jit(solution)/shard_map/ppermute | solution.py:428
  33.1 0.6 collective-permute-start.6
  33.7 0.2 collective-permute-done.2.refs_3_
  34.0 0.3 collective-permute-start.7
  34.2 2.3 %collective-permute-start.8 = (bf16[96,384]{1,0:T(8,128)(2,1)S(1)}, bf16[96,384]{1,0:T(8,128)(2,1)S(1)}, u32[]{:S(2)}, u32[]{:S(2)}) collective-permute-start(bf16[96,384]{1,0:T(8,128)(2,1)S(1)} %copy-done.22), channel_id=1, source_target_pairs={{0,9},{1,8},{2,11},{3,10},{4,13},{5,12},{6,15},{7,14},{8,1},{9,0},... | collective-permute-start | bytes 221192 | tf_op jit(solution)/shard_map/ppermute | solution.py:428
  36.5 3.3 %collective-permute-start.9 = (bf16[96,384]{1,0:T(8,128)(2,1)S(1)}, bf16[96,384]{1,0:T(8,128)(2,1)S(1)}, u32[]{:S(2)}, u32[]{:S(2)}) collective-permute-start(bf16[96,384]{1,0:T(8,128)(2,1)S(1)} %copy-done.21), channel_id=1, source_target_pairs={{0,10},{1,11},{2,8},{3,9},{4,14},{5,15},{6,12},{7,13},{8,2},{9,3},... | collective-permute-start | bytes 221192 | tf_op jit(solution)/shard_map/ppermute | solution.py:428
  39.8 3.8 %collective-permute-done.5.refs_6_ = bf16[96,384]{1,0:T(8,128)(2,1)S(1)} collective-permute-done((bf16[96,384]{1,0:T(8,128)(2,1)S(1)}, bf16[96,384]{1,0:T(8,128)(2,1)S(1)}, u32[]{:S(2)}, u32[]{:S(2)}) %collective-permute-start.5) | collective-permute-done | bytes 73760 | tf_op jit(solution)/shard_map/ppermute | solution.py:428
  43.6 0.8 collective-permute-done.6.refs_7_
  44.4 10.3 %collective-permute-done.7.refs_8_ = bf16[96,384]{1,0:T(8,128)(2,1)S(1)} collective-permute-done((bf16[96,384]{1,0:T(8,128)(2,1)S(1)}, bf16[96,384]{1,0:T(8,128)(2,1)S(1)}, u32[]{:S(2)}, u32[]{:S(2)}) %collective-permute-start.7) | collective-permute-done | bytes 73760 | tf_op jit(solution)/shard_map/ppermute | solution.py:428
  54.8 2.0 %collective-permute-start.12 = (bf16[96,384]{1,0:T(8,128)(2,1)}, bf16[96,384]{1,0:T(8,128)(2,1)S(1)}, u32[]{:S(2)}, u32[]{:S(2)}) collective-permute-start(bf16[96,384]{1,0:T(8,128)(2,1)} %get-tuple-element.53), channel_id=1, source_target_pairs={{0,13},{1,12},{2,15},{3,14},{4,9},{5,8},{6,11},{7,10},{8,5},{9,4},... | collective-permute-start | bytes 221192 | tf_op jit(solution)/shard_map/ppermute | solution.py:428
  56.8 2.8 %collective-permute-start.13 = (bf16[96,384]{1,0:T(8,128)(2,1)}, bf16[96,384]{1,0:T(8,128)(2,1)S(1)}, u32[]{:S(2)}, u32[]{:S(2)}) collective-permute-start(bf16[96,384]{1,0:T(8,128)(2,1)} %get-tuple-element.54), channel_id=1, source_target_pairs={{0,14},{1,15},{2,12},{3,13},{4,10},{5,11},{6,8},{7,9},{8,6},{9,7},... | collective-permute-start | bytes 221192 | tf_op jit(solution)/shard_map/ppermute | solution.py:428
  59.6 1.7 collective-permute-start.14
  61.3 1.5 collective-permute-done.12.refs_13_
  62.8 2.9 %collective-permute-done.13.refs_14_ = bf16[96,384]{1,0:T(8,128)(2,1)S(1)} collective-permute-done((bf16[96,384]{1,0:T(8,128)(2,1)}, bf16[96,384]{1,0:T(8,128)(2,1)S(1)}, u32[]{:S(2)}, u32[]{:S(2)}) %collective-permute-start.13) | collective-permute-done | bytes 73760 | tf_op jit(solution)/shard_map/ppermute | solution.py:428
  65.7 2.7 %collective-permute-done.14.refs_15_ = bf16[96,384]{1,0:T(8,128)(2,1)S(1)} collective-permute-done((bf16[96,384]{1,0:T(8,128)(2,1)}, bf16[96,384]{1,0:T(8,128)(2,1)S(1)}, u32[]{:S(2)}, u32[]{:S(2)}) %collective-permute-start.14) | collective-permute-done | bytes 73760 | tf_op jit(solution)/shard_map/ppermute | solution.py:428
  68.4 2.7 %shard_map.110 = bf16[16,96,384]{2,1,0:T(8,128)(2,1)} custom-call(bf16[32,96,384]{2,1,0:T(8,128)(2,1)S(1)} %all-to-all-done.recv, bf16[96,384]{1,0:T(8,128)(2,1)S(1)} %copy-done.12, bf16[96,384]{1,0:T(8,128)(2,1)S(1)} %collective-permute-done.refs_1_, bf16[96,384]{1,0:T(8,128)(2,1)S(1)} %collective-permute-done.1.refs_2_, ...), custom_call_target="tpu_custom_call" | custom-call | flops 452984832 | bytes 4718592 | tf_op jit(solution)/shard_map/pallas_call | solution.py:368
  71.1 0.0 copy-start.14
  71.1 0.0 copy-start.16
  71.1 0.0 copy-start.17
  71.1 0.0 copy-start.18
  71.1 0.0 copy-start.19
  71.1 0.0 copy-start.20
  71.2 4.5 %all-to-all-start.1 = ((bf16[16,96,384]{2,1,0:T(8,128)(2,1)}), bf16[16,96,384]{2,1,0:T(8,128)(2,1)S(1)}, u32[]{:S(2)}, u32[]{:S(2)}) async-start(bf16[16,96,384]{2,1,0:T(8,128)(2,1)} %shard_map.110), calls=%async_computation.1 | async-start | bytes 2359296 | tf_op jit(solution)/shard_map/all_to_all | solution.py:414
  75.8 1.9 shard_map.111
  77.7 1.4 copy-done.2
  79.1 14.3 %all-to-all-done.1.recv = bf16[16,96,384]{2,1,0:T(8,128)(2,1)S(1)} async-done(((bf16[16,96,384]{2,1,0:T(8,128)(2,1)}), bf16[16,96,384]{2,1,0:T(8,128)(2,1)S(1)}, u32[]{:S(2)}, u32[]{:S(2)}) %all-to-all-start.1) | async-done | bytes 1179680 | tf_op jit(solution)/shard_map/all_to_all | solution.py:414
  93.4 1.7 copy-done.3
  95.1 3.8 %shard_map.112 = (bf16[32,96,384]{2,1,0:T(8,128)(2,1)S(1)}, bf16[12,128,384]{2,1,0:T(8,128)(2,1)S(1)}) custom-call(bf16[16,96,384]{2,1,0:T(8,128)(2,1)S(1)} %all-to-all-done.1.recv, f32[12,128,384]{2,1,0:T(8,128)S(1)} %copy-done.3, bf16[12,128,384]{2,1,0:T(8,128)(2,1)S(1)} %copy-done, f32[2,384]{1,0:T(2,128)S(1)} %copy-done.15, ...), custom_call_target="tpu_custom_call" | custom-call | flops 754974720 | bytes 8965120 | tf_op jit(solution)/shard_map/pallas_call | solution.py:368
  98.9 1.4 copy-done.1
  100.3 1.0 copy-done.6
  101.3 5.0 %all-to-all-start.2 = ((bf16[32,96,384]{2,1,0:T(8,128)(2,1)}), bf16[32,96,384]{2,1,0:T(8,128)(2,1)S(1)}, u32[]{:S(2)}, u32[]{:S(2)}) async-start(bf16[32,96,384]{2,1,0:T(8,128)(2,1)} %copy-done.1), calls=%async_computation.2 | async-start | bytes 4718592 | tf_op jit(solution)/shard_map/all_to_all | solution.py:414
  106.3 0.0 copy-start.7
  106.4 1.3 copy-done.7
  107.6 1.5 shard_map.113
  109.1 1.4 copy-done.4
  110.6 1.0 copy-done.8
  111.6 49.3 %all-to-all-done.2.recv = bf16[32,96,384]{2,1,0:T(8,128)(2,1)S(1)} async-done(((bf16[32,96,384]{2,1,0:T(8,128)(2,1)}), bf16[32,96,384]{2,1,0:T(8,128)(2,1)S(1)}, u32[]{:S(2)}, u32[]{:S(2)}) %all-to-all-start.2) | async-done | bytes 2359328 | tf_op jit(solution)/shard_map/all_to_all | solution.py:414
  160.9 1.3 shard_map.114
  162.2 34.5 %all_to_all.20.recv = bf16[32,48,384]{2,1,0:T(8,128)(2,1)S(1)} all-to-all(bf16[32,48,384]{2,1,0:T(8,128)(2,1)S(1)} %shard_map.114), channel_id=1, replica_groups=mesh['grp'=1,'row'=32] {'row'}, dimensions={0} | all-to-all | bytes 2359296 | tf_op jit(solution)/shard_map/all_to_all | solution.py:414
  196.7 2.5 %shard_map.115 = bf16[12,384,128]{2,1,0:T(8,128)(2,1)} custom-call(bf16[32,48,384]{2,1,0:T(8,128)(2,1)S(1)} %all_to_all.20.recv, f32[12,128,384]{2,1,0:T(8,128)S(1)} %copy-done.5, bf16[12,128,384]{2,1,0:T(8,128)(2,1)S(1)} %copy-done.9, bf16[128,128]{1,0:T(8,128)(2,1)S(1)} %get-tuple-element.71.w_t, f32[2,128,128]{2,1,0:T(8,128)S(1)} %get-tuple-element.72.vectors), custom_call_target="tpu_custom_call" | custom-call | flops 150994944 | bytes 6062080 | tf_op jit(solution)/shard_map/pallas_call | solution.py:368
  (58 shorter events, 0.1 us)
Async XLA Ops:
  6.2 7.4 %copy-start.30 = (bf16[96,384]{1,0:T(8,128)(2,1)S(1)}, bf16[96,384]{1,0:T(8,128)(2,1)}, u32[]{:S(2)}) copy-start(bf16[96,384]{1,0:T(8,128)(2,1)} %get-tuple-element.41) | copy-start | bytes 221188
  6.2 7.7 %copy-start.29 = (bf16[96,384]{1,0:T(8,128)(2,1)S(1)}, bf16[96,384]{1,0:T(8,128)(2,1)}, u32[]{:S(2)}) copy-start(bf16[96,384]{1,0:T(8,128)(2,1)} %get-tuple-element.42) | copy-start | bytes 221188
  6.2 9.4 %copy-start.28 = (bf16[96,384]{1,0:T(8,128)(2,1)S(1)}, bf16[96,384]{1,0:T(8,128)(2,1)}, u32[]{:S(2)}) copy-start(bf16[96,384]{1,0:T(8,128)(2,1)} %get-tuple-element.43) | copy-start | bytes 221188
  6.2 9.4 %copy-start.27 = (bf16[96,384]{1,0:T(8,128)(2,1)S(1)}, bf16[96,384]{1,0:T(8,128)(2,1)}, u32[]{:S(2)}) copy-start(bf16[96,384]{1,0:T(8,128)(2,1)} %get-tuple-element.44) | copy-start | bytes 221188
  6.2 11.1 %copy-start.26 = (bf16[96,384]{1,0:T(8,128)(2,1)S(1)}, bf16[96,384]{1,0:T(8,128)(2,1)}, u32[]{:S(2)}) copy-start(bf16[96,384]{1,0:T(8,128)(2,1)} %get-tuple-element.45) | copy-start | bytes 221188
  6.2 11.2 %copy-start.25 = (bf16[96,384]{1,0:T(8,128)(2,1)S(1)}, bf16[96,384]{1,0:T(8,128)(2,1)}, u32[]{:S(2)}) copy-start(bf16[96,384]{1,0:T(8,128)(2,1)} %get-tuple-element.46) | copy-start | bytes 221188
  6.2 26.9 %copy-start.24 = (bf16[96,384]{1,0:T(8,128)(2,1)S(1)}, bf16[96,384]{1,0:T(8,128)(2,1)}, u32[]{:S(2)}) copy-start(bf16[96,384]{1,0:T(8,128)(2,1)} %get-tuple-element.47) | copy-start | bytes 221188
  6.2 27.7 %copy-start.23 = (bf16[96,384]{1,0:T(8,128)(2,1)S(1)}, bf16[96,384]{1,0:T(8,128)(2,1)}, u32[]{:S(2)}) copy-start(bf16[96,384]{1,0:T(8,128)(2,1)} %get-tuple-element.48) | copy-start | bytes 221188
  6.2 28.0 %copy-start.22 = (bf16[96,384]{1,0:T(8,128)(2,1)S(1)}, bf16[96,384]{1,0:T(8,128)(2,1)}, u32[]{:S(2)}) copy-start(bf16[96,384]{1,0:T(8,128)(2,1)} %get-tuple-element.49) | copy-start | bytes 221188
  6.2 30.3 %copy-start.21 = (bf16[96,384]{1,0:T(8,128)(2,1)S(1)}, bf16[96,384]{1,0:T(8,128)(2,1)}, u32[]{:S(2)}) copy-start(bf16[96,384]{1,0:T(8,128)(2,1)} %get-tuple-element.50) | copy-start | bytes 221188
  6.3 62.1 %copy-start.12 = (bf16[96,384]{1,0:T(8,128)(2,1)S(1)}, bf16[96,384]{1,0:T(8,128)(2,1)}, u32[]{:S(2)}) copy-start(bf16[96,384]{1,0:T(8,128)(2,1)} %get-tuple-element.40.refs_0_) | copy-start | bytes 221188
  6.3 62.1 %all-to-all-start = ((bf16[32,96,384]{2,1,0:T(8,128)(2,1)}), bf16[32,96,384]{2,1,0:T(8,128)(2,1)S(1)}, u32[]{:S(2)}, u32[]{:S(2)}) async-start(bf16[32,96,384]{2,1,0:T(8,128)(2,1)} %get-tuple-element.39), calls=%async_computation | async-start | bytes 4718592 | tf_op jit(solution)/shard_map/all_to_all | solution.py:414
  13.6 3.8 %collective-permute-start = (bf16[96,384]{1,0:T(8,128)(2,1)S(1)}, bf16[96,384]{1,0:T(8,128)(2,1)S(1)}, u32[]{:S(2)}, u32[]{:S(2)}) collective-permute-start(bf16[96,384]{1,0:T(8,128)(2,1)S(1)} %copy-done.30), channel_id=1, source_target_pairs={{0,1},{1,0},{2,3},{3,2},{4,5},{5,4},{6,7},{7,6},{8,9},{9,8},{10,11... | collective-permute-start | bytes 221192 | tf_op jit(solution)/shard_map/ppermute | solution.py:428
  13.9 19.2 %collective-permute-start.1 = (bf16[96,384]{1,0:T(8,128)(2,1)S(1)}, bf16[96,384]{1,0:T(8,128)(2,1)S(1)}, u32[]{:S(2)}, u32[]{:S(2)}) collective-permute-start(bf16[96,384]{1,0:T(8,128)(2,1)S(1)} %copy-done.29), channel_id=1, source_target_pairs={{0,2},{1,3},{2,0},{3,1},{4,6},{5,7},{6,4},{7,5},{8,10},{9,11},{10,... | collective-permute-start | bytes 221192 | tf_op jit(solution)/shard_map/ppermute | solution.py:428
  15.6 18.4 %collective-permute-start.2 = (bf16[96,384]{1,0:T(8,128)(2,1)S(1)}, bf16[96,384]{1,0:T(8,128)(2,1)S(1)}, u32[]{:S(2)}, u32[]{:S(2)}) collective-permute-start(bf16[96,384]{1,0:T(8,128)(2,1)S(1)} %copy-done.28), channel_id=1, source_target_pairs={{0,3},{1,2},{2,1},{3,0},{4,7},{5,6},{6,5},{7,4},{8,11},{9,10},{10,... | collective-permute-start | bytes 221192 | tf_op jit(solution)/shard_map/ppermute | solution.py:428
  15.6 18.6 %collective-permute-start.3 = (bf16[96,384]{1,0:T(8,128)(2,1)S(1)}, bf16[96,384]{1,0:T(8,128)(2,1)S(1)}, u32[]{:S(2)}, u32[]{:S(2)}) collective-permute-start(bf16[96,384]{1,0:T(8,128)(2,1)S(1)} %copy-done.27), channel_id=1, source_target_pairs={{0,4},{1,5},{2,6},{3,7},{4,0},{5,1},{6,2},{7,3},{8,12},{9,13},{10,... | collective-permute-start | bytes 221192 | tf_op jit(solution)/shard_map/ppermute | solution.py:428
  17.3 19.2 %collective-permute-start.4 = (bf16[96,384]{1,0:T(8,128)(2,1)S(1)}, bf16[96,384]{1,0:T(8,128)(2,1)S(1)}, u32[]{:S(2)}, u32[]{:S(2)}) collective-permute-start(bf16[96,384]{1,0:T(8,128)(2,1)S(1)} %copy-done.26), channel_id=1, source_target_pairs={{0,5},{1,4},{2,7},{3,6},{4,1},{5,0},{6,3},{7,2},{8,13},{9,12},{10,... | collective-permute-start | bytes 221192 | tf_op jit(solution)/shard_map/ppermute | solution.py:428
  17.4 26.2 %collective-permute-start.5 = (bf16[96,384]{1,0:T(8,128)(2,1)S(1)}, bf16[96,384]{1,0:T(8,128)(2,1)S(1)}, u32[]{:S(2)}, u32[]{:S(2)}) collective-permute-start(bf16[96,384]{1,0:T(8,128)(2,1)S(1)} %copy-done.25), channel_id=1, source_target_pairs={{0,6},{1,7},{2,4},{3,5},{4,2},{5,3},{6,0},{7,1},{8,14},{9,15},{10,... | collective-permute-start | bytes 221192 | tf_op jit(solution)/shard_map/ppermute | solution.py:428
  33.1 11.3 %collective-permute-start.6 = (bf16[96,384]{1,0:T(8,128)(2,1)S(1)}, bf16[96,384]{1,0:T(8,128)(2,1)S(1)}, u32[]{:S(2)}, u32[]{:S(2)}) collective-permute-start(bf16[96,384]{1,0:T(8,128)(2,1)S(1)} %copy-done.24), channel_id=1, source_target_pairs={{0,7},{1,6},{2,5},{3,4},{4,3},{5,2},{6,1},{7,0},{8,15},{9,14},{10,... | collective-permute-start | bytes 221192 | tf_op jit(solution)/shard_map/ppermute | solution.py:428
  34.0 20.8 %collective-permute-start.7 = (bf16[96,384]{1,0:T(8,128)(2,1)S(1)}, bf16[96,384]{1,0:T(8,128)(2,1)S(1)}, u32[]{:S(2)}, u32[]{:S(2)}) collective-permute-start(bf16[96,384]{1,0:T(8,128)(2,1)S(1)} %copy-done.23), channel_id=1, source_target_pairs={{0,8},{1,9},{2,10},{3,11},{4,12},{5,13},{6,14},{7,15},{8,0},{9,1},... | collective-permute-start | bytes 221192 | tf_op jit(solution)/shard_map/ppermute | solution.py:428
  34.2 22.6 %collective-permute-start.8 = (bf16[96,384]{1,0:T(8,128)(2,1)S(1)}, bf16[96,384]{1,0:T(8,128)(2,1)S(1)}, u32[]{:S(2)}, u32[]{:S(2)}) collective-permute-start(bf16[96,384]{1,0:T(8,128)(2,1)S(1)} %copy-done.22), channel_id=1, source_target_pairs={{0,9},{1,8},{2,11},{3,10},{4,13},{5,12},{6,15},{7,14},{8,1},{9,0},... | collective-permute-start | bytes 221192 | tf_op jit(solution)/shard_map/ppermute | solution.py:428
  36.5 23.1 %collective-permute-start.9 = (bf16[96,384]{1,0:T(8,128)(2,1)S(1)}, bf16[96,384]{1,0:T(8,128)(2,1)S(1)}, u32[]{:S(2)}, u32[]{:S(2)}) collective-permute-start(bf16[96,384]{1,0:T(8,128)(2,1)S(1)} %copy-done.21), channel_id=1, source_target_pairs={{0,10},{1,11},{2,8},{3,9},{4,14},{5,15},{6,12},{7,13},{8,2},{9,3},... | collective-permute-start | bytes 221192 | tf_op jit(solution)/shard_map/ppermute | solution.py:428
  43.6 17.7 %collective-permute-start.10 = (bf16[96,384]{1,0:T(8,128)(2,1)}, bf16[96,384]{1,0:T(8,128)(2,1)S(1)}, u32[]{:S(2)}, u32[]{:S(2)}) collective-permute-start(bf16[96,384]{1,0:T(8,128)(2,1)} %get-tuple-element.51), channel_id=1, source_target_pairs={{0,11},{1,10},{2,9},{3,8},{4,15},{5,14},{6,13},{7,12},{8,3},{9,2},... | collective-permute-start | bytes 221192 | tf_op jit(solution)/shard_map/ppermute | solution.py:428
  44.4 16.9 %collective-permute-start.11 = (bf16[96,384]{1,0:T(8,128)(2,1)}, bf16[96,384]{1,0:T(8,128)(2,1)S(1)}, u32[]{:S(2)}, u32[]{:S(2)}) collective-permute-start(bf16[96,384]{1,0:T(8,128)(2,1)} %get-tuple-element.52), channel_id=1, source_target_pairs={{0,12},{1,13},{2,14},{3,15},{4,8},{5,9},{6,10},{7,11},{8,4},{9,5},... | collective-permute-start | bytes 221192 | tf_op jit(solution)/shard_map/ppermute | solution.py:428
  54.8 8.0 %collective-permute-start.12 = (bf16[96,384]{1,0:T(8,128)(2,1)}, bf16[96,384]{1,0:T(8,128)(2,1)S(1)}, u32[]{:S(2)}, u32[]{:S(2)}) collective-permute-start(bf16[96,384]{1,0:T(8,128)(2,1)} %get-tuple-element.53), channel_id=1, source_target_pairs={{0,13},{1,12},{2,15},{3,14},{4,9},{5,8},{6,11},{7,10},{8,5},{9,4},... | collective-permute-start | bytes 221192 | tf_op jit(solution)/shard_map/ppermute | solution.py:428
  56.8 8.9 %collective-permute-start.13 = (bf16[96,384]{1,0:T(8,128)(2,1)}, bf16[96,384]{1,0:T(8,128)(2,1)S(1)}, u32[]{:S(2)}, u32[]{:S(2)}) collective-permute-start(bf16[96,384]{1,0:T(8,128)(2,1)} %get-tuple-element.54), channel_id=1, source_target_pairs={{0,14},{1,15},{2,12},{3,13},{4,10},{5,11},{6,8},{7,9},{8,6},{9,7},... | collective-permute-start | bytes 221192 | tf_op jit(solution)/shard_map/ppermute | solution.py:428
  59.6 8.8 %collective-permute-start.14 = (bf16[96,384]{1,0:T(8,128)(2,1)}, bf16[96,384]{1,0:T(8,128)(2,1)S(1)}, u32[]{:S(2)}, u32[]{:S(2)}) collective-permute-start(bf16[96,384]{1,0:T(8,128)(2,1)} %get-tuple-element.55), channel_id=1, source_target_pairs={{0,15},{1,14},{2,13},{3,12},{4,11},{5,10},{6,9},{7,8},{8,7},{9,6},... | collective-permute-start | bytes 221192 | tf_op jit(solution)/shard_map/ppermute | solution.py:428
  71.1 4.6 %copy-start = (bf16[12,128,384]{2,1,0:T(8,128)(2,1)S(1)}, bf16[12,128,384]{2,1,0:T(8,128)(2,1)}, u32[]{:S(2)}) copy-start(bf16[12,128,384]{2,1,0:T(8,128)(2,1)} %get-tuple-element.56.x_t) | copy-start | bytes 3538948
  71.1 4.6 %copy-start.10 = (bf16[2,128,512]{2,1,0:T(8,128)(2,1)S(1)}, bf16[2,128,512]{2,1,0:T(8,128)(2,1)}, u32[]{:S(2)}) copy-start(bf16[2,128,512]{2,1,0:T(8,128)(2,1)} %w_ab.3) | copy-start | bytes 786436
  71.1 4.6 %copy-start.11 = (f32[2,16,128]{2,1,0:T(8,128)S(1)}, f32[2,16,128]{2,1,0:T(8,128)}, u32[]{:S(2)}) copy-start(f32[2,16,128]{2,1,0:T(8,128)} %get-tuple-element.58.row_marks) | copy-start | bytes 49156
  71.1 4.6 %copy-start.13 = (bf16[2,128,128]{2,1,0:T(8,128)(2,1)S(1)}, bf16[2,128,128]{2,1,0:T(8,128)(2,1)}, u32[]{:S(2)}) copy-start(bf16[2,128,128]{2,1,0:T(8,128)(2,1)} %w_gate.1) | copy-start | bytes 196612
  71.1 4.6 %copy-start.14 = (bf16[2,128,128]{2,1,0:T(8,128)(2,1)S(1)}, bf16[2,128,128]{2,1,0:T(8,128)(2,1)}, u32[]{:S(2)}) copy-start(bf16[2,128,128]{2,1,0:T(8,128)(2,1)} %w_out.1) | copy-start | bytes 196612
  71.1 4.6 %copy-start.15 = (f32[2,384]{1,0:T(2,128)S(1)}, f32[2,384]{1,0:T(2,128)}, u32[]{:S(2)}) copy-start(f32[2,384]{1,0:T(2,128)} %get-tuple-element.57.marks) | copy-start | bytes 9220
  71.1 4.6 %copy-start.16 = (f32[2,128]{1,0:T(2,128)S(1)}, f32[2,128]{1,0:T(2,128)}, u32[]{:S(2)}) copy-start(f32[2,128]{1,0:T(2,128)} %gain.3) | copy-start | bytes 3076
  71.1 4.6 %copy-start.17 = (f32[2,128]{1,0:T(2,128)S(1)}, f32[2,128]{1,0:T(2,128)}, u32[]{:S(2)}) copy-start(f32[2,128]{1,0:T(2,128)} %bias.3) | copy-start | bytes 3076
  71.1 4.6 %copy-start.18 = (f32[2,128]{1,0:T(2,128)S(1)}, f32[2,128]{1,0:T(2,128)}, u32[]{:S(2)}) copy-start(f32[2,128]{1,0:T(2,128)} %embed.3) | copy-start | bytes 3076
  71.1 4.6 %copy-start.19 = (f32[2,128]{1,0:T(2,128)S(1)}, f32[2,128]{1,0:T(2,128)}, u32[]{:S(2)}) copy-start(f32[2,128]{1,0:T(2,128)} %mid_gain.1) | copy-start | bytes 3076
  71.1 4.6 %copy-start.20 = (f32[2,128]{1,0:T(2,128)S(1)}, f32[2,128]{1,0:T(2,128)}, u32[]{:S(2)}) copy-start(f32[2,128]{1,0:T(2,128)} %mid_bias.1) | copy-start | bytes 3076
  71.2 22.3 %all-to-all-start.1 = ((bf16[16,96,384]{2,1,0:T(8,128)(2,1)}), bf16[16,96,384]{2,1,0:T(8,128)(2,1)S(1)}, u32[]{:S(2)}, u32[]{:S(2)}) async-start(bf16[16,96,384]{2,1,0:T(8,128)(2,1)} %shard_map.110), calls=%async_computation.1 | async-start | bytes 2359296 | tf_op jit(solution)/shard_map/all_to_all | solution.py:414
  77.7 1.4 copy-start.2
  93.4 1.7 copy-start.3
  98.9 1.4 copy-start.1
  100.3 1.0 copy-start.6
  101.3 59.6 %all-to-all-start.2 = ((bf16[32,96,384]{2,1,0:T(8,128)(2,1)}), bf16[32,96,384]{2,1,0:T(8,128)(2,1)S(1)}, u32[]{:S(2)}, u32[]{:S(2)}) async-start(bf16[32,96,384]{2,1,0:T(8,128)(2,1)} %copy-done.1), calls=%async_computation.2 | async-start | bytes 4718592 | tf_op jit(solution)/shard_map/all_to_all | solution.py:414
  106.3 1.3 copy-start.7
  109.1 1.5 copy-start.4
  160.9 35.8 %copy-start.9 = (bf16[12,128,384]{2,1,0:T(8,128)(2,1)S(1)}, bf16[12,128,384]{2,1,0:T(8,128)(2,1)}, u32[]{:S(2)}) copy-start(bf16[12,128,384]{2,1,0:T(8,128)(2,1)} %copy-done.8) | copy-start | bytes 3538948
  162.2 34.5 %copy-start.5 = (f32[12,128,384]{2,1,0:T(8,128)S(1)}, f32[12,128,384]{2,1,0:T(8,128)}, u32[]{:S(2)}) copy-start(f32[12,128,384]{2,1,0:T(8,128)} %copy-done.4) | copy-start | bytes 7077892
  (1 other events, 1.0 us)

commit v10 on v9

--- a/solution.py
+++ b/solution.py
@@ -13,7 +13,7 @@
 F32 = jnp.float32
 BF16 = jnp.bfloat16
 VMEM_LIMIT = 32 * 1024 * 1024
-PRODUCTS_VMEM_LIMIT = 48 * 1024 * 1024
+PRODUCTS_VMEM_LIMIT = 60 * 1024 * 1024
 FIRST_VMEM_LIMIT = 60 * 1024 * 1024
 GROUP = 4
 
@@ -425,12 +425,13 @@
         (), (residue_mask, chain_ids, pair, *norms, w_ab), 2 * pairs * C * 4 * HC, FIRST_VMEM_LIMIT,
     )
     recv = exchange(slabs)
-    own = [own[0]] + [lax.ppermute(own[o], "row", [(i, i ^ o) for i in range(devices)]) for o in range(1, half)]
     gate, weights, vectors = call(
         gate_kernel, [gate_t, turned, columns],
         [pltpu.VMEM((5, 2, C), F32), pltpu.VMEM((2, 2, C, C), BF16), w_wide, sems(8)],
         (x_t, marks, row_marks), (*norms, w_gate, w_ab, ln_mid_gain, ln_mid_bias, w_out), 2 * pairs * C * C,
     )
+    gate, weights, vectors, *own[5:] = lax.optimization_barrier((gate, weights, vectors, *own[5:]))
+    own = [own[0]] + [lax.ppermute(own[o], "row", [(i, i ^ o) for i in range(devices)]) for o in range(1, half)]
     products = call(
         functools.partial(first_products_kernel, rows), [own_back],
         [

time: 200 us -> 198 us (0.990)
  waiting for transfers between devices: 99 us -> 74 us
  blocking collectives: 34.5 us -> 56.7 us
  starting transfers between devices: 36.1 us -> 28 us
  local copies, waits for them, and re-layouts: 9.32 us -> 17 us
  Pallas kernels: 19.8 us -> 21.9 us
    all_to_all x1 -> x2, blocking collectives: 34.5 us -> 56.7 us  [exchange(): lax.all_to_all(slabs, 'row', split_axis=0, concat_axis=0, tiled=True, axi...]
    all_to_all x3 -> x2, waiting for transfers between devices: 63.6 us -> 46.6 us  [exchange(): lax.all_to_all(slabs, 'row', split_axis=0, concat_axis=0, tiled=True, axi...]
    ppermute x15, waiting for transfers between devices: 35.5 us -> 27.4 us  [local(): lax.ppermute(own[o], 'row', [(i, i ^ o) for i in range(devices)])]
    unnamed x62 -> x60, local copies, waits for them, and re-layouts: 9.32 us -> 17 us
    all_to_all x3 -> x2, starting transfers between devices: 16.8 us -> 10.9 us  [exchange(): lax.all_to_all(slabs, 'row', split_axis=0, concat_axis=0, tiled=True, axi...]
    ppermute x15, starting transfers between devices: 19.3 us -> 17.1 us  [local(): lax.ppermute(own[o], 'row', [(i, i ^ o) for i in range(devices)])]
    pallas_call x7, Pallas kernels: 19.8 us -> 21.9 us  [call(): pl.pallas_call(kernel, out_shape=outs, in_specs=[WHOLE] * len(arrays) + [...]
  transfers between devices with their start and end apart: 18 -> 17, of which waited for: 10 -> 9; matrix products, arithmetic and copies ran while one was open for 0% -> 0% of each run, Pallas kernels for 2% -> 2%
where the time goes in v10:
time: 198 us
  waiting for transfers between devices  74 us (37%)
  blocking collectives  56.7 us (29%)
  starting transfers between devices  28 us (14%)
  Pallas kernels  21.9 us (11%)
  local copies, waits for them, and re-layouts  17 us (9%)
    all_to_all x2, blocking collectives, exchange(): lax.all_to_all(slabs, 'row', split_axis=0, concat_axis=0, tiled=True, axi...  56.7 us
    all_to_all x2, waiting for transfers between devices, exchange(): lax.all_to_all(slabs, 'row', split_axis=0, concat_axis=0, tiled=True, axi...  46.6 us
    ppermute x15, waiting for transfers between devices, local(): lax.ppermute(own[o], 'row', [(i, i ^ o) for i in range(devices)])  27.4 us
    pallas_call x7, Pallas kernels, call(): pl.pallas_call(kernel, out_shape=outs, in_specs=[WHOLE] * len(arrays) + [...  21.9 us
    ppermute x15, starting transfers between devices, local(): lax.ppermute(own[o], 'row', [(i, i ^ o) for i in range(devices)])  17.1 us
    unnamed x60, local copies, waits for them, and re-layouts  17 us
    all_to_all x2, starting transfers between devices, exchange(): lax.all_to_all(slabs, 'row', split_axis=0, concat_axis=0, tiled=True, axi...  10.9 us
  transfers between devices with their start and end apart: 17, of which 9 were waited for; matrix products, arithmetic and copies ran while one was open for 0% of the time, Pallas kernels for 2%

profile of v10, /device:TPU:0, one launch (start us, length us, event | category | flops | bytes accessed | tf_op | source)
XLA Modules:
  0.0 197.6 jit_solution(18250809034864084364)
XLA Ops:
  0.0 6.1 %shard_map.109 = (bf16[96,384]{1,0:T(8,128)(2,1)}, bf16[96,384]{1,0:T(8,128)(2,1)}, bf16[96,384]{1,0:T(8,128)(2,1)}, bf16[96,384]{1,0:T(8,128)(2,1)}, bf16[96,38...) custom-call(s32[384]{0:T(512)} %residue_mask.1, ...), custom_call_target="tpu_custom_call" | custom-call | flops 603979776 | bytes 4738048 | tf_op jit(solution)/shard_map/pallas_call | solution.py:368
  6.2 7.4 %all-to-all-start = ((bf16[32,96,384]{2,1,0:T(8,128)(2,1)}), bf16[32,96,384]{2,1,0:T(8,128)(2,1)}, u32[]{:S(2)}, u32[]{:S(2)}) async-start(bf16[32,96,384]{2,1,0:T(8,128)(2,1)} %get-tuple-element.53), calls=%async_computation | async-start | bytes 4718592 | tf_op jit(solution)/shard_map/all_to_all | solution.py:414
  13.9 1.7 collective-permute-start.1
  15.6 1.7 collective-permute-start.3
  17.2 0.9 copy-done.14
  18.2 0.8 copy-done.18
  19.0 0.8 copy-done.19
  19.9 0.7 copy-done.22
  20.6 0.7 copy-done.25
  21.2 0.7 copy-done.26
  21.9 0.7 copy-done.27
  22.6 0.7 copy-done.28
  23.3 0.7 copy-done.29
  23.9 1.9 shard_map.110
  25.9 0.8 copy-done.4
  26.6 0.7 copy-done.11
  27.5 2.6 %collective-permute-start.5 = (bf16[96,384]{1,0:T(8,128)(2,1)}, bf16[96,384]{1,0:T(8,128)(2,1)}, u32[]{:S(2)}, u32[]{:S(2)}) collective-permute-start(bf16[96,384]{1,0:T(8,128)(2,1)} %get-tuple-element.77), channel_id=1, source_target_pairs={{0,6},{1,7},{2,4},{3,5},{4,2},{5,3},{6,0},{7,1},{8,14},{9,15},{10,... | collective-permute-start | bytes 221192 | tf_op jit(solution)/shard_map/ppermute | solution.py:434
  30.0 3.1 %collective-permute-done.1.refs_2_ = bf16[96,384]{1,0:T(8,128)(2,1)} collective-permute-done((bf16[96,384]{1,0:T(8,128)(2,1)}, bf16[96,384]{1,0:T(8,128)(2,1)}, u32[]{:S(2)}, u32[]{:S(2)}) %collective-permute-start.1) | collective-permute-done | bytes 73760 | tf_op jit(solution)/shard_map/ppermute | solution.py:434
  33.1 0.6 collective-permute-start.6
  34.2 2.3 %collective-permute-start.8 = (bf16[96,384]{1,0:T(8,128)(2,1)}, bf16[96,384]{1,0:T(8,128)(2,1)}, u32[]{:S(2)}, u32[]{:S(2)}) collective-permute-start(bf16[96,384]{1,0:T(8,128)(2,1)} %get-tuple-element.80), channel_id=1, source_target_pairs={{0,9},{1,8},{2,11},{3,10},{4,13},{5,12},{6,15},{7,14},{8,1},{9,0},... | collective-permute-start | bytes 221192 | tf_op jit(solution)/shard_map/ppermute | solution.py:434
  36.5 1.1 collective-permute-start.9
  37.7 6.0 %collective-permute-done.5.refs_6_ = bf16[96,384]{1,0:T(8,128)(2,1)} collective-permute-done((bf16[96,384]{1,0:T(8,128)(2,1)}, bf16[96,384]{1,0:T(8,128)(2,1)}, u32[]{:S(2)}, u32[]{:S(2)}) %collective-permute-start.5) | collective-permute-done | bytes 73760 | tf_op jit(solution)/shard_map/ppermute | solution.py:434
  43.7 0.8 collective-permute-done.6.refs_7_
  44.4 10.4 %collective-permute-done.7.refs_8_ = bf16[96,384]{1,0:T(8,128)(2,1)} collective-permute-done((bf16[96,384]{1,0:T(8,128)(2,1)}, bf16[96,384]{1,0:T(8,128)(2,1)}, u32[]{:S(2)}, u32[]{:S(2)}) %collective-permute-start.7) | collective-permute-done | bytes 73760 | tf_op jit(solution)/shard_map/ppermute | solution.py:434
  54.8 2.0 collective-permute-start.12
  56.8 2.8 %collective-permute-start.13 = (bf16[96,384]{1,0:T(8,128)(2,1)}, bf16[96,384]{1,0:T(8,128)(2,1)}, u32[]{:S(2)}, u32[]{:S(2)}) collective-permute-start(bf16[96,384]{1,0:T(8,128)(2,1)} %get-tuple-element.85), channel_id=1, source_target_pairs={{0,14},{1,15},{2,12},{3,13},{4,10},{5,11},{6,8},{7,9},{8,6},{9,7},... | collective-permute-start | bytes 221192 | tf_op jit(solution)/shard_map/ppermute | solution.py:434
  59.6 1.7 collective-permute-start.14
  61.3 1.4 collective-permute-done.12.refs_13_
  62.7 2.9 %collective-permute-done.13.refs_14_ = bf16[96,384]{1,0:T(8,128)(2,1)} collective-permute-done((bf16[96,384]{1,0:T(8,128)(2,1)}, bf16[96,384]{1,0:T(8,128)(2,1)}, u32[]{:S(2)}, u32[]{:S(2)}) %collective-permute-start.13) | collective-permute-done | bytes 73760 | tf_op jit(solution)/shard_map/ppermute | solution.py:434
  65.7 2.5 %collective-permute-done.14.refs_15_ = bf16[96,384]{1,0:T(8,128)(2,1)} collective-permute-done((bf16[96,384]{1,0:T(8,128)(2,1)}, bf16[96,384]{1,0:T(8,128)(2,1)}, u32[]{:S(2)}, u32[]{:S(2)}) %collective-permute-start.14) | collective-permute-done | bytes 73760 | tf_op jit(solution)/shard_map/ppermute | solution.py:434
  68.2 4.7 %shard_map.111 = bf16[16,96,384]{2,1,0:T(8,128)(2,1)} custom-call(bf16[32,96,384]{2,1,0:T(8,128)(2,1)} %all-to-all-done.recv, bf16[96,384]{1,0:T(8,128)(2,1)} %get-tuple-element.54.refs_0_, bf16[96,384]{1,0:T(8,128)(2,1)} %collective-permute-done.refs_1_, bf16[96,384]{1,0:T(8,128)(2,1)} %collective-permute-done.1.refs_2_, ...), custom_call_target="tpu_custom_call" | custom-call | flops 452984832 | bytes 4718592 | tf_op jit(solution)/shard_map/pallas_call | solution.py:368
  72.9 22.3 %all_to_all.20.recv = bf16[16,96,384]{2,1,0:T(8,128)(2,1)S(1)} all-to-all(bf16[16,96,384]{2,1,0:T(8,128)(2,1)} %shard_map.111), channel_id=1, replica_groups={{0,1,2,3,4,5,6,7,8,9,10,11,12,13,14,15},{16,17,18,19,20,21,22,23,24,25,..., dimensions={0} | all-to-all | bytes 2359296 | tf_op jit(solution)/shard_map/all_to_all | solution.py:414
  95.2 3.8 %shard_map.112 = (bf16[32,96,384]{2,1,0:T(8,128)(2,1)S(1)}, bf16[12,128,384]{2,1,0:T(8,128)(2,1)S(1)}) custom-call(bf16[16,96,384]{2,1,0:T(8,128)(2,1)S(1)} %all_to_all.20.recv, f32[12,128,384]{2,1,0:T(8,128)S(1)} %get-tuple-element.87.gate, bf16[12,128,384]{2,1,0:T(8,128)(2,1)S(1)} %copy-done, f32[2,384]{1,0:T(2,128)S(1)} %copy-done.23, ...), custom_call_target="tpu_custom_call" | custom-call | flops 754974720 | bytes 8965120 | tf_op jit(solution)/shard_map/pallas_call | solution.py:368
  99.0 1.4 copy-done.1
  100.4 1.0 copy-done.7
  101.4 3.5 %all-to-all-start.2 = ((bf16[32,96,384]{2,1,0:T(8,128)(2,1)}), bf16[32,96,384]{2,1,0:T(8,128)(2,1)S(1)}, u32[]{:S(2)}, u32[]{:S(2)}) async-start(bf16[32,96,384]{2,1,0:T(8,128)(2,1)} %copy-done.1), calls=%async_computation.2 | async-start | bytes 4718592 | tf_op jit(solution)/shard_map/all_to_all | solution.py:414
  105.0 1.0 copy-done.6
  106.0 0.9 copy-done.13
  106.9 0.7 copy-done.24
  107.6 1.5 shard_map.113
  109.1 1.4 copy-done.2
  110.6 1.0 copy-done.9
  111.6 0.7 copy-done.16
  112.2 0.6 copy-done.20
  112.8 46.5 %all-to-all-done.2.recv = bf16[32,96,384]{2,1,0:T(8,128)(2,1)S(1)} async-done(((bf16[32,96,384]{2,1,0:T(8,128)(2,1)}), bf16[32,96,384]{2,1,0:T(8,128)(2,1)S(1)}, u32[]{:S(2)}, u32[]{:S(2)}) %all-to-all-start.2) | async-done | bytes 2359328 | tf_op jit(solution)/shard_map/all_to_all | solution.py:414
  159.4 1.3 shard_map.114
  160.7 34.4 %all_to_all.21.recv = bf16[32,48,384]{2,1,0:T(8,128)(2,1)S(1)} all-to-all(bf16[32,48,384]{2,1,0:T(8,128)(2,1)S(1)} %shard_map.114), channel_id=1, replica_groups=mesh['grp'=1,'row'=32] {'row'}, dimensions={0} | all-to-all | bytes 2359296 | tf_op jit(solution)/shard_map/all_to_all | solution.py:414
  195.1 2.5 %shard_map.115 = bf16[12,384,128]{2,1,0:T(8,128)(2,1)} custom-call(bf16[32,48,384]{2,1,0:T(8,128)(2,1)S(1)} %all_to_all.21.recv, f32[12,128,384]{2,1,0:T(8,128)S(1)} %copy-done.3, bf16[12,128,384]{2,1,0:T(8,128)(2,1)S(1)} %copy-done.10, bf16[128,128]{1,0:T(8,128)(2,1)S(1)} %copy-done.21, f32[2,128,128]{2,1,0:T(8,128)S(1)} %copy-done.17), custom_call_target="tpu_custom_call" | custom-call | flops 150994944 | bytes 6062080 | tf_op jit(solution)/shard_map/pallas_call | solution.py:368
  (55 shorter events, 1.0 us)
Async XLA Ops:
  6.1 11.1 %copy-start = (bf16[12,128,384]{2,1,0:T(8,128)(2,1)S(1)}, bf16[12,128,384]{2,1,0:T(8,128)(2,1)}, u32[]{:S(2)}) copy-start(bf16[12,128,384]{2,1,0:T(8,128)(2,1)} %get-tuple-element.59.x_t) | copy-start | bytes 3538948
  6.2 11.1 %copy-start.15 = (f32[2,16,128]{2,1,0:T(8,128)S(1)}, f32[2,16,128]{2,1,0:T(8,128)}, u32[]{:S(2)}) copy-start(f32[2,16,128]{2,1,0:T(8,128)} %get-tuple-element.61.row_marks) | copy-start | bytes 49156
  6.2 62.1 %all-to-all-start = ((bf16[32,96,384]{2,1,0:T(8,128)(2,1)}), bf16[32,96,384]{2,1,0:T(8,128)(2,1)}, u32[]{:S(2)}, u32[]{:S(2)}) async-start(bf16[32,96,384]{2,1,0:T(8,128)(2,1)} %get-tuple-element.53), calls=%async_computation | async-start | bytes 4718592 | tf_op jit(solution)/shard_map/all_to_all | solution.py:414
  13.6 13.9 %collective-permute-start = (bf16[96,384]{1,0:T(8,128)(2,1)}, bf16[96,384]{1,0:T(8,128)(2,1)}, u32[]{:S(2)}, u32[]{:S(2)}) collective-permute-start(bf16[96,384]{1,0:T(8,128)(2,1)} %get-tuple-element.55), channel_id=1, source_target_pairs={{0,1},{1,0},{2,3},{3,2},{4,5},{5,4},{6,7},{7,6},{8,9},{9,8},{10,11... | collective-permute-start | bytes 221192 | tf_op jit(solution)/shard_map/ppermute | solution.py:434
  13.9 19.3 %collective-permute-start.1 = (bf16[96,384]{1,0:T(8,128)(2,1)}, bf16[96,384]{1,0:T(8,128)(2,1)}, u32[]{:S(2)}, u32[]{:S(2)}) collective-permute-start(bf16[96,384]{1,0:T(8,128)(2,1)} %get-tuple-element.56), channel_id=1, source_target_pairs={{0,2},{1,3},{2,0},{3,1},{4,6},{5,7},{6,4},{7,5},{8,10},{9,11},{10,... | collective-permute-start | bytes 221192 | tf_op jit(solution)/shard_map/ppermute | solution.py:434
  15.5 18.4 %collective-permute-start.2 = (bf16[96,384]{1,0:T(8,128)(2,1)}, bf16[96,384]{1,0:T(8,128)(2,1)}, u32[]{:S(2)}, u32[]{:S(2)}) collective-permute-start(bf16[96,384]{1,0:T(8,128)(2,1)} %get-tuple-element.57), channel_id=1, source_target_pairs={{0,3},{1,2},{2,1},{3,0},{4,7},{5,6},{6,5},{7,4},{8,11},{9,10},{10,... | collective-permute-start | bytes 221192 | tf_op jit(solution)/shard_map/ppermute | solution.py:434
  15.6 18.7 %collective-permute-start.3 = (bf16[96,384]{1,0:T(8,128)(2,1)}, bf16[96,384]{1,0:T(8,128)(2,1)}, u32[]{:S(2)}, u32[]{:S(2)}) collective-permute-start(bf16[96,384]{1,0:T(8,128)(2,1)} %get-tuple-element.58), channel_id=1, source_target_pairs={{0,4},{1,5},{2,6},{3,7},{4,0},{5,1},{6,2},{7,3},{8,12},{9,13},{10,... | collective-permute-start | bytes 221192 | tf_op jit(solution)/shard_map/ppermute | solution.py:434
  17.2 1.0 copy-start.14
  18.2 0.8 copy-start.18
  19.0 0.8 copy-start.19
  19.9 0.7 copy-start.22
  20.6 0.7 copy-start.25
  21.2 0.7 copy-start.26
  21.9 0.7 copy-start.27
  22.6 0.7 copy-start.28
  23.3 0.7 copy-start.29
  25.9 0.8 copy-start.4
  26.6 0.7 copy-start.11
  27.3 9.2 %collective-permute-start.4 = (bf16[96,384]{1,0:T(8,128)(2,1)}, bf16[96,384]{1,0:T(8,128)(2,1)}, u32[]{:S(2)}, u32[]{:S(2)}) collective-permute-start(bf16[96,384]{1,0:T(8,128)(2,1)} %get-tuple-element.76), channel_id=1, source_target_pairs={{0,5},{1,4},{2,7},{3,6},{4,1},{5,0},{6,3},{7,2},{8,13},{9,12},{10,... | collective-permute-start | bytes 221192 | tf_op jit(solution)/shard_map/ppermute | solution.py:434
  27.5 16.2 %collective-permute-start.5 = (bf16[96,384]{1,0:T(8,128)(2,1)}, bf16[96,384]{1,0:T(8,128)(2,1)}, u32[]{:S(2)}, u32[]{:S(2)}) collective-permute-start(bf16[96,384]{1,0:T(8,128)(2,1)} %get-tuple-element.77), channel_id=1, source_target_pairs={{0,6},{1,7},{2,4},{3,5},{4,2},{5,3},{6,0},{7,1},{8,14},{9,15},{10,... | collective-permute-start | bytes 221192 | tf_op jit(solution)/shard_map/ppermute | solution.py:434
  33.1 11.3 %collective-permute-start.6 = (bf16[96,384]{1,0:T(8,128)(2,1)}, bf16[96,384]{1,0:T(8,128)(2,1)}, u32[]{:S(2)}, u32[]{:S(2)}) collective-permute-start(bf16[96,384]{1,0:T(8,128)(2,1)} %get-tuple-element.78), channel_id=1, source_target_pairs={{0,7},{1,6},{2,5},{3,4},{4,3},{5,2},{6,1},{7,0},{8,15},{9,14},{10,... | collective-permute-start | bytes 221192 | tf_op jit(solution)/shard_map/ppermute | solution.py:434
  34.0 20.9 %collective-permute-start.7 = (bf16[96,384]{1,0:T(8,128)(2,1)}, bf16[96,384]{1,0:T(8,128)(2,1)}, u32[]{:S(2)}, u32[]{:S(2)}) collective-permute-start(bf16[96,384]{1,0:T(8,128)(2,1)} %get-tuple-element.79), channel_id=1, source_target_pairs={{0,8},{1,9},{2,10},{3,11},{4,12},{5,13},{6,14},{7,15},{8,0},{9,1},... | collective-permute-start | bytes 221192 | tf_op jit(solution)/shard_map/ppermute | solution.py:434
  34.2 22.6 %collective-permute-start.8 = (bf16[96,384]{1,0:T(8,128)(2,1)}, bf16[96,384]{1,0:T(8,128)(2,1)}, u32[]{:S(2)}, u32[]{:S(2)}) collective-permute-start(bf16[96,384]{1,0:T(8,128)(2,1)} %get-tuple-element.80), channel_id=1, source_target_pairs={{0,9},{1,8},{2,11},{3,10},{4,13},{5,12},{6,15},{7,14},{8,1},{9,0},... | collective-permute-start | bytes 221192 | tf_op jit(solution)/shard_map/ppermute | solution.py:434
  36.5 23.1 %collective-permute-start.9 = (bf16[96,384]{1,0:T(8,128)(2,1)}, bf16[96,384]{1,0:T(8,128)(2,1)}, u32[]{:S(2)}, u32[]{:S(2)}) collective-permute-start(bf16[96,384]{1,0:T(8,128)(2,1)} %get-tuple-element.81), channel_id=1, source_target_pairs={{0,10},{1,11},{2,8},{3,9},{4,14},{5,15},{6,12},{7,13},{8,2},{9,3},... | collective-permute-start | bytes 221192 | tf_op jit(solution)/shard_map/ppermute | solution.py:434
  43.6 17.7 %collective-permute-start.10 = (bf16[96,384]{1,0:T(8,128)(2,1)}, bf16[96,384]{1,0:T(8,128)(2,1)}, u32[]{:S(2)}, u32[]{:S(2)}) collective-permute-start(bf16[96,384]{1,0:T(8,128)(2,1)} %get-tuple-element.82), channel_id=1, source_target_pairs={{0,11},{1,10},{2,9},{3,8},{4,15},{5,14},{6,13},{7,12},{8,3},{9,2},... | collective-permute-start | bytes 221192 | tf_op jit(solution)/shard_map/ppermute | solution.py:434
  44.4 16.9 %collective-permute-start.11 = (bf16[96,384]{1,0:T(8,128)(2,1)}, bf16[96,384]{1,0:T(8,128)(2,1)}, u32[]{:S(2)}, u32[]{:S(2)}) collective-permute-start(bf16[96,384]{1,0:T(8,128)(2,1)} %get-tuple-element.83), channel_id=1, source_target_pairs={{0,12},{1,13},{2,14},{3,15},{4,8},{5,9},{6,10},{7,11},{8,4},{9,5},... | collective-permute-start | bytes 221192 | tf_op jit(solution)/shard_map/ppermute | solution.py:434
  54.8 7.9 %collective-permute-start.12 = (bf16[96,384]{1,0:T(8,128)(2,1)}, bf16[96,384]{1,0:T(8,128)(2,1)}, u32[]{:S(2)}, u32[]{:S(2)}) collective-permute-start(bf16[96,384]{1,0:T(8,128)(2,1)} %get-tuple-element.84), channel_id=1, source_target_pairs={{0,13},{1,12},{2,15},{3,14},{4,9},{5,8},{6,11},{7,10},{8,5},{9,4},... | collective-permute-start | bytes 221192 | tf_op jit(solution)/shard_map/ppermute | solution.py:434
  56.8 8.9 %collective-permute-start.13 = (bf16[96,384]{1,0:T(8,128)(2,1)}, bf16[96,384]{1,0:T(8,128)(2,1)}, u32[]{:S(2)}, u32[]{:S(2)}) collective-permute-start(bf16[96,384]{1,0:T(8,128)(2,1)} %get-tuple-element.85), channel_id=1, source_target_pairs={{0,14},{1,15},{2,12},{3,13},{4,10},{5,11},{6,8},{7,9},{8,6},{9,7},... | collective-permute-start | bytes 221192 | tf_op jit(solution)/shard_map/ppermute | solution.py:434
  59.6 8.6 %collective-permute-start.14 = (bf16[96,384]{1,0:T(8,128)(2,1)}, bf16[96,384]{1,0:T(8,128)(2,1)}, u32[]{:S(2)}, u32[]{:S(2)}) collective-permute-start(bf16[96,384]{1,0:T(8,128)(2,1)} %get-tuple-element.86), channel_id=1, source_target_pairs={{0,15},{1,14},{2,13},{3,12},{4,11},{5,10},{6,9},{7,8},{8,7},{9,6},... | collective-permute-start | bytes 221192 | tf_op jit(solution)/shard_map/ppermute | solution.py:434
  72.9 22.3 %copy-start.5 = (f32[7,128,128]{2,1,0:T(8,128)S(1)}, f32[7,128,128]{2,1,0:T(8,128)}, u32[]{:S(2)}) copy-start(f32[7,128,128]{2,1,0:T(8,128)} %copy-done.4) | copy-start | bytes 1376260
  72.9 22.3 %copy-start.12 = (bf16[896,128]{1,0:T(8,128)(2,1)S(1)}, bf16[896,128]{1,0:T(8,128)(2,1)}, u32[]{:S(2)}) copy-start(bf16[896,128]{1,0:T(8,128)(2,1)} %copy-done.11) | copy-start | bytes 688132
  72.9 22.3 %copy-start.23 = (f32[2,384]{1,0:T(2,128)S(1)}, f32[2,384]{1,0:T(2,128)}, u32[]{:S(2)}) copy-start(f32[2,384]{1,0:T(2,128)} %get-tuple-element.60.marks) | copy-start | bytes 9220
  99.0 1.4 copy-start.1
  100.4 1.0 copy-start.7
  101.4 3.5 %copy-start.8 = (bf16[12,128,384]{2,1,0:T(8,128)(2,1)S(1)}, bf16[12,128,384]{2,1,0:T(8,128)(2,1)}, u32[]{:S(2)}) copy-start(bf16[12,128,384]{2,1,0:T(8,128)(2,1)} %copy-done.7) | copy-start | bytes 3538948
  101.4 57.9 %all-to-all-start.2 = ((bf16[32,96,384]{2,1,0:T(8,128)(2,1)}), bf16[32,96,384]{2,1,0:T(8,128)(2,1)S(1)}, u32[]{:S(2)}, u32[]{:S(2)}) async-start(bf16[32,96,384]{2,1,0:T(8,128)(2,1)} %copy-done.1), calls=%async_computation.2 | async-start | bytes 4718592 | tf_op jit(solution)/shard_map/all_to_all | solution.py:414
  104.9 1.0 copy-start.6
  106.0 0.9 copy-start.13
  106.9 0.7 copy-start.24
  109.1 1.4 copy-start.2
  110.5 1.0 copy-start.9
  111.6 0.7 copy-start.16
  112.2 0.6 copy-start.20
  159.3 35.8 %copy-start.10 = (bf16[12,128,384]{2,1,0:T(8,128)(2,1)S(1)}, bf16[12,128,384]{2,1,0:T(8,128)(2,1)}, u32[]{:S(2)}) copy-start(bf16[12,128,384]{2,1,0:T(8,128)(2,1)} %copy-done.9) | copy-start | bytes 3538948
  159.4 35.8 %copy-start.17 = (f32[2,128,128]{2,1,0:T(8,128)S(1)}, f32[2,128,128]{2,1,0:T(8,128)}, u32[]{:S(2)}) copy-start(f32[2,128,128]{2,1,0:T(8,128)} %copy-done.16) | copy-start | bytes 393220
  159.4 35.8 %copy-start.21 = (bf16[128,128]{1,0:T(8,128)(2,1)S(1)}, bf16[128,128]{1,0:T(8,128)(2,1)}, u32[]{:S(2)}) copy-start(bf16[128,128]{1,0:T(8,128)(2,1)} %copy-done.20) | copy-start | bytes 98308
  160.7 34.4 %copy-start.3 = (f32[12,128,384]{2,1,0:T(8,128)S(1)}, f32[12,128,384]{2,1,0:T(8,128)}, u32[]{:S(2)}) copy-start(f32[12,128,384]{2,1,0:T(8,128)} %copy-done.2) | copy-start | bytes 7077892

commit v11 on v10

--- a/solution.py
+++ b/solution.py
@@ -15,7 +15,7 @@
 VMEM_LIMIT = 32 * 1024 * 1024
 PRODUCTS_VMEM_LIMIT = 60 * 1024 * 1024
 FIRST_VMEM_LIMIT = 60 * 1024 * 1024
-GROUP = 4
+GROUP = 6
 
 WHOLE = pl.BlockSpec(memory_space=pltpu.VMEM)
 ANYWHERE = pl.BlockSpec(memory_space=pl.ANY)

time: 198 us -> 198 us (level)
  no operation moved by 1% of the time
where the time goes in v11:
time: 198 us; the launch traced here: 197 us
  waiting for transfers between devices  74 us (37%)
  blocking collectives  56.7 us (29%)
  starting transfers between devices  28 us (14%)
  Pallas kernels  21.6 us (11%)
  local copies, waits for them, and re-layouts  17 us (9%)
    all_to_all x2, blocking collectives, exchange(): lax.all_to_all(slabs, 'row', split_axis=0, concat_axis=0, tiled=True, axi...  56.7 us
    all_to_all x2, waiting for transfers between devices, exchange(): lax.all_to_all(slabs, 'row', split_axis=0, concat_axis=0, tiled=True, axi...  46.6 us
    ppermute x15, waiting for transfers between devices, local(): lax.ppermute(own[o], 'row', [(i, i ^ o) for i in range(devices)])  27.4 us
    pallas_call x7, Pallas kernels, call(): pl.pallas_call(kernel, out_shape=outs, in_specs=[WHOLE] * len(arrays) + [...  21.6 us
    ppermute x15, starting transfers between devices, local(): lax.ppermute(own[o], 'row', [(i, i ^ o) for i in range(devices)])  17.1 us
    unnamed x60, local copies, waits for them, and re-layouts  17 us
    all_to_all x2, starting transfers between devices, exchange(): lax.all_to_all(slabs, 'row', split_axis=0, concat_axis=0, tiled=True, axi...  10.9 us
  transfers between devices with their start and end apart: 17, of which 9 were waited for; matrix products, arithmetic and copies ran while one was open for 0% of the time, Pallas kernels for 2%

profile of v11, /device:TPU:0, one launch (start us, length us, event | category | flops | bytes accessed | tf_op | source)
XLA Modules:
  0.0 197.4 jit_solution(13013056199951395154)
XLA Ops:
  0.0 6.0 %shard_map.109 = (bf16[96,384]{1,0:T(8,128)(2,1)}, bf16[96,384]{1,0:T(8,128)(2,1)}, bf16[96,384]{1,0:T(8,128)(2,1)}, bf16[96,384]{1,0:T(8,128)(2,1)}, bf16[96,38...) custom-call(s32[384]{0:T(512)} %residue_mask.1, ...), custom_call_target="tpu_custom_call" | custom-call | flops 603979776 | bytes 4738048 | tf_op jit(solution)/shard_map/pallas_call | solution.py:368
  6.0 7.4 %all-to-all-start = ((bf16[32,96,384]{2,1,0:T(8,128)(2,1)}), bf16[32,96,384]{2,1,0:T(8,128)(2,1)}, u32[]{:S(2)}, u32[]{:S(2)}) async-start(bf16[32,96,384]{2,1,0:T(8,128)(2,1)} %get-tuple-element.53), calls=%async_computation | async-start | bytes 4718592 | tf_op jit(solution)/shard_map/all_to_all | solution.py:414
  13.7 1.7 collective-permute-start.1
  15.4 1.7 collective-permute-start.3
  17.1 0.9 copy-done.14
  18.1 0.8 copy-done.18
  18.9 0.8 copy-done.19
  19.7 0.7 copy-done.22
  20.4 0.7 copy-done.25
  21.1 0.7 copy-done.26
  21.8 0.7 copy-done.27
  22.5 0.7 copy-done.28
  23.1 0.7 copy-done.29
  23.8 1.9 shard_map.110
  25.7 0.8 copy-done.4
  26.5 0.7 copy-done.11
  27.3 2.6 %collective-permute-start.5 = (bf16[96,384]{1,0:T(8,128)(2,1)}, bf16[96,384]{1,0:T(8,128)(2,1)}, u32[]{:S(2)}, u32[]{:S(2)}) collective-permute-start(bf16[96,384]{1,0:T(8,128)(2,1)} %get-tuple-element.77), channel_id=1, source_target_pairs={{0,6},{1,7},{2,4},{3,5},{4,2},{5,3},{6,0},{7,1},{8,14},{9,15},{10,... | collective-permute-start | bytes 221192 | tf_op jit(solution)/shard_map/ppermute | solution.py:434
  29.9 3.1 %collective-permute-done.1.refs_2_ = bf16[96,384]{1,0:T(8,128)(2,1)} collective-permute-done((bf16[96,384]{1,0:T(8,128)(2,1)}, bf16[96,384]{1,0:T(8,128)(2,1)}, u32[]{:S(2)}, u32[]{:S(2)}) %collective-permute-start.1) | collective-permute-done | bytes 73760 | tf_op jit(solution)/shard_map/ppermute | solution.py:434
  33.0 0.6 collective-permute-start.6
  34.1 2.3 %collective-permute-start.8 = (bf16[96,384]{1,0:T(8,128)(2,1)}, bf16[96,384]{1,0:T(8,128)(2,1)}, u32[]{:S(2)}, u32[]{:S(2)}) collective-permute-start(bf16[96,384]{1,0:T(8,128)(2,1)} %get-tuple-element.80), channel_id=1, source_target_pairs={{0,9},{1,8},{2,11},{3,10},{4,13},{5,12},{6,15},{7,14},{8,1},{9,0},... | collective-permute-start | bytes 221192 | tf_op jit(solution)/shard_map/ppermute | solution.py:434
  36.4 1.1 collective-permute-start.9
  37.5 6.0 %collective-permute-done.5.refs_6_ = bf16[96,384]{1,0:T(8,128)(2,1)} collective-permute-done((bf16[96,384]{1,0:T(8,128)(2,1)}, bf16[96,384]{1,0:T(8,128)(2,1)}, u32[]{:S(2)}, u32[]{:S(2)}) %collective-permute-start.5) | collective-permute-done | bytes 73760 | tf_op jit(solution)/shard_map/ppermute | solution.py:434
  43.5 0.8 collective-permute-done.6.refs_7_
  44.3 10.4 %collective-permute-done.7.refs_8_ = bf16[96,384]{1,0:T(8,128)(2,1)} collective-permute-done((bf16[96,384]{1,0:T(8,128)(2,1)}, bf16[96,384]{1,0:T(8,128)(2,1)}, u32[]{:S(2)}, u32[]{:S(2)}) %collective-permute-start.7) | collective-permute-done | bytes 73760 | tf_op jit(solution)/shard_map/ppermute | solution.py:434
  54.7 2.0 collective-permute-start.12
  56.7 2.8 %collective-permute-start.13 = (bf16[96,384]{1,0:T(8,128)(2,1)}, bf16[96,384]{1,0:T(8,128)(2,1)}, u32[]{:S(2)}, u32[]{:S(2)}) collective-permute-start(bf16[96,384]{1,0:T(8,128)(2,1)} %get-tuple-element.85), channel_id=1, source_target_pairs={{0,14},{1,15},{2,12},{3,13},{4,10},{5,11},{6,8},{7,9},{8,6},{9,7},... | collective-permute-start | bytes 221192 | tf_op jit(solution)/shard_map/ppermute | solution.py:434
  59.5 1.7 collective-permute-start.14
  61.2 1.4 collective-permute-done.12.refs_13_
  62.6 2.9 %collective-permute-done.13.refs_14_ = bf16[96,384]{1,0:T(8,128)(2,1)} collective-permute-done((bf16[96,384]{1,0:T(8,128)(2,1)}, bf16[96,384]{1,0:T(8,128)(2,1)}, u32[]{:S(2)}, u32[]{:S(2)}) %collective-permute-start.13) | collective-permute-done | bytes 73760 | tf_op jit(solution)/shard_map/ppermute | solution.py:434
  65.5 2.5 %collective-permute-done.14.refs_15_ = bf16[96,384]{1,0:T(8,128)(2,1)} collective-permute-done((bf16[96,384]{1,0:T(8,128)(2,1)}, bf16[96,384]{1,0:T(8,128)(2,1)}, u32[]{:S(2)}, u32[]{:S(2)}) %collective-permute-start.14) | collective-permute-done | bytes 73760 | tf_op jit(solution)/shard_map/ppermute | solution.py:434
  68.1 4.7 %shard_map.111 = bf16[16,96,384]{2,1,0:T(8,128)(2,1)} custom-call(bf16[32,96,384]{2,1,0:T(8,128)(2,1)} %all-to-all-done.recv, bf16[96,384]{1,0:T(8,128)(2,1)} %get-tuple-element.54.refs_0_, bf16[96,384]{1,0:T(8,128)(2,1)} %collective-permute-done.refs_1_, bf16[96,384]{1,0:T(8,128)(2,1)} %collective-permute-done.1.refs_2_, ...), custom_call_target="tpu_custom_call" | custom-call | flops 452984832 | bytes 4718592 | tf_op jit(solution)/shard_map/pallas_call | solution.py:368
  72.8 22.3 %all_to_all.20.recv = bf16[16,96,384]{2,1,0:T(8,128)(2,1)S(1)} all-to-all(bf16[16,96,384]{2,1,0:T(8,128)(2,1)} %shard_map.111), channel_id=1, replica_groups={{0,1,2,3,4,5,6,7,8,9,10,11,12,13,14,15},{16,17,18,19,20,21,22,23,24,25,..., dimensions={0} | all-to-all | bytes 2359296 | tf_op jit(solution)/shard_map/all_to_all | solution.py:414
  95.1 3.7 %shard_map.112 = (bf16[32,96,384]{2,1,0:T(8,128)(2,1)S(1)}, bf16[12,128,384]{2,1,0:T(8,128)(2,1)S(1)}) custom-call(bf16[16,96,384]{2,1,0:T(8,128)(2,1)S(1)} %all_to_all.20.recv, f32[12,128,384]{2,1,0:T(8,128)S(1)} %get-tuple-element.87.gate, bf16[12,128,384]{2,1,0:T(8,128)(2,1)S(1)} %copy-done, f32[2,384]{1,0:T(2,128)S(1)} %copy-done.23, ...), custom_call_target="tpu_custom_call" | custom-call | flops 754974720 | bytes 8965120 | tf_op jit(solution)/shard_map/pallas_call | solution.py:368
  98.8 1.4 copy-done.1
  100.2 1.0 copy-done.7
  101.2 3.5 %all-to-all-start.2 = ((bf16[32,96,384]{2,1,0:T(8,128)(2,1)}), bf16[32,96,384]{2,1,0:T(8,128)(2,1)S(1)}, u32[]{:S(2)}, u32[]{:S(2)}) async-start(bf16[32,96,384]{2,1,0:T(8,128)(2,1)} %copy-done.1), calls=%async_computation.2 | async-start | bytes 4718592 | tf_op jit(solution)/shard_map/all_to_all | solution.py:414
  104.7 1.0 copy-done.6
  105.7 0.9 copy-done.13
  106.7 0.7 copy-done.24
  107.4 1.5 shard_map.113
  108.9 1.4 copy-done.2
  110.3 1.0 copy-done.9
  111.3 0.7 copy-done.16
  112.0 0.6 copy-done.20
  112.6 46.5 %all-to-all-done.2.recv = bf16[32,96,384]{2,1,0:T(8,128)(2,1)S(1)} async-done(((bf16[32,96,384]{2,1,0:T(8,128)(2,1)}), bf16[32,96,384]{2,1,0:T(8,128)(2,1)S(1)}, u32[]{:S(2)}, u32[]{:S(2)}) %all-to-all-start.2) | async-done | bytes 2359328 | tf_op jit(solution)/shard_map/all_to_all | solution.py:414
  159.1 1.3 shard_map.114
  160.5 34.4 %all_to_all.21.recv = bf16[32,48,384]{2,1,0:T(8,128)(2,1)S(1)} all-to-all(bf16[32,48,384]{2,1,0:T(8,128)(2,1)S(1)} %shard_map.114), channel_id=1, replica_groups=mesh['grp'=1,'row'=32] {'row'}, dimensions={0} | all-to-all | bytes 2359296 | tf_op jit(solution)/shard_map/all_to_all | solution.py:414
  194.9 2.5 %shard_map.115 = bf16[12,384,128]{2,1,0:T(8,128)(2,1)} custom-call(bf16[32,48,384]{2,1,0:T(8,128)(2,1)S(1)} %all_to_all.21.recv, f32[12,128,384]{2,1,0:T(8,128)S(1)} %copy-done.3, bf16[12,128,384]{2,1,0:T(8,128)(2,1)S(1)} %copy-done.10, bf16[128,128]{1,0:T(8,128)(2,1)S(1)} %copy-done.21, f32[2,128,128]{2,1,0:T(8,128)S(1)} %copy-done.17), custom_call_target="tpu_custom_call" | custom-call | flops 150994944 | bytes 6062080 | tf_op jit(solution)/shard_map/pallas_call | solution.py:368
  (55 shorter events, 1.0 us)
Async XLA Ops:
  6.0 11.1 %copy-start = (bf16[12,128,384]{2,1,0:T(8,128)(2,1)S(1)}, bf16[12,128,384]{2,1,0:T(8,128)(2,1)}, u32[]{:S(2)}) copy-start(bf16[12,128,384]{2,1,0:T(8,128)(2,1)} %get-tuple-element.59.x_t) | copy-start | bytes 3538948
  6.0 11.1 %copy-start.15 = (f32[2,16,128]{2,1,0:T(8,128)S(1)}, f32[2,16,128]{2,1,0:T(8,128)}, u32[]{:S(2)}) copy-start(f32[2,16,128]{2,1,0:T(8,128)} %get-tuple-element.61.row_marks) | copy-start | bytes 49156
  6.0 62.1 %all-to-all-start = ((bf16[32,96,384]{2,1,0:T(8,128)(2,1)}), bf16[32,96,384]{2,1,0:T(8,128)(2,1)}, u32[]{:S(2)}, u32[]{:S(2)}) async-start(bf16[32,96,384]{2,1,0:T(8,128)(2,1)} %get-tuple-element.53), calls=%async_computation | async-start | bytes 4718592 | tf_op jit(solution)/shard_map/all_to_all | solution.py:414
  13.5 13.9 %collective-permute-start = (bf16[96,384]{1,0:T(8,128)(2,1)}, bf16[96,384]{1,0:T(8,128)(2,1)}, u32[]{:S(2)}, u32[]{:S(2)}) collective-permute-start(bf16[96,384]{1,0:T(8,128)(2,1)} %get-tuple-element.55), channel_id=1, source_target_pairs={{0,1},{1,0},{2,3},{3,2},{4,5},{5,4},{6,7},{7,6},{8,9},{9,8},{10,11... | collective-permute-start | bytes 221192 | tf_op jit(solution)/shard_map/ppermute | solution.py:434
  13.7 19.3 %collective-permute-start.1 = (bf16[96,384]{1,0:T(8,128)(2,1)}, bf16[96,384]{1,0:T(8,128)(2,1)}, u32[]{:S(2)}, u32[]{:S(2)}) collective-permute-start(bf16[96,384]{1,0:T(8,128)(2,1)} %get-tuple-element.56), channel_id=1, source_target_pairs={{0,2},{1,3},{2,0},{3,1},{4,6},{5,7},{6,4},{7,5},{8,10},{9,11},{10,... | collective-permute-start | bytes 221192 | tf_op jit(solution)/shard_map/ppermute | solution.py:434
  15.4 18.4 %collective-permute-start.2 = (bf16[96,384]{1,0:T(8,128)(2,1)}, bf16[96,384]{1,0:T(8,128)(2,1)}, u32[]{:S(2)}, u32[]{:S(2)}) collective-permute-start(bf16[96,384]{1,0:T(8,128)(2,1)} %get-tuple-element.57), channel_id=1, source_target_pairs={{0,3},{1,2},{2,1},{3,0},{4,7},{5,6},{6,5},{7,4},{8,11},{9,10},{10,... | collective-permute-start | bytes 221192 | tf_op jit(solution)/shard_map/ppermute | solution.py:434
  15.4 18.7 %collective-permute-start.3 = (bf16[96,384]{1,0:T(8,128)(2,1)}, bf16[96,384]{1,0:T(8,128)(2,1)}, u32[]{:S(2)}, u32[]{:S(2)}) collective-permute-start(bf16[96,384]{1,0:T(8,128)(2,1)} %get-tuple-element.58), channel_id=1, source_target_pairs={{0,4},{1,5},{2,6},{3,7},{4,0},{5,1},{6,2},{7,3},{8,12},{9,13},{10,... | collective-permute-start | bytes 221192 | tf_op jit(solution)/shard_map/ppermute | solution.py:434
  17.1 1.0 copy-start.14
  18.1 0.8 copy-start.18
  18.9 0.8 copy-start.19
  19.7 0.7 copy-start.22
  20.4 0.7 copy-start.25
  21.1 0.7 copy-start.26
  21.8 0.7 copy-start.27
  22.5 0.7 copy-start.28
  23.1 0.7 copy-start.29
  25.7 0.8 copy-start.4
  26.5 0.7 copy-start.11
  27.2 9.2 %collective-permute-start.4 = (bf16[96,384]{1,0:T(8,128)(2,1)}, bf16[96,384]{1,0:T(8,128)(2,1)}, u32[]{:S(2)}, u32[]{:S(2)}) collective-permute-start(bf16[96,384]{1,0:T(8,128)(2,1)} %get-tuple-element.76), channel_id=1, source_target_pairs={{0,5},{1,4},{2,7},{3,6},{4,1},{5,0},{6,3},{7,2},{8,13},{9,12},{10,... | collective-permute-start | bytes 221192 | tf_op jit(solution)/shard_map/ppermute | solution.py:434
  27.3 16.2 %collective-permute-start.5 = (bf16[96,384]{1,0:T(8,128)(2,1)}, bf16[96,384]{1,0:T(8,128)(2,1)}, u32[]{:S(2)}, u32[]{:S(2)}) collective-permute-start(bf16[96,384]{1,0:T(8,128)(2,1)} %get-tuple-element.77), channel_id=1, source_target_pairs={{0,6},{1,7},{2,4},{3,5},{4,2},{5,3},{6,0},{7,1},{8,14},{9,15},{10,... | collective-permute-start | bytes 221192 | tf_op jit(solution)/shard_map/ppermute | solution.py:434
  33.0 11.3 %collective-permute-start.6 = (bf16[96,384]{1,0:T(8,128)(2,1)}, bf16[96,384]{1,0:T(8,128)(2,1)}, u32[]{:S(2)}, u32[]{:S(2)}) collective-permute-start(bf16[96,384]{1,0:T(8,128)(2,1)} %get-tuple-element.78), channel_id=1, source_target_pairs={{0,7},{1,6},{2,5},{3,4},{4,3},{5,2},{6,1},{7,0},{8,15},{9,14},{10,... | collective-permute-start | bytes 221192 | tf_op jit(solution)/shard_map/ppermute | solution.py:434
  33.8 20.9 %collective-permute-start.7 = (bf16[96,384]{1,0:T(8,128)(2,1)}, bf16[96,384]{1,0:T(8,128)(2,1)}, u32[]{:S(2)}, u32[]{:S(2)}) collective-permute-start(bf16[96,384]{1,0:T(8,128)(2,1)} %get-tuple-element.79), channel_id=1, source_target_pairs={{0,8},{1,9},{2,10},{3,11},{4,12},{5,13},{6,14},{7,15},{8,0},{9,1},... | collective-permute-start | bytes 221192 | tf_op jit(solution)/shard_map/ppermute | solution.py:434
  34.1 22.6 %collective-permute-start.8 = (bf16[96,384]{1,0:T(8,128)(2,1)}, bf16[96,384]{1,0:T(8,128)(2,1)}, u32[]{:S(2)}, u32[]{:S(2)}) collective-permute-start(bf16[96,384]{1,0:T(8,128)(2,1)} %get-tuple-element.80), channel_id=1, source_target_pairs={{0,9},{1,8},{2,11},{3,10},{4,13},{5,12},{6,15},{7,14},{8,1},{9,0},... | collective-permute-start | bytes 221192 | tf_op jit(solution)/shard_map/ppermute | solution.py:434
  36.4 23.1 %collective-permute-start.9 = (bf16[96,384]{1,0:T(8,128)(2,1)}, bf16[96,384]{1,0:T(8,128)(2,1)}, u32[]{:S(2)}, u32[]{:S(2)}) collective-permute-start(bf16[96,384]{1,0:T(8,128)(2,1)} %get-tuple-element.81), channel_id=1, source_target_pairs={{0,10},{1,11},{2,8},{3,9},{4,14},{5,15},{6,12},{7,13},{8,2},{9,3},... | collective-permute-start | bytes 221192 | tf_op jit(solution)/shard_map/ppermute | solution.py:434
  43.5 17.7 %collective-permute-start.10 = (bf16[96,384]{1,0:T(8,128)(2,1)}, bf16[96,384]{1,0:T(8,128)(2,1)}, u32[]{:S(2)}, u32[]{:S(2)}) collective-permute-start(bf16[96,384]{1,0:T(8,128)(2,1)} %get-tuple-element.82), channel_id=1, source_target_pairs={{0,11},{1,10},{2,9},{3,8},{4,15},{5,14},{6,13},{7,12},{8,3},{9,2},... | collective-permute-start | bytes 221192 | tf_op jit(solution)/shard_map/ppermute | solution.py:434
  44.3 16.9 %collective-permute-start.11 = (bf16[96,384]{1,0:T(8,128)(2,1)}, bf16[96,384]{1,0:T(8,128)(2,1)}, u32[]{:S(2)}, u32[]{:S(2)}) collective-permute-start(bf16[96,384]{1,0:T(8,128)(2,1)} %get-tuple-element.83), channel_id=1, source_target_pairs={{0,12},{1,13},{2,14},{3,15},{4,8},{5,9},{6,10},{7,11},{8,4},{9,5},... | collective-permute-start | bytes 221192 | tf_op jit(solution)/shard_map/ppermute | solution.py:434
  54.7 7.9 %collective-permute-start.12 = (bf16[96,384]{1,0:T(8,128)(2,1)}, bf16[96,384]{1,0:T(8,128)(2,1)}, u32[]{:S(2)}, u32[]{:S(2)}) collective-permute-start(bf16[96,384]{1,0:T(8,128)(2,1)} %get-tuple-element.84), channel_id=1, source_target_pairs={{0,13},{1,12},{2,15},{3,14},{4,9},{5,8},{6,11},{7,10},{8,5},{9,4},... | collective-permute-start | bytes 221192 | tf_op jit(solution)/shard_map/ppermute | solution.py:434
  56.7 8.9 %collective-permute-start.13 = (bf16[96,384]{1,0:T(8,128)(2,1)}, bf16[96,384]{1,0:T(8,128)(2,1)}, u32[]{:S(2)}, u32[]{:S(2)}) collective-permute-start(bf16[96,384]{1,0:T(8,128)(2,1)} %get-tuple-element.85), channel_id=1, source_target_pairs={{0,14},{1,15},{2,12},{3,13},{4,10},{5,11},{6,8},{7,9},{8,6},{9,7},... | collective-permute-start | bytes 221192 | tf_op jit(solution)/shard_map/ppermute | solution.py:434
  59.5 8.6 %collective-permute-start.14 = (bf16[96,384]{1,0:T(8,128)(2,1)}, bf16[96,384]{1,0:T(8,128)(2,1)}, u32[]{:S(2)}, u32[]{:S(2)}) collective-permute-start(bf16[96,384]{1,0:T(8,128)(2,1)} %get-tuple-element.86), channel_id=1, source_target_pairs={{0,15},{1,14},{2,13},{3,12},{4,11},{5,10},{6,9},{7,8},{8,7},{9,6},... | collective-permute-start | bytes 221192 | tf_op jit(solution)/shard_map/ppermute | solution.py:434
  72.8 22.3 %copy-start.5 = (f32[7,128,128]{2,1,0:T(8,128)S(1)}, f32[7,128,128]{2,1,0:T(8,128)}, u32[]{:S(2)}) copy-start(f32[7,128,128]{2,1,0:T(8,128)} %copy-done.4) | copy-start | bytes 1376260
  72.8 22.3 %copy-start.12 = (bf16[896,128]{1,0:T(8,128)(2,1)S(1)}, bf16[896,128]{1,0:T(8,128)(2,1)}, u32[]{:S(2)}) copy-start(bf16[896,128]{1,0:T(8,128)(2,1)} %copy-done.11) | copy-start | bytes 688132
  72.8 22.3 %copy-start.23 = (f32[2,384]{1,0:T(2,128)S(1)}, f32[2,384]{1,0:T(2,128)}, u32[]{:S(2)}) copy-start(f32[2,384]{1,0:T(2,128)} %get-tuple-element.60.marks) | copy-start | bytes 9220
  98.8 1.4 copy-start.1
  100.2 1.0 copy-start.7
  101.2 3.5 %copy-start.8 = (bf16[12,128,384]{2,1,0:T(8,128)(2,1)S(1)}, bf16[12,128,384]{2,1,0:T(8,128)(2,1)}, u32[]{:S(2)}) copy-start(bf16[12,128,384]{2,1,0:T(8,128)(2,1)} %copy-done.7) | copy-start | bytes 3538948
  101.2 57.9 %all-to-all-start.2 = ((bf16[32,96,384]{2,1,0:T(8,128)(2,1)}), bf16[32,96,384]{2,1,0:T(8,128)(2,1)S(1)}, u32[]{:S(2)}, u32[]{:S(2)}) async-start(bf16[32,96,384]{2,1,0:T(8,128)(2,1)} %copy-done.1), calls=%async_computation.2 | async-start | bytes 4718592 | tf_op jit(solution)/shard_map/all_to_all | solution.py:414
  104.7 1.0 copy-start.6
  105.7 0.9 copy-start.13
  106.7 0.7 copy-start.24
  108.9 1.4 copy-start.2
  110.3 1.0 copy-start.9
  111.3 0.7 copy-start.16
  112.0 0.6 copy-start.20
  159.1 35.8 %copy-start.10 = (bf16[12,128,384]{2,1,0:T(8,128)(2,1)S(1)}, bf16[12,128,384]{2,1,0:T(8,128)(2,1)}, u32[]{:S(2)}) copy-start(bf16[12,128,384]{2,1,0:T(8,128)(2,1)} %copy-done.9) | copy-start | bytes 3538948
  159.1 35.8 %copy-start.17 = (f32[2,128,128]{2,1,0:T(8,128)S(1)}, f32[2,128,128]{2,1,0:T(8,128)}, u32[]{:S(2)}) copy-start(f32[2,128,128]{2,1,0:T(8,128)} %copy-done.16) | copy-start | bytes 393220
  159.1 35.8 %copy-start.21 = (bf16[128,128]{1,0:T(8,128)(2,1)S(1)}, bf16[128,128]{1,0:T(8,128)(2,1)}, u32[]{:S(2)}) copy-start(bf16[128,128]{1,0:T(8,128)(2,1)} %copy-done.20) | copy-start | bytes 98308
  160.5 34.4 %copy-start.3 = (f32[12,128,384]{2,1,0:T(8,128)S(1)}, f32[12,128,384]{2,1,0:T(8,128)}, u32[]{:S(2)}) copy-start(f32[12,128,384]{2,1,0:T(8,128)} %copy-done.2) | copy-start | bytes 7077892
